TPU v7x, 256 devices: a whole 4x4x8 slice. The times are simulated.
256 devices in a mesh: grp: 2 (over y_hi), row: 16 (over x, y_lo, core), col: 8 (over z).
Axes of the slice: x: 4, y: 4 (y_hi: 2, y_lo: 2; y = y_hi * 2 + y_lo), z: 8, core: 2. Of those that a mesh axis runs over, the one named last changes fastest.
Arguments:
- orbital_b: bfloat16 [4096, 12288], P(('grp', 'row'), 'col'), may hold values from -0.5 to 0.5
- gaps: float32 [4096], P(('grp', 'row')), may hold values from 0.5 to 20
- block_inverse: float32 [1024, 1024], replicated, may hold values from -0.1875 to 0.1875
Outputs:
- sigma: float32 [4096], P(('grp', 'row'))
- w_panel: float32 [8, 1536, 1024], P('col', ('grp', 'row'))
All inputs are finite; a program needn't handle non-finite values.
Results may differ from a plain program's by a relative error of at most 0.0028.
Values may be sent and summed in bfloat16 or wider, within the bound.
No kernel may reach another device: no remote copies, remote signals or barrier semaphores. Data moves between devices by JAX's collectives and lax.ppermute only.
A program may use at most 64 MiB of HBM per device.

v0:
```python
import jax
import jax.numpy as jnp
from jax import lax
from jax.sharding import PartitionSpec as P


def broadcast(value, axis, source):
    kept = jnp.where(lax.axis_index(axis) == source, value, 0).astype(value.dtype)
    return lax.psum(kept, axis)


def unit_rows(start, count, panel):
    rows = lax.iota(jnp.int32, count)[:, None] + start
    return (rows == lax.iota(jnp.int32, panel)[None, :]).astype(jnp.float32)


def body(orbital_b, gaps, block_inverse):
    width = orbital_b.shape[1]
    panel = block_inverse.shape[0]
    panel_b = broadcast(orbital_b[:, :panel], "col", 0)
    weight = 2.0 * gaps / (gaps * gaps + 1.0)
    weighted = (weight[:, None] * panel_b.astype(jnp.float32)).astype(jnp.bfloat16)
    partial_value = lax.dot_general(
        orbital_b, weighted, (((0,), (0,)), ((), ())), preferred_element_type=jnp.float32
    )
    offset = lax.axis_index("col") * width
    summed = lax.psum(partial_value, ("grp", "row"))
    screened_all = jnp.dot(
        unit_rows(offset, width, panel) + summed, block_inverse, precision=lax.Precision.HIGHEST
    )
    count = width // lax.axis_size(("grp", "row"))
    first = lax.axis_index(("grp", "row")) * count
    w_panel = lax.dynamic_slice_in_dim(screened_all, first, count, 0)
    screened_low = screened_all.astype(jnp.bfloat16)
    contracted = jnp.dot(orbital_b, screened_low, preferred_element_type=jnp.float32)
    local_sigma = -jnp.sum(contracted * panel_b.astype(jnp.float32), axis=1)
    sigma = lax.psum(local_sigma, "col")
    return (sigma, w_panel[None])


def solution(mesh):
    return jax.shard_map(
        body,
        mesh=mesh,
        in_specs=(P(("grp", "row"), "col"), P(("grp", "row")), P()),
        out_specs=(P(("grp", "row")), P("col", ("grp", "row"), None)),
        check_vma=False,
    )
```

profile of v0, /device:TPU:1, one launch (start us, length us, event | category | flops | bytes accessed | tf_op | source)
XLA Modules:
  0.0 263.0 jit_solution(14071542001386800117)
XLA Ops:
  7.2 0.0 all-reduce.3.cloned.1.call-start
  7.2 1.0 slice.3
  8.2 0.2 copy.6
  8.4 0.7 broadcast_select_fusion
  9.1 0.0 all-reduce.3.cloned.1.call-update
  9.1 0.0 all-reduce.5.cloned.1.call-start
  9.2 0.7 add_divide_fusion
  9.8 72.2 %all-reduce.3.cloned.1.call-done = bf16[128,1024]{0,1:T(8,128)(2,1)} async-done(((bf16[128,1024]{0,1:T(8,128)(2,1)}), bf16[128,1024]{0,1:T(8,128)(2,1)}) %all-reduce.3.cloned.1.call-update) | async-done | bytes 262160 | tf_op jit(solution)/shard_map/psum | solution.py:9
  82.0 4.8 %convolution_bitcast_fusion = f32[1536,1024]{1,0:T(8,128)} fusion(bf16[128,1536]{1,0:T(8,128)(2,1)} %param.3, bf16[128,1024]{0,1:T(8,128)(2,1)} %all-reduce.3.cloned.1.call-done, f32[128]{0:T(128)S(1)} %add_divide_fusion), kind=kOutput, calls=%fused_computation.4 | convolution fusion | flops 403046400 | bytes 6947328 | tf_op jit(solution)/shard_map/dot_general | solution.py:23
  86.8 0.0 all-reduce.5.cloned.1.call-update
  86.8 0.0 copy-start
  86.9 0.0 copy-start.1
  86.9 129.0 %all-reduce.5.cloned.1.call-done = f32[1536,1024]{1,0:T(8,128)} async-done(((f32[1536,1024]{1,0:T(8,128)}), f32[1536,1024]{1,0:T(8,128)}) %all-reduce.5.cloned.1.call-update) | async-done | bytes 6291472 | tf_op jit(solution)/shard_map/psum | solution.py:27
  215.9 24.3 %fusion = f32[1536,1024]{1,0:T(8,128)S(1)} fusion(f32[1024,1024]{1,0:T(8,128)} %param.5, f32[1536,1024]{1,0:T(8,128)} %all-reduce.5.cloned.1.call-done, s32[1536]{0:T(1024)S(1)} %iota_add_fusion), kind=kOutput, calls=%fused_computation | convolution fusion | flops 19332071424 | bytes 16783360 | tf_op jit(solution)/shard_map/dot_general | solution.py:28
  240.2 0.7 dynamic-slice_bitcast_fusion
  240.9 0.0 copy-done
  240.9 0.0 copy-done.1
  240.9 1.1 fusion.12
  242.0 14.2 %psum.23 = f32[128]{0:T(128)} all-reduce(f32[128]{0:T(128)S(1)} %neg.3), channel_id=1, replica_groups=mesh['grp'=2,'row'=16,'col'=8] {'col'}, use_global_device_ids=true, to_apply=%region_3.4 | all-reduce | flops 128 | bytes 1024 | tf_op jit(solution)/shard_map/psum | solution.py:37
  (2 shorter events, 0.0 us)
Async XLA Ops:
  7.2 74.9 %all-reduce.3.cloned.1.call-start = ((), (), s32[]{:S(2)}) async-start(), calls=%async_computation | async-start | bytes 524288 | tf_op jit(solution)/shard_map/psum | solution.py:9
  9.1 206.8 %all-reduce.5.cloned.1.call-start = ((), (), s32[]{:S(2)}) async-start(), calls=%async_computation.1 | async-start | bytes 12582912 | tf_op jit(solution)/shard_map/psum | solution.py:27
  86.8 154.1 %copy-start = (bf16[128,1536]{1,0:T(8,128)(2,1)S(1)}, bf16[128,1536]{1,0:T(8,128)(2,1)}, u32[]{:S(2)}) copy-start(bf16[128,1536]{1,0:T(8,128)(2,1)} %param.3) | copy-start | bytes 1179652
  86.9 154.1 %copy-start.1 = (bf16[128,1024]{0,1:T(8,128)(2,1)S(1)}, bf16[128,1024]{0,1:T(8,128)(2,1)}, u32[]{:S(2)}) copy-start(bf16[128,1024]{0,1:T(8,128)(2,1)} %all-reduce.3.cloned.1.call-done) | copy-start | bytes 786436
Sparse Core Ops, SparseCore 0:
  10.3 71.6 all-reduce.2
  86.9 128.8 all-reduce.4
where the time goes:
time: 267 us; the launch traced here: 263 us
  waiting for transfers between devices  201 us (75%)
  matrix products  30.2 us (11%)
  blocking collectives  14.2 us (5%)
  between operations  14.1 us (5%)
    psum x1, waiting for transfers between devices, body(): summed = lax.psum(partial_value, ('grp', 'row'))  129 us
    psum x1, waiting for transfers between devices, broadcast(): return lax.psum(kept, axis)  72.2 us
    dot_general x1, matrix products, body(): jnp.dot(unit_rows(offset, width, panel) + summed, block_inverse, precisio...  24.3 us
    psum x1, blocking collectives, body(): sigma = lax.psum(local_sigma, 'col')  14.2 us
  transfers between devices with their start and end apart: 2, of which 2 were waited for; matrix products, arithmetic and copies ran while one was open for 0% of the time, Pallas kernels for 0%

commit v1 on v0

v1 whole, which is shorter than its diff:
```python
import jax
import jax.numpy as jnp
from jax import lax
from jax.sharding import Mesh, PartitionSpec as P

X, Y, Z, CORE = "x", ("grp", "ylo"), "col", "core"
PLANE = ("grp", "x", "ylo", "core")


def shift(value, axis, size, step):
    return lax.ppermute(value, axis, [(i, (i + step) % size) for i in range(size)])


def spread(panel):
    z = lax.axis_index(Z)
    a = lax.ppermute(panel, Z, [(0, 3)])
    b = lax.ppermute(panel, Z, [(0, 5)])
    held = jnp.where(z == 3, a, jnp.where(z == 5, b, panel))
    a = lax.ppermute(held, Z, [(0, 1), (3, 4), (5, 6)])
    b = lax.ppermute(held, Z, [(0, 7), (3, 2)])
    up = (z == 1) | (z == 4) | (z == 6)
    down = (z == 7) | (z == 2)
    return jnp.where(up, a, jnp.where(down, b, held))


def body(orbital_b, gaps, block_inverse):
    own, width = orbital_b.shape
    panel = block_inverse.shape[0]
    nx, ny = lax.axis_size(X), lax.axis_size(Y)
    x, y, z, core = (lax.axis_index(a) for a in (X, Y, Z, CORE))
    count = width // lax.axis_size(PLANE)
    low, f32 = jnp.bfloat16, jnp.float32

    panels = [spread(orbital_b[:, :panel])]
    blocks = orbital_b.T.reshape(2, nx, -1, own)

    def rows_of(i):
        return lax.dynamic_index_in_dim(blocks, i, 1, False).reshape(-1, own)

    factors = jnp.concatenate(
        [rows_of(x)] + [shift(rows_of((x + k) % nx), X, nx, k) for k in range(1, nx)], axis=1
    )
    gap_list = [gaps] + [shift(gaps, X, nx, k) for k in range(1, nx)]
    half = own // 2
    right = shift(panels[0], X, nx, 1)
    left = shift(panels[0], X, nx, -1)
    far_a = shift(right[:half], X, nx, 1)
    far_b = shift(left[half:], X, nx, -1)
    panels += [right, jnp.concatenate([far_a, far_b], axis=0), left]
    panels = jnp.concatenate(panels, axis=0)
    gap_all = jnp.concatenate(gap_list)
    weight = 2.0 * gap_all / (gap_all * gap_all + 1.0)
    weighted = (weight[:, None] * panels.astype(f32)).astype(low)
    part = jnp.dot(factors, weighted, preferred_element_type=f32)

    part = part.reshape(ny, 2, count, panel)
    kept = lax.dynamic_index_in_dim(part, core, 1, False)
    sent = lax.dynamic_index_in_dim(part, 1 - core, 1, False)
    kept = kept + shift(sent, CORE, 2, 1)
    total = lax.dynamic_index_in_dim(kept, y, 0, False)
    for k in range(1, ny):
        piece = lax.dynamic_index_in_dim(kept, (y + k) % ny, 0, False).astype(low)
        total = total + shift(piece, Y, ny, k).astype(f32)
    first = z * width + lax.axis_index(PLANE) * count
    rows = lax.iota(jnp.int32, count)[:, None] + first
    unit = (rows == lax.iota(jnp.int32, panel)[None, :]).astype(f32)
    screened = jnp.dot(unit + total, block_inverse, precision=lax.Precision.HIGH)

    mine = screened.astype(low)
    gathered = jnp.stack([mine] + [shift(mine, Y, ny, k) for k in range(1, ny)])
    other = shift(gathered, CORE, 2, 1)
    both = jnp.concatenate([gathered, other], axis=0).reshape(-1, panel)
    by_y = factors.reshape(ny, 2, count, -1)
    ordered = jnp.stack(
        [
            lax.dynamic_slice(by_y, ((y - k) % ny, (core + c) % 2, 0, 0), (1, 1, count, nx * own))
            for c in range(2)
            for k in range(ny)
        ]
    ).reshape(-1, nx * own)
    products = lax.dot_general(both, panels, (((1,), (1,)), ((), ())), preferred_element_type=f32)
    local = -jnp.sum(products * ordered.astype(f32), axis=0).reshape(nx, own)
    by_x = jnp.stack([lax.dynamic_index_in_dim(local, (x - i) % nx, 0, False) for i in range(nx)])
    copies = jnp.broadcast_to(by_x[:, None], (nx, lax.axis_size(Z), own)).reshape(-1, own)
    terms = lax.all_to_all(copies, (X, Z), 0, 0, tiled=True)
    sigma = jnp.sum(terms, axis=0)
    return sigma, screened[None]


def solution(mesh):
    split = Mesh(mesh.devices.reshape(2, 4, 2, 2, 8), ("grp", "x", "ylo", "core", "col"))
    return jax.shard_map(
        body,
        mesh=split,
        in_specs=(P(PLANE, Z), P(PLANE), P()),
        out_specs=(P(PLANE), P(Z, PLANE, None)),
        check_vma=False,
    )
```

time: 267 us -> 92.8 us (0.35); the launches traced: 263 us -> 92.5 us
  waiting for transfers between devices: 201 us -> 23.3 us
  starting transfers between devices: 0.08 us -> 40.6 us
  matrix products: 30.2 us -> 3.59 us
  between operations: 14.1 us -> 1.27 us
  blocking collectives: 14.2 us -> 18.6 us
    psum x2 -> x0, waiting for transfers between devices: 201 us -> none  [the longest x1 129 us: body(): summed = lax.psum(partial_value, ('grp', 'row'))]
    ppermute x0 -> x22, starting transfers between devices: none -> 40.6 us  [the longest x18 28.1 us: shift(): lax.ppermute(value, axis, [(i, (i + step) % size) for i in range(size)])]
    dot_general x3, matrix products: 30.2 us -> 3.59 us  [the longest x1 2.29 us: body(): jnp.dot(unit + total, block_inverse, precision=lax.Precision.HIGH)]
    ppermute x0 -> x22, waiting for transfers between devices: none -> 23.3 us  [the longest x18 22.7 us: shift(): lax.ppermute(value, axis, [(i, (i + step) % size) for i in range(size)])]
    all_to_all x0 -> x1, blocking collectives: none -> 18.6 us  [body(): terms = lax.all_to_all(copies, (X, Z), 0, 0, tiled=True)]
    psum x1 -> x0, blocking collectives: 14.2 us -> none  [body(): sigma = lax.psum(local_sigma, 'col')]
  transfers between devices with their start and end apart: 2 -> 22, of which waited for: 2 -> 9; matrix products, arithmetic and copies ran while one was open for 0% -> 4% of each run, Pallas kernels for 0% -> 0%
where the time goes in v1:
time: 92.8 us; the launch traced here: 92.5 us
  starting transfers between devices  40.6 us (44%)
  waiting for transfers between devices  23.3 us (25%)
  blocking collectives  18.6 us (20%)
  matrix products  3.59 us (4%)
  local copies, waits for them, and re-layouts  3.29 us (4%)
  other arithmetic  1.9 us (2%)
  between operations  1.27 us (1%)
    ppermute x18, starting transfers between devices, shift(): lax.ppermute(value, axis, [(i, (i + step) % size) for i in range(size)])  28.1 us
    ppermute x18, waiting for transfers between devices, shift(): lax.ppermute(value, axis, [(i, (i + step) % size) for i in range(size)])  22.7 us
    all_to_all x1, blocking collectives, body(): terms = lax.all_to_all(copies, (X, Z), 0, 0, tiled=True)  18.6 us
    ppermute x1, starting transfers between devices, spread(): a = lax.ppermute(panel, Z, [(0, 3)])  7.09 us
    ppermute x1, starting transfers between devices, spread(): b = lax.ppermute(panel, Z, [(0, 5)])  2.8 us
    dot_general x1, matrix products, body(): jnp.dot(unit + total, block_inverse, precision=lax.Precision.HIGH)  2.29 us
    unnamed x19, local copies, waits for them, and re-layouts  2.07 us
  transfers between devices with their start and end apart: 22, of which 9 were waited for; matrix products, arithmetic and copies ran while one was open for 4% of the time, Pallas kernels for 0%

profile of v1, /device:TPU:1, one launch (start us, length us, event | category | flops | bytes accessed | tf_op | source)
XLA Modules:
  0.0 92.5 jit_solution(6040748692399922557)
XLA Ops:
  0.6 1.0 %slice.9 = bf16[128,1024]{1,0:T(8,128)(2,1)S(1)} slice(bf16[128,1536]{1,0:T(8,128)(2,1)} %param.3), slice={[0:128], [0:1024]} | slice | bytes 524288 | tf_op jit(solution)/shard_map/slice | solution.py:34
  1.6 7.1 %collective-permute-start.6 = (bf16[128,1024]{1,0:T(8,128)(2,1)S(1)}, bf16[128,1024]{1,0:T(8,128)(2,1)S(1)}, u32[]{:S(2)}, u32[]{:S(2)}) collective-permute-start(bf16[128,1024]{1,0:T(8,128)(2,1)S(1)} %slice.9), channel_id=1, source_target_pairs={{0,3},{8,11},{16,19},{24,27},{32,35},{40,43},{48,51},{56,59},{64,6... | collective-permute-start | bytes 786440 | tf_op jit(solution)/shard_map/ppermute | solution.py:16
  8.7 2.8 %collective-permute-start.7 = (bf16[128,1024]{1,0:T(8,128)(2,1)S(1)}, bf16[128,1024]{1,0:T(8,128)(2,1)S(1)}, u32[]{:S(2)}, u32[]{:S(2)}) collective-permute-start(bf16[128,1024]{1,0:T(8,128)(2,1)S(1)} %slice.9), channel_id=1, source_target_pairs={{0,5},{8,13},{16,21},{24,29},{32,37},{40,45},{48,53},{56,61},{64,6... | collective-permute-start | bytes 786440 | tf_op jit(solution)/shard_map/ppermute | solution.py:17
  11.5 1.3 %collective-permute-start.3 = (f32[128]{0:T(128)}, f32[128]{0:T(128)S(1)}, u32[]{:S(2)}, u32[]{:S(2)}) collective-permute-start(f32[128]{0:T(128)} %param.4), channel_id=1, source_target_pairs={{0,32},{32,64},{64,96},{96,0},{1,33},{33,65},{65,97},{97,1},{2,34}... | collective-permute-start | bytes 1544 | tf_op jit(solution)/shard_map/ppermute | solution.py:11
  12.8 2.5 %collective-permute-start.4 = (f32[128]{0:T(128)}, f32[128]{0:T(128)S(1)}, u32[]{:S(2)}, u32[]{:S(2)}) collective-permute-start(f32[128]{0:T(128)} %param.4), channel_id=1, source_target_pairs={{0,64},{32,96},{64,0},{96,32},{1,65},{33,97},{65,1},{97,33},{2,66}... | collective-permute-start | bytes 1544 | tf_op jit(solution)/shard_map/ppermute | solution.py:11
  15.2 1.2 %collective-permute-start.5 = (f32[128]{0:T(128)}, f32[128]{0:T(128)S(1)}, u32[]{:S(2)}, u32[]{:S(2)}) collective-permute-start(f32[128]{0:T(128)} %param.4), channel_id=1, source_target_pairs={{0,96},{32,0},{64,32},{96,64},{1,97},{33,1},{65,33},{97,65},{2,98}... | collective-permute-start | bytes 1544 | tf_op jit(solution)/shard_map/ppermute | solution.py:11
  16.4 0.0 collective-permute-done.6
  16.4 0.0 collective-permute-done.7
  16.4 1.0 %select_select_fusion.1 = bf16[128,1024]{1,0:T(8,128)(2,1)S(1)} fusion(bf16[128,1024]{1,0:T(8,128)(2,1)S(1)} %collective-permute-done.6, bf16[128,1024]{1,0:T(8,128)(2,1)S(1)} %collective-permute-done.7, pred[]{:T(512)S(6)} %eq.68, pred[]{:T(512)S(6)} %eq.67, bf16[128,1536]{1,0:T(8,128)(2,1)} %param.3), kind=kLoop, calls=%fused_computation.17 | loop fusion | flops 262144 | bytes 1048578 | tf_op jit(solution)/shard_map/jit(_where)/select_n | solution.py:18
  17.4 1.3 %collective-permute-start.8 = (bf16[128,1024]{1,0:T(8,128)(2,1)S(1)}, bf16[128,1024]{1,0:T(8,128)(2,1)S(1)}, u32[]{:S(2)}, u32[]{:S(2)}) collective-permute-start(bf16[128,1024]{1,0:T(8,128)(2,1)S(1)} %select_select_fusion.1), channel_id=1, source_target_pairs={{0,1},{3,4},{5,6},{8,9},{11,12},{13,14},{16,17},{19,20},{21,22},{2... | collective-permute-start | bytes 786440 | tf_op jit(solution)/shard_map/ppermute | solution.py:19
  18.8 1.3 %collective-permute-start.9 = (bf16[128,1024]{1,0:T(8,128)(2,1)S(1)}, bf16[128,1024]{1,0:T(8,128)(2,1)S(1)}, u32[]{:S(2)}, u32[]{:S(2)}) collective-permute-start(bf16[128,1024]{1,0:T(8,128)(2,1)S(1)} %select_select_fusion.1), channel_id=1, source_target_pairs={{0,7},{3,2},{8,15},{11,10},{16,23},{19,18},{24,31},{27,26},{32,39}... | collective-permute-start | bytes 786440 | tf_op jit(solution)/shard_map/ppermute | solution.py:20
  20.1 0.7 constant_dynamic-update-slice_fusion
  20.7 1.2 %copy.6 = bf16[128,1536]{0,1:T(8,128)(2,1)S(1)} copy(bf16[128,1536]{1,0:T(8,128)(2,1)} %param.3) | data formatting | bytes 786432 | tf_op args[0]
  22.3 0.5 collective-permute-done.8
  22.8 2.7 %collective-permute-start.2 = (bf16[384,128]{1,0:T(8,128)(2,1)S(1)}, bf16[384,128]{1,0:T(8,128)(2,1)S(1)}, u32[]{:S(2)}, u32[]{:S(2)}) collective-permute-start(bf16[384,128]{1,0:T(8,128)(2,1)S(1)} %bitcast.81), channel_id=1, source_target_pairs={{0,96},{32,0},{64,32},{96,64},{1,97},{33,1},{65,33},{97,65},{2,98}... | collective-permute-start | bytes 294920 | tf_op jit(solution)/shard_map/ppermute | solution.py:11
  25.5 1.6 %collective-permute-start.1 = (bf16[384,128]{1,0:T(8,128)(2,1)S(1)}, bf16[384,128]{1,0:T(8,128)(2,1)S(1)}, u32[]{:S(2)}, u32[]{:S(2)}) collective-permute-start(bf16[384,128]{1,0:T(8,128)(2,1)S(1)} %bitcast.79), channel_id=1, source_target_pairs={{0,64},{32,96},{64,0},{96,32},{1,65},{33,97},{65,1},{97,33},{2,66}... | collective-permute-start | bytes 294920 | tf_op jit(solution)/shard_map/ppermute | solution.py:11
  27.1 0.1 constant_dynamic-update-slice_fusion.5
  27.2 0.0 collective-permute-done.3
  27.3 0.4 collective-permute-start.10
  27.7 0.0 collective-permute-done.4
  27.7 0.8 collective-permute-start
  28.5 0.0 collective-permute-done.5
  28.5 2.0 %collective-permute-start.12 = (bf16[128,1024]{1,0:T(8,128)(2,1)S(1)}, bf16[128,1024]{1,0:T(8,128)(2,1)S(1)}, u32[]{:S(2)}, u32[]{:S(2)}) collective-permute-start(bf16[128,1024]{1,0:T(8,128)(2,1)S(1)} %get-tuple-element.5), channel_id=1, source_target_pairs={{0,96},{32,0},{64,32},{96,64},{1,97},{33,1},{65,33},{97,65},{2,98}... | collective-permute-start | bytes 786440 | tf_op jit(solution)/shard_map/ppermute | solution.py:11
  30.5 5.1 %collective-permute-done.10 = bf16[128,1024]{1,0:T(8,128)(2,1)S(1)} collective-permute-done((bf16[128,1024]{1,0:T(8,128)(2,1)S(1)}, bf16[128,1024]{1,0:T(8,128)(2,1)S(1)}, u32[]{:S(2)}, u32[]{:S(2)}) %collective-permute-start.10) | collective-permute-done | bytes 262176 | tf_op jit(solution)/shard_map/ppermute | solution.py:11
  35.7 0.1 collective-permute-start.11
  35.8 2.7 %collective-permute-start.13 = (bf16[64,1024]{1,0:T(8,128)(2,1)S(1)}, bf16[64,1024]{1,0:T(8,128)(2,1)S(1)}, u32[]{:S(2)}, u32[]{:S(2)}) collective-permute-start(bf16[64,1024]{1,0:T(8,128)(2,1)S(1)} %slice.13), channel_id=1, source_target_pairs={{0,96},{32,0},{64,32},{96,64},{1,97},{33,1},{65,33},{97,65},{2,98}... | collective-permute-start | bytes 393224 | tf_op jit(solution)/shard_map/ppermute | solution.py:11
  38.5 2.6 %collective-permute-done.11 = bf16[64,1024]{1,0:T(8,128)(2,1)S(1)} collective-permute-done((bf16[64,1024]{1,0:T(8,128)(2,1)S(1)}, bf16[64,1024]{1,0:T(8,128)(2,1)S(1)}, u32[]{:S(2)}, u32[]{:S(2)}) %collective-permute-start.11) | collective-permute-done | bytes 131104 | tf_op jit(solution)/shard_map/ppermute | solution.py:11
  41.2 0.7 fusion.1
  41.9 0.1 dynamic-slice_bitcast_fusion
  42.0 4.6 %collective-permute-start.14 = (f32[4,48,1024]{2,1,0:T(8,128)S(1)}, f32[4,48,1024]{2,1,0:T(8,128)S(1)}, u32[]{:S(2)}, u32[]{:S(2)}) collective-permute-start(f32[4,48,1024]{2,1,0:T(8,128)S(1)} %dynamic-slice_bitcast_fusion), channel_id=1, source_target_pairs={{0,8},{8,0},{1,9},{9,1},{2,10},{10,2},{3,11},{11,3},{4,12},{12,4},... | collective-permute-start | bytes 2359304 | tf_op jit(solution)/shard_map/ppermute | solution.py:11
  46.8 1.7 %collective-permute-done.14 = f32[4,48,1024]{2,1,0:T(8,128)S(1)} collective-permute-done((f32[4,48,1024]{2,1,0:T(8,128)S(1)}, f32[4,48,1024]{2,1,0:T(8,128)S(1)}, u32[]{:S(2)}, u32[]{:S(2)}) %collective-permute-start.14) | collective-permute-done | bytes 786464 | tf_op jit(solution)/shard_map/ppermute | solution.py:11
  48.5 0.1 bitcast_add_fusion
  48.7 2.8 %collective-permute-start.17 = (bf16[48,1024]{1,0:T(8,128)(2,1)S(1)}, bf16[48,1024]{1,0:T(8,128)(2,1)S(1)}, u32[]{:S(2)}, u32[]{:S(2)}) collective-permute-start(bf16[48,1024]{1,0:T(8,128)(2,1)S(1)} %get-tuple-element.7), channel_id=1, source_target_pairs={{0,144},{16,0},{128,16},{144,128},{1,145},{17,1},{129,17},{145,129... | collective-permute-start | bytes 294920 | tf_op jit(solution)/shard_map/ppermute | solution.py:11
  51.5 0.3 collective-permute-start.16
  51.8 0.7 collective-permute-start.15
  52.5 2.7 %collective-permute-done.17 = bf16[48,1024]{1,0:T(8,128)(2,1)S(1)} collective-permute-done((bf16[48,1024]{1,0:T(8,128)(2,1)S(1)}, bf16[48,1024]{1,0:T(8,128)(2,1)S(1)}, u32[]{:S(2)}, u32[]{:S(2)}) %collective-permute-start.17) | collective-permute-done | bytes 98336 | tf_op jit(solution)/shard_map/ppermute | solution.py:11
  55.3 1.3 %collective-permute-done.16 = bf16[48,1024]{1,0:T(8,128)(2,1)S(1)} collective-permute-done((bf16[48,1024]{1,0:T(8,128)(2,1)S(1)}, bf16[48,1024]{1,0:T(8,128)(2,1)S(1)}, u32[]{:S(2)}, u32[]{:S(2)}) %collective-permute-start.16) | collective-permute-done | bytes 98336 | tf_op jit(solution)/shard_map/ppermute | solution.py:11
  56.5 3.1 %collective-permute-done.15 = bf16[48,1024]{1,0:T(8,128)(2,1)S(1)} collective-permute-done((bf16[48,1024]{1,0:T(8,128)(2,1)S(1)}, bf16[48,1024]{1,0:T(8,128)(2,1)S(1)}, u32[]{:S(2)}, u32[]{:S(2)}) %collective-permute-start.15) | collective-permute-done | bytes 98336 | tf_op jit(solution)/shard_map/ppermute | solution.py:11
  59.7 2.3 %constant_dynamic-update-slice_fusion.10 = (bf16[8,48,1024]{2,1,0:T(8,128)(2,1)S(1)}, bf16[48,1024]{1,0:T(8,128)(2,1)S(1)}, f32[48,1024]{1,0:T(8,128)}) fusion(f32[1024,1024]{1,0:T(8,128)S(1)} %copy-done, bf16[48,1024]{1,0:T(8,128)(2,1)S(1)} %collective-permute-done.17, bf16[48,1024]{1,0:T(8,128)(2,1)S(1)} %collective-permute-done.16, ...), kind=kOutput, calls=%fused_computation.54 | convolution fusion | flops 302481408 | bytes 5079556 | tf_op jit(solution)/shard_map/dot_general | solution.py:67
  62.0 0.6 collective-permute-start.19
  62.5 2.1 %collective-permute-start.20 = (bf16[48,1024]{1,0:T(8,128)(2,1)S(1)}, bf16[48,1024]{1,0:T(8,128)(2,1)S(1)}, u32[]{:S(2)}, u32[]{:S(2)}) collective-permute-start(bf16[48,1024]{1,0:T(8,128)(2,1)S(1)} %get-tuple-element.3), channel_id=1, source_target_pairs={{0,144},{16,0},{128,16},{144,128},{1,145},{17,1},{129,17},{145,129... | collective-permute-start | bytes 294920 | tf_op jit(solution)/shard_map/ppermute | solution.py:11
  64.6 4.8 %collective-permute-done.18 = bf16[48,1024]{1,0:T(8,128)(2,1)S(1)} collective-permute-done((bf16[48,1024]{1,0:T(8,128)(2,1)S(1)}, bf16[48,1024]{1,0:T(8,128)(2,1)S(1)}, u32[]{:S(2)}, u32[]{:S(2)}) %collective-permute-start.18) | collective-permute-done | bytes 98336 | tf_op jit(solution)/shard_map/ppermute | solution.py:11
  69.4 0.1 pad_maximum_fusion
  69.5 1.8 %collective-permute-start.21 = (bf16[4,48,1024]{2,1,0:T(8,128)(2,1)S(1)}, bf16[4,48,1024]{2,1,0:T(8,128)(2,1)S(1)}, u32[]{:S(2)}, u32[]{:S(2)}) collective-permute-start(bf16[4,48,1024]{2,1,0:T(8,128)(2,1)S(1)} %pad_maximum_fusion), channel_id=1, source_target_pairs={{0,8},{8,0},{1,9},{9,1},{2,10},{10,2},{3,11},{11,3},{4,12},{12,4},... | collective-permute-start | bytes 1179656 | tf_op jit(solution)/shard_map/ppermute | solution.py:11
  71.3 1.3 %collective-permute-done.21 = bf16[4,48,1024]{2,1,0:T(8,128)(2,1)S(1)} collective-permute-done((bf16[4,48,1024]{2,1,0:T(8,128)(2,1)S(1)}, bf16[4,48,1024]{2,1,0:T(8,128)(2,1)S(1)}, u32[]{:S(2)}, u32[]{:S(2)}) %collective-permute-start.21) | collective-permute-done | bytes 393248 | tf_op jit(solution)/shard_map/ppermute | solution.py:11
  72.6 0.6 fusion
  73.3 18.6 %all_to_all.9 = f32[32,1,128]{2,1,0:T(1,128)S(1)} all-to-all(f32[32,1,128]{2,1,0:T(1,128)S(1)} %bitcast.83), channel_id=1, replica_groups=mesh['grp'=2,'x'=4,'ylo'=2,'core'=2,'col'=8] {'x','col'}, dimensions={0} | all-to-all | bytes 32768 | tf_op jit(solution)/shard_map/all_to_all | solution.py:85
  91.9 0.6 reduce_sum.19
  (42 shorter events, 0.5 us)
Async XLA Ops:
  1.6 14.8 %collective-permute-start.6 = (bf16[128,1024]{1,0:T(8,128)(2,1)S(1)}, bf16[128,1024]{1,0:T(8,128)(2,1)S(1)}, u32[]{:S(2)}, u32[]{:S(2)}) collective-permute-start(bf16[128,1024]{1,0:T(8,128)(2,1)S(1)} %slice.9), channel_id=1, source_target_pairs={{0,3},{8,11},{16,19},{24,27},{32,35},{40,43},{48,51},{56,59},{64,6... | collective-permute-start | bytes 786440 | tf_op jit(solution)/shard_map/ppermute | solution.py:16
  8.7 7.7 %collective-permute-start.7 = (bf16[128,1024]{1,0:T(8,128)(2,1)S(1)}, bf16[128,1024]{1,0:T(8,128)(2,1)S(1)}, u32[]{:S(2)}, u32[]{:S(2)}) collective-permute-start(bf16[128,1024]{1,0:T(8,128)(2,1)S(1)} %slice.9), channel_id=1, source_target_pairs={{0,5},{8,13},{16,21},{24,29},{32,37},{40,45},{48,53},{56,61},{64,6... | collective-permute-start | bytes 786440 | tf_op jit(solution)/shard_map/ppermute | solution.py:17
  11.5 15.7 %collective-permute-start.3 = (f32[128]{0:T(128)}, f32[128]{0:T(128)S(1)}, u32[]{:S(2)}, u32[]{:S(2)}) collective-permute-start(f32[128]{0:T(128)} %param.4), channel_id=1, source_target_pairs={{0,32},{32,64},{64,96},{96,0},{1,33},{33,65},{65,97},{97,1},{2,34}... | collective-permute-start | bytes 1544 | tf_op jit(solution)/shard_map/ppermute | solution.py:11
  12.8 14.9 %collective-permute-start.4 = (f32[128]{0:T(128)}, f32[128]{0:T(128)S(1)}, u32[]{:S(2)}, u32[]{:S(2)}) collective-permute-start(f32[128]{0:T(128)} %param.4), channel_id=1, source_target_pairs={{0,64},{32,96},{64,0},{96,32},{1,65},{33,97},{65,1},{97,33},{2,66}... | collective-permute-start | bytes 1544 | tf_op jit(solution)/shard_map/ppermute | solution.py:11
  15.2 13.3 %collective-permute-start.5 = (f32[128]{0:T(128)}, f32[128]{0:T(128)S(1)}, u32[]{:S(2)}, u32[]{:S(2)}) collective-permute-start(f32[128]{0:T(128)} %param.4), channel_id=1, source_target_pairs={{0,96},{32,0},{64,32},{96,64},{1,97},{33,1},{65,33},{97,65},{2,98}... | collective-permute-start | bytes 1544 | tf_op jit(solution)/shard_map/ppermute | solution.py:11
  17.4 5.4 %collective-permute-start.8 = (bf16[128,1024]{1,0:T(8,128)(2,1)S(1)}, bf16[128,1024]{1,0:T(8,128)(2,1)S(1)}, u32[]{:S(2)}, u32[]{:S(2)}) collective-permute-start(bf16[128,1024]{1,0:T(8,128)(2,1)S(1)} %select_select_fusion.1), channel_id=1, source_target_pairs={{0,1},{3,4},{5,6},{8,9},{11,12},{13,14},{16,17},{19,20},{21,22},{2... | collective-permute-start | bytes 786440 | tf_op jit(solution)/shard_map/ppermute | solution.py:19
  18.8 6.8 %collective-permute-start.9 = (bf16[128,1024]{1,0:T(8,128)(2,1)S(1)}, bf16[128,1024]{1,0:T(8,128)(2,1)S(1)}, u32[]{:S(2)}, u32[]{:S(2)}) collective-permute-start(bf16[128,1024]{1,0:T(8,128)(2,1)S(1)} %select_select_fusion.1), channel_id=1, source_target_pairs={{0,7},{3,2},{8,15},{11,10},{16,23},{19,18},{24,31},{27,26},{32,39}... | collective-permute-start | bytes 786440 | tf_op jit(solution)/shard_map/ppermute | solution.py:20
  22.8 18.4 %collective-permute-start.2 = (bf16[384,128]{1,0:T(8,128)(2,1)S(1)}, bf16[384,128]{1,0:T(8,128)(2,1)S(1)}, u32[]{:S(2)}, u32[]{:S(2)}) collective-permute-start(bf16[384,128]{1,0:T(8,128)(2,1)S(1)} %bitcast.81), channel_id=1, source_target_pairs={{0,96},{32,0},{64,32},{96,64},{1,97},{33,1},{65,33},{97,65},{2,98}... | collective-permute-start | bytes 294920 | tf_op jit(solution)/shard_map/ppermute | solution.py:11
  25.5 15.7 %collective-permute-start.1 = (bf16[384,128]{1,0:T(8,128)(2,1)S(1)}, bf16[384,128]{1,0:T(8,128)(2,1)S(1)}, u32[]{:S(2)}, u32[]{:S(2)}) collective-permute-start(bf16[384,128]{1,0:T(8,128)(2,1)S(1)} %bitcast.79), channel_id=1, source_target_pairs={{0,64},{32,96},{64,0},{96,32},{1,65},{33,97},{65,1},{97,33},{2,66}... | collective-permute-start | bytes 294920 | tf_op jit(solution)/shard_map/ppermute | solution.py:11
  27.3 8.4 %collective-permute-start.10 = (bf16[128,1024]{1,0:T(8,128)(2,1)S(1)}, bf16[128,1024]{1,0:T(8,128)(2,1)S(1)}, u32[]{:S(2)}, u32[]{:S(2)}) collective-permute-start(bf16[128,1024]{1,0:T(8,128)(2,1)S(1)} %get-tuple-element.5), channel_id=1, source_target_pairs={{0,32},{32,64},{64,96},{96,0},{1,33},{33,65},{65,97},{97,1},{2,34}... | collective-permute-start | bytes 786440 | tf_op jit(solution)/shard_map/ppermute | solution.py:11
  27.7 13.6 %collective-permute-start = (bf16[384,128]{1,0:T(8,128)(2,1)S(1)}, bf16[384,128]{1,0:T(8,128)(2,1)S(1)}, u32[]{:S(2)}, u32[]{:S(2)}) collective-permute-start(bf16[384,128]{1,0:T(8,128)(2,1)S(1)} %bitcast.78), channel_id=1, source_target_pairs={{0,32},{32,64},{64,96},{96,0},{1,33},{33,65},{65,97},{97,1},{2,34}... | collective-permute-start | bytes 294920 | tf_op jit(solution)/shard_map/ppermute | solution.py:11
  28.5 7.3 %collective-permute-start.12 = (bf16[128,1024]{1,0:T(8,128)(2,1)S(1)}, bf16[128,1024]{1,0:T(8,128)(2,1)S(1)}, u32[]{:S(2)}, u32[]{:S(2)}) collective-permute-start(bf16[128,1024]{1,0:T(8,128)(2,1)S(1)} %get-tuple-element.5), channel_id=1, source_target_pairs={{0,96},{32,0},{64,32},{96,64},{1,97},{33,1},{65,33},{97,65},{2,98}... | collective-permute-start | bytes 786440 | tf_op jit(solution)/shard_map/ppermute | solution.py:11
  35.7 5.5 %collective-permute-start.11 = (bf16[64,1024]{1,0:T(8,128)(2,1)S(1)}, bf16[64,1024]{1,0:T(8,128)(2,1)S(1)}, u32[]{:S(2)}, u32[]{:S(2)}) collective-permute-start(bf16[64,1024]{1,0:T(8,128)(2,1)S(1)} %slice.12), channel_id=1, source_target_pairs={{0,32},{32,64},{64,96},{96,0},{1,33},{33,65},{65,97},{97,1},{2,34}... | collective-permute-start | bytes 393224 | tf_op jit(solution)/shard_map/ppermute | solution.py:11
  35.8 5.4 %collective-permute-start.13 = (bf16[64,1024]{1,0:T(8,128)(2,1)S(1)}, bf16[64,1024]{1,0:T(8,128)(2,1)S(1)}, u32[]{:S(2)}, u32[]{:S(2)}) collective-permute-start(bf16[64,1024]{1,0:T(8,128)(2,1)S(1)} %slice.13), channel_id=1, source_target_pairs={{0,96},{32,0},{64,32},{96,64},{1,97},{33,1},{65,33},{97,65},{2,98}... | collective-permute-start | bytes 393224 | tf_op jit(solution)/shard_map/ppermute | solution.py:11
  42.0 6.5 %collective-permute-start.14 = (f32[4,48,1024]{2,1,0:T(8,128)S(1)}, f32[4,48,1024]{2,1,0:T(8,128)S(1)}, u32[]{:S(2)}, u32[]{:S(2)}) collective-permute-start(f32[4,48,1024]{2,1,0:T(8,128)S(1)} %dynamic-slice_bitcast_fusion), channel_id=1, source_target_pairs={{0,8},{8,0},{1,9},{9,1},{2,10},{10,2},{3,11},{11,3},{4,12},{12,4},... | collective-permute-start | bytes 2359304 | tf_op jit(solution)/shard_map/ppermute | solution.py:11
  46.6 13.1 %copy-start = (f32[1024,1024]{1,0:T(8,128)S(1)}, f32[1024,1024]{1,0:T(8,128)}, u32[]{:S(2)}) copy-start(f32[1024,1024]{1,0:T(8,128)} %param.5) | copy-start | bytes 12582916
  48.7 6.6 %collective-permute-start.17 = (bf16[48,1024]{1,0:T(8,128)(2,1)S(1)}, bf16[48,1024]{1,0:T(8,128)(2,1)S(1)}, u32[]{:S(2)}, u32[]{:S(2)}) collective-permute-start(bf16[48,1024]{1,0:T(8,128)(2,1)S(1)} %get-tuple-element.7), channel_id=1, source_target_pairs={{0,144},{16,0},{128,16},{144,128},{1,145},{17,1},{129,17},{145,129... | collective-permute-start | bytes 294920 | tf_op jit(solution)/shard_map/ppermute | solution.py:11
  51.5 5.1 %collective-permute-start.16 = (bf16[48,1024]{1,0:T(8,128)(2,1)S(1)}, bf16[48,1024]{1,0:T(8,128)(2,1)S(1)}, u32[]{:S(2)}, u32[]{:S(2)}) collective-permute-start(bf16[48,1024]{1,0:T(8,128)(2,1)S(1)} %get-tuple-element.8), channel_id=1, source_target_pairs={{0,128},{16,144},{128,0},{144,16},{1,129},{17,145},{129,1},{145,17... | collective-permute-start | bytes 294920 | tf_op jit(solution)/shard_map/ppermute | solution.py:11
  51.8 7.8 %collective-permute-start.15 = (bf16[48,1024]{1,0:T(8,128)(2,1)S(1)}, bf16[48,1024]{1,0:T(8,128)(2,1)S(1)}, u32[]{:S(2)}, u32[]{:S(2)}) collective-permute-start(bf16[48,1024]{1,0:T(8,128)(2,1)S(1)} %get-tuple-element.6), channel_id=1, source_target_pairs={{0,16},{16,128},{128,144},{144,0},{1,17},{17,129},{129,145},{145,1... | collective-permute-start | bytes 294920 | tf_op jit(solution)/shard_map/ppermute | solution.py:11
  62.0 7.5 %collective-permute-start.18 = (bf16[48,1024]{1,0:T(8,128)(2,1)S(1)}, bf16[48,1024]{1,0:T(8,128)(2,1)S(1)}, u32[]{:S(2)}, u32[]{:S(2)}) collective-permute-start(bf16[48,1024]{1,0:T(8,128)(2,1)S(1)} %get-tuple-element.3), channel_id=1, source_target_pairs={{0,16},{16,128},{128,144},{144,0},{1,17},{17,129},{129,145},{145,1... | collective-permute-start | bytes 294920 | tf_op jit(solution)/shard_map/ppermute | solution.py:11
  62.0 7.5 %collective-permute-start.19 = (bf16[48,1024]{1,0:T(8,128)(2,1)S(1)}, bf16[48,1024]{1,0:T(8,128)(2,1)S(1)}, u32[]{:S(2)}, u32[]{:S(2)}) collective-permute-start(bf16[48,1024]{1,0:T(8,128)(2,1)S(1)} %get-tuple-element.3), channel_id=1, source_target_pairs={{0,128},{16,144},{128,0},{144,16},{1,129},{17,145},{129,1},{145,17... | collective-permute-start | bytes 294920 | tf_op jit(solution)/shard_map/ppermute | solution.py:11
  62.5 6.9 %collective-permute-start.20 = (bf16[48,1024]{1,0:T(8,128)(2,1)S(1)}, bf16[48,1024]{1,0:T(8,128)(2,1)S(1)}, u32[]{:S(2)}, u32[]{:S(2)}) collective-permute-start(bf16[48,1024]{1,0:T(8,128)(2,1)S(1)} %get-tuple-element.3), channel_id=1, source_target_pairs={{0,144},{16,0},{128,16},{144,128},{1,145},{17,1},{129,17},{145,129... | collective-permute-start | bytes 294920 | tf_op jit(solution)/shard_map/ppermute | solution.py:11
  69.5 3.1 %collective-permute-start.21 = (bf16[4,48,1024]{2,1,0:T(8,128)(2,1)S(1)}, bf16[4,48,1024]{2,1,0:T(8,128)(2,1)S(1)}, u32[]{:S(2)}, u32[]{:S(2)}) collective-permute-start(bf16[4,48,1024]{2,1,0:T(8,128)(2,1)S(1)} %pad_maximum_fusion), channel_id=1, source_target_pairs={{0,8},{8,0},{1,9},{9,1},{2,10},{10,2},{3,11},{11,3},{4,12},{12,4},... | collective-permute-start | bytes 1179656 | tf_op jit(solution)/shard_map/ppermute | solution.py:11

commit v2 on v0

v2 whole, which is shorter than its diff:
```python
import jax
import jax.numpy as jnp
from jax import lax
from jax.sharding import Mesh, PartitionSpec as P

X, Y, Z, CORE = "x", ("grp", "ylo"), "col", "core"
PLANE = ("grp", "x", "ylo", "core")
LOW, F32 = jnp.bfloat16, jnp.float32
HOLDER = (0, 0, 0, 0, 0, 1, 1, 1)


def shift(value, axis, size, step):
    return lax.ppermute(value, axis, [(i, (i + step) % size) for i in range(size)])


def along_z(value, pairs):
    return lax.ppermute(value, (CORE, Z), [(b * 8 + a, d * 8 + c) for (a, b), (c, d) in pairs])


def along_x(value, nx, step, target):
    pairs = []
    for x in range(nx):
        for z, core in enumerate(HOLDER):
            source = target if z == 0 else core
            to = (x + step) % nx
            pairs.append(((x * 2 + source) * 8 + z, (to * 2 + target) * 8 + z))
    return lax.ppermute(value, (X, CORE, Z), pairs)


def swap(value):
    return lax.ppermute(value, CORE, [(0, 1), (1, 0)])


def parts_of(value):
    out = []
    for _ in range(3):
        part = lax.reduce_precision(value, 8, 7)
        out.append(part.astype(LOW))
        value = value - part
    return out


def body(orbital_b, gaps, block_inverse):
    own, width = orbital_b.shape
    panel = block_inverse.shape[0]
    nx, ny, nz = lax.axis_size(X), lax.axis_size(Y), lax.axis_size(Z)
    x, y, z, core = (lax.axis_index(a) for a in (X, Y, Z, CORE))
    count = width // lax.axis_size(PLANE)
    is0 = core == 0

    def order(a, b, axis):
        return jnp.concatenate([jnp.where(is0, a, b), jnp.where(is0, b, a)], axis=axis)

    with jax.named_scope("panel_z"):
        piece = orbital_b[:, :panel]
        chip = order(piece, swap(piece), 0)
        far = along_z(chip, [((0, 0), (3, 0)), ((0, 1), (6, 1))])
        near = along_z(chip, [((0, 0), (1, 0)), ((0, 1), (7, 1))])
        next_a = along_z(far, [((3, 0), (4, 0)), ((6, 1), (5, 1))])
        next_b = along_z(far, [((3, 0), (2, 0))])
        chip = jnp.where((z == 3) | (z == 6), far, jnp.where((z == 1) | (z == 7), near, chip))
        chip = jnp.where((z == 4) | (z == 5), next_a, jnp.where(z == 2, next_b, chip))

    with jax.named_scope("blocks"):
        weight = 2.0 * gaps / (gaps * gaps + 1.0)
        rows = orbital_b.T.reshape(2, nx, 2, 2, count, own)
        extra = jnp.concatenate(
            [jnp.stack(parts_of(weight)), jnp.zeros((13, own), LOW)], axis=0
        )
        mine = lax.dynamic_index_in_dim(rows, core, 3, False).reshape(-1, own)
        mine = jnp.concatenate([mine, extra], axis=0)
        sent = lax.dynamic_index_in_dim(rows, 1 - core, 3, False).reshape(-1, own)
        sent = jnp.concatenate([sent, extra], axis=0)
        pair = order(mine, swap(sent), 1)
        blocks = pair[:-16].reshape(2, nx, 2 * count, 2 * own)

        def rows_of(i):
            block = lax.dynamic_index_in_dim(blocks, i, 1, False).reshape(-1, 2 * own)
            return jnp.concatenate([block, pair[-16:]], axis=0)

        b0 = rows_of(x)
        b1, b2, b3 = (shift(rows_of((x + k) % nx), X, nx, k) for k in range(1, nx))
        b2 = order(b2[:, :own], b2[:, own:], 1)
        factors = jnp.concatenate([b0, order(b1, b3, 1), b2], axis=1)
        weight = jnp.sum(factors[-16:-13].astype(F32)[::-1], axis=0)
        factors = factors[:-16]

    with jax.named_scope("panel_x"):
        up = along_x(chip, nx, 1, 0)
        down = along_x(chip, nx, -1, 1)
        first = jnp.where(is0, up, down)
        half = jnp.where(is0, up[:own], down[own:])
        second = lax.ppermute(
            half,
            (X, CORE),
            [(i * 2, (i + 1) % nx * 2) for i in range(nx)]
            + [(i * 2 + 1, (i - 1) % nx * 2 + 1) for i in range(nx)],
        )
        given = along_z(chip, [((i, h), (i, 1 - h)) for i, h in enumerate(HOLDER) if i])
        holder = jnp.where(z >= 5, 1, 0)
        chip = jnp.where((z == 0) | (core == holder), chip, given)
        early = [chip, first, swap(first)]
        late = [second, swap(second)]

    with jax.named_scope("response"):
        start = 0
        part = 0.0
        for group in (early, late):
            block = jnp.concatenate(group, axis=0)
            stop = start + block.shape[0]
            weighted = (weight[start:stop, None] * block.astype(F32)).astype(LOW)
            part = part + jnp.dot(factors[:, start:stop], weighted, preferred_element_type=F32)
            start = stop

    with jax.named_scope("sum_y"):
        kept = part.reshape(ny, count, panel)
        total = lax.dynamic_index_in_dim(kept, y, 0, False)
        for k in (2, 1, 3):
            piece = lax.dynamic_index_in_dim(kept, (y + k) % ny, 0, False).astype(LOW)
            total = total + shift(piece, Y, ny, k).astype(F32)

    with jax.named_scope("screen"):
        place = z * width + lax.axis_index(PLANE) * count
        unit = (lax.iota(jnp.int32, count)[:, None] + place) == lax.iota(jnp.int32, panel)[None, :]
        screened = jnp.dot(
            unit.astype(F32) + total, block_inverse, precision=lax.Precision.HIGH
        )

    with jax.named_scope("gather_y"):
        low = screened.astype(LOW)
        steps = (0, 2, 1, 3)
        gathered = jnp.concatenate([low] + [shift(low, Y, ny, k) for k in steps[1:]], axis=0)
        by_y = factors.reshape(ny, count, -1)
        ordered = jnp.concatenate(
            [lax.dynamic_index_in_dim(by_y, (y - k) % ny, 0, False) for k in steps], axis=0
        )

    with jax.named_scope("sigma"):
        panels = jnp.concatenate(early + late, axis=0)
        products = lax.dot_general(
            gathered, panels, (((1,), (1,)), ((), ())), preferred_element_type=F32
        )
        local = -jnp.sum(products * ordered.astype(F32), axis=0).reshape(2 * nx, own)
        a, b, c = local[2:4], local[4:6], local[6:]
        offsets = [
            local[:2],
            jnp.where(is0, b, a),
            jnp.where(is0, c, c[::-1]),
            jnp.where(is0, a, b),
        ]
        to = (lax.iota(jnp.int32, nx) - x) % nx
        by_x = sum(
            jnp.where((to == k)[:, None, None], offsets[k][None], 0.0) for k in range(nx)
        )
        copies = jnp.broadcast_to(by_x[:, :, None], (nx, 2, nz, own)).reshape(-1, own)
        terms = lax.all_to_all(copies, (X, CORE, Z), 0, 0, tiled=True)
        sigma = jnp.sum(terms, axis=0)
    return sigma, screened[None]


def solution(mesh):
    split = Mesh(mesh.devices.reshape(2, 4, 2, 2, 8), ("grp", "x", "ylo", "core", "col"))
    return jax.shard_map(
        body,
        mesh=split,
        in_specs=(P(PLANE, Z), P(PLANE), P()),
        out_specs=(P(PLANE), P(Z, PLANE, None)),
        check_vma=False,
    )
```

time: 267 us -> 93.1 us (0.35); the launches traced: 263 us -> 92.8 us
  waiting for transfers between devices: 201 us -> 28.6 us
  starting transfers between devices: 0.08 us -> 33.7 us
  matrix products: 30.2 us -> 4.12 us
  between operations: 14.1 us -> 1.35 us
  blocking collectives: 14.2 us -> 19.2 us
    psum x2 -> x0, waiting for transfers between devices: 201 us -> none  [the longest x1 129 us: body(): summed = lax.psum(partial_value, ('grp', 'row'))]
    ppermute x0 -> x21, starting transfers between devices: none -> 33.7 us  [the longest x9 10.2 us: shift(): lax.ppermute(value, axis, [(i, (i + step) % size) for i in range(size)])]
    ppermute x0 -> x21, waiting for transfers between devices: none -> 28.6 us  [the longest x9 14.6 us: shift(): lax.ppermute(value, axis, [(i, (i + step) % size) for i in range(size)])]
    dot_general x3 -> x4, matrix products: 30.2 us -> 4.12 us  [the longest x1 2.3 us: body(): jnp.dot(unit.astype(F32) + total, block_inverse, precision=lax.Precision....]
    all_to_all x0 -> x1, blocking collectives: none -> 19.2 us  [body(): terms = lax.all_to_all(copies, (X, CORE, Z), 0, 0, tiled=True)]
    psum x1 -> x0, blocking collectives: 14.2 us -> none  [body(): sigma = lax.psum(local_sigma, 'col')]
  transfers between devices with their start and end apart: 2 -> 21, of which waited for: 2 -> 10; matrix products, arithmetic and copies ran while one was open for 0% -> 5% of each run, Pallas kernels for 0% -> 0%
where the time goes in v2:
time: 93.1 us; the launch traced here: 92.8 us
  starting transfers between devices  33.7 us (36%)
  waiting for transfers between devices  28.6 us (31%)
  blocking collectives  19.2 us (21%)
  matrix products  4.12 us (4%)
  local copies, waits for them, and re-layouts  3.24 us (3%)
  other arithmetic  2.65 us (3%)
  between operations  1.35 us (1%)
    all_to_all x1, blocking collectives, body(): terms = lax.all_to_all(copies, (X, CORE, Z), 0, 0, tiled=True)  19.2 us
    ppermute x9, waiting for transfers between devices, shift(): lax.ppermute(value, axis, [(i, (i + step) % size) for i in range(size)])  14.6 us
    ppermute x9, starting transfers between devices, shift(): lax.ppermute(value, axis, [(i, (i + step) % size) for i in range(size)])  10.2 us
    ppermute x5, starting transfers between devices, along_z(): lax.ppermute(value, (CORE, Z), [(b * 8 + a, d * 8 + c) for (a, b), (c, d)...  9.61 us
    ppermute x4, starting transfers between devices, swap(): return lax.ppermute(value, CORE, [(0, 1), (1, 0)])  8.37 us
    ppermute x2, waiting for transfers between devices, along_x(): return lax.ppermute(value, (X, CORE, Z), pairs)  6.48 us
    ppermute x5, waiting for transfers between devices, along_z(): lax.ppermute(value, (CORE, Z), [(b * 8 + a, d * 8 + c) for (a, b), (c, d)...  4.04 us
    ppermute x2, starting transfers between devices, along_x(): return lax.ppermute(value, (X, CORE, Z), pairs)  3.55 us
  transfers between devices with their start and end apart: 21, of which 10 were waited for; matrix products, arithmetic and copies ran while one was open for 5% of the time, Pallas kernels for 0%

profile of v2, /device:TPU:1, one launch (start us, length us, event | category | flops | bytes accessed | tf_op | source)
XLA Modules:
  0.0 92.8 jit_solution(9669697873384353610)
XLA Ops:
  0.6 1.0 %slice.73 = bf16[128,1024]{1,0:T(8,128)(2,1)S(1)} slice(bf16[128,1536]{1,0:T(8,128)(2,1)} %param.3), slice={[0:128], [0:1024]} | slice | bytes 524288 | tf_op jit(solution)/shard_map/panel_z/slice | solution.py:55
  1.7 3.3 %collective-permute-start.4 = (bf16[128,1024]{1,0:T(8,128)(2,1)S(1)}, bf16[128,1024]{1,0:T(8,128)(2,1)S(1)}, u32[]{:S(2)}, u32[]{:S(2)}) collective-permute-start(bf16[128,1024]{1,0:T(8,128)(2,1)S(1)} %slice.73), channel_id=1, source_target_pairs={{0,8},{8,0},{1,9},{9,1},{2,10},{10,2},{3,11},{11,3},{4,12},{12,4},... | collective-permute-start | bytes 786440 | tf_op jit(solution)/shard_map/panel_z/ppermute | solution.py:31
  5.0 0.7 fusion.44
  5.7 1.2 %copy.6 = bf16[128,1536]{0,1:T(8,128)(2,1)S(1)} copy(bf16[128,1536]{1,0:T(8,128)(2,1)} %param.3) | data formatting | bytes 786432 | tf_op args[0]
  7.0 0.2 concatenate.52
  7.2 0.1 collective-permute-start
  7.5 6.2 %collective-permute-start.5 = (bf16[256,1024]{1,0:T(8,128)(2,1)S(1)}, bf16[256,1024]{1,0:T(8,128)(2,1)S(1)}, u32[]{:S(2)}, u32[]{:S(2)}) collective-permute-start(bf16[256,1024]{1,0:T(8,128)(2,1)S(1)} %pad_maximum_fusion), channel_id=1, source_target_pairs={{0,3},{8,14},{16,19},{24,30},{32,35},{40,46},{48,51},{56,62},{64,6... | collective-permute-start | bytes 1572872 | tf_op jit(solution)/shard_map/panel_z/ppermute | solution.py:17
  13.9 0.2 concatenate.51
  14.3 0.1 fusion.14
  14.4 1.3 %collective-permute-start.8 = (bf16[256,1024]{1,0:T(8,128)(2,1)S(1)}, bf16[256,1024]{1,0:T(8,128)(2,1)S(1)}, u32[]{:S(2)}, u32[]{:S(2)}) collective-permute-start(bf16[256,1024]{1,0:T(8,128)(2,1)S(1)} %pad_maximum_fusion), channel_id=1, source_target_pairs={{0,1},{8,15},{16,17},{24,31},{32,33},{40,47},{48,49},{56,63},{64,6... | collective-permute-start | bytes 1572872 | tf_op jit(solution)/shard_map/panel_z/ppermute | solution.py:17
  15.7 4.0 %collective-permute-done.5 = bf16[256,1024]{1,0:T(8,128)(2,1)S(1)} collective-permute-done((bf16[256,1024]{1,0:T(8,128)(2,1)S(1)}, bf16[256,1024]{1,0:T(8,128)(2,1)S(1)}, u32[]{:S(2)}, u32[]{:S(2)}) %collective-permute-start.5) | collective-permute-done | bytes 524320 | tf_op jit(solution)/shard_map/panel_z/ppermute | solution.py:17
  19.8 0.7 collective-permute-start.6
  20.4 0.7 collective-permute-start.7
  21.2 1.3 %collective-permute-start.1 = (bf16[208,256]{1,0:T(8,128)(2,1)S(1)}, bf16[208,256]{1,0:T(8,128)(2,1)S(1)}, u32[]{:S(2)}, u32[]{:S(2)}) collective-permute-start(bf16[208,256]{1,0:T(8,128)(2,1)S(1)} %get-tuple-element.36), channel_id=1, source_target_pairs={{0,32},{32,64},{64,96},{96,0},{1,33},{33,65},{65,97},{97,1},{2,34}... | collective-permute-start | bytes 319496 | tf_op jit(solution)/shard_map/blocks/ppermute | solution.py:13
  22.5 1.5 %collective-permute-start.2 = (bf16[208,256]{1,0:T(8,128)(2,1)S(1)}, bf16[208,256]{1,0:T(8,128)(2,1)S(1)}, u32[]{:S(2)}, u32[]{:S(2)}) collective-permute-start(bf16[208,256]{1,0:T(8,128)(2,1)S(1)} %get-tuple-element.34), channel_id=1, source_target_pairs={{0,96},{32,0},{64,32},{96,64},{1,97},{33,1},{65,33},{97,65},{2,98}... | collective-permute-start | bytes 319496 | tf_op jit(solution)/shard_map/blocks/ppermute | solution.py:13
  24.0 3.4 %collective-permute-done.1 = bf16[208,256]{1,0:T(8,128)(2,1)S(1)} collective-permute-done((bf16[208,256]{1,0:T(8,128)(2,1)S(1)}, bf16[208,256]{1,0:T(8,128)(2,1)S(1)}, u32[]{:S(2)}, u32[]{:S(2)}) %collective-permute-start.1) | collective-permute-done | bytes 106528 | tf_op jit(solution)/shard_map/blocks/ppermute | solution.py:13
  27.4 1.5 %collective-permute-start.3 = (bf16[208,256]{1,0:T(8,128)(2,1)S(1)}, bf16[208,256]{1,0:T(8,128)(2,1)S(1)}, u32[]{:S(2)}, u32[]{:S(2)}) collective-permute-start(bf16[208,256]{1,0:T(8,128)(2,1)S(1)} %get-tuple-element.33), channel_id=1, source_target_pairs={{0,64},{32,96},{64,0},{96,32},{1,65},{33,97},{65,1},{97,33},{2,66}... | collective-permute-start | bytes 319496 | tf_op jit(solution)/shard_map/blocks/ppermute | solution.py:13
  29.0 0.5 select_select_fusion
  29.4 0.7 collective-permute-start.10
  30.1 2.9 %collective-permute-start.11 = (bf16[256,1024]{1,0:T(8,128)(2,1)S(1)}, bf16[256,1024]{1,0:T(8,128)(2,1)S(1)}, u32[]{:S(2)}, u32[]{:S(2)}) collective-permute-start(bf16[256,1024]{1,0:T(8,128)(2,1)S(1)} %select_select_fusion), channel_id=1, source_target_pairs={{8,104},{1,105},{2,106},{3,107},{4,108},{13,109},{14,110},{15,111}... | collective-permute-start | bytes 1572872 | tf_op jit(solution)/shard_map/panel_x/ppermute | solution.py:27
  33.1 0.7 collective-permute-start.9
  33.9 6.5 %collective-permute-done.11 = bf16[256,1024]{1,0:T(8,128)(2,1)S(1)} collective-permute-done((bf16[256,1024]{1,0:T(8,128)(2,1)S(1)}, bf16[256,1024]{1,0:T(8,128)(2,1)S(1)}, u32[]{:S(2)}, u32[]{:S(2)}) %collective-permute-start.11) | collective-permute-done | bytes 524320 | tf_op jit(solution)/shard_map/panel_x/ppermute | solution.py:27
  40.4 1.9 %collective-permute-start.13 = (bf16[128,1024]{1,0:T(8,128)(2,1)S(1)}, bf16[128,1024]{1,0:T(8,128)(2,1)S(1)}, u32[]{:S(2)}, u32[]{:S(2)}) collective-permute-start(bf16[128,1024]{1,0:T(8,128)(2,1)S(1)} %slice_select_fusion), channel_id=1, source_target_pairs={{0,32},{32,64},{64,96},{96,0},{8,104},{40,8},{72,40},{104,72},{1,3... | collective-permute-start | bytes 786440 | tf_op jit(solution)/shard_map/panel_x/ppermute | solution.py:93
  42.3 0.2 constant_dynamic-update-slice_fusion.8
  42.5 0.2 constant_dynamic-update-slice_fusion.7
  42.7 0.4 collective-permute-start.12
  43.2 2.5 %collective-permute-done.13 = bf16[128,1024]{1,0:T(8,128)(2,1)S(1)} collective-permute-done((bf16[128,1024]{1,0:T(8,128)(2,1)S(1)}, bf16[128,1024]{1,0:T(8,128)(2,1)S(1)}, u32[]{:S(2)}, u32[]{:S(2)}) %collective-permute-start.13) | collective-permute-done | bytes 262176 | tf_op jit(solution)/shard_map/panel_x/ppermute | solution.py:93
  45.7 4.5 %collective-permute-start.14 = (bf16[128,1024]{1,0:T(8,128)(2,1)S(1)}, bf16[128,1024]{1,0:T(8,128)(2,1)S(1)}, u32[]{:S(2)}, u32[]{:S(2)}) collective-permute-start(bf16[128,1024]{1,0:T(8,128)(2,1)S(1)} %collective-permute-done.13), channel_id=1, source_target_pairs={{0,8},{8,0},{1,9},{9,1},{2,10},{10,2},{3,11},{11,3},{4,12},{12,4},... | collective-permute-start | bytes 786440 | tf_op jit(solution)/shard_map/panel_x/ppermute | solution.py:31
  50.2 0.2 rev.6
  50.5 0.9 collective-permute-done.14
  51.4 0.4 fusion.9
  51.8 0.0 copy-start
  51.8 0.6 fusion.7
  52.4 2.8 %collective-permute-start.17 = (bf16[48,1024]{1,0:T(8,128)(2,1)S(1)}, bf16[48,1024]{1,0:T(8,128)(2,1)S(1)}, u32[]{:S(2)}, u32[]{:S(2)}) collective-permute-start(bf16[48,1024]{1,0:T(8,128)(2,1)S(1)} %get-tuple-element.17), channel_id=1, source_target_pairs={{0,144},{16,0},{128,16},{144,128},{1,145},{17,1},{129,17},{145,129... | collective-permute-start | bytes 294920 | tf_op jit(solution)/shard_map/sum_y/ppermute | solution.py:13
  55.3 1.6 %collective-permute-start.15 = (bf16[48,1024]{1,0:T(8,128)(2,1)S(1)}, bf16[48,1024]{1,0:T(8,128)(2,1)S(1)}, u32[]{:S(2)}, u32[]{:S(2)}) collective-permute-start(bf16[48,1024]{1,0:T(8,128)(2,1)S(1)} %get-tuple-element.16), channel_id=1, source_target_pairs={{0,128},{16,144},{128,0},{144,16},{1,129},{17,145},{129,1},{145,17... | collective-permute-start | bytes 294920 | tf_op jit(solution)/shard_map/sum_y/ppermute | solution.py:13
  57.0 0.1 collective-permute-done.17
  57.1 5.6 %collective-permute-done.16 = bf16[48,1024]{1,0:T(8,128)(2,1)S(1)} collective-permute-done((bf16[48,1024]{1,0:T(8,128)(2,1)S(1)}, bf16[48,1024]{1,0:T(8,128)(2,1)S(1)}, u32[]{:S(2)}, u32[]{:S(2)}) %collective-permute-start.16) | collective-permute-done | bytes 98336 | tf_op jit(solution)/shard_map/sum_y/ppermute | solution.py:13
  62.7 2.3 %fusion.49 = (bf16[48,1024]{1,0:T(8,128)(2,1)S(1)}, f32[48,1024]{1,0:T(8,128)}) fusion(f32[1024,1024]{1,0:T(8,128)S(1)} %copy-done, bf16[48,1024]{1,0:T(8,128)(2,1)S(1)} %collective-permute-done.17, bf16[48,1024]{1,0:T(8,128)(2,1)S(1)} %collective-permute-done.16, bf16[48,1024]{1,0:T(8,128)(2,1)S(1)} %collective-permute-done.15, ...), kind=kOutput, calls=%fused_computation.119 | convolution fusion | flops 302481408 | bytes 4981252 | tf_op jit(solution)/shard_map/screen/dot_general | solution.py:125
  65.0 0.2 collective-permute-start.20
  65.2 1.2 %collective-permute-start.19 = (bf16[48,1024]{1,0:T(8,128)(2,1)S(1)}, bf16[48,1024]{1,0:T(8,128)(2,1)S(1)}, u32[]{:S(2)}, u32[]{:S(2)}) collective-permute-start(bf16[48,1024]{1,0:T(8,128)(2,1)S(1)} %get-tuple-element.43), channel_id=1, source_target_pairs={{0,16},{16,128},{128,144},{144,0},{1,17},{17,129},{129,145},{145,1... | collective-permute-start | bytes 294920 | tf_op jit(solution)/shard_map/gather_y/ppermute | solution.py:13
  66.4 0.0 collective-permute-start.18
  66.5 2.0 %collective-permute-done.20 = bf16[48,1024]{1,0:T(8,128)(2,1)S(1)} collective-permute-done((bf16[48,1024]{1,0:T(8,128)(2,1)S(1)}, bf16[48,1024]{1,0:T(8,128)(2,1)S(1)}, u32[]{:S(2)}, u32[]{:S(2)}) %collective-permute-start.20) | collective-permute-done | bytes 98336 | tf_op jit(solution)/shard_map/gather_y/ppermute | solution.py:13
  68.4 1.4 %collective-permute-done.19 = bf16[48,1024]{1,0:T(8,128)(2,1)S(1)} collective-permute-done((bf16[48,1024]{1,0:T(8,128)(2,1)S(1)}, bf16[48,1024]{1,0:T(8,128)(2,1)S(1)}, u32[]{:S(2)}, u32[]{:S(2)}) %collective-permute-start.19) | collective-permute-done | bytes 98336 | tf_op jit(solution)/shard_map/gather_y/ppermute | solution.py:13
  69.9 2.1 %collective-permute-done.18 = bf16[48,1024]{1,0:T(8,128)(2,1)S(1)} collective-permute-done((bf16[48,1024]{1,0:T(8,128)(2,1)S(1)}, bf16[48,1024]{1,0:T(8,128)(2,1)S(1)}, u32[]{:S(2)}, u32[]{:S(2)}) %collective-permute-start.18) | collective-permute-done | bytes 98336 | tf_op jit(solution)/shard_map/gather_y/ppermute | solution.py:13
  72.0 0.9 fusion.8
  73.0 0.1 select_add_fusion
  73.1 19.2 %all_to_all.9 = f32[64,1,128]{2,1,0:T(1,128)S(1)} all-to-all(f32[64,1,128]{2,1,0:T(1,128)S(1)} %bitcast.71), channel_id=1, replica_groups=mesh['grp'=2,'x'=4,'ylo'=2,'core'=2,'col'=8] {'x','core','col'}, dimensions={0} | all-to-all | bytes 65536 | tf_op jit(solution)/shard_map/sigma/all_to_all | solution.py:156
  92.2 0.6 reduce_sum.29
  (50 shorter events, 0.7 us)
Async XLA Ops:
  0.6 6.7 %copy-start.1 = (bf16[128,1536]{1,0:T(8,128)(2,1)S(1)}, bf16[128,1536]{1,0:T(8,128)(2,1)}, u32[]{:S(2)}) copy-start(bf16[128,1536]{1,0:T(8,128)(2,1)} %param.3) | copy-start | bytes 1179652
  1.7 5.7 %collective-permute-start.4 = (bf16[128,1024]{1,0:T(8,128)(2,1)S(1)}, bf16[128,1024]{1,0:T(8,128)(2,1)S(1)}, u32[]{:S(2)}, u32[]{:S(2)}) collective-permute-start(bf16[128,1024]{1,0:T(8,128)(2,1)S(1)} %slice.73), channel_id=1, source_target_pairs={{0,8},{8,0},{1,9},{9,1},{2,10},{10,2},{3,11},{11,3},{4,12},{12,4},... | collective-permute-start | bytes 786440 | tf_op jit(solution)/shard_map/panel_z/ppermute | solution.py:31
  7.2 7.0 %collective-permute-start = (bf16[784,128]{1,0:T(8,128)(2,1)S(1)}, bf16[784,128]{1,0:T(8,128)(2,1)S(1)}, u32[]{:S(2)}, u32[]{:S(2)}) collective-permute-start(bf16[784,128]{1,0:T(8,128)(2,1)S(1)} %concatenate.52), channel_id=1, source_target_pairs={{0,8},{8,0},{1,9},{9,1},{2,10},{10,2},{3,11},{11,3},{4,12},{12,4},... | collective-permute-start | bytes 602120 | tf_op jit(solution)/shard_map/blocks/ppermute | solution.py:31
  7.5 12.3 %collective-permute-start.5 = (bf16[256,1024]{1,0:T(8,128)(2,1)S(1)}, bf16[256,1024]{1,0:T(8,128)(2,1)S(1)}, u32[]{:S(2)}, u32[]{:S(2)}) collective-permute-start(bf16[256,1024]{1,0:T(8,128)(2,1)S(1)} %pad_maximum_fusion), channel_id=1, source_target_pairs={{0,3},{8,14},{16,19},{24,30},{32,35},{40,46},{48,51},{56,62},{64,6... | collective-permute-start | bytes 1572872 | tf_op jit(solution)/shard_map/panel_z/ppermute | solution.py:17
  14.4 14.5 %collective-permute-start.8 = (bf16[256,1024]{1,0:T(8,128)(2,1)S(1)}, bf16[256,1024]{1,0:T(8,128)(2,1)S(1)}, u32[]{:S(2)}, u32[]{:S(2)}) collective-permute-start(bf16[256,1024]{1,0:T(8,128)(2,1)S(1)} %pad_maximum_fusion), channel_id=1, source_target_pairs={{0,1},{8,15},{16,17},{24,31},{32,33},{40,47},{48,49},{56,63},{64,6... | collective-permute-start | bytes 1572872 | tf_op jit(solution)/shard_map/panel_z/ppermute | solution.py:17
  19.8 9.2 %collective-permute-start.6 = (bf16[256,1024]{1,0:T(8,128)(2,1)S(1)}, bf16[256,1024]{1,0:T(8,128)(2,1)S(1)}, u32[]{:S(2)}, u32[]{:S(2)}) collective-permute-start(bf16[256,1024]{1,0:T(8,128)(2,1)S(1)} %collective-permute-done.5), channel_id=1, source_target_pairs={{3,4},{14,13},{19,20},{30,29},{35,36},{46,45},{51,52},{62,61},{67,... | collective-permute-start | bytes 1572872 | tf_op jit(solution)/shard_map/panel_z/ppermute | solution.py:17
  20.4 8.5 %collective-permute-start.7 = (bf16[256,1024]{1,0:T(8,128)(2,1)S(1)}, bf16[256,1024]{1,0:T(8,128)(2,1)S(1)}, u32[]{:S(2)}, u32[]{:S(2)}) collective-permute-start(bf16[256,1024]{1,0:T(8,128)(2,1)S(1)} %collective-permute-done.5), channel_id=1, source_target_pairs={{3,2},{19,18},{35,34},{51,50},{67,66},{83,82},{99,98},{115,114},{1... | collective-permute-start | bytes 1572872 | tf_op jit(solution)/shard_map/panel_z/ppermute | solution.py:17
  21.2 6.2 %collective-permute-start.1 = (bf16[208,256]{1,0:T(8,128)(2,1)S(1)}, bf16[208,256]{1,0:T(8,128)(2,1)S(1)}, u32[]{:S(2)}, u32[]{:S(2)}) collective-permute-start(bf16[208,256]{1,0:T(8,128)(2,1)S(1)} %get-tuple-element.36), channel_id=1, source_target_pairs={{0,32},{32,64},{64,96},{96,0},{1,33},{33,65},{65,97},{97,1},{2,34}... | collective-permute-start | bytes 319496 | tf_op jit(solution)/shard_map/blocks/ppermute | solution.py:13
  22.5 6.4 %collective-permute-start.2 = (bf16[208,256]{1,0:T(8,128)(2,1)S(1)}, bf16[208,256]{1,0:T(8,128)(2,1)S(1)}, u32[]{:S(2)}, u32[]{:S(2)}) collective-permute-start(bf16[208,256]{1,0:T(8,128)(2,1)S(1)} %get-tuple-element.34), channel_id=1, source_target_pairs={{0,96},{32,0},{64,32},{96,64},{1,97},{33,1},{65,33},{97,65},{2,98}... | collective-permute-start | bytes 319496 | tf_op jit(solution)/shard_map/blocks/ppermute | solution.py:13
  27.4 6.4 %collective-permute-start.3 = (bf16[208,256]{1,0:T(8,128)(2,1)S(1)}, bf16[208,256]{1,0:T(8,128)(2,1)S(1)}, u32[]{:S(2)}, u32[]{:S(2)}) collective-permute-start(bf16[208,256]{1,0:T(8,128)(2,1)S(1)} %get-tuple-element.33), channel_id=1, source_target_pairs={{0,64},{32,96},{64,0},{96,32},{1,65},{33,97},{65,1},{97,33},{2,66}... | collective-permute-start | bytes 319496 | tf_op jit(solution)/shard_map/blocks/ppermute | solution.py:13
  29.4 4.4 %collective-permute-start.10 = (bf16[256,1024]{1,0:T(8,128)(2,1)S(1)}, bf16[256,1024]{1,0:T(8,128)(2,1)S(1)}, u32[]{:S(2)}, u32[]{:S(2)}) collective-permute-start(bf16[256,1024]{1,0:T(8,128)(2,1)S(1)} %select_select_fusion), channel_id=1, source_target_pairs={{0,32},{1,33},{2,34},{3,35},{4,36},{13,37},{14,38},{15,39},{32,64}... | collective-permute-start | bytes 1572872 | tf_op jit(solution)/shard_map/panel_x/ppermute | solution.py:27
  30.1 10.2 %collective-permute-start.11 = (bf16[256,1024]{1,0:T(8,128)(2,1)S(1)}, bf16[256,1024]{1,0:T(8,128)(2,1)S(1)}, u32[]{:S(2)}, u32[]{:S(2)}) collective-permute-start(bf16[256,1024]{1,0:T(8,128)(2,1)S(1)} %select_select_fusion), channel_id=1, source_target_pairs={{8,104},{1,105},{2,106},{3,107},{4,108},{13,109},{14,110},{15,111}... | collective-permute-start | bytes 1572872 | tf_op jit(solution)/shard_map/panel_x/ppermute | solution.py:27
  33.1 9.3 %collective-permute-start.9 = (bf16[256,1024]{1,0:T(8,128)(2,1)S(1)}, bf16[256,1024]{1,0:T(8,128)(2,1)S(1)}, u32[]{:S(2)}, u32[]{:S(2)}) collective-permute-start(bf16[256,1024]{1,0:T(8,128)(2,1)S(1)} %select_select_fusion), channel_id=1, source_target_pairs={{1,9},{2,10},{3,11},{4,12},{13,5},{14,6},{15,7},{17,25},{18,26},{1... | collective-permute-start | bytes 1572872 | tf_op jit(solution)/shard_map/panel_x/ppermute | solution.py:17
  40.4 5.3 %collective-permute-start.13 = (bf16[128,1024]{1,0:T(8,128)(2,1)S(1)}, bf16[128,1024]{1,0:T(8,128)(2,1)S(1)}, u32[]{:S(2)}, u32[]{:S(2)}) collective-permute-start(bf16[128,1024]{1,0:T(8,128)(2,1)S(1)} %slice_select_fusion), channel_id=1, source_target_pairs={{0,32},{32,64},{64,96},{96,0},{8,104},{40,8},{72,40},{104,72},{1,3... | collective-permute-start | bytes 786440 | tf_op jit(solution)/shard_map/panel_x/ppermute | solution.py:93
  42.7 3.0 %copy-start.2 = (bf16[1024,1024]{1,0:T(8,128)(2,1)}, bf16[1024,1024]{1,0:T(8,128)(2,1)S(1)}, u32[]{:S(2)}) copy-start(bf16[1024,1024]{1,0:T(8,128)(2,1)S(1)} %get-tuple-element.12) | copy-start | bytes 6291460
  42.7 9.0 %collective-permute-start.12 = (bf16[256,1024]{1,0:T(8,128)(2,1)S(1)}, bf16[256,1024]{1,0:T(8,128)(2,1)S(1)}, u32[]{:S(2)}, u32[]{:S(2)}) collective-permute-start(bf16[256,1024]{1,0:T(8,128)(2,1)S(1)} %get-tuple-element.13), channel_id=1, source_target_pairs={{0,8},{8,0},{1,9},{9,1},{2,10},{10,2},{3,11},{11,3},{4,12},{12,4},... | collective-permute-start | bytes 1572872 | tf_op jit(solution)/shard_map/panel_x/ppermute | solution.py:31
  45.7 5.7 %collective-permute-start.14 = (bf16[128,1024]{1,0:T(8,128)(2,1)S(1)}, bf16[128,1024]{1,0:T(8,128)(2,1)S(1)}, u32[]{:S(2)}, u32[]{:S(2)}) collective-permute-start(bf16[128,1024]{1,0:T(8,128)(2,1)S(1)} %collective-permute-done.13), channel_id=1, source_target_pairs={{0,8},{8,0},{1,9},{9,1},{2,10},{10,2},{3,11},{11,3},{4,12},{12,4},... | collective-permute-start | bytes 786440 | tf_op jit(solution)/shard_map/panel_x/ppermute | solution.py:31
  51.8 5.1 %copy-start.3 = (bf16[1024,1024]{1,0:T(8,128)(2,1)S(1)}, bf16[1024,1024]{1,0:T(8,128)(2,1)}, u32[]{:S(2)}) copy-start(bf16[1024,1024]{1,0:T(8,128)(2,1)} %copy-done.2) | copy-start | bytes 6291460
  51.8 10.9 %copy-start = (f32[1024,1024]{1,0:T(8,128)S(1)}, f32[1024,1024]{1,0:T(8,128)}, u32[]{:S(2)}) copy-start(f32[1024,1024]{1,0:T(8,128)} %param.5) | copy-start | bytes 12582916
  52.4 4.6 %collective-permute-start.17 = (bf16[48,1024]{1,0:T(8,128)(2,1)S(1)}, bf16[48,1024]{1,0:T(8,128)(2,1)S(1)}, u32[]{:S(2)}, u32[]{:S(2)}) collective-permute-start(bf16[48,1024]{1,0:T(8,128)(2,1)S(1)} %get-tuple-element.17), channel_id=1, source_target_pairs={{0,144},{16,0},{128,16},{144,128},{1,145},{17,1},{129,17},{145,129... | collective-permute-start | bytes 294920 | tf_op jit(solution)/shard_map/sum_y/ppermute | solution.py:13
  55.3 7.4 %collective-permute-start.16 = (bf16[48,1024]{1,0:T(8,128)(2,1)S(1)}, bf16[48,1024]{1,0:T(8,128)(2,1)S(1)}, u32[]{:S(2)}, u32[]{:S(2)}) collective-permute-start(bf16[48,1024]{1,0:T(8,128)(2,1)S(1)} %get-tuple-element.18), channel_id=1, source_target_pairs={{0,16},{16,128},{128,144},{144,0},{1,17},{17,129},{129,145},{145,1... | collective-permute-start | bytes 294920 | tf_op jit(solution)/shard_map/sum_y/ppermute | solution.py:13
  55.3 7.4 %collective-permute-start.15 = (bf16[48,1024]{1,0:T(8,128)(2,1)S(1)}, bf16[48,1024]{1,0:T(8,128)(2,1)S(1)}, u32[]{:S(2)}, u32[]{:S(2)}) collective-permute-start(bf16[48,1024]{1,0:T(8,128)(2,1)S(1)} %get-tuple-element.16), channel_id=1, source_target_pairs={{0,128},{16,144},{128,0},{144,16},{1,129},{17,145},{129,1},{145,17... | collective-permute-start | bytes 294920 | tf_op jit(solution)/shard_map/sum_y/ppermute | solution.py:13
  65.0 3.5 %collective-permute-start.20 = (bf16[48,1024]{1,0:T(8,128)(2,1)S(1)}, bf16[48,1024]{1,0:T(8,128)(2,1)S(1)}, u32[]{:S(2)}, u32[]{:S(2)}) collective-permute-start(bf16[48,1024]{1,0:T(8,128)(2,1)S(1)} %get-tuple-element.43), channel_id=1, source_target_pairs={{0,144},{16,0},{128,16},{144,128},{1,145},{17,1},{129,17},{145,129... | collective-permute-start | bytes 294920 | tf_op jit(solution)/shard_map/gather_y/ppermute | solution.py:13
  65.2 4.7 %collective-permute-start.19 = (bf16[48,1024]{1,0:T(8,128)(2,1)S(1)}, bf16[48,1024]{1,0:T(8,128)(2,1)S(1)}, u32[]{:S(2)}, u32[]{:S(2)}) collective-permute-start(bf16[48,1024]{1,0:T(8,128)(2,1)S(1)} %get-tuple-element.43), channel_id=1, source_target_pairs={{0,16},{16,128},{128,144},{144,0},{1,17},{17,129},{129,145},{145,1... | collective-permute-start | bytes 294920 | tf_op jit(solution)/shard_map/gather_y/ppermute | solution.py:13
  66.4 5.6 %collective-permute-start.18 = (bf16[48,1024]{1,0:T(8,128)(2,1)S(1)}, bf16[48,1024]{1,0:T(8,128)(2,1)S(1)}, u32[]{:S(2)}, u32[]{:S(2)}) collective-permute-start(bf16[48,1024]{1,0:T(8,128)(2,1)S(1)} %get-tuple-element.43), channel_id=1, source_target_pairs={{0,128},{16,144},{128,0},{144,16},{1,129},{17,145},{129,1},{145,17... | collective-permute-start | bytes 294920 | tf_op jit(solution)/shard_map/gather_y/ppermute | solution.py:13

commit v3 on v2

v3 whole, which is shorter than its diff:
```python
import jax
import jax.numpy as jnp
from jax import lax
from jax.sharding import Mesh, PartitionSpec as P

X, Y, Z, CORE = "x", ("grp", "ylo"), "col", "core"
PLANE = ("grp", "x", "ylo", "core")
LOW, F32 = jnp.bfloat16, jnp.float32
def shift(value, axis, size, step):
    return lax.ppermute(value, axis, [(i, (i + step) % size) for i in range(size)])


def along_z(value, *pairs):
    return lax.ppermute(value, Z, pairs)


def swap(value):
    return lax.ppermute(value, CORE, [(0, 1), (1, 0)])


def parts_of(value):
    out = []
    for _ in range(3):
        part = lax.reduce_precision(value, 8, 7)
        out.append(part.astype(LOW))
        value = value - part
    return out


def body(orbital_b, gaps, block_inverse):
    own, width = orbital_b.shape
    panel = block_inverse.shape[0]
    nx, ny, nz = lax.axis_size(X), lax.axis_size(Y), lax.axis_size(Z)
    x, y, z, core = (lax.axis_index(a) for a in (X, Y, Z, CORE))
    count = width // lax.axis_size(PLANE)
    steps = (0, 2, 1, 3)

    with jax.named_scope("panel_z"):
        piece = orbital_b[:, :panel]
        far_a = along_z(piece, (0, 3))
        far_b = along_z(piece, (0, 6))
        near_a = along_z(piece, (0, 1))
        near_b = along_z(piece, (0, 7))

    with jax.named_scope("blocks"):
        weight = 2.0 * gaps / (gaps * gaps + 1.0)
        rows = orbital_b.T.reshape(2, nx, 2, 2, count, own)
        extra = jnp.concatenate(
            [jnp.stack(parts_of(weight)), jnp.zeros((13, own), LOW)], axis=0
        )
        mine = lax.dynamic_index_in_dim(rows, core, 3, False).reshape(-1, own)
        mine = jnp.concatenate([mine, extra], axis=0)
        sent = lax.dynamic_index_in_dim(rows, 1 - core, 3, False).reshape(-1, own)
        sent = jnp.concatenate([sent, extra], axis=0)
        mine, sent, far_a, far_b = lax.optimization_barrier((mine, sent, far_a, far_b))

    with jax.named_scope("panel_z"):
        next_a = along_z(far_a, (3, 4))
        next_b = along_z(far_b, (6, 5))
        next_c = along_z(far_a, (3, 2))
    with jax.named_scope("blocks"):
        pair = jnp.concatenate([mine, swap(sent)], axis=1)
        blocks = pair[:-16].reshape(2, nx, 2 * count, 2 * own)

        def rows_of(i):
            block = lax.dynamic_index_in_dim(blocks, i, 1, False).reshape(-1, 2 * own)
            return jnp.concatenate([block, pair[-16:]], axis=0)

        factors = jnp.concatenate(
            [rows_of(x)] + [shift(rows_of((x + k) % nx), X, nx, k) for k in steps[1:]], axis=1
        )
        weight = jnp.sum(factors[-16:-13].astype(F32), axis=0)
        factors = factors[:-16]

    with jax.named_scope("panel_z"):
        held = jnp.where(z == 3, far_a, jnp.where(z == 6, far_b, piece))
        held = jnp.where(z == 1, near_a, jnp.where(z == 7, near_b, held))
        held = jnp.where(z == 4, next_a, jnp.where(z == 5, next_b, jnp.where(z == 2, next_c, held)))

    with jax.named_scope("panel_x"):
        got = [held] + [shift(held, X, nx, k) for k in steps[1:]]
        panels = [part for one in got for part in (one, swap(one))]

    with jax.named_scope("response"):
        part = 0.0
        half = len(panels) // 2
        for group in (slice(0, half), slice(half, None)):
            block = jnp.concatenate(panels[group], axis=0)
            columns = slice(group.start * own, (group.stop or 2 * half) * own)
            weighted = (weight[columns, None] * block.astype(F32)).astype(LOW)
            part = part + jnp.dot(factors[:, columns], weighted, preferred_element_type=F32)

    with jax.named_scope("sum_y"):
        kept = part.reshape(ny, count, panel)
        total = lax.dynamic_index_in_dim(kept, y, 0, False)
        for k in (2, 1, 3):
            piece = lax.dynamic_index_in_dim(kept, (y + k) % ny, 0, False).astype(LOW)
            total = total + shift(piece, Y, ny, k).astype(F32)

    with jax.named_scope("screen"):
        place = z * width + lax.axis_index(PLANE) * count
        unit = (lax.iota(jnp.int32, count)[:, None] + place) == lax.iota(jnp.int32, panel)[None, :]
        screened = jnp.dot(
            unit.astype(F32) + total, block_inverse, precision=lax.Precision.HIGH
        )

    with jax.named_scope("gather_y"):
        low = screened.astype(LOW)
        gathered = jnp.concatenate([low] + [shift(low, Y, ny, k) for k in steps[1:]], axis=0)
        by_y = factors.reshape(ny, count, -1)
        ordered = jnp.concatenate(
            [lax.dynamic_index_in_dim(by_y, (y - k) % ny, 0, False) for k in steps], axis=0
        )

    with jax.named_scope("sigma"):
        block = jnp.concatenate(panels, axis=0)
        products = lax.dot_general(
            gathered, block, (((1,), (1,)), ((), ())), preferred_element_type=F32
        )
        local = -jnp.sum(products * ordered.astype(F32), axis=0).reshape(nx, 2, own)
        local = local[:, 0] + swap(local[:, 1])
        back = (x - lax.iota(jnp.int32, nx)) % nx
        by_x = sum(
            jnp.where((back == k)[:, None], local[i][None], 0.0) for i, k in enumerate(steps)
        )
        copies = jnp.broadcast_to(by_x[:, None], (nx, nz, own)).reshape(-1, own)
        terms = lax.all_to_all(copies, (X, Z), 0, 0, tiled=True)
        sigma = jnp.sum(terms, axis=0)
    return sigma, screened[None]


def solution(mesh):
    split = Mesh(mesh.devices.reshape(2, 4, 2, 2, 8), ("grp", "x", "ylo", "core", "col"))
    return jax.shard_map(
        body,
        mesh=split,
        in_specs=(P(PLANE, Z), P(PLANE), P()),
        out_specs=(P(PLANE), P(Z, PLANE, None)),
        check_vma=False,
    )
```

time: 93.1 us -> 90.1 us (0.968)
  waiting for transfers between devices: 28.6 us -> 26.5 us
    ppermute x8 -> x7, waiting for transfers between devices: 13.1 us -> 0.02 us  [along_z(): return lax.ppermute(value, Z, pairs)]
    ppermute x9 -> x12, waiting for transfers between devices: 14.6 us -> 24.8 us  [shift(): lax.ppermute(value, axis, [(i, (i + step) % size) for i in range(size)])]
    ppermute x9 -> x12, starting transfers between devices: 10.2 us -> 12 us  [shift(): lax.ppermute(value, axis, [(i, (i + step) % size) for i in range(size)])]
    ppermute x8 -> x7, starting transfers between devices: 15.1 us -> 14.1 us  [along_z(): return lax.ppermute(value, Z, pairs)]
    ppermute x4 -> x6, starting transfers between devices: 8.37 us -> 8.35 us  [swap(): return lax.ppermute(value, CORE, [(0, 1), (1, 0)])]
  transfers between devices with their start and end apart: 21 -> 25, of which waited for: 10 -> 10; matrix products, arithmetic and copies ran while one was open for 5% -> 4% of each run, Pallas kernels for 0% -> 0%
where the time goes in v3:
time: 90.1 us; the launch traced here: 89.8 us
  starting transfers between devices  34.4 us (38%)
  waiting for transfers between devices  26.5 us (29%)
  blocking collectives  18.7 us (21%)
  matrix products  4.12 us (5%)
  local copies, waits for them, and re-layouts  3.11 us (3%)
  other arithmetic  1.79 us (2%)
  between operations  1.23 us (1%)
    ppermute x12, waiting for transfers between devices, shift(): lax.ppermute(value, axis, [(i, (i + step) % size) for i in range(size)])  24.8 us
    all_to_all x1, blocking collectives, body(): terms = lax.all_to_all(copies, (X, Z), 0, 0, tiled=True)  18.7 us
    ppermute x7, starting transfers between devices, along_z(): return lax.ppermute(value, Z, pairs)  14.1 us
    ppermute x12, starting transfers between devices, shift(): lax.ppermute(value, axis, [(i, (i + step) % size) for i in range(size)])  12 us
    ppermute x6, starting transfers between devices, swap(): return lax.ppermute(value, CORE, [(0, 1), (1, 0)])  8.35 us
    dot_general x1, matrix products, body(): jnp.dot(unit.astype(F32) + total, block_inverse, precision=lax.Precision....  2.29 us
  transfers between devices with their start and end apart: 25, of which 10 were waited for; matrix products, arithmetic and copies ran while one was open for 4% of the time, Pallas kernels for 0%

profile of v3, /device:TPU:1, one launch (start us, length us, event | category | flops | bytes accessed | tf_op | source)
XLA Modules:
  0.0 89.8 jit_solution(15551005700178050959)
XLA Ops:
  0.6 1.0 %slice.52 = bf16[128,1024]{1,0:T(8,128)(2,1)S(1)} slice(bf16[128,1536]{1,0:T(8,128)(2,1)} %param.3), slice={[0:128], [0:1024]} | slice | bytes 524288 | tf_op jit(solution)/shard_map/panel_z/slice | solution.py:39
  1.6 7.1 %collective-permute-start = (bf16[128,1024]{1,0:T(8,128)(2,1)S(1)}, bf16[128,1024]{1,0:T(8,128)(2,1)S(1)}, u32[]{:S(2)}, u32[]{:S(2)}) collective-permute-start(bf16[128,1024]{1,0:T(8,128)(2,1)S(1)} %slice.52), channel_id=1, source_target_pairs={{0,3},{8,11},{16,19},{24,27},{32,35},{40,43},{48,51},{56,59},{64,6... | collective-permute-start | bytes 786440 | tf_op jit(solution)/shard_map/panel_z/ppermute | solution.py:14
  8.7 2.4 %collective-permute-start.1 = (bf16[128,1024]{1,0:T(8,128)(2,1)S(1)}, bf16[128,1024]{1,0:T(8,128)(2,1)S(1)}, u32[]{:S(2)}, u32[]{:S(2)}) collective-permute-start(bf16[128,1024]{1,0:T(8,128)(2,1)S(1)} %slice.52), channel_id=1, source_target_pairs={{0,6},{8,14},{16,22},{24,30},{32,38},{40,46},{48,54},{56,62},{64,7... | collective-permute-start | bytes 786440 | tf_op jit(solution)/shard_map/panel_z/ppermute | solution.py:14
  11.1 1.3 %collective-permute-start.9 = (bf16[128,1024]{1,0:T(8,128)(2,1)S(1)}, bf16[128,1024]{1,0:T(8,128)(2,1)S(1)}, u32[]{:S(2)}, u32[]{:S(2)}) collective-permute-start(bf16[128,1024]{1,0:T(8,128)(2,1)S(1)} %slice.52), channel_id=1, source_target_pairs={{0,1},{8,9},{16,17},{24,25},{32,33},{40,41},{48,49},{56,57},{64,65... | collective-permute-start | bytes 786440 | tf_op jit(solution)/shard_map/panel_z/ppermute | solution.py:14
  12.4 1.3 %collective-permute-start.10 = (bf16[128,1024]{1,0:T(8,128)(2,1)S(1)}, bf16[128,1024]{1,0:T(8,128)(2,1)S(1)}, u32[]{:S(2)}, u32[]{:S(2)}) collective-permute-start(bf16[128,1024]{1,0:T(8,128)(2,1)S(1)} %slice.52), channel_id=1, source_target_pairs={{0,7},{8,15},{16,23},{24,31},{32,39},{40,47},{48,55},{56,63},{64,7... | collective-permute-start | bytes 786440 | tf_op jit(solution)/shard_map/panel_z/ppermute | solution.py:14
  13.7 0.7 fusion.46
  14.4 1.2 %copy.7 = bf16[128,1536]{0,1:T(8,128)(2,1)S(1)} copy(bf16[128,1536]{1,0:T(8,128)(2,1)} %param.3) | data formatting | bytes 786432 | tf_op args[0]
  15.8 0.0 copy-start.1
  15.8 0.2 concatenate.48
  16.1 0.2 concatenate.49
  16.4 2.3 %collective-permute-start.2 = (bf16[784,128]{1,0:T(8,128)(2,1)S(1)}, bf16[784,128]{1,0:T(8,128)(2,1)S(1)}, u32[]{:S(2)}, u32[]{:S(2)}) collective-permute-start(bf16[784,128]{1,0:T(8,128)(2,1)S(1)} %concatenate.49), channel_id=1, source_target_pairs={{0,8},{8,0},{1,9},{9,1},{2,10},{10,2},{3,11},{11,3},{4,12},{12,4},... | collective-permute-start | bytes 602120 | tf_op jit(solution)/shard_map/blocks/ppermute | solution.py:18
  18.7 0.7 collective-permute-start.6
  19.4 0.7 collective-permute-start.8
  20.1 0.7 collective-permute-start.7
  20.8 0.1 constant_dynamic-update-slice_fusion
  21.0 2.6 %collective-permute-start.5 = (bf16[208,256]{1,0:T(8,128)(2,1)S(1)}, bf16[208,256]{1,0:T(8,128)(2,1)S(1)}, u32[]{:S(2)}, u32[]{:S(2)}) collective-permute-start(bf16[208,256]{1,0:T(8,128)(2,1)S(1)} %get-tuple-element.29), channel_id=1, source_target_pairs={{0,96},{32,0},{64,32},{96,64},{1,97},{33,1},{65,33},{97,65},{2,98}... | collective-permute-start | bytes 319496 | tf_op jit(solution)/shard_map/blocks/ppermute | solution.py:10
  23.6 1.7 %collective-permute-start.3 = (bf16[208,256]{1,0:T(8,128)(2,1)S(1)}, bf16[208,256]{1,0:T(8,128)(2,1)S(1)}, u32[]{:S(2)}, u32[]{:S(2)}) collective-permute-start(bf16[208,256]{1,0:T(8,128)(2,1)S(1)} %get-tuple-element.27), channel_id=1, source_target_pairs={{0,64},{32,96},{64,0},{96,32},{1,65},{33,97},{65,1},{97,33},{2,66}... | collective-permute-start | bytes 319496 | tf_op jit(solution)/shard_map/blocks/ppermute | solution.py:10
  25.3 0.4 constant_dynamic-update-slice_fusion.9
  25.7 2.2 %collective-permute-start.11 = (bf16[128,1024]{1,0:T(8,128)(2,1)S(1)}, bf16[128,1024]{1,0:T(8,128)(2,1)S(1)}, u32[]{:S(2)}, u32[]{:S(2)}) collective-permute-start(bf16[128,1024]{1,0:T(8,128)(2,1)S(1)} %get-tuple-element.11), channel_id=1, source_target_pairs={{0,8},{8,0},{1,9},{9,1},{2,10},{10,2},{3,11},{11,3},{4,12},{12,4},... | collective-permute-start | bytes 786440 | tf_op jit(solution)/shard_map/panel_x/ppermute | solution.py:18
  27.9 0.5 collective-permute-start.12
  28.4 1.2 %collective-permute-start.14 = (bf16[128,1024]{1,0:T(8,128)(2,1)S(1)}, bf16[128,1024]{1,0:T(8,128)(2,1)S(1)}, u32[]{:S(2)}, u32[]{:S(2)}) collective-permute-start(bf16[128,1024]{1,0:T(8,128)(2,1)S(1)} %get-tuple-element.11), channel_id=1, source_target_pairs={{0,32},{32,64},{64,96},{96,0},{1,33},{33,65},{65,97},{97,1},{2,34}... | collective-permute-start | bytes 786440 | tf_op jit(solution)/shard_map/panel_x/ppermute | solution.py:10
  29.6 2.0 %collective-permute-done.4 = bf16[208,256]{1,0:T(8,128)(2,1)S(1)} collective-permute-done((bf16[208,256]{1,0:T(8,128)(2,1)S(1)}, bf16[208,256]{1,0:T(8,128)(2,1)S(1)}, u32[]{:S(2)}, u32[]{:S(2)}) %collective-permute-start.4) | collective-permute-done | bytes 106528 | tf_op jit(solution)/shard_map/blocks/ppermute | solution.py:10
  31.7 11.6 %collective-permute-done.14 = bf16[128,1024]{1,0:T(8,128)(2,1)S(1)} collective-permute-done((bf16[128,1024]{1,0:T(8,128)(2,1)S(1)}, bf16[128,1024]{1,0:T(8,128)(2,1)S(1)}, u32[]{:S(2)}, u32[]{:S(2)}) %collective-permute-start.14) | collective-permute-done | bytes 262176 | tf_op jit(solution)/shard_map/panel_x/ppermute | solution.py:10
  43.3 0.5 collective-permute-start.15
  43.7 0.1 collective-permute-start.17
  43.8 0.5 collective-permute-start.13
  44.4 0.5 collective-permute-done.15
  44.9 0.4 collective-permute-done.17
  45.3 0.5 fusion.1
  45.8 0.0 copy-start
  45.8 0.5 convolution_add_fusion
  46.3 2.8 %collective-permute-start.20 = (bf16[48,1024]{1,0:T(8,128)(2,1)S(1)}, bf16[48,1024]{1,0:T(8,128)(2,1)S(1)}, u32[]{:S(2)}, u32[]{:S(2)}) collective-permute-start(bf16[48,1024]{1,0:T(8,128)(2,1)S(1)} %get-tuple-element.15), channel_id=1, source_target_pairs={{0,144},{16,0},{128,16},{144,128},{1,145},{17,1},{129,17},{145,129... | collective-permute-start | bytes 294920 | tf_op jit(solution)/shard_map/sum_y/ppermute | solution.py:10
  49.1 1.6 %collective-permute-start.18 = (bf16[48,1024]{1,0:T(8,128)(2,1)S(1)}, bf16[48,1024]{1,0:T(8,128)(2,1)S(1)}, u32[]{:S(2)}, u32[]{:S(2)}) collective-permute-start(bf16[48,1024]{1,0:T(8,128)(2,1)S(1)} %get-tuple-element.14), channel_id=1, source_target_pairs={{0,128},{16,144},{128,0},{144,16},{1,129},{17,145},{129,1},{145,17... | collective-permute-start | bytes 294920 | tf_op jit(solution)/shard_map/sum_y/ppermute | solution.py:10
  50.9 0.1 collective-permute-done.20
  51.0 5.6 %collective-permute-done.19 = bf16[48,1024]{1,0:T(8,128)(2,1)S(1)} collective-permute-done((bf16[48,1024]{1,0:T(8,128)(2,1)S(1)}, bf16[48,1024]{1,0:T(8,128)(2,1)S(1)}, u32[]{:S(2)}, u32[]{:S(2)}) %collective-permute-start.19) | collective-permute-done | bytes 98336 | tf_op jit(solution)/shard_map/sum_y/ppermute | solution.py:10
  56.6 2.3 %fusion.53 = (bf16[48,1024]{1,0:T(8,128)(2,1)S(1)}, f32[48,1024]{1,0:T(8,128)}) fusion(f32[1024,1024]{1,0:T(8,128)S(1)} %copy-done, bf16[48,1024]{1,0:T(8,128)(2,1)S(1)} %collective-permute-done.20, bf16[48,1024]{1,0:T(8,128)(2,1)S(1)} %collective-permute-done.19, bf16[48,1024]{1,0:T(8,128)(2,1)S(1)} %collective-permute-done.18, ...), kind=kOutput, calls=%fused_computation.111 | convolution fusion | flops 302481408 | bytes 4981252 | tf_op jit(solution)/shard_map/screen/dot_general | solution.py:103
  58.9 0.2 collective-permute-start.23
  59.1 1.2 %collective-permute-start.22 = (bf16[48,1024]{1,0:T(8,128)(2,1)S(1)}, bf16[48,1024]{1,0:T(8,128)(2,1)S(1)}, u32[]{:S(2)}, u32[]{:S(2)}) collective-permute-start(bf16[48,1024]{1,0:T(8,128)(2,1)S(1)} %get-tuple-element.40), channel_id=1, source_target_pairs={{0,16},{16,128},{128,144},{144,0},{1,17},{17,129},{129,145},{145,1... | collective-permute-start | bytes 294920 | tf_op jit(solution)/shard_map/gather_y/ppermute | solution.py:10
  60.3 0.0 collective-permute-start.21
  60.4 2.0 %collective-permute-done.23 = bf16[48,1024]{1,0:T(8,128)(2,1)S(1)} collective-permute-done((bf16[48,1024]{1,0:T(8,128)(2,1)S(1)}, bf16[48,1024]{1,0:T(8,128)(2,1)S(1)}, u32[]{:S(2)}, u32[]{:S(2)}) %collective-permute-start.23) | collective-permute-done | bytes 98336 | tf_op jit(solution)/shard_map/gather_y/ppermute | solution.py:10
  62.3 1.4 %collective-permute-done.22 = bf16[48,1024]{1,0:T(8,128)(2,1)S(1)} collective-permute-done((bf16[48,1024]{1,0:T(8,128)(2,1)S(1)}, bf16[48,1024]{1,0:T(8,128)(2,1)S(1)}, u32[]{:S(2)}, u32[]{:S(2)}) %collective-permute-start.22) | collective-permute-done | bytes 98336 | tf_op jit(solution)/shard_map/gather_y/ppermute | solution.py:10
  63.8 2.1 %collective-permute-done.21 = bf16[48,1024]{1,0:T(8,128)(2,1)S(1)} collective-permute-done((bf16[48,1024]{1,0:T(8,128)(2,1)S(1)}, bf16[48,1024]{1,0:T(8,128)(2,1)S(1)}, u32[]{:S(2)}, u32[]{:S(2)}) %collective-permute-start.21) | collective-permute-done | bytes 98336 | tf_op jit(solution)/shard_map/gather_y/ppermute | solution.py:10
  65.9 0.9 fusion
  66.8 2.9 %collective-permute-start.24 = (f32[4,128]{1,0:T(4,128)S(1)}, f32[4,128]{1,0:T(4,128)S(1)}, u32[]{:S(2)}, u32[]{:S(2)}) collective-permute-start(f32[4,128]{1,0:T(4,128)S(1)} %bitcast.77), channel_id=1, source_target_pairs={{0,8},{8,0},{1,9},{9,1},{2,10},{10,2},{3,11},{11,3},{4,12},{12,4},... | collective-permute-start | bytes 6152 | tf_op jit(solution)/shard_map/sigma/ppermute | solution.py:18
  69.7 0.8 collective-permute-done.24
  70.5 0.1 select_add_fusion
  70.6 18.7 %all_to_all.9 = f32[32,1,128]{2,1,0:T(1,128)S(1)} all-to-all(f32[32,1,128]{2,1,0:T(1,128)S(1)} %bitcast.74), channel_id=1, replica_groups=mesh['grp'=2,'x'=4,'ylo'=2,'core'=2,'col'=8] {'x','col'}, dimensions={0} | all-to-all | bytes 32768 | tf_op jit(solution)/shard_map/sigma/all_to_all | solution.py:127
  89.2 0.6 reduce_sum.29
  (48 shorter events, 0.5 us)
Async XLA Ops:
  1.6 14.8 %collective-permute-start = (bf16[128,1024]{1,0:T(8,128)(2,1)S(1)}, bf16[128,1024]{1,0:T(8,128)(2,1)S(1)}, u32[]{:S(2)}, u32[]{:S(2)}) collective-permute-start(bf16[128,1024]{1,0:T(8,128)(2,1)S(1)} %slice.52), channel_id=1, source_target_pairs={{0,3},{8,11},{16,19},{24,27},{32,35},{40,43},{48,51},{56,59},{64,6... | collective-permute-start | bytes 786440 | tf_op jit(solution)/shard_map/panel_z/ppermute | solution.py:14
  8.7 7.7 %collective-permute-start.1 = (bf16[128,1024]{1,0:T(8,128)(2,1)S(1)}, bf16[128,1024]{1,0:T(8,128)(2,1)S(1)}, u32[]{:S(2)}, u32[]{:S(2)}) collective-permute-start(bf16[128,1024]{1,0:T(8,128)(2,1)S(1)} %slice.52), channel_id=1, source_target_pairs={{0,6},{8,14},{16,22},{24,30},{32,38},{40,46},{48,54},{56,62},{64,7... | collective-permute-start | bytes 786440 | tf_op jit(solution)/shard_map/panel_z/ppermute | solution.py:14
  11.1 9.9 %collective-permute-start.9 = (bf16[128,1024]{1,0:T(8,128)(2,1)S(1)}, bf16[128,1024]{1,0:T(8,128)(2,1)S(1)}, u32[]{:S(2)}, u32[]{:S(2)}) collective-permute-start(bf16[128,1024]{1,0:T(8,128)(2,1)S(1)} %slice.52), channel_id=1, source_target_pairs={{0,1},{8,9},{16,17},{24,25},{32,33},{40,41},{48,49},{56,57},{64,65... | collective-permute-start | bytes 786440 | tf_op jit(solution)/shard_map/panel_z/ppermute | solution.py:14
  12.4 11.2 %collective-permute-start.10 = (bf16[128,1024]{1,0:T(8,128)(2,1)S(1)}, bf16[128,1024]{1,0:T(8,128)(2,1)S(1)}, u32[]{:S(2)}, u32[]{:S(2)}) collective-permute-start(bf16[128,1024]{1,0:T(8,128)(2,1)S(1)} %slice.52), channel_id=1, source_target_pairs={{0,7},{8,15},{16,23},{24,31},{32,39},{40,47},{48,55},{56,63},{64,7... | collective-permute-start | bytes 786440 | tf_op jit(solution)/shard_map/panel_z/ppermute | solution.py:14
  15.8 9.5 %copy-start.1 = (bf16[128,1536]{1,0:T(8,128)(2,1)S(1)}, bf16[128,1536]{1,0:T(8,128)(2,1)}, u32[]{:S(2)}) copy-start(bf16[128,1536]{1,0:T(8,128)(2,1)} %param.3) | copy-start | bytes 1179652
  16.4 3.7 %collective-permute-start.2 = (bf16[784,128]{1,0:T(8,128)(2,1)S(1)}, bf16[784,128]{1,0:T(8,128)(2,1)S(1)}, u32[]{:S(2)}, u32[]{:S(2)}) collective-permute-start(bf16[784,128]{1,0:T(8,128)(2,1)S(1)} %concatenate.49), channel_id=1, source_target_pairs={{0,8},{8,0},{1,9},{9,1},{2,10},{10,2},{3,11},{11,3},{4,12},{12,4},... | collective-permute-start | bytes 602120 | tf_op jit(solution)/shard_map/blocks/ppermute | solution.py:18
  18.7 4.9 %collective-permute-start.6 = (bf16[128,1024]{1,0:T(8,128)(2,1)S(1)}, bf16[128,1024]{1,0:T(8,128)(2,1)S(1)}, u32[]{:S(2)}, u32[]{:S(2)}) collective-permute-start(bf16[128,1024]{1,0:T(8,128)(2,1)S(1)} %collective-permute-done), channel_id=1, source_target_pairs={{3,4},{11,12},{19,20},{27,28},{35,36},{43,44},{51,52},{59,60},{67,... | collective-permute-start | bytes 786440 | tf_op jit(solution)/shard_map/panel_z/ppermute | solution.py:14
  19.4 5.9 %collective-permute-start.8 = (bf16[128,1024]{1,0:T(8,128)(2,1)S(1)}, bf16[128,1024]{1,0:T(8,128)(2,1)S(1)}, u32[]{:S(2)}, u32[]{:S(2)}) collective-permute-start(bf16[128,1024]{1,0:T(8,128)(2,1)S(1)} %collective-permute-done), channel_id=1, source_target_pairs={{3,2},{11,10},{19,18},{27,26},{35,34},{43,42},{51,50},{59,58},{67,... | collective-permute-start | bytes 786440 | tf_op jit(solution)/shard_map/panel_z/ppermute | solution.py:14
  20.1 5.2 %collective-permute-start.7 = (bf16[128,1024]{1,0:T(8,128)(2,1)S(1)}, bf16[128,1024]{1,0:T(8,128)(2,1)S(1)}, u32[]{:S(2)}, u32[]{:S(2)}) collective-permute-start(bf16[128,1024]{1,0:T(8,128)(2,1)S(1)} %collective-permute-done.1), channel_id=1, source_target_pairs={{6,5},{14,13},{22,21},{30,29},{38,37},{46,45},{54,53},{62,61},{70,... | collective-permute-start | bytes 786440 | tf_op jit(solution)/shard_map/panel_z/ppermute | solution.py:14
  21.0 7.4 %collective-permute-start.5 = (bf16[208,256]{1,0:T(8,128)(2,1)S(1)}, bf16[208,256]{1,0:T(8,128)(2,1)S(1)}, u32[]{:S(2)}, u32[]{:S(2)}) collective-permute-start(bf16[208,256]{1,0:T(8,128)(2,1)S(1)} %get-tuple-element.29), channel_id=1, source_target_pairs={{0,96},{32,0},{64,32},{96,64},{1,97},{33,1},{65,33},{97,65},{2,98}... | collective-permute-start | bytes 319496 | tf_op jit(solution)/shard_map/blocks/ppermute | solution.py:10
  23.6 8.0 %collective-permute-start.4 = (bf16[208,256]{1,0:T(8,128)(2,1)S(1)}, bf16[208,256]{1,0:T(8,128)(2,1)S(1)}, u32[]{:S(2)}, u32[]{:S(2)}) collective-permute-start(bf16[208,256]{1,0:T(8,128)(2,1)S(1)} %get-tuple-element.28), channel_id=1, source_target_pairs={{0,32},{32,64},{64,96},{96,0},{1,33},{33,65},{65,97},{97,1},{2,34}... | collective-permute-start | bytes 319496 | tf_op jit(solution)/shard_map/blocks/ppermute | solution.py:10
  23.6 8.0 %collective-permute-start.3 = (bf16[208,256]{1,0:T(8,128)(2,1)S(1)}, bf16[208,256]{1,0:T(8,128)(2,1)S(1)}, u32[]{:S(2)}, u32[]{:S(2)}) collective-permute-start(bf16[208,256]{1,0:T(8,128)(2,1)S(1)} %get-tuple-element.27), channel_id=1, source_target_pairs={{0,64},{32,96},{64,0},{96,32},{1,65},{33,97},{65,1},{97,33},{2,66}... | collective-permute-start | bytes 319496 | tf_op jit(solution)/shard_map/blocks/ppermute | solution.py:10
  25.7 18.7 %collective-permute-start.11 = (bf16[128,1024]{1,0:T(8,128)(2,1)S(1)}, bf16[128,1024]{1,0:T(8,128)(2,1)S(1)}, u32[]{:S(2)}, u32[]{:S(2)}) collective-permute-start(bf16[128,1024]{1,0:T(8,128)(2,1)S(1)} %get-tuple-element.11), channel_id=1, source_target_pairs={{0,8},{8,0},{1,9},{9,1},{2,10},{10,2},{3,11},{11,3},{4,12},{12,4},... | collective-permute-start | bytes 786440 | tf_op jit(solution)/shard_map/panel_x/ppermute | solution.py:18
  27.9 16.0 %collective-permute-start.12 = (bf16[128,1024]{1,0:T(8,128)(2,1)S(1)}, bf16[128,1024]{1,0:T(8,128)(2,1)S(1)}, u32[]{:S(2)}, u32[]{:S(2)}) collective-permute-start(bf16[128,1024]{1,0:T(8,128)(2,1)S(1)} %get-tuple-element.11), channel_id=1, source_target_pairs={{0,64},{32,96},{64,0},{96,32},{1,65},{33,97},{65,1},{97,33},{2,66}... | collective-permute-start | bytes 786440 | tf_op jit(solution)/shard_map/panel_x/ppermute | solution.py:10
  28.4 14.9 %collective-permute-start.14 = (bf16[128,1024]{1,0:T(8,128)(2,1)S(1)}, bf16[128,1024]{1,0:T(8,128)(2,1)S(1)}, u32[]{:S(2)}, u32[]{:S(2)}) collective-permute-start(bf16[128,1024]{1,0:T(8,128)(2,1)S(1)} %get-tuple-element.11), channel_id=1, source_target_pairs={{0,32},{32,64},{64,96},{96,0},{1,33},{33,65},{65,97},{97,1},{2,34}... | collective-permute-start | bytes 786440 | tf_op jit(solution)/shard_map/panel_x/ppermute | solution.py:10
  31.6 12.1 %collective-permute-start.16 = (bf16[128,1024]{1,0:T(8,128)(2,1)S(1)}, bf16[128,1024]{1,0:T(8,128)(2,1)S(1)}, u32[]{:S(2)}, u32[]{:S(2)}) collective-permute-start(bf16[128,1024]{1,0:T(8,128)(2,1)S(1)} %get-tuple-element.11), channel_id=1, source_target_pairs={{0,96},{32,0},{64,32},{96,64},{1,97},{33,1},{65,33},{97,65},{2,98}... | collective-permute-start | bytes 786440 | tf_op jit(solution)/shard_map/panel_x/ppermute | solution.py:10
  43.3 1.6 %collective-permute-start.15 = (bf16[128,1024]{1,0:T(8,128)(2,1)S(1)}, bf16[128,1024]{1,0:T(8,128)(2,1)S(1)}, u32[]{:S(2)}, u32[]{:S(2)}) collective-permute-start(bf16[128,1024]{1,0:T(8,128)(2,1)S(1)} %collective-permute-done.14), channel_id=1, source_target_pairs={{0,8},{8,0},{1,9},{9,1},{2,10},{10,2},{3,11},{11,3},{4,12},{12,4},... | collective-permute-start | bytes 786440 | tf_op jit(solution)/shard_map/panel_x/ppermute | solution.py:18
  43.7 1.5 %collective-permute-start.17 = (bf16[128,1024]{1,0:T(8,128)(2,1)S(1)}, bf16[128,1024]{1,0:T(8,128)(2,1)S(1)}, u32[]{:S(2)}, u32[]{:S(2)}) collective-permute-start(bf16[128,1024]{1,0:T(8,128)(2,1)S(1)} %collective-permute-done.16), channel_id=1, source_target_pairs={{0,8},{8,0},{1,9},{9,1},{2,10},{10,2},{3,11},{11,3},{4,12},{12,4},... | collective-permute-start | bytes 786440 | tf_op jit(solution)/shard_map/panel_x/ppermute | solution.py:18
  43.8 1.9 %collective-permute-start.13 = (bf16[128,1024]{1,0:T(8,128)(2,1)S(1)}, bf16[128,1024]{1,0:T(8,128)(2,1)S(1)}, u32[]{:S(2)}, u32[]{:S(2)}) collective-permute-start(bf16[128,1024]{1,0:T(8,128)(2,1)S(1)} %collective-permute-done.12), channel_id=1, source_target_pairs={{0,8},{8,0},{1,9},{9,1},{2,10},{10,2},{3,11},{11,3},{4,12},{12,4},... | collective-permute-start | bytes 786440 | tf_op jit(solution)/shard_map/panel_x/ppermute | solution.py:18
  45.8 10.8 %copy-start = (f32[1024,1024]{1,0:T(8,128)S(1)}, f32[1024,1024]{1,0:T(8,128)}, u32[]{:S(2)}) copy-start(f32[1024,1024]{1,0:T(8,128)} %param.5) | copy-start | bytes 12582916
  46.3 4.6 %collective-permute-start.20 = (bf16[48,1024]{1,0:T(8,128)(2,1)S(1)}, bf16[48,1024]{1,0:T(8,128)(2,1)S(1)}, u32[]{:S(2)}, u32[]{:S(2)}) collective-permute-start(bf16[48,1024]{1,0:T(8,128)(2,1)S(1)} %get-tuple-element.15), channel_id=1, source_target_pairs={{0,144},{16,0},{128,16},{144,128},{1,145},{17,1},{129,17},{145,129... | collective-permute-start | bytes 294920 | tf_op jit(solution)/shard_map/sum_y/ppermute | solution.py:10
  49.1 7.4 %collective-permute-start.19 = (bf16[48,1024]{1,0:T(8,128)(2,1)S(1)}, bf16[48,1024]{1,0:T(8,128)(2,1)S(1)}, u32[]{:S(2)}, u32[]{:S(2)}) collective-permute-start(bf16[48,1024]{1,0:T(8,128)(2,1)S(1)} %get-tuple-element.16), channel_id=1, source_target_pairs={{0,16},{16,128},{128,144},{144,0},{1,17},{17,129},{129,145},{145,1... | collective-permute-start | bytes 294920 | tf_op jit(solution)/shard_map/sum_y/ppermute | solution.py:10
  49.1 7.4 %collective-permute-start.18 = (bf16[48,1024]{1,0:T(8,128)(2,1)S(1)}, bf16[48,1024]{1,0:T(8,128)(2,1)S(1)}, u32[]{:S(2)}, u32[]{:S(2)}) collective-permute-start(bf16[48,1024]{1,0:T(8,128)(2,1)S(1)} %get-tuple-element.14), channel_id=1, source_target_pairs={{0,128},{16,144},{128,0},{144,16},{1,129},{17,145},{129,1},{145,17... | collective-permute-start | bytes 294920 | tf_op jit(solution)/shard_map/sum_y/ppermute | solution.py:10
  58.9 3.5 %collective-permute-start.23 = (bf16[48,1024]{1,0:T(8,128)(2,1)S(1)}, bf16[48,1024]{1,0:T(8,128)(2,1)S(1)}, u32[]{:S(2)}, u32[]{:S(2)}) collective-permute-start(bf16[48,1024]{1,0:T(8,128)(2,1)S(1)} %get-tuple-element.40), channel_id=1, source_target_pairs={{0,144},{16,0},{128,16},{144,128},{1,145},{17,1},{129,17},{145,129... | collective-permute-start | bytes 294920 | tf_op jit(solution)/shard_map/gather_y/ppermute | solution.py:10
  59.1 4.7 %collective-permute-start.22 = (bf16[48,1024]{1,0:T(8,128)(2,1)S(1)}, bf16[48,1024]{1,0:T(8,128)(2,1)S(1)}, u32[]{:S(2)}, u32[]{:S(2)}) collective-permute-start(bf16[48,1024]{1,0:T(8,128)(2,1)S(1)} %get-tuple-element.40), channel_id=1, source_target_pairs={{0,16},{16,128},{128,144},{144,0},{1,17},{17,129},{129,145},{145,1... | collective-permute-start | bytes 294920 | tf_op jit(solution)/shard_map/gather_y/ppermute | solution.py:10
  60.3 5.6 %collective-permute-start.21 = (bf16[48,1024]{1,0:T(8,128)(2,1)S(1)}, bf16[48,1024]{1,0:T(8,128)(2,1)S(1)}, u32[]{:S(2)}, u32[]{:S(2)}) collective-permute-start(bf16[48,1024]{1,0:T(8,128)(2,1)S(1)} %get-tuple-element.40), channel_id=1, source_target_pairs={{0,128},{16,144},{128,0},{144,16},{1,129},{17,145},{129,1},{145,17... | collective-permute-start | bytes 294920 | tf_op jit(solution)/shard_map/gather_y/ppermute | solution.py:10
  66.8 3.7 %collective-permute-start.24 = (f32[4,128]{1,0:T(4,128)S(1)}, f32[4,128]{1,0:T(4,128)S(1)}, u32[]{:S(2)}, u32[]{:S(2)}) collective-permute-start(f32[4,128]{1,0:T(4,128)S(1)} %bitcast.77), channel_id=1, source_target_pairs={{0,8},{8,0},{1,9},{9,1},{2,10},{10,2},{3,11},{11,3},{4,12},{12,4},... | collective-permute-start | bytes 6152 | tf_op jit(solution)/shard_map/sigma/ppermute | solution.py:18

commit v4 on v3

--- a/solution.py
+++ b/solution.py
@@ -27,6 +27,11 @@
     return out
 
 
+def two_parts(value):
+    high = lax.reduce_precision(value, 8, 7)
+    return high.astype(LOW), (value - high).astype(LOW)
+
+
 def body(orbital_b, gaps, block_inverse):
     own, width = orbital_b.shape
     panel = block_inverse.shape[0]
@@ -37,10 +42,8 @@
 
     with jax.named_scope("panel_z"):
         piece = orbital_b[:, :panel]
+        far_b = along_z(piece, (0, 6))
         far_a = along_z(piece, (0, 3))
-        far_b = along_z(piece, (0, 6))
-        near_a = along_z(piece, (0, 1))
-        near_b = along_z(piece, (0, 7))
 
     with jax.named_scope("blocks"):
         weight = 2.0 * gaps / (gaps * gaps + 1.0)
@@ -55,9 +58,16 @@
         mine, sent, far_a, far_b = lax.optimization_barrier((mine, sent, far_a, far_b))
 
     with jax.named_scope("panel_z"):
-        next_a = along_z(far_a, (3, 4))
-        next_b = along_z(far_b, (6, 5))
-        next_c = along_z(far_a, (3, 2))
+        held = jnp.where(z == 3, far_a, jnp.where(z == 6, far_b, piece))
+        near_a = along_z(held, (0, 1), (3, 4), (6, 5))
+        near_b = along_z(held, (0, 7), (3, 2))
+        inv_high, inv_rest = two_parts(block_inverse)
+        near_a, near_b, inv_high, inv_rest = lax.optimization_barrier(
+            (near_a, near_b, inv_high, inv_rest)
+        )
+        held = jnp.where((z == 1) | (z == 4) | (z == 5), near_a, held)
+        held = jnp.where((z == 7) | (z == 2), near_b, held)
+
     with jax.named_scope("blocks"):
         pair = jnp.concatenate([mine, swap(sent)], axis=1)
         blocks = pair[:-16].reshape(2, nx, 2 * count, 2 * own)
@@ -71,11 +81,6 @@
         )
         weight = jnp.sum(factors[-16:-13].astype(F32), axis=0)
         factors = factors[:-16]
-
-    with jax.named_scope("panel_z"):
-        held = jnp.where(z == 3, far_a, jnp.where(z == 6, far_b, piece))
-        held = jnp.where(z == 1, near_a, jnp.where(z == 7, near_b, held))
-        held = jnp.where(z == 4, next_a, jnp.where(z == 5, next_b, jnp.where(z == 2, next_c, held)))
 
     with jax.named_scope("panel_x"):
         got = [held] + [shift(held, X, nx, k) for k in steps[1:]]
@@ -100,9 +105,13 @@
     with jax.named_scope("screen"):
         place = z * width + lax.axis_index(PLANE) * count
         unit = (lax.iota(jnp.int32, count)[:, None] + place) == lax.iota(jnp.int32, panel)[None, :]
+        total = unit.astype(F32) + total
+        high, rest = two_parts(total)
         screened = jnp.dot(
-            unit.astype(F32) + total, block_inverse, precision=lax.Precision.HIGH
+            jnp.concatenate([high, rest], axis=0), inv_high, preferred_element_type=F32
         )
+        screened = screened[:count] + screened[count:]
+        screened = screened + jnp.dot(high, inv_rest, preferred_element_type=F32)
 
     with jax.named_scope("gather_y"):
         low = screened.astype(LOW)

time: 90.1 us -> 86.2 us (0.957)
  waiting for transfers between devices: 26.5 us -> 9.32 us
  starting transfers between devices: 34.4 us -> 46.2 us
  other arithmetic: 1.79 us -> 6.19 us
  blocking collectives: 18.7 us -> 15.8 us
    ppermute x12, waiting for transfers between devices: 24.8 us -> 7.79 us  [shift(): lax.ppermute(value, axis, [(i, (i + step) % size) for i in range(size)])]
    ppermute x12, starting transfers between devices: 12 us -> 19.6 us  [shift(): lax.ppermute(value, axis, [(i, (i + step) % size) for i in range(size)])]
    ppermute x6, starting transfers between devices: 8.35 us -> 13.8 us  [swap(): return lax.ppermute(value, CORE, [(0, 1), (1, 0)])]
    convert_element_type x0 -> x2, other arithmetic: none -> 4.58 us  [two_parts(): return (high.astype(LOW), (value - high).astype(LOW))]
    all_to_all x1, blocking collectives: 18.7 us -> 15.8 us  [body(): terms = lax.all_to_all(copies, (X, Z), 0, 0, tiled=True)]
    ppermute x7 -> x4, starting transfers between devices: 14.1 us -> 12.8 us  [along_z(): return lax.ppermute(value, Z, pairs)]
    dot_general x1 -> x2, matrix products: 2.29 us -> 1.64 us  [the longest x1 1.16 us: body(): screened = screened + jnp.dot(high, inv_rest, preferred_element_type=F32)]
  transfers between devices with their start and end apart: 25 -> 22, of which waited for: 10 -> 9; matrix products, arithmetic and copies ran while one was open for 4% -> 9% of each run, Pallas kernels for 0% -> 0%
where the time goes in v4:
time: 86.2 us; the launch traced here: 85.9 us
  starting transfers between devices  46.2 us (54%)
  blocking collectives  15.8 us (18%)
  waiting for transfers between devices  9.32 us (11%)
  other arithmetic  6.19 us (7%)
  local copies, waits for them, and re-layouts  3.79 us (4%)
  matrix products  3.46 us (4%)
  between operations  1.22 us (1%)
    ppermute x12, starting transfers between devices, shift(): lax.ppermute(value, axis, [(i, (i + step) % size) for i in range(size)])  19.6 us
    all_to_all x1, blocking collectives, body(): terms = lax.all_to_all(copies, (X, Z), 0, 0, tiled=True)  15.8 us
    ppermute x6, starting transfers between devices, swap(): return lax.ppermute(value, CORE, [(0, 1), (1, 0)])  13.8 us
    ppermute x4, starting transfers between devices, along_z(): return lax.ppermute(value, Z, pairs)  12.8 us
    ppermute x12, waiting for transfers between devices, shift(): lax.ppermute(value, axis, [(i, (i + step) % size) for i in range(size)])  7.79 us
    convert_element_type x2, other arithmetic, two_parts(): return (high.astype(LOW), (value - high).astype(LOW))  4.58 us
  transfers between devices with their start and end apart: 22, of which 9 were waited for; matrix products, arithmetic and copies ran while one was open for 9% of the time, Pallas kernels for 0%

profile of v4, /device:TPU:1, one launch (start us, length us, event | category | flops | bytes accessed | tf_op | source)
XLA Modules:
  0.0 85.9 jit_solution(1531871426708142138)
XLA Ops:
  0.6 1.7 %slice.58 = bf16[128,1024]{1,0:T(8,128)(2,1)} slice(bf16[128,1536]{1,0:T(8,128)(2,1)} %param.3), slice={[0:128], [0:1024]} | slice | bytes 524288 | tf_op jit(solution)/shard_map/panel_z/slice | solution.py:44
  2.3 7.1 %collective-permute-start = (bf16[128,1024]{1,0:T(8,128)(2,1)}, bf16[128,1024]{1,0:T(8,128)(2,1)S(1)}, u32[]{:S(2)}, u32[]{:S(2)}) collective-permute-start(bf16[128,1024]{1,0:T(8,128)(2,1)} %slice.58), channel_id=1, source_target_pairs={{0,3},{8,11},{16,19},{24,27},{32,35},{40,43},{48,51},{56,59},{64,6... | collective-permute-start | bytes 786440 | tf_op jit(solution)/shard_map/panel_z/ppermute | solution.py:14
  9.4 3.1 %collective-permute-start.1 = (bf16[128,1024]{1,0:T(8,128)(2,1)}, bf16[128,1024]{1,0:T(8,128)(2,1)}, u32[]{:S(2)}, u32[]{:S(2)}) collective-permute-start(bf16[128,1024]{1,0:T(8,128)(2,1)} %slice.58), channel_id=1, source_target_pairs={{0,6},{8,14},{16,22},{24,30},{32,38},{40,46},{48,54},{56,62},{64,7... | collective-permute-start | bytes 786440 | tf_op jit(solution)/shard_map/panel_z/ppermute | solution.py:14
  12.5 1.2 %copy.7 = bf16[128,1536]{0,1:T(8,128)(2,1)S(1)} copy(bf16[128,1536]{1,0:T(8,128)(2,1)} %param.3) | data formatting | bytes 786432 | tf_op args[0]
  13.7 0.7 fusion.43
  14.4 4.5 %fusion = (bf16[1024,1024]{1,0:T(8,128)(2,1)S(1)}, bf16[1024,1024]{1,0:T(8,128)(2,1)}) fusion(f32[1024,1024]{1,0:T(8,128)} %param.5), kind=kLoop, calls=%fused_computation.2 | loop fusion | flops 4194304 | bytes 8388608 | tf_op jit(solution)/shard_map/panel_z/convert_element_type | solution.py:32
  19.0 0.2 concatenate.52
  19.3 0.2 concatenate.51
  19.7 1.0 %collective-permute-start.2 = (bf16[784,128]{1,0:T(8,128)(2,1)S(1)}, bf16[784,128]{1,0:T(8,128)(2,1)S(1)}, u32[]{:S(2)}, u32[]{:S(2)}) collective-permute-start(bf16[784,128]{1,0:T(8,128)(2,1)S(1)} %concatenate.52), channel_id=1, source_target_pairs={{0,8},{8,0},{1,9},{9,1},{2,10},{10,2},{3,11},{11,3},{4,12},{12,4},... | collective-permute-start | bytes 602120 | tf_op jit(solution)/shard_map/blocks/ppermute | solution.py:18
  20.8 1.3 %collective-permute-start.6 = (bf16[128,1024]{1,0:T(8,128)(2,1)S(1)}, bf16[128,1024]{1,0:T(8,128)(2,1)S(1)}, u32[]{:S(2)}, u32[]{:S(2)}) collective-permute-start(bf16[128,1024]{1,0:T(8,128)(2,1)S(1)} %select_select_fusion.1), channel_id=1, source_target_pairs={{0,1},{3,4},{6,5},{8,9},{11,12},{14,13},{16,17},{19,20},{22,21},{2... | collective-permute-start | bytes 786440 | tf_op jit(solution)/shard_map/panel_z/ppermute | solution.py:14
  22.1 1.3 %collective-permute-start.7 = (bf16[128,1024]{1,0:T(8,128)(2,1)S(1)}, bf16[128,1024]{1,0:T(8,128)(2,1)S(1)}, u32[]{:S(2)}, u32[]{:S(2)}) collective-permute-start(bf16[128,1024]{1,0:T(8,128)(2,1)S(1)} %select_select_fusion.1), channel_id=1, source_target_pairs={{0,7},{3,2},{8,15},{11,10},{16,23},{19,18},{24,31},{27,26},{32,39}... | collective-permute-start | bytes 786440 | tf_op jit(solution)/shard_map/panel_z/ppermute | solution.py:14
  23.4 0.1 constant_dynamic-update-slice_fusion
  23.6 2.8 %collective-permute-start.3 = (bf16[208,256]{1,0:T(8,128)(2,1)S(1)}, bf16[208,256]{1,0:T(8,128)(2,1)S(1)}, u32[]{:S(2)}, u32[]{:S(2)}) collective-permute-start(bf16[208,256]{1,0:T(8,128)(2,1)S(1)} %get-tuple-element.39), channel_id=1, source_target_pairs={{0,64},{32,96},{64,0},{96,32},{1,65},{33,97},{65,1},{97,33},{2,66}... | collective-permute-start | bytes 319496 | tf_op jit(solution)/shard_map/blocks/ppermute | solution.py:10
  26.5 0.3 collective-permute-start.4
  26.8 2.4 %collective-permute-start.5 = (bf16[208,256]{1,0:T(8,128)(2,1)S(1)}, bf16[208,256]{1,0:T(8,128)(2,1)S(1)}, u32[]{:S(2)}, u32[]{:S(2)}) collective-permute-start(bf16[208,256]{1,0:T(8,128)(2,1)S(1)} %get-tuple-element.41), channel_id=1, source_target_pairs={{0,96},{32,0},{64,32},{96,64},{1,97},{33,1},{65,33},{97,65},{2,98}... | collective-permute-start | bytes 319496 | tf_op jit(solution)/shard_map/blocks/ppermute | solution.py:10
  29.1 0.1 collective-permute-done.7
  29.2 0.1 constant_dynamic-update-slice_fusion.9
  29.4 1.3 %collective-permute-start.11 = (bf16[128,1024]{1,0:T(8,128)(2,1)S(1)}, bf16[128,1024]{1,0:T(8,128)(2,1)S(1)}, u32[]{:S(2)}, u32[]{:S(2)}) collective-permute-start(bf16[128,1024]{1,0:T(8,128)(2,1)S(1)} %get-tuple-element.19), channel_id=1, source_target_pairs={{0,32},{32,64},{64,96},{96,0},{1,33},{33,65},{65,97},{97,1},{2,34}... | collective-permute-start | bytes 786440 | tf_op jit(solution)/shard_map/panel_x/ppermute | solution.py:10
  30.7 1.5 %collective-permute-start.13 = (bf16[128,1024]{1,0:T(8,128)(2,1)S(1)}, bf16[128,1024]{1,0:T(8,128)(2,1)S(1)}, u32[]{:S(2)}, u32[]{:S(2)}) collective-permute-start(bf16[128,1024]{1,0:T(8,128)(2,1)S(1)} %get-tuple-element.19), channel_id=1, source_target_pairs={{0,96},{32,0},{64,32},{96,64},{1,97},{33,1},{65,33},{97,65},{2,98}... | collective-permute-start | bytes 786440 | tf_op jit(solution)/shard_map/panel_x/ppermute | solution.py:10
  32.2 1.5 %collective-permute-start.9 = (bf16[128,1024]{1,0:T(8,128)(2,1)S(1)}, bf16[128,1024]{1,0:T(8,128)(2,1)S(1)}, u32[]{:S(2)}, u32[]{:S(2)}) collective-permute-start(bf16[128,1024]{1,0:T(8,128)(2,1)S(1)} %get-tuple-element.19), channel_id=1, source_target_pairs={{0,64},{32,96},{64,0},{96,32},{1,65},{33,97},{65,1},{97,33},{2,66}... | collective-permute-start | bytes 786440 | tf_op jit(solution)/shard_map/panel_x/ppermute | solution.py:10
  33.7 1.5 %collective-permute-start.8 = (bf16[128,1024]{1,0:T(8,128)(2,1)S(1)}, bf16[128,1024]{1,0:T(8,128)(2,1)S(1)}, u32[]{:S(2)}, u32[]{:S(2)}) collective-permute-start(bf16[128,1024]{1,0:T(8,128)(2,1)S(1)} %get-tuple-element.19), channel_id=1, source_target_pairs={{0,8},{8,0},{1,9},{9,1},{2,10},{10,2},{3,11},{11,3},{4,12},{12,4},... | collective-permute-start | bytes 786440 | tf_op jit(solution)/shard_map/panel_x/ppermute | solution.py:18
  35.2 2.5 %collective-permute-done.11 = bf16[128,1024]{1,0:T(8,128)(2,1)S(1)} collective-permute-done((bf16[128,1024]{1,0:T(8,128)(2,1)S(1)}, bf16[128,1024]{1,0:T(8,128)(2,1)S(1)}, u32[]{:S(2)}, u32[]{:S(2)}) %collective-permute-start.11) | collective-permute-done | bytes 262176 | tf_op jit(solution)/shard_map/panel_x/ppermute | solution.py:10
  37.7 1.8 %collective-permute-start.12 = (bf16[128,1024]{1,0:T(8,128)(2,1)S(1)}, bf16[128,1024]{1,0:T(8,128)(2,1)S(1)}, u32[]{:S(2)}, u32[]{:S(2)}) collective-permute-start(bf16[128,1024]{1,0:T(8,128)(2,1)S(1)} %collective-permute-done.11), channel_id=1, source_target_pairs={{0,8},{8,0},{1,9},{9,1},{2,10},{10,2},{3,11},{11,3},{4,12},{12,4},... | collective-permute-start | bytes 786440 | tf_op jit(solution)/shard_map/panel_x/ppermute | solution.py:18
  39.5 4.8 %collective-permute-start.14 = (bf16[128,1024]{1,0:T(8,128)(2,1)S(1)}, bf16[128,1024]{1,0:T(8,128)(2,1)S(1)}, u32[]{:S(2)}, u32[]{:S(2)}) collective-permute-start(bf16[128,1024]{1,0:T(8,128)(2,1)S(1)} %collective-permute-done.13), channel_id=1, source_target_pairs={{0,8},{8,0},{1,9},{9,1},{2,10},{10,2},{3,11},{11,3},{4,12},{12,4},... | collective-permute-start | bytes 786440 | tf_op jit(solution)/shard_map/panel_x/ppermute | solution.py:18
  44.3 0.2 collective-permute-done.9
  44.5 1.5 %collective-permute-start.10 = (bf16[128,1024]{1,0:T(8,128)(2,1)S(1)}, bf16[128,1024]{1,0:T(8,128)(2,1)S(1)}, u32[]{:S(2)}, u32[]{:S(2)}) collective-permute-start(bf16[128,1024]{1,0:T(8,128)(2,1)S(1)} %collective-permute-done.9), channel_id=1, source_target_pairs={{0,8},{8,0},{1,9},{9,1},{2,10},{10,2},{3,11},{11,3},{4,12},{12,4},... | collective-permute-start | bytes 786440 | tf_op jit(solution)/shard_map/panel_x/ppermute | solution.py:18
  46.1 0.5 fusion.2
  46.6 0.6 collective-permute-done.10
  47.2 0.5 convolution_add_fusion
  47.7 3.0 %collective-permute-start.15 = (bf16[48,1024]{1,0:T(8,128)(2,1)S(1)}, bf16[48,1024]{1,0:T(8,128)(2,1)S(1)}, u32[]{:S(2)}, u32[]{:S(2)}) collective-permute-start(bf16[48,1024]{1,0:T(8,128)(2,1)S(1)} %get-tuple-element.26), channel_id=1, source_target_pairs={{0,128},{16,144},{128,0},{144,16},{1,129},{17,145},{129,1},{145,17... | collective-permute-start | bytes 294920 | tf_op jit(solution)/shard_map/sum_y/ppermute | solution.py:10
  50.7 0.4 collective-permute-start.16
  51.1 2.3 %collective-permute-start.17 = (bf16[48,1024]{1,0:T(8,128)(2,1)S(1)}, bf16[48,1024]{1,0:T(8,128)(2,1)S(1)}, u32[]{:S(2)}, u32[]{:S(2)}) collective-permute-start(bf16[48,1024]{1,0:T(8,128)(2,1)S(1)} %get-tuple-element.27), channel_id=1, source_target_pairs={{0,144},{16,0},{128,16},{144,128},{1,145},{17,1},{129,17},{145,129... | collective-permute-start | bytes 294920 | tf_op jit(solution)/shard_map/sum_y/ppermute | solution.py:10
  53.5 1.9 %collective-permute-done.16 = bf16[48,1024]{1,0:T(8,128)(2,1)S(1)} collective-permute-done((bf16[48,1024]{1,0:T(8,128)(2,1)S(1)}, bf16[48,1024]{1,0:T(8,128)(2,1)S(1)}, u32[]{:S(2)}, u32[]{:S(2)}) %collective-permute-start.16) | collective-permute-done | bytes 98336 | tf_op jit(solution)/shard_map/sum_y/ppermute | solution.py:10
  55.4 0.4 collective-permute-done.17
  55.8 0.1 fusion.26
  55.9 0.5 fusion.29
  56.4 1.2 %fusion.51 = (bf16[48,1024]{1,0:T(8,128)(2,1)S(1)}, f32[48,1024]{1,0:T(8,128)}) fusion(bf16[48,1024]{1,0:T(8,128)(2,1)S(1)} %get-tuple-element.25, bf16[1024,1024]{1,0:T(8,128)(2,1)S(1)} %get-tuple-element.17, f32[96,1024]{1,0:T(8,128)S(1)} %fusion.29), kind=kOutput, calls=%fused_computation.117 | convolution fusion | flops 100810752 | bytes 2883584 | tf_op jit(solution)/shard_map/screen/dot_general | solution.py:114
  57.5 1.5 %collective-permute-start.18 = (bf16[48,1024]{1,0:T(8,128)(2,1)S(1)}, bf16[48,1024]{1,0:T(8,128)(2,1)S(1)}, u32[]{:S(2)}, u32[]{:S(2)}) collective-permute-start(bf16[48,1024]{1,0:T(8,128)(2,1)S(1)} %get-tuple-element.52), channel_id=1, source_target_pairs={{0,128},{16,144},{128,0},{144,16},{1,129},{17,145},{129,1},{145,17... | collective-permute-start | bytes 294920 | tf_op jit(solution)/shard_map/gather_y/ppermute | solution.py:10
  59.0 1.5 %collective-permute-start.19 = (bf16[48,1024]{1,0:T(8,128)(2,1)S(1)}, bf16[48,1024]{1,0:T(8,128)(2,1)S(1)}, u32[]{:S(2)}, u32[]{:S(2)}) collective-permute-start(bf16[48,1024]{1,0:T(8,128)(2,1)S(1)} %get-tuple-element.52), channel_id=1, source_target_pairs={{0,16},{16,128},{128,144},{144,0},{1,17},{17,129},{129,145},{145,1... | collective-permute-start | bytes 294920 | tf_op jit(solution)/shard_map/gather_y/ppermute | solution.py:10
  60.5 1.2 %collective-permute-start.20 = (bf16[48,1024]{1,0:T(8,128)(2,1)S(1)}, bf16[48,1024]{1,0:T(8,128)(2,1)S(1)}, u32[]{:S(2)}, u32[]{:S(2)}) collective-permute-start(bf16[48,1024]{1,0:T(8,128)(2,1)S(1)} %get-tuple-element.52), channel_id=1, source_target_pairs={{0,144},{16,0},{128,16},{144,128},{1,145},{17,1},{129,17},{145,129... | collective-permute-start | bytes 294920 | tf_op jit(solution)/shard_map/gather_y/ppermute | solution.py:10
  61.7 0.8 collective-permute-done.18
  62.5 2.1 %collective-permute-done.19 = bf16[48,1024]{1,0:T(8,128)(2,1)S(1)} collective-permute-done((bf16[48,1024]{1,0:T(8,128)(2,1)S(1)}, bf16[48,1024]{1,0:T(8,128)(2,1)S(1)}, u32[]{:S(2)}, u32[]{:S(2)}) %collective-permute-start.19) | collective-permute-done | bytes 98336 | tf_op jit(solution)/shard_map/gather_y/ppermute | solution.py:10
  64.6 0.9 fusion.1
  65.5 3.2 %collective-permute-start.21 = (f32[4,128]{1,0:T(4,128)S(1)}, f32[4,128]{1,0:T(4,128)S(1)}, u32[]{:S(2)}, u32[]{:S(2)}) collective-permute-start(f32[4,128]{1,0:T(4,128)S(1)} %bitcast.80), channel_id=1, source_target_pairs={{0,8},{8,0},{1,9},{9,1},{2,10},{10,2},{3,11},{11,3},{4,12},{12,4},... | collective-permute-start | bytes 6152 | tf_op jit(solution)/shard_map/sigma/ppermute | solution.py:18
  68.7 0.8 collective-permute-done.21
  69.5 0.1 select_add_fusion
  69.6 15.8 %all_to_all.9 = f32[32,1,128]{2,1,0:T(1,128)S(1)} all-to-all(f32[32,1,128]{2,1,0:T(1,128)S(1)} %bitcast.77), channel_id=1, replica_groups=mesh['grp'=2,'x'=4,'ylo'=2,'core'=2,'col'=8] {'x','col'}, dimensions={0} | all-to-all | bytes 32768 | tf_op jit(solution)/shard_map/sigma/all_to_all | solution.py:136
  85.3 0.6 reduce_sum.29
  (46 shorter events, 0.6 us)
Async XLA Ops:
  2.3 17.4 %collective-permute-start = (bf16[128,1024]{1,0:T(8,128)(2,1)}, bf16[128,1024]{1,0:T(8,128)(2,1)S(1)}, u32[]{:S(2)}, u32[]{:S(2)}) collective-permute-start(bf16[128,1024]{1,0:T(8,128)(2,1)} %slice.58), channel_id=1, source_target_pairs={{0,3},{8,11},{16,19},{24,27},{32,35},{40,43},{48,51},{56,59},{64,6... | collective-permute-start | bytes 786440 | tf_op jit(solution)/shard_map/panel_z/ppermute | solution.py:14
  9.4 10.3 %collective-permute-start.1 = (bf16[128,1024]{1,0:T(8,128)(2,1)}, bf16[128,1024]{1,0:T(8,128)(2,1)}, u32[]{:S(2)}, u32[]{:S(2)}) collective-permute-start(bf16[128,1024]{1,0:T(8,128)(2,1)} %slice.58), channel_id=1, source_target_pairs={{0,6},{8,14},{16,22},{24,30},{32,38},{40,46},{48,54},{56,62},{64,7... | collective-permute-start | bytes 786440 | tf_op jit(solution)/shard_map/panel_z/ppermute | solution.py:14
  18.8 1.9 %copy-start.1 = (bf16[128,1536]{1,0:T(8,128)(2,1)S(1)}, bf16[128,1536]{1,0:T(8,128)(2,1)}, u32[]{:S(2)}) copy-start(bf16[128,1536]{1,0:T(8,128)(2,1)} %param.3) | copy-start | bytes 1179652
  19.7 3.8 %collective-permute-start.2 = (bf16[784,128]{1,0:T(8,128)(2,1)S(1)}, bf16[784,128]{1,0:T(8,128)(2,1)S(1)}, u32[]{:S(2)}, u32[]{:S(2)}) collective-permute-start(bf16[784,128]{1,0:T(8,128)(2,1)S(1)} %concatenate.52), channel_id=1, source_target_pairs={{0,8},{8,0},{1,9},{9,1},{2,10},{10,2},{3,11},{11,3},{4,12},{12,4},... | collective-permute-start | bytes 602120 | tf_op jit(solution)/shard_map/blocks/ppermute | solution.py:18
  20.8 8.4 %collective-permute-start.6 = (bf16[128,1024]{1,0:T(8,128)(2,1)S(1)}, bf16[128,1024]{1,0:T(8,128)(2,1)S(1)}, u32[]{:S(2)}, u32[]{:S(2)}) collective-permute-start(bf16[128,1024]{1,0:T(8,128)(2,1)S(1)} %select_select_fusion.1), channel_id=1, source_target_pairs={{0,1},{3,4},{6,5},{8,9},{11,12},{14,13},{16,17},{19,20},{22,21},{2... | collective-permute-start | bytes 786440 | tf_op jit(solution)/shard_map/panel_z/ppermute | solution.py:14
  22.1 7.2 %collective-permute-start.7 = (bf16[128,1024]{1,0:T(8,128)(2,1)S(1)}, bf16[128,1024]{1,0:T(8,128)(2,1)S(1)}, u32[]{:S(2)}, u32[]{:S(2)}) collective-permute-start(bf16[128,1024]{1,0:T(8,128)(2,1)S(1)} %select_select_fusion.1), channel_id=1, source_target_pairs={{0,7},{3,2},{8,15},{11,10},{16,23},{19,18},{24,31},{27,26},{32,39}... | collective-permute-start | bytes 786440 | tf_op jit(solution)/shard_map/panel_z/ppermute | solution.py:14
  23.6 8.5 %collective-permute-start.3 = (bf16[208,256]{1,0:T(8,128)(2,1)S(1)}, bf16[208,256]{1,0:T(8,128)(2,1)S(1)}, u32[]{:S(2)}, u32[]{:S(2)}) collective-permute-start(bf16[208,256]{1,0:T(8,128)(2,1)S(1)} %get-tuple-element.39), channel_id=1, source_target_pairs={{0,64},{32,96},{64,0},{96,32},{1,65},{33,97},{65,1},{97,33},{2,66}... | collective-permute-start | bytes 319496 | tf_op jit(solution)/shard_map/blocks/ppermute | solution.py:10
  26.5 7.2 %collective-permute-start.4 = (bf16[208,256]{1,0:T(8,128)(2,1)S(1)}, bf16[208,256]{1,0:T(8,128)(2,1)S(1)}, u32[]{:S(2)}, u32[]{:S(2)}) collective-permute-start(bf16[208,256]{1,0:T(8,128)(2,1)S(1)} %get-tuple-element.40), channel_id=1, source_target_pairs={{0,32},{32,64},{64,96},{96,0},{1,33},{33,65},{65,97},{97,1},{2,34}... | collective-permute-start | bytes 319496 | tf_op jit(solution)/shard_map/blocks/ppermute | solution.py:10
  26.8 8.4 %collective-permute-start.5 = (bf16[208,256]{1,0:T(8,128)(2,1)S(1)}, bf16[208,256]{1,0:T(8,128)(2,1)S(1)}, u32[]{:S(2)}, u32[]{:S(2)}) collective-permute-start(bf16[208,256]{1,0:T(8,128)(2,1)S(1)} %get-tuple-element.41), channel_id=1, source_target_pairs={{0,96},{32,0},{64,32},{96,64},{1,97},{33,1},{65,33},{97,65},{2,98}... | collective-permute-start | bytes 319496 | tf_op jit(solution)/shard_map/blocks/ppermute | solution.py:10
  29.4 8.3 %collective-permute-start.11 = (bf16[128,1024]{1,0:T(8,128)(2,1)S(1)}, bf16[128,1024]{1,0:T(8,128)(2,1)S(1)}, u32[]{:S(2)}, u32[]{:S(2)}) collective-permute-start(bf16[128,1024]{1,0:T(8,128)(2,1)S(1)} %get-tuple-element.19), channel_id=1, source_target_pairs={{0,32},{32,64},{64,96},{96,0},{1,33},{33,65},{65,97},{97,1},{2,34}... | collective-permute-start | bytes 786440 | tf_op jit(solution)/shard_map/panel_x/ppermute | solution.py:10
  30.7 8.8 %collective-permute-start.13 = (bf16[128,1024]{1,0:T(8,128)(2,1)S(1)}, bf16[128,1024]{1,0:T(8,128)(2,1)S(1)}, u32[]{:S(2)}, u32[]{:S(2)}) collective-permute-start(bf16[128,1024]{1,0:T(8,128)(2,1)S(1)} %get-tuple-element.19), channel_id=1, source_target_pairs={{0,96},{32,0},{64,32},{96,64},{1,97},{33,1},{65,33},{97,65},{2,98}... | collective-permute-start | bytes 786440 | tf_op jit(solution)/shard_map/panel_x/ppermute | solution.py:10
  32.2 12.4 %collective-permute-start.9 = (bf16[128,1024]{1,0:T(8,128)(2,1)S(1)}, bf16[128,1024]{1,0:T(8,128)(2,1)S(1)}, u32[]{:S(2)}, u32[]{:S(2)}) collective-permute-start(bf16[128,1024]{1,0:T(8,128)(2,1)S(1)} %get-tuple-element.19), channel_id=1, source_target_pairs={{0,64},{32,96},{64,0},{96,32},{1,65},{33,97},{65,1},{97,33},{2,66}... | collective-permute-start | bytes 786440 | tf_op jit(solution)/shard_map/panel_x/ppermute | solution.py:10
  33.7 12.3 %collective-permute-start.8 = (bf16[128,1024]{1,0:T(8,128)(2,1)S(1)}, bf16[128,1024]{1,0:T(8,128)(2,1)S(1)}, u32[]{:S(2)}, u32[]{:S(2)}) collective-permute-start(bf16[128,1024]{1,0:T(8,128)(2,1)S(1)} %get-tuple-element.19), channel_id=1, source_target_pairs={{0,8},{8,0},{1,9},{9,1},{2,10},{10,2},{3,11},{11,3},{4,12},{12,4},... | collective-permute-start | bytes 786440 | tf_op jit(solution)/shard_map/panel_x/ppermute | solution.py:18
  37.7 8.3 %collective-permute-start.12 = (bf16[128,1024]{1,0:T(8,128)(2,1)S(1)}, bf16[128,1024]{1,0:T(8,128)(2,1)S(1)}, u32[]{:S(2)}, u32[]{:S(2)}) collective-permute-start(bf16[128,1024]{1,0:T(8,128)(2,1)S(1)} %collective-permute-done.11), channel_id=1, source_target_pairs={{0,8},{8,0},{1,9},{9,1},{2,10},{10,2},{3,11},{11,3},{4,12},{12,4},... | collective-permute-start | bytes 786440 | tf_op jit(solution)/shard_map/panel_x/ppermute | solution.py:18
  39.5 6.6 %collective-permute-start.14 = (bf16[128,1024]{1,0:T(8,128)(2,1)S(1)}, bf16[128,1024]{1,0:T(8,128)(2,1)S(1)}, u32[]{:S(2)}, u32[]{:S(2)}) collective-permute-start(bf16[128,1024]{1,0:T(8,128)(2,1)S(1)} %collective-permute-done.13), channel_id=1, source_target_pairs={{0,8},{8,0},{1,9},{9,1},{2,10},{10,2},{3,11},{11,3},{4,12},{12,4},... | collective-permute-start | bytes 786440 | tf_op jit(solution)/shard_map/panel_x/ppermute | solution.py:18
  44.5 2.7 %collective-permute-start.10 = (bf16[128,1024]{1,0:T(8,128)(2,1)S(1)}, bf16[128,1024]{1,0:T(8,128)(2,1)S(1)}, u32[]{:S(2)}, u32[]{:S(2)}) collective-permute-start(bf16[128,1024]{1,0:T(8,128)(2,1)S(1)} %collective-permute-done.9), channel_id=1, source_target_pairs={{0,8},{8,0},{1,9},{9,1},{2,10},{10,2},{3,11},{11,3},{4,12},{12,4},... | collective-permute-start | bytes 786440 | tf_op jit(solution)/shard_map/panel_x/ppermute | solution.py:18
  47.7 8.2 %copy-start = (bf16[1024,1024]{1,0:T(8,128)(2,1)S(1)}, bf16[1024,1024]{1,0:T(8,128)(2,1)}, u32[]{:S(2)}) copy-start(bf16[1024,1024]{1,0:T(8,128)(2,1)} %get-tuple-element.16) | copy-start | bytes 6291460
  47.7 5.8 %collective-permute-start.15 = (bf16[48,1024]{1,0:T(8,128)(2,1)S(1)}, bf16[48,1024]{1,0:T(8,128)(2,1)S(1)}, u32[]{:S(2)}, u32[]{:S(2)}) collective-permute-start(bf16[48,1024]{1,0:T(8,128)(2,1)S(1)} %get-tuple-element.26), channel_id=1, source_target_pairs={{0,128},{16,144},{128,0},{144,16},{1,129},{17,145},{129,1},{145,17... | collective-permute-start | bytes 294920 | tf_op jit(solution)/shard_map/sum_y/ppermute | solution.py:10
  50.7 4.7 %collective-permute-start.16 = (bf16[48,1024]{1,0:T(8,128)(2,1)S(1)}, bf16[48,1024]{1,0:T(8,128)(2,1)S(1)}, u32[]{:S(2)}, u32[]{:S(2)}) collective-permute-start(bf16[48,1024]{1,0:T(8,128)(2,1)S(1)} %get-tuple-element.28), channel_id=1, source_target_pairs={{0,16},{16,128},{128,144},{144,0},{1,17},{17,129},{129,145},{145,1... | collective-permute-start | bytes 294920 | tf_op jit(solution)/shard_map/sum_y/ppermute | solution.py:10
  51.1 4.6 %collective-permute-start.17 = (bf16[48,1024]{1,0:T(8,128)(2,1)S(1)}, bf16[48,1024]{1,0:T(8,128)(2,1)S(1)}, u32[]{:S(2)}, u32[]{:S(2)}) collective-permute-start(bf16[48,1024]{1,0:T(8,128)(2,1)S(1)} %get-tuple-element.27), channel_id=1, source_target_pairs={{0,144},{16,0},{128,16},{144,128},{1,145},{17,1},{129,17},{145,129... | collective-permute-start | bytes 294920 | tf_op jit(solution)/shard_map/sum_y/ppermute | solution.py:10
  57.5 5.0 %collective-permute-start.18 = (bf16[48,1024]{1,0:T(8,128)(2,1)S(1)}, bf16[48,1024]{1,0:T(8,128)(2,1)S(1)}, u32[]{:S(2)}, u32[]{:S(2)}) collective-permute-start(bf16[48,1024]{1,0:T(8,128)(2,1)S(1)} %get-tuple-element.52), channel_id=1, source_target_pairs={{0,128},{16,144},{128,0},{144,16},{1,129},{17,145},{129,1},{145,17... | collective-permute-start | bytes 294920 | tf_op jit(solution)/shard_map/gather_y/ppermute | solution.py:10
  59.0 5.6 %collective-permute-start.19 = (bf16[48,1024]{1,0:T(8,128)(2,1)S(1)}, bf16[48,1024]{1,0:T(8,128)(2,1)S(1)}, u32[]{:S(2)}, u32[]{:S(2)}) collective-permute-start(bf16[48,1024]{1,0:T(8,128)(2,1)S(1)} %get-tuple-element.52), channel_id=1, source_target_pairs={{0,16},{16,128},{128,144},{144,0},{1,17},{17,129},{129,145},{145,1... | collective-permute-start | bytes 294920 | tf_op jit(solution)/shard_map/gather_y/ppermute | solution.py:10
  60.5 4.1 %collective-permute-start.20 = (bf16[48,1024]{1,0:T(8,128)(2,1)S(1)}, bf16[48,1024]{1,0:T(8,128)(2,1)S(1)}, u32[]{:S(2)}, u32[]{:S(2)}) collective-permute-start(bf16[48,1024]{1,0:T(8,128)(2,1)S(1)} %get-tuple-element.52), channel_id=1, source_target_pairs={{0,144},{16,0},{128,16},{144,128},{1,145},{17,1},{129,17},{145,129... | collective-permute-start | bytes 294920 | tf_op jit(solution)/shard_map/gather_y/ppermute | solution.py:10
  65.5 4.0 %collective-permute-start.21 = (f32[4,128]{1,0:T(4,128)S(1)}, f32[4,128]{1,0:T(4,128)S(1)}, u32[]{:S(2)}, u32[]{:S(2)}) collective-permute-start(f32[4,128]{1,0:T(4,128)S(1)} %bitcast.80), channel_id=1, source_target_pairs={{0,8},{8,0},{1,9},{9,1},{2,10},{10,2},{3,11},{11,3},{4,12},{12,4},... | collective-permute-start | bytes 6152 | tf_op jit(solution)/shard_map/sigma/ppermute | solution.py:18

commit v5 on v4

v5 whole, which is shorter than its diff:
```python
import jax
import jax.numpy as jnp
from jax import lax
from jax.sharding import Mesh, PartitionSpec as P

X, Y, Z, CORE = "x", ("grp", "ylo"), "col", "core"
PLANE = ("grp", "x", "ylo", "core")
LOW, F32 = jnp.bfloat16, jnp.float32
def shift(value, axis, size, step):
    return lax.ppermute(value, axis, [(i, (i + step) % size) for i in range(size)])


def along_z(value, *pairs):
    return lax.ppermute(value, Z, pairs)


def swap(value):
    return lax.ppermute(value, CORE, [(0, 1), (1, 0)])


def parts_of(value):
    out = []
    for _ in range(3):
        part = lax.reduce_precision(value, 8, 7)
        out.append(part.astype(LOW))
        value = value - part
    return out


def two_parts(value):
    high = lax.reduce_precision(value, 8, 7)
    return high.astype(LOW), (value - high).astype(LOW)


def body(orbital_b, gaps, block_inverse):
    own, width = orbital_b.shape
    panel = block_inverse.shape[0]
    nx, ny, nz = lax.axis_size(X), lax.axis_size(Y), lax.axis_size(Z)
    x, y, z, core = (lax.axis_index(a) for a in (X, Y, Z, CORE))
    count = width // lax.axis_size(PLANE)
    steps = (0, 2, 1, 3)

    with jax.named_scope("panel_z"):
        piece = orbital_b[:, :panel]
        far_a = along_z(piece, (0, 3))
        far_b = along_z(piece, (0, 6))

    with jax.named_scope("blocks"):
        weight = 2.0 * gaps / (gaps * gaps + 1.0)
        extra = jnp.concatenate(
            [jnp.stack(parts_of(weight)), jnp.zeros((13, own), LOW)], axis=0
        )
        blocks = orbital_b.T.reshape(2, nx, -1, own)

        def rows_of(i):
            block = lax.dynamic_index_in_dim(blocks, i, 1, False).reshape(-1, own)
            return jnp.concatenate([block, extra], axis=0)

        rows = [rows_of((x + k) % nx) for k in steps]
        factors = [rows[0]] + [shift(row, X, nx, k) for row, k in zip(rows[1:], steps[1:])]

    with jax.named_scope("panel_z"):
        far_a, far_b, block_inverse, *_ = lax.optimization_barrier(
            (far_a, far_b, block_inverse, *rows)
        )
        held = jnp.where(z == 3, far_a, jnp.where(z == 6, far_b, piece))
        near_a = along_z(held, (0, 1), (3, 4), (6, 5))
        near_b = along_z(held, (0, 7), (3, 2))
        inv_high, inv_rest = two_parts(block_inverse)
        near_a, near_b, inv_high, inv_rest, *factors = lax.optimization_barrier(
            (near_a, near_b, inv_high, inv_rest, *factors)
        )
        held = jnp.where((z == 1) | (z == 4) | (z == 5), near_a, held)
        held = jnp.where((z == 7) | (z == 2), near_b, held)

    with jax.named_scope("panel_x"):
        panels = [held] + [shift(held, X, nx, k) for k in steps[1:]]
        panels = jnp.concatenate(panels, axis=0)

    with jax.named_scope("response"):
        factors = jnp.concatenate(factors, axis=1)
        weight = jnp.sum(factors[-16:-13].astype(F32), axis=0)
        factors = factors[:-16]
        weighted = (weight[:, None] * panels.astype(F32)).astype(LOW)
        part = jnp.dot(factors, weighted, preferred_element_type=F32)

    with jax.named_scope("sum_core"):
        part = part.reshape(ny, 2, count, panel)
        sent = lax.dynamic_index_in_dim(part, 1 - core, 1, False)
        kept = lax.dynamic_index_in_dim(part, core, 1, False) + swap(sent)

    with jax.named_scope("sum_y"):
        total = lax.dynamic_index_in_dim(kept, y, 0, False)
        for k in (2, 1, 3):
            piece = lax.dynamic_index_in_dim(kept, (y + k) % ny, 0, False).astype(LOW)
            total = total + shift(piece, Y, ny, k).astype(F32)

    with jax.named_scope("screen"):
        place = z * width + lax.axis_index(PLANE) * count
        unit = (lax.iota(jnp.int32, count)[:, None] + place) == lax.iota(jnp.int32, panel)[None, :]
        total = unit.astype(F32) + total
        high, rest = two_parts(total)
        screened = jnp.dot(
            jnp.concatenate([high, rest], axis=0), inv_high, preferred_element_type=F32
        )
        screened = screened[:count] + screened[count:]
        screened = screened + jnp.dot(high, inv_rest, preferred_element_type=F32)

    with jax.named_scope("gather_y"):
        low = screened.astype(LOW)
        gathered = jnp.concatenate([low] + [shift(low, Y, ny, k) for k in steps[1:]], axis=0)
        gathered = jnp.concatenate([gathered, swap(gathered)], axis=0)
        by_y = factors.reshape(ny, 2, count, -1)
        ordered = jnp.concatenate(
            [
                lax.dynamic_slice(by_y, ((y - k) % ny, c, 0, 0), (1, 1, count, nx * own))
                for c in (core, 1 - core)
                for k in steps
            ]
        ).reshape(-1, nx * own)

    with jax.named_scope("sigma"):
        products = lax.dot_general(
            gathered, panels, (((1,), (1,)), ((), ())), preferred_element_type=F32
        )
        local = -jnp.sum(products * ordered.astype(F32), axis=0).reshape(nx, own)
        back = (x - lax.iota(jnp.int32, nx)) % nx
        by_x = sum(
            jnp.where((back == k)[:, None], local[i][None], 0.0) for i, k in enumerate(steps)
        )
        copies = jnp.broadcast_to(by_x[:, None], (nx, nz, own)).reshape(-1, own)
        terms = lax.all_to_all(copies, (X, Z), 0, 0, tiled=True)
        sigma = jnp.sum(terms, axis=0)
    return sigma, screened[None]


def solution(mesh):
    split = Mesh(mesh.devices.reshape(2, 4, 2, 2, 8), ("grp", "x", "ylo", "core", "col"))
    return jax.shard_map(
        body,
        mesh=split,
        in_specs=(P(PLANE, Z), P(PLANE), P()),
        out_specs=(P(PLANE), P(Z, PLANE, None)),
        check_vma=False,
    )
```

time: 86.2 us -> 82.2 us (0.954)
  starting transfers between devices: 46.2 us -> 34.3 us
  waiting for transfers between devices: 9.32 us -> 21.2 us
  blocking collectives: 15.8 us -> 14.1 us
  other arithmetic: 6.19 us -> 4.79 us
    ppermute x6 -> x2, starting transfers between devices: 13.8 us -> 3.94 us  [swap(): return lax.ppermute(value, CORE, [(0, 1), (1, 0)])]
    ppermute x12, waiting for transfers between devices: 7.79 us -> 17.3 us  [shift(): lax.ppermute(value, axis, [(i, (i + step) % size) for i in range(size)])]
    all_to_all x1, blocking collectives: 15.8 us -> 14.1 us  [body(): terms = lax.all_to_all(copies, (X, Z), 0, 0, tiled=True)]
    ppermute x6 -> x2, waiting for transfers between devices: 1.41 us -> 3.05 us  [swap(): return lax.ppermute(value, CORE, [(0, 1), (1, 0)])]
    convert_element_type x2, other arithmetic: 4.58 us -> 3.22 us  [two_parts(): return (high.astype(LOW), (value - high).astype(LOW))]
    ppermute x12, starting transfers between devices: 19.6 us -> 18.4 us  [shift(): lax.ppermute(value, axis, [(i, (i + step) % size) for i in range(size)])]
    dot_general x3 -> x2, matrix products: 1.82 us -> 1.3 us  [the longest x1 0.67 us: body(): part = jnp.dot(factors, weighted, preferred_element_type=F32)]
  transfers between devices with their start and end apart: 22 -> 18, of which waited for: 9 -> 9; matrix products, arithmetic and copies ran while one was open for 9% -> 7% of each run, Pallas kernels for 0% -> 0%
where the time goes in v5:
time: 82.2 us; the launch traced here: 81.9 us
  starting transfers between devices  34.3 us (42%)
  waiting for transfers between devices  21.2 us (26%)
  blocking collectives  14.1 us (17%)
  other arithmetic  4.79 us (6%)
  local copies, waits for them, and re-layouts  3.34 us (4%)
  matrix products  2.95 us (4%)
  between operations  1.13 us (1%)
    ppermute x12, starting transfers between devices, shift(): lax.ppermute(value, axis, [(i, (i + step) % size) for i in range(size)])  18.4 us
    ppermute x12, waiting for transfers between devices, shift(): lax.ppermute(value, axis, [(i, (i + step) % size) for i in range(size)])  17.3 us
    all_to_all x1, blocking collectives, body(): terms = lax.all_to_all(copies, (X, Z), 0, 0, tiled=True)  14.1 us
    ppermute x4, starting transfers between devices, along_z(): return lax.ppermute(value, Z, pairs)  12.1 us
    ppermute x2, starting transfers between devices, swap(): return lax.ppermute(value, CORE, [(0, 1), (1, 0)])  3.94 us
    convert_element_type x2, other arithmetic, two_parts(): return (high.astype(LOW), (value - high).astype(LOW))  3.22 us
    ppermute x2, waiting for transfers between devices, swap(): return lax.ppermute(value, CORE, [(0, 1), (1, 0)])  3.05 us
  transfers between devices with their start and end apart: 18, of which 9 were waited for; matrix products, arithmetic and copies ran while one was open for 7% of the time, Pallas kernels for 0%

profile of v5, /device:TPU:1, one launch (start us, length us, event | category | flops | bytes accessed | tf_op | source)
XLA Modules:
  0.0 81.9 jit_solution(18288609905050743145)
XLA Ops:
  0.6 0.0 copy-start
  0.6 1.0 %slice.31 = bf16[128,1024]{1,0:T(8,128)(2,1)S(1)} slice(bf16[128,1536]{1,0:T(8,128)(2,1)} %param.3), slice={[0:128], [0:1024]} | slice | bytes 524288 | tf_op jit(solution)/shard_map/panel_z/slice | solution.py:44
  1.7 7.1 %collective-permute-start = (bf16[128,1024]{1,0:T(8,128)(2,1)S(1)}, bf16[128,1024]{1,0:T(8,128)(2,1)S(1)}, u32[]{:S(2)}, u32[]{:S(2)}) collective-permute-start(bf16[128,1024]{1,0:T(8,128)(2,1)S(1)} %slice.31), channel_id=1, source_target_pairs={{0,3},{8,11},{16,19},{24,27},{32,35},{40,43},{48,51},{56,59},{64,6... | collective-permute-start | bytes 786440 | tf_op jit(solution)/shard_map/panel_z/ppermute | solution.py:14
  8.8 2.4 %collective-permute-start.1 = (bf16[128,1024]{1,0:T(8,128)(2,1)S(1)}, bf16[128,1024]{1,0:T(8,128)(2,1)S(1)}, u32[]{:S(2)}, u32[]{:S(2)}) collective-permute-start(bf16[128,1024]{1,0:T(8,128)(2,1)S(1)} %slice.31), channel_id=1, source_target_pairs={{0,6},{8,14},{16,22},{24,30},{32,38},{40,46},{48,54},{56,62},{64,7... | collective-permute-start | bytes 786440 | tf_op jit(solution)/shard_map/panel_z/ppermute | solution.py:14
  11.1 0.7 fusion.19
  11.9 1.2 %copy.18 = bf16[128,1536]{0,1:T(8,128)(2,1)S(1)} copy(bf16[128,1536]{1,0:T(8,128)(2,1)} %param.3) | data formatting | bytes 786432 | tf_op args[0]
  13.2 0.2 concatenate.37
  13.3 2.8 %collective-permute-start.4 = (bf16[400,128]{1,0:T(8,128)(2,1)S(1)}, bf16[400,128]{1,0:T(8,128)(2,1)S(1)}, u32[]{:S(2)}, u32[]{:S(2)}) collective-permute-start(bf16[400,128]{1,0:T(8,128)(2,1)S(1)} %concatenate.37), channel_id=1, source_target_pairs={{0,64},{32,96},{64,0},{96,32},{1,65},{33,97},{65,1},{97,33},{2,66}... | collective-permute-start | bytes 307208 | tf_op jit(solution)/shard_map/blocks/ppermute | solution.py:10
  16.2 0.2 concatenate.38
  16.3 0.4 collective-permute-start.5
  16.7 0.2 concatenate.39
  16.9 2.4 %collective-permute-start.6 = (bf16[400,128]{1,0:T(8,128)(2,1)S(1)}, bf16[400,128]{1,0:T(8,128)(2,1)S(1)}, u32[]{:S(2)}, u32[]{:S(2)}) collective-permute-start(bf16[400,128]{1,0:T(8,128)(2,1)S(1)} %concatenate.39), channel_id=1, source_target_pairs={{0,96},{32,0},{64,32},{96,64},{1,97},{33,1},{65,33},{97,65},{2,98}... | collective-permute-start | bytes 307208 | tf_op jit(solution)/shard_map/blocks/ppermute | solution.py:10
  19.3 0.2 concatenate.36
  19.6 0.0 collective-permute-done.1
  19.7 1.3 %collective-permute-start.2 = (bf16[128,1024]{1,0:T(8,128)(2,1)S(1)}, bf16[128,1024]{1,0:T(8,128)(2,1)S(1)}, u32[]{:S(2)}, u32[]{:S(2)}) collective-permute-start(bf16[128,1024]{1,0:T(8,128)(2,1)S(1)} %select_select_fusion.1), channel_id=1, source_target_pairs={{0,1},{3,4},{6,5},{8,9},{11,12},{14,13},{16,17},{19,20},{22,21},{2... | collective-permute-start | bytes 786440 | tf_op jit(solution)/shard_map/panel_z/ppermute | solution.py:14
  21.0 1.3 %collective-permute-start.3 = (bf16[128,1024]{1,0:T(8,128)(2,1)S(1)}, bf16[128,1024]{1,0:T(8,128)(2,1)S(1)}, u32[]{:S(2)}, u32[]{:S(2)}) collective-permute-start(bf16[128,1024]{1,0:T(8,128)(2,1)S(1)} %select_select_fusion.1), channel_id=1, source_target_pairs={{0,7},{3,2},{8,15},{11,10},{16,23},{19,18},{24,31},{27,26},{32,39}... | collective-permute-start | bytes 786440 | tf_op jit(solution)/shard_map/panel_z/ppermute | solution.py:14
  22.3 3.1 %fusion = (bf16[1024,1024]{1,0:T(8,128)(2,1)S(1)}, bf16[1024,1024]{1,0:T(8,128)(2,1)S(1)}) fusion(f32[1024,1024]{1,0:T(8,128)} %param.5), kind=kLoop, calls=%fused_computation.2 | loop fusion | flops 4194304 | bytes 8388608 | tf_op jit(solution)/shard_map/panel_z/convert_element_type | solution.py:32
  25.4 0.0 collective-permute-done.5
  25.5 0.9 %collective-permute-done.3 = bf16[128,1024]{1,0:T(8,128)(2,1)S(1)} collective-permute-done((bf16[128,1024]{1,0:T(8,128)(2,1)S(1)}, bf16[128,1024]{1,0:T(8,128)(2,1)S(1)}, u32[]{:S(2)}, u32[]{:S(2)}) %collective-permute-start.3) | collective-permute-done | bytes 262176 | tf_op jit(solution)/shard_map/panel_z/ppermute | solution.py:14
  26.4 0.1 collective-permute-start.7
  26.5 1.0 %collective-permute-start.8 = (bf16[128,1024]{1,0:T(8,128)(2,1)S(1)}, bf16[128,1024]{1,0:T(8,128)(2,1)S(1)}, u32[]{:S(2)}, u32[]{:S(2)}) collective-permute-start(bf16[128,1024]{1,0:T(8,128)(2,1)S(1)} %select_select_fusion), channel_id=1, source_target_pairs={{0,32},{32,64},{64,96},{96,0},{1,33},{33,65},{65,97},{97,1},{2,34}... | collective-permute-start | bytes 786440 | tf_op jit(solution)/shard_map/panel_x/ppermute | solution.py:10
  27.5 1.8 %collective-permute-start.9 = (bf16[128,1024]{1,0:T(8,128)(2,1)S(1)}, bf16[128,1024]{1,0:T(8,128)(2,1)S(1)}, u32[]{:S(2)}, u32[]{:S(2)}) collective-permute-start(bf16[128,1024]{1,0:T(8,128)(2,1)S(1)} %select_select_fusion), channel_id=1, source_target_pairs={{0,96},{32,0},{64,32},{96,64},{1,97},{33,1},{65,33},{97,65},{2,98}... | collective-permute-start | bytes 786440 | tf_op jit(solution)/shard_map/panel_x/ppermute | solution.py:10
  29.4 3.9 %collective-permute-done.7 = bf16[128,1024]{1,0:T(8,128)(2,1)S(1)} collective-permute-done((bf16[128,1024]{1,0:T(8,128)(2,1)S(1)}, bf16[128,1024]{1,0:T(8,128)(2,1)S(1)}, u32[]{:S(2)}, u32[]{:S(2)}) %collective-permute-start.7) | collective-permute-done | bytes 262176 | tf_op jit(solution)/shard_map/panel_x/ppermute | solution.py:10
  33.3 8.1 %collective-permute-done.8 = bf16[128,1024]{1,0:T(8,128)(2,1)S(1)} collective-permute-done((bf16[128,1024]{1,0:T(8,128)(2,1)S(1)}, bf16[128,1024]{1,0:T(8,128)(2,1)S(1)}, u32[]{:S(2)}, u32[]{:S(2)}) %collective-permute-start.8) | collective-permute-done | bytes 262176 | tf_op jit(solution)/shard_map/panel_x/ppermute | solution.py:10
  41.4 0.7 fusion.2
  42.1 0.1 dynamic-slice_bitcast_fusion
  42.2 0.8 collective-permute-start.10
  43.1 1.7 %collective-permute-done.10 = f32[4,48,1024]{2,1,0:T(8,128)S(1)} collective-permute-done((f32[4,48,1024]{2,1,0:T(8,128)S(1)}, f32[4,48,1024]{2,1,0:T(8,128)S(1)}, u32[]{:S(2)}, u32[]{:S(2)}) %collective-permute-start.10) | collective-permute-done | bytes 786464 | tf_op jit(solution)/shard_map/sum_core/ppermute | solution.py:18
  44.9 0.1 bitcast_add_fusion
  45.0 3.0 %collective-permute-start.11 = (bf16[48,1024]{1,0:T(8,128)(2,1)S(1)}, bf16[48,1024]{1,0:T(8,128)(2,1)S(1)}, u32[]{:S(2)}, u32[]{:S(2)}) collective-permute-start(bf16[48,1024]{1,0:T(8,128)(2,1)S(1)} %get-tuple-element.32), channel_id=1, source_target_pairs={{0,128},{16,144},{128,0},{144,16},{1,129},{17,145},{129,1},{145,17... | collective-permute-start | bytes 294920 | tf_op jit(solution)/shard_map/sum_y/ppermute | solution.py:10
  48.0 0.4 collective-permute-start.12
  48.4 2.3 %collective-permute-start.13 = (bf16[48,1024]{1,0:T(8,128)(2,1)S(1)}, bf16[48,1024]{1,0:T(8,128)(2,1)S(1)}, u32[]{:S(2)}, u32[]{:S(2)}) collective-permute-start(bf16[48,1024]{1,0:T(8,128)(2,1)S(1)} %get-tuple-element.33), channel_id=1, source_target_pairs={{0,144},{16,0},{128,16},{144,128},{1,145},{17,1},{129,17},{145,129... | collective-permute-start | bytes 294920 | tf_op jit(solution)/shard_map/sum_y/ppermute | solution.py:10
  50.7 2.0 %collective-permute-done.12 = bf16[48,1024]{1,0:T(8,128)(2,1)S(1)} collective-permute-done((bf16[48,1024]{1,0:T(8,128)(2,1)S(1)}, bf16[48,1024]{1,0:T(8,128)(2,1)S(1)}, u32[]{:S(2)}, u32[]{:S(2)}) %collective-permute-start.12) | collective-permute-done | bytes 98336 | tf_op jit(solution)/shard_map/sum_y/ppermute | solution.py:10
  52.7 0.4 collective-permute-done.13
  53.1 0.1 fusion.4
  53.2 0.5 fusion.5
  53.7 1.2 %constant_dynamic-update-slice_fusion.8 = (bf16[384,1024]{1,0:T(8,128)(2,1)S(1)}, bf16[48,1024]{1,0:T(8,128)(2,1)S(1)}, f32[48,1024]{1,0:T(8,128)}) fusion(bf16[48,1024]{1,0:T(8,128)(2,1)S(1)} %get-tuple-element.31, bf16[1024,1024]{1,0:T(8,128)(2,1)S(1)} %get-tuple-element.23, f32[96,1024]{1,0:T(8,128)S(1)} %fusion.5), kind=kOutput, calls=%fused_computation.50 | convolution fusion | flops 100810752 | bytes 2981888 | tf_op jit(solution)/shard_map/screen/dot_general | solution.py:107
  54.9 1.5 %collective-permute-start.14 = (bf16[48,1024]{1,0:T(8,128)(2,1)S(1)}, bf16[48,1024]{1,0:T(8,128)(2,1)S(1)}, u32[]{:S(2)}, u32[]{:S(2)}) collective-permute-start(bf16[48,1024]{1,0:T(8,128)(2,1)S(1)} %get-tuple-element.25), channel_id=1, source_target_pairs={{0,128},{16,144},{128,0},{144,16},{1,129},{17,145},{129,1},{145,17... | collective-permute-start | bytes 294920 | tf_op jit(solution)/shard_map/gather_y/ppermute | solution.py:10
  56.3 1.5 %collective-permute-start.15 = (bf16[48,1024]{1,0:T(8,128)(2,1)S(1)}, bf16[48,1024]{1,0:T(8,128)(2,1)S(1)}, u32[]{:S(2)}, u32[]{:S(2)}) collective-permute-start(bf16[48,1024]{1,0:T(8,128)(2,1)S(1)} %get-tuple-element.25), channel_id=1, source_target_pairs={{0,16},{16,128},{128,144},{144,0},{1,17},{17,129},{129,145},{145,1... | collective-permute-start | bytes 294920 | tf_op jit(solution)/shard_map/gather_y/ppermute | solution.py:10
  57.9 1.2 %collective-permute-start.16 = (bf16[48,1024]{1,0:T(8,128)(2,1)S(1)}, bf16[48,1024]{1,0:T(8,128)(2,1)S(1)}, u32[]{:S(2)}, u32[]{:S(2)}) collective-permute-start(bf16[48,1024]{1,0:T(8,128)(2,1)S(1)} %get-tuple-element.25), channel_id=1, source_target_pairs={{0,144},{16,0},{128,16},{144,128},{1,145},{17,1},{129,17},{145,129... | collective-permute-start | bytes 294920 | tf_op jit(solution)/shard_map/gather_y/ppermute | solution.py:10
  59.0 0.8 collective-permute-done.14
  59.8 2.1 %collective-permute-done.15 = bf16[48,1024]{1,0:T(8,128)(2,1)S(1)} collective-permute-done((bf16[48,1024]{1,0:T(8,128)(2,1)S(1)}, bf16[48,1024]{1,0:T(8,128)(2,1)S(1)}, u32[]{:S(2)}, u32[]{:S(2)}) %collective-permute-start.15) | collective-permute-done | bytes 98336 | tf_op jit(solution)/shard_map/gather_y/ppermute | solution.py:10
  62.0 3.2 %collective-permute-start.17 = (bf16[192,1024]{1,0:T(8,128)(2,1)S(1)}, bf16[192,1024]{1,0:T(8,128)(2,1)S(1)}, u32[]{:S(2)}, u32[]{:S(2)}) collective-permute-start(bf16[192,1024]{1,0:T(8,128)(2,1)S(1)} %pad_maximum_fusion.1), channel_id=1, source_target_pairs={{0,8},{8,0},{1,9},{9,1},{2,10},{10,2},{3,11},{11,3},{4,12},{12,4},... | collective-permute-start | bytes 1179656 | tf_op jit(solution)/shard_map/gather_y/ppermute | solution.py:18
  65.2 1.3 %collective-permute-done.17 = bf16[192,1024]{1,0:T(8,128)(2,1)S(1)} collective-permute-done((bf16[192,1024]{1,0:T(8,128)(2,1)S(1)}, bf16[192,1024]{1,0:T(8,128)(2,1)S(1)}, u32[]{:S(2)}, u32[]{:S(2)}) %collective-permute-start.17) | collective-permute-done | bytes 393248 | tf_op jit(solution)/shard_map/gather_y/ppermute | solution.py:18
  66.5 0.6 fusion.1
  67.2 0.1 select_add_fusion
  67.2 14.1 %all_to_all.9 = f32[32,1,128]{2,1,0:T(1,128)S(1)} all-to-all(f32[32,1,128]{2,1,0:T(1,128)S(1)} %bitcast.61), channel_id=1, replica_groups=mesh['grp'=2,'x'=4,'ylo'=2,'core'=2,'col'=8] {'x','col'}, dimensions={0} | all-to-all | bytes 32768 | tf_op jit(solution)/shard_map/sigma/all_to_all | solution.py:132
  81.3 0.6 reduce_sum.29
  (39 shorter events, 0.5 us)
Async XLA Ops:
  0.6 19.0 %copy-start = (bf16[128,1536]{1,0:T(8,128)(2,1)S(1)}, bf16[128,1536]{1,0:T(8,128)(2,1)}, u32[]{:S(2)}) copy-start(bf16[128,1536]{1,0:T(8,128)(2,1)} %param.3) | copy-start | bytes 1179652
  1.7 17.9 %collective-permute-start = (bf16[128,1024]{1,0:T(8,128)(2,1)S(1)}, bf16[128,1024]{1,0:T(8,128)(2,1)S(1)}, u32[]{:S(2)}, u32[]{:S(2)}) collective-permute-start(bf16[128,1024]{1,0:T(8,128)(2,1)S(1)} %slice.31), channel_id=1, source_target_pairs={{0,3},{8,11},{16,19},{24,27},{32,35},{40,43},{48,51},{56,59},{64,6... | collective-permute-start | bytes 786440 | tf_op jit(solution)/shard_map/panel_z/ppermute | solution.py:14
  8.8 10.8 %collective-permute-start.1 = (bf16[128,1024]{1,0:T(8,128)(2,1)S(1)}, bf16[128,1024]{1,0:T(8,128)(2,1)S(1)}, u32[]{:S(2)}, u32[]{:S(2)}) collective-permute-start(bf16[128,1024]{1,0:T(8,128)(2,1)S(1)} %slice.31), channel_id=1, source_target_pairs={{0,6},{8,14},{16,22},{24,30},{32,38},{40,46},{48,54},{56,62},{64,7... | collective-permute-start | bytes 786440 | tf_op jit(solution)/shard_map/panel_z/ppermute | solution.py:14
  13.3 12.1 %collective-permute-start.4 = (bf16[400,128]{1,0:T(8,128)(2,1)S(1)}, bf16[400,128]{1,0:T(8,128)(2,1)S(1)}, u32[]{:S(2)}, u32[]{:S(2)}) collective-permute-start(bf16[400,128]{1,0:T(8,128)(2,1)S(1)} %concatenate.37), channel_id=1, source_target_pairs={{0,64},{32,96},{64,0},{96,32},{1,65},{33,97},{65,1},{97,33},{2,66}... | collective-permute-start | bytes 307208 | tf_op jit(solution)/shard_map/blocks/ppermute | solution.py:10
  16.3 9.1 %collective-permute-start.5 = (bf16[400,128]{1,0:T(8,128)(2,1)S(1)}, bf16[400,128]{1,0:T(8,128)(2,1)S(1)}, u32[]{:S(2)}, u32[]{:S(2)}) collective-permute-start(bf16[400,128]{1,0:T(8,128)(2,1)S(1)} %concatenate.38), channel_id=1, source_target_pairs={{0,32},{32,64},{64,96},{96,0},{1,33},{33,65},{65,97},{97,1},{2,34}... | collective-permute-start | bytes 307208 | tf_op jit(solution)/shard_map/blocks/ppermute | solution.py:10
  16.9 8.5 %collective-permute-start.6 = (bf16[400,128]{1,0:T(8,128)(2,1)S(1)}, bf16[400,128]{1,0:T(8,128)(2,1)S(1)}, u32[]{:S(2)}, u32[]{:S(2)}) collective-permute-start(bf16[400,128]{1,0:T(8,128)(2,1)S(1)} %concatenate.39), channel_id=1, source_target_pairs={{0,96},{32,0},{64,32},{96,64},{1,97},{33,1},{65,33},{97,65},{2,98}... | collective-permute-start | bytes 307208 | tf_op jit(solution)/shard_map/blocks/ppermute | solution.py:10
  19.7 5.8 %collective-permute-start.2 = (bf16[128,1024]{1,0:T(8,128)(2,1)S(1)}, bf16[128,1024]{1,0:T(8,128)(2,1)S(1)}, u32[]{:S(2)}, u32[]{:S(2)}) collective-permute-start(bf16[128,1024]{1,0:T(8,128)(2,1)S(1)} %select_select_fusion.1), channel_id=1, source_target_pairs={{0,1},{3,4},{6,5},{8,9},{11,12},{14,13},{16,17},{19,20},{22,21},{2... | collective-permute-start | bytes 786440 | tf_op jit(solution)/shard_map/panel_z/ppermute | solution.py:14
  21.0 5.4 %collective-permute-start.3 = (bf16[128,1024]{1,0:T(8,128)(2,1)S(1)}, bf16[128,1024]{1,0:T(8,128)(2,1)S(1)}, u32[]{:S(2)}, u32[]{:S(2)}) collective-permute-start(bf16[128,1024]{1,0:T(8,128)(2,1)S(1)} %select_select_fusion.1), channel_id=1, source_target_pairs={{0,7},{3,2},{8,15},{11,10},{16,23},{19,18},{24,31},{27,26},{32,39}... | collective-permute-start | bytes 786440 | tf_op jit(solution)/shard_map/panel_z/ppermute | solution.py:14
  26.4 6.9 %collective-permute-start.7 = (bf16[128,1024]{1,0:T(8,128)(2,1)S(1)}, bf16[128,1024]{1,0:T(8,128)(2,1)S(1)}, u32[]{:S(2)}, u32[]{:S(2)}) collective-permute-start(bf16[128,1024]{1,0:T(8,128)(2,1)S(1)} %select_select_fusion), channel_id=1, source_target_pairs={{0,64},{32,96},{64,0},{96,32},{1,65},{33,97},{65,1},{97,33},{2,66}... | collective-permute-start | bytes 786440 | tf_op jit(solution)/shard_map/panel_x/ppermute | solution.py:10
  26.5 14.9 %collective-permute-start.8 = (bf16[128,1024]{1,0:T(8,128)(2,1)S(1)}, bf16[128,1024]{1,0:T(8,128)(2,1)S(1)}, u32[]{:S(2)}, u32[]{:S(2)}) collective-permute-start(bf16[128,1024]{1,0:T(8,128)(2,1)S(1)} %select_select_fusion), channel_id=1, source_target_pairs={{0,32},{32,64},{64,96},{96,0},{1,33},{33,65},{65,97},{97,1},{2,34}... | collective-permute-start | bytes 786440 | tf_op jit(solution)/shard_map/panel_x/ppermute | solution.py:10
  27.5 13.9 %collective-permute-start.9 = (bf16[128,1024]{1,0:T(8,128)(2,1)S(1)}, bf16[128,1024]{1,0:T(8,128)(2,1)S(1)}, u32[]{:S(2)}, u32[]{:S(2)}) collective-permute-start(bf16[128,1024]{1,0:T(8,128)(2,1)S(1)} %select_select_fusion), channel_id=1, source_target_pairs={{0,96},{32,0},{64,32},{96,64},{1,97},{33,1},{65,33},{97,65},{2,98}... | collective-permute-start | bytes 786440 | tf_op jit(solution)/shard_map/panel_x/ppermute | solution.py:10
  42.2 2.7 %collective-permute-start.10 = (f32[4,48,1024]{2,1,0:T(8,128)S(1)}, f32[4,48,1024]{2,1,0:T(8,128)S(1)}, u32[]{:S(2)}, u32[]{:S(2)}) collective-permute-start(f32[4,48,1024]{2,1,0:T(8,128)S(1)} %dynamic-slice_bitcast_fusion), channel_id=1, source_target_pairs={{0,8},{8,0},{1,9},{9,1},{2,10},{10,2},{3,11},{11,3},{4,12},{12,4},... | collective-permute-start | bytes 2359304 | tf_op jit(solution)/shard_map/sum_core/ppermute | solution.py:18
  45.0 5.7 %collective-permute-start.11 = (bf16[48,1024]{1,0:T(8,128)(2,1)S(1)}, bf16[48,1024]{1,0:T(8,128)(2,1)S(1)}, u32[]{:S(2)}, u32[]{:S(2)}) collective-permute-start(bf16[48,1024]{1,0:T(8,128)(2,1)S(1)} %get-tuple-element.32), channel_id=1, source_target_pairs={{0,128},{16,144},{128,0},{144,16},{1,129},{17,145},{129,1},{145,17... | collective-permute-start | bytes 294920 | tf_op jit(solution)/shard_map/sum_y/ppermute | solution.py:10
  48.0 4.7 %collective-permute-start.12 = (bf16[48,1024]{1,0:T(8,128)(2,1)S(1)}, bf16[48,1024]{1,0:T(8,128)(2,1)S(1)}, u32[]{:S(2)}, u32[]{:S(2)}) collective-permute-start(bf16[48,1024]{1,0:T(8,128)(2,1)S(1)} %get-tuple-element.34), channel_id=1, source_target_pairs={{0,16},{16,128},{128,144},{144,0},{1,17},{17,129},{129,145},{145,1... | collective-permute-start | bytes 294920 | tf_op jit(solution)/shard_map/sum_y/ppermute | solution.py:10
  48.4 4.6 %collective-permute-start.13 = (bf16[48,1024]{1,0:T(8,128)(2,1)S(1)}, bf16[48,1024]{1,0:T(8,128)(2,1)S(1)}, u32[]{:S(2)}, u32[]{:S(2)}) collective-permute-start(bf16[48,1024]{1,0:T(8,128)(2,1)S(1)} %get-tuple-element.33), channel_id=1, source_target_pairs={{0,144},{16,0},{128,16},{144,128},{1,145},{17,1},{129,17},{145,129... | collective-permute-start | bytes 294920 | tf_op jit(solution)/shard_map/sum_y/ppermute | solution.py:10
  54.9 5.0 %collective-permute-start.14 = (bf16[48,1024]{1,0:T(8,128)(2,1)S(1)}, bf16[48,1024]{1,0:T(8,128)(2,1)S(1)}, u32[]{:S(2)}, u32[]{:S(2)}) collective-permute-start(bf16[48,1024]{1,0:T(8,128)(2,1)S(1)} %get-tuple-element.25), channel_id=1, source_target_pairs={{0,128},{16,144},{128,0},{144,16},{1,129},{17,145},{129,1},{145,17... | collective-permute-start | bytes 294920 | tf_op jit(solution)/shard_map/gather_y/ppermute | solution.py:10
  56.3 5.6 %collective-permute-start.15 = (bf16[48,1024]{1,0:T(8,128)(2,1)S(1)}, bf16[48,1024]{1,0:T(8,128)(2,1)S(1)}, u32[]{:S(2)}, u32[]{:S(2)}) collective-permute-start(bf16[48,1024]{1,0:T(8,128)(2,1)S(1)} %get-tuple-element.25), channel_id=1, source_target_pairs={{0,16},{16,128},{128,144},{144,0},{1,17},{17,129},{129,145},{145,1... | collective-permute-start | bytes 294920 | tf_op jit(solution)/shard_map/gather_y/ppermute | solution.py:10
  57.9 4.1 %collective-permute-start.16 = (bf16[48,1024]{1,0:T(8,128)(2,1)S(1)}, bf16[48,1024]{1,0:T(8,128)(2,1)S(1)}, u32[]{:S(2)}, u32[]{:S(2)}) collective-permute-start(bf16[48,1024]{1,0:T(8,128)(2,1)S(1)} %get-tuple-element.25), channel_id=1, source_target_pairs={{0,144},{16,0},{128,16},{144,128},{1,145},{17,1},{129,17},{145,129... | collective-permute-start | bytes 294920 | tf_op jit(solution)/shard_map/gather_y/ppermute | solution.py:10
  62.0 4.5 %collective-permute-start.17 = (bf16[192,1024]{1,0:T(8,128)(2,1)S(1)}, bf16[192,1024]{1,0:T(8,128)(2,1)S(1)}, u32[]{:S(2)}, u32[]{:S(2)}) collective-permute-start(bf16[192,1024]{1,0:T(8,128)(2,1)S(1)} %pad_maximum_fusion.1), channel_id=1, source_target_pairs={{0,8},{8,0},{1,9},{9,1},{2,10},{10,2},{3,11},{11,3},{4,12},{12,4},... | collective-permute-start | bytes 1179656 | tf_op jit(solution)/shard_map/gather_y/ppermute | solution.py:18

commit v6 on v5

--- a/solution.py
+++ b/solution.py
@@ -12,6 +12,17 @@
 
 def along_z(value, *pairs):
     return lax.ppermute(value, Z, pairs)
+
+
+def from_zero(value, *targets):
+    return lax.ppermute(value, (CORE, Z), [(c * 8, c * 8 + z) for c, z in enumerate(targets)])
+
+
+def turn(value, size, step):
+    pairs = []
+    for x in range(size):
+        pairs += [(x * 2, (x + step) % size * 2), (x * 2 + 1, (x - step) % size * 2 + 1)]
+    return lax.ppermute(value, (X, CORE), pairs)
 
 
 def swap(value):
@@ -39,11 +50,13 @@
     x, y, z, core = (lax.axis_index(a) for a in (X, Y, Z, CORE))
     count = width // lax.axis_size(PLANE)
     steps = (0, 2, 1, 3)
+    way = 1 - 2 * core
 
     with jax.named_scope("panel_z"):
         piece = orbital_b[:, :panel]
-        far_a = along_z(piece, (0, 3))
-        far_b = along_z(piece, (0, 6))
+        far_a = from_zero(piece, 3, 6)
+        far_b = from_zero(piece, 6, 3)
+        first = along_z(piece, (0, 1))
 
     with jax.named_scope("blocks"):
         weight = 2.0 * gaps / (gaps * gaps + 1.0)
@@ -56,26 +69,29 @@
             block = lax.dynamic_index_in_dim(blocks, i, 1, False).reshape(-1, own)
             return jnp.concatenate([block, extra], axis=0)
 
-        rows = [rows_of((x + k) % nx) for k in steps]
-        factors = [rows[0]] + [shift(row, X, nx, k) for row, k in zip(rows[1:], steps[1:])]
+        rows = [rows_of((x + way * k) % nx) for k in steps]
+        factors = [rows[0]] + [turn(row, nx, k) for row, k in zip(rows[1:], steps[1:])]
 
     with jax.named_scope("panel_z"):
         far_a, far_b, block_inverse, *_ = lax.optimization_barrier(
             (far_a, far_b, block_inverse, *rows)
         )
-        held = jnp.where(z == 3, far_a, jnp.where(z == 6, far_b, piece))
-        near_a = along_z(held, (0, 1), (3, 4), (6, 5))
-        near_b = along_z(held, (0, 7), (3, 2))
+        held = jnp.where(z == jnp.where(core == 0, 3, 6), far_a, piece)
+        held = jnp.where(z == jnp.where(core == 0, 6, 3), far_b, held)
+        near_a = along_z(held, (3, 4), (6, 5))
+        near_b = along_z(held, (3, 2), (6, 7))
         inv_high, inv_rest = two_parts(block_inverse)
         near_a, near_b, inv_high, inv_rest, *factors = lax.optimization_barrier(
             (near_a, near_b, inv_high, inv_rest, *factors)
         )
-        held = jnp.where((z == 1) | (z == 4) | (z == 5), near_a, held)
+        held = jnp.where(z == 1, first, held)
+        held = jnp.where((z == 4) | (z == 5), near_a, held)
         held = jnp.where((z == 7) | (z == 2), near_b, held)
 
     with jax.named_scope("panel_x"):
-        panels = [held] + [shift(held, X, nx, k) for k in steps[1:]]
-        panels = jnp.concatenate(panels, axis=0)
+        ahead = turn(held, nx, 1)
+        behind = turn(held, nx, 3)
+        panels = jnp.concatenate([held, turn(ahead, nx, 1), ahead, behind], axis=0)
 
     with jax.named_scope("response"):
         factors = jnp.concatenate(factors, axis=1)
@@ -124,7 +140,7 @@
             gathered, panels, (((1,), (1,)), ((), ())), preferred_element_type=F32
         )
         local = -jnp.sum(products * ordered.astype(F32), axis=0).reshape(nx, own)
-        back = (x - lax.iota(jnp.int32, nx)) % nx
+        back = way * (x - lax.iota(jnp.int32, nx)) % nx
         by_x = sum(
             jnp.where((back == k)[:, None], local[i][None], 0.0) for i, k in enumerate(steps)
         )

time: 82.2 us -> 86.6 us (1.054)
  starting transfers between devices: 34.3 us -> 43.7 us
  waiting for transfers between devices: 21.2 us -> 14.8 us
  other arithmetic: 4.79 us -> 6.19 us
    ppermute x0 -> x8, starting transfers between devices: none -> 20.1 us  [the longest x2 10.1 us: from_zero(): lax.ppermute(value, (CORE, Z), [(c * 8, c * 8 + z) for c, z in enumerate(...]
    ppermute x12 -> x6, waiting for transfers between devices: 17.3 us -> 5.26 us  [shift(): lax.ppermute(value, axis, [(i, (i + step) % size) for i in range(size)])]
    ppermute x4 -> x3, starting transfers between devices: 12.1 us -> 2.66 us  [along_z(): return lax.ppermute(value, Z, pairs)]
    ppermute x12 -> x6, starting transfers between devices: 18.4 us -> 9.84 us  [shift(): lax.ppermute(value, axis, [(i, (i + step) % size) for i in range(size)])]
    ppermute x2, starting transfers between devices: 3.94 us -> 11 us  [swap(): return lax.ppermute(value, CORE, [(0, 1), (1, 0)])]
    ppermute x0 -> x8, waiting for transfers between devices: none -> 6.5 us  [the longest x6 6.49 us: turn(): return lax.ppermute(value, (X, CORE), pairs)]
    convert_element_type x2, other arithmetic: 3.22 us -> 4.56 us  [two_parts(): return (high.astype(LOW), (value - high).astype(LOW))]
    ppermute x4 -> x3, waiting for transfers between devices: 0.9 us -> 0.01 us  [along_z(): return lax.ppermute(value, Z, pairs)]
  transfers between devices with their start and end apart: 18 -> 19, of which waited for: 9 -> 9; matrix products, arithmetic and copies ran while one was open for 7% -> 9% of each run, Pallas kernels for 0% -> 0%
where the time goes in v6:
time: 86.6 us; the launch traced here: 86.3 us
  starting transfers between devices  43.7 us (50%)
  waiting for transfers between devices  14.8 us (17%)
  blocking collectives  14.3 us (17%)
  other arithmetic  6.19 us (7%)
  local copies, waits for them, and re-layouts  3.35 us (4%)
  matrix products  2.92 us (3%)
  between operations  1.11 us (1%)
    all_to_all x1, blocking collectives, body(): terms = lax.all_to_all(copies, (X, Z), 0, 0, tiled=True)  14.3 us
    ppermute x2, starting transfers between devices, swap(): return lax.ppermute(value, CORE, [(0, 1), (1, 0)])  11 us
    ppermute x2, starting transfers between devices, from_zero(): lax.ppermute(value, (CORE, Z), [(c * 8, c * 8 + z) for c, z in enumerate(...  10.1 us
    ppermute x6, starting transfers between devices, turn(): return lax.ppermute(value, (X, CORE), pairs)  10.1 us
    ppermute x6, starting transfers between devices, shift(): lax.ppermute(value, axis, [(i, (i + step) % size) for i in range(size)])  9.84 us
    ppermute x6, waiting for transfers between devices, turn(): return lax.ppermute(value, (X, CORE), pairs)  6.49 us
    ppermute x6, waiting for transfers between devices, shift(): lax.ppermute(value, axis, [(i, (i + step) % size) for i in range(size)])  5.26 us
    convert_element_type x2, other arithmetic, two_parts(): return (high.astype(LOW), (value - high).astype(LOW))  4.56 us
  transfers between devices with their start and end apart: 19, of which 9 were waited for; matrix products, arithmetic and copies ran while one was open for 9% of the time, Pallas kernels for 0%

profile of v6, /device:TPU:1, one launch (start us, length us, event | category | flops | bytes accessed | tf_op | source)
XLA Modules:
  0.0 86.3 jit_solution(5587504351022417802)
XLA Ops:
  0.6 0.0 copy-start.1
  0.6 1.0 %slice.31 = bf16[128,1024]{1,0:T(8,128)(2,1)S(1)} slice(bf16[128,1536]{1,0:T(8,128)(2,1)} %param.3), slice={[0:128], [0:1024]} | slice | bytes 524288 | tf_op jit(solution)/shard_map/panel_z/slice | solution.py:56
  1.7 8.8 %collective-permute-start = (bf16[128,1024]{1,0:T(8,128)(2,1)S(1)}, bf16[128,1024]{1,0:T(8,128)(2,1)S(1)}, u32[]{:S(2)}, u32[]{:S(2)}) collective-permute-start(bf16[128,1024]{1,0:T(8,128)(2,1)S(1)} %slice.31), channel_id=1, source_target_pairs={{0,3},{8,14},{16,19},{24,30},{32,35},{40,46},{48,51},{56,62},{64,6... | collective-permute-start | bytes 786440 | tf_op jit(solution)/shard_map/panel_z/ppermute | solution.py:18
  10.5 1.3 %collective-permute-start.1 = (bf16[128,1024]{1,0:T(8,128)(2,1)S(1)}, bf16[128,1024]{1,0:T(8,128)(2,1)S(1)}, u32[]{:S(2)}, u32[]{:S(2)}) collective-permute-start(bf16[128,1024]{1,0:T(8,128)(2,1)S(1)} %slice.31), channel_id=1, source_target_pairs={{0,6},{8,11},{16,22},{24,27},{32,38},{40,43},{48,54},{56,59},{64,7... | collective-permute-start | bytes 786440 | tf_op jit(solution)/shard_map/panel_z/ppermute | solution.py:18
  11.8 1.3 %collective-permute-start.7 = (bf16[128,1024]{1,0:T(8,128)(2,1)S(1)}, bf16[128,1024]{1,0:T(8,128)(2,1)S(1)}, u32[]{:S(2)}, u32[]{:S(2)}) collective-permute-start(bf16[128,1024]{1,0:T(8,128)(2,1)S(1)} %slice.31), channel_id=1, source_target_pairs={{0,1},{8,9},{16,17},{24,25},{32,33},{40,41},{48,49},{56,57},{64,65... | collective-permute-start | bytes 786440 | tf_op jit(solution)/shard_map/panel_z/ppermute | solution.py:14
  13.1 0.7 fusion.19
  13.8 1.2 %copy.18 = bf16[128,1536]{0,1:T(8,128)(2,1)S(1)} copy(bf16[128,1536]{1,0:T(8,128)(2,1)} %param.3) | data formatting | bytes 786432 | tf_op args[0]
  15.1 0.2 concatenate.37
  15.3 2.8 %collective-permute-start.4 = (bf16[400,128]{1,0:T(8,128)(2,1)S(1)}, bf16[400,128]{1,0:T(8,128)(2,1)S(1)}, u32[]{:S(2)}, u32[]{:S(2)}) collective-permute-start(bf16[400,128]{1,0:T(8,128)(2,1)S(1)} %concatenate.37), channel_id=1, source_target_pairs={{0,64},{8,72},{32,96},{40,104},{64,0},{72,8},{96,32},{104,40},{1,6... | collective-permute-start | bytes 307208 | tf_op jit(solution)/shard_map/blocks/ppermute | solution.py:25
  18.1 0.2 concatenate.38
  18.3 0.9 %collective-permute-start.5 = (bf16[400,128]{1,0:T(8,128)(2,1)S(1)}, bf16[400,128]{1,0:T(8,128)(2,1)S(1)}, u32[]{:S(2)}, u32[]{:S(2)}) collective-permute-start(bf16[400,128]{1,0:T(8,128)(2,1)S(1)} %concatenate.38), channel_id=1, source_target_pairs={{0,32},{8,104},{32,64},{40,8},{64,96},{72,40},{96,0},{104,72},{1,3... | collective-permute-start | bytes 307208 | tf_op jit(solution)/shard_map/blocks/ppermute | solution.py:25
  19.2 0.2 concatenate.39
  19.4 0.2 concatenate.36
  19.7 0.7 collective-permute-start.6
  20.4 0.0 collective-permute-done.1
  20.4 0.7 collective-permute-start.2
  21.1 0.7 collective-permute-start.3
  21.8 4.5 %fusion = (bf16[1024,1024]{1,0:T(8,128)(2,1)S(1)}, bf16[1024,1024]{1,0:T(8,128)(2,1)}) fusion(f32[1024,1024]{1,0:T(8,128)} %param.5), kind=kLoop, calls=%fused_computation.2 | loop fusion | flops 4194304 | bytes 8388608 | tf_op jit(solution)/shard_map/panel_z/convert_element_type | solution.py:43
  26.3 0.1 select_select_fusion
  26.3 2.5 %collective-permute-start.8 = (bf16[128,1024]{1,0:T(8,128)(2,1)S(1)}, bf16[128,1024]{1,0:T(8,128)(2,1)S(1)}, u32[]{:S(2)}, u32[]{:S(2)}) collective-permute-start(bf16[128,1024]{1,0:T(8,128)(2,1)S(1)} %select_select_fusion), channel_id=1, source_target_pairs={{0,32},{8,104},{32,64},{40,8},{64,96},{72,40},{96,0},{104,72},{1,3... | collective-permute-start | bytes 786440 | tf_op jit(solution)/shard_map/panel_x/ppermute | solution.py:25
  28.9 3.3 %collective-permute-done.8 = bf16[128,1024]{1,0:T(8,128)(2,1)S(1)} collective-permute-done((bf16[128,1024]{1,0:T(8,128)(2,1)S(1)}, bf16[128,1024]{1,0:T(8,128)(2,1)S(1)}, u32[]{:S(2)}, u32[]{:S(2)}) %collective-permute-start.8) | collective-permute-done | bytes 262176 | tf_op jit(solution)/shard_map/panel_x/ppermute | solution.py:25
  32.2 3.1 %collective-permute-start.9 = (bf16[128,1024]{1,0:T(8,128)(2,1)S(1)}, bf16[128,1024]{1,0:T(8,128)(2,1)S(1)}, u32[]{:S(2)}, u32[]{:S(2)}) collective-permute-start(bf16[128,1024]{1,0:T(8,128)(2,1)S(1)} %collective-permute-done.8), channel_id=1, source_target_pairs={{0,32},{8,104},{32,64},{40,8},{64,96},{72,40},{96,0},{104,72},{1,3... | collective-permute-start | bytes 786440 | tf_op jit(solution)/shard_map/panel_x/ppermute | solution.py:25
  35.4 2.7 %collective-permute-done.10 = bf16[128,1024]{1,0:T(8,128)(2,1)S(1)} collective-permute-done((bf16[128,1024]{1,0:T(8,128)(2,1)S(1)}, bf16[128,1024]{1,0:T(8,128)(2,1)S(1)}, u32[]{:S(2)}, u32[]{:S(2)}) %collective-permute-start.10) | collective-permute-done | bytes 262176 | tf_op jit(solution)/shard_map/panel_x/ppermute | solution.py:25
  38.0 0.5 collective-permute-done.9
  38.6 0.7 fusion.2
  39.3 0.1 dynamic-slice_bitcast_fusion
  39.4 7.9 %collective-permute-start.11 = (f32[4,48,1024]{2,1,0:T(8,128)S(1)}, f32[4,48,1024]{2,1,0:T(8,128)S(1)}, u32[]{:S(2)}, u32[]{:S(2)}) collective-permute-start(f32[4,48,1024]{2,1,0:T(8,128)S(1)} %dynamic-slice_bitcast_fusion), channel_id=1, source_target_pairs={{0,8},{8,0},{1,9},{9,1},{2,10},{10,2},{3,11},{11,3},{4,12},{12,4},... | collective-permute-start | bytes 2359304 | tf_op jit(solution)/shard_map/sum_core/ppermute | solution.py:29
  47.4 1.8 %collective-permute-done.11 = f32[4,48,1024]{2,1,0:T(8,128)S(1)} collective-permute-done((f32[4,48,1024]{2,1,0:T(8,128)S(1)}, f32[4,48,1024]{2,1,0:T(8,128)S(1)}, u32[]{:S(2)}, u32[]{:S(2)}) %collective-permute-start.11) | collective-permute-done | bytes 786464 | tf_op jit(solution)/shard_map/sum_core/ppermute | solution.py:29
  49.1 0.1 bitcast_add_fusion
  49.3 3.0 %collective-permute-start.12 = (bf16[48,1024]{1,0:T(8,128)(2,1)S(1)}, bf16[48,1024]{1,0:T(8,128)(2,1)S(1)}, u32[]{:S(2)}, u32[]{:S(2)}) collective-permute-start(bf16[48,1024]{1,0:T(8,128)(2,1)S(1)} %get-tuple-element.34), channel_id=1, source_target_pairs={{0,128},{16,144},{128,0},{144,16},{1,129},{17,145},{129,1},{145,17... | collective-permute-start | bytes 294920 | tf_op jit(solution)/shard_map/sum_y/ppermute | solution.py:10
  52.3 0.4 collective-permute-start.13
  52.7 2.3 %collective-permute-start.14 = (bf16[48,1024]{1,0:T(8,128)(2,1)S(1)}, bf16[48,1024]{1,0:T(8,128)(2,1)S(1)}, u32[]{:S(2)}, u32[]{:S(2)}) collective-permute-start(bf16[48,1024]{1,0:T(8,128)(2,1)S(1)} %get-tuple-element.35), channel_id=1, source_target_pairs={{0,144},{16,0},{128,16},{144,128},{1,145},{17,1},{129,17},{145,129... | collective-permute-start | bytes 294920 | tf_op jit(solution)/shard_map/sum_y/ppermute | solution.py:10
  55.0 2.0 %collective-permute-done.13 = bf16[48,1024]{1,0:T(8,128)(2,1)S(1)} collective-permute-done((bf16[48,1024]{1,0:T(8,128)(2,1)S(1)}, bf16[48,1024]{1,0:T(8,128)(2,1)S(1)}, u32[]{:S(2)}, u32[]{:S(2)}) %collective-permute-start.13) | collective-permute-done | bytes 98336 | tf_op jit(solution)/shard_map/sum_y/ppermute | solution.py:10
  57.0 0.4 collective-permute-done.14
  57.3 0.1 fusion.4
  57.5 0.5 fusion.5
  57.9 1.2 %constant_dynamic-update-slice_fusion.8 = (bf16[384,1024]{1,0:T(8,128)(2,1)S(1)}, bf16[48,1024]{1,0:T(8,128)(2,1)S(1)}, f32[48,1024]{1,0:T(8,128)}) fusion(bf16[48,1024]{1,0:T(8,128)(2,1)S(1)} %get-tuple-element.33, bf16[1024,1024]{1,0:T(8,128)(2,1)S(1)} %get-tuple-element.23, f32[96,1024]{1,0:T(8,128)S(1)} %fusion.5), kind=kOutput, calls=%fused_computation.50 | convolution fusion | flops 100810752 | bytes 2981888 | tf_op jit(solution)/shard_map/screen/dot_general | solution.py:123
  59.1 1.5 %collective-permute-start.15 = (bf16[48,1024]{1,0:T(8,128)(2,1)S(1)}, bf16[48,1024]{1,0:T(8,128)(2,1)S(1)}, u32[]{:S(2)}, u32[]{:S(2)}) collective-permute-start(bf16[48,1024]{1,0:T(8,128)(2,1)S(1)} %get-tuple-element.27), channel_id=1, source_target_pairs={{0,128},{16,144},{128,0},{144,16},{1,129},{17,145},{129,1},{145,17... | collective-permute-start | bytes 294920 | tf_op jit(solution)/shard_map/gather_y/ppermute | solution.py:10
  60.6 1.5 %collective-permute-start.16 = (bf16[48,1024]{1,0:T(8,128)(2,1)S(1)}, bf16[48,1024]{1,0:T(8,128)(2,1)S(1)}, u32[]{:S(2)}, u32[]{:S(2)}) collective-permute-start(bf16[48,1024]{1,0:T(8,128)(2,1)S(1)} %get-tuple-element.27), channel_id=1, source_target_pairs={{0,16},{16,128},{128,144},{144,0},{1,17},{17,129},{129,145},{145,1... | collective-permute-start | bytes 294920 | tf_op jit(solution)/shard_map/gather_y/ppermute | solution.py:10
  62.1 1.2 %collective-permute-start.17 = (bf16[48,1024]{1,0:T(8,128)(2,1)S(1)}, bf16[48,1024]{1,0:T(8,128)(2,1)S(1)}, u32[]{:S(2)}, u32[]{:S(2)}) collective-permute-start(bf16[48,1024]{1,0:T(8,128)(2,1)S(1)} %get-tuple-element.27), channel_id=1, source_target_pairs={{0,144},{16,0},{128,16},{144,128},{1,145},{17,1},{129,17},{145,129... | collective-permute-start | bytes 294920 | tf_op jit(solution)/shard_map/gather_y/ppermute | solution.py:10
  63.3 0.8 collective-permute-done.15
  64.1 2.1 %collective-permute-done.16 = bf16[48,1024]{1,0:T(8,128)(2,1)S(1)} collective-permute-done((bf16[48,1024]{1,0:T(8,128)(2,1)S(1)}, bf16[48,1024]{1,0:T(8,128)(2,1)S(1)}, u32[]{:S(2)}, u32[]{:S(2)}) %collective-permute-start.16) | collective-permute-done | bytes 98336 | tf_op jit(solution)/shard_map/gather_y/ppermute | solution.py:10
  66.2 3.2 %collective-permute-start.18 = (bf16[192,1024]{1,0:T(8,128)(2,1)S(1)}, bf16[192,1024]{1,0:T(8,128)(2,1)S(1)}, u32[]{:S(2)}, u32[]{:S(2)}) collective-permute-start(bf16[192,1024]{1,0:T(8,128)(2,1)S(1)} %pad_maximum_fusion.1), channel_id=1, source_target_pairs={{0,8},{8,0},{1,9},{9,1},{2,10},{10,2},{3,11},{11,3},{4,12},{12,4},... | collective-permute-start | bytes 1179656 | tf_op jit(solution)/shard_map/gather_y/ppermute | solution.py:29
  69.4 1.3 %collective-permute-done.18 = bf16[192,1024]{1,0:T(8,128)(2,1)S(1)} collective-permute-done((bf16[192,1024]{1,0:T(8,128)(2,1)S(1)}, bf16[192,1024]{1,0:T(8,128)(2,1)S(1)}, u32[]{:S(2)}, u32[]{:S(2)}) %collective-permute-start.18) | collective-permute-done | bytes 393248 | tf_op jit(solution)/shard_map/gather_y/ppermute | solution.py:29
  70.8 0.6 fusion.1
  71.4 0.1 select_add_fusion
  71.5 14.3 %all_to_all.9 = f32[32,1,128]{2,1,0:T(1,128)S(1)} all-to-all(f32[32,1,128]{2,1,0:T(1,128)S(1)} %bitcast.61), channel_id=1, replica_groups=mesh['grp'=2,'x'=4,'ylo'=2,'core'=2,'col'=8] {'x','col'}, dimensions={0} | all-to-all | bytes 32768 | tf_op jit(solution)/shard_map/sigma/all_to_all | solution.py:148
  85.8 0.6 reduce_sum.29
  (43 shorter events, 0.5 us)
Async XLA Ops:
  0.6 19.7 %copy-start.1 = (bf16[128,1536]{1,0:T(8,128)(2,1)S(1)}, bf16[128,1536]{1,0:T(8,128)(2,1)}, u32[]{:S(2)}) copy-start(bf16[128,1536]{1,0:T(8,128)(2,1)} %param.3) | copy-start | bytes 1179652
  1.7 18.0 %collective-permute-start = (bf16[128,1024]{1,0:T(8,128)(2,1)S(1)}, bf16[128,1024]{1,0:T(8,128)(2,1)S(1)}, u32[]{:S(2)}, u32[]{:S(2)}) collective-permute-start(bf16[128,1024]{1,0:T(8,128)(2,1)S(1)} %slice.31), channel_id=1, source_target_pairs={{0,3},{8,14},{16,19},{24,30},{32,35},{40,46},{48,51},{56,62},{64,6... | collective-permute-start | bytes 786440 | tf_op jit(solution)/shard_map/panel_z/ppermute | solution.py:18
  10.5 9.9 %collective-permute-start.1 = (bf16[128,1024]{1,0:T(8,128)(2,1)S(1)}, bf16[128,1024]{1,0:T(8,128)(2,1)S(1)}, u32[]{:S(2)}, u32[]{:S(2)}) collective-permute-start(bf16[128,1024]{1,0:T(8,128)(2,1)S(1)} %slice.31), channel_id=1, source_target_pairs={{0,6},{8,11},{16,22},{24,27},{32,38},{40,43},{48,54},{56,59},{64,7... | collective-permute-start | bytes 786440 | tf_op jit(solution)/shard_map/panel_z/ppermute | solution.py:18
  11.8 14.5 %collective-permute-start.7 = (bf16[128,1024]{1,0:T(8,128)(2,1)S(1)}, bf16[128,1024]{1,0:T(8,128)(2,1)S(1)}, u32[]{:S(2)}, u32[]{:S(2)}) collective-permute-start(bf16[128,1024]{1,0:T(8,128)(2,1)S(1)} %slice.31), channel_id=1, source_target_pairs={{0,1},{8,9},{16,17},{24,25},{32,33},{40,41},{48,49},{56,57},{64,65... | collective-permute-start | bytes 786440 | tf_op jit(solution)/shard_map/panel_z/ppermute | solution.py:14
  15.3 5.8 %collective-permute-start.4 = (bf16[400,128]{1,0:T(8,128)(2,1)S(1)}, bf16[400,128]{1,0:T(8,128)(2,1)S(1)}, u32[]{:S(2)}, u32[]{:S(2)}) collective-permute-start(bf16[400,128]{1,0:T(8,128)(2,1)S(1)} %concatenate.37), channel_id=1, source_target_pairs={{0,64},{8,72},{32,96},{40,104},{64,0},{72,8},{96,32},{104,40},{1,6... | collective-permute-start | bytes 307208 | tf_op jit(solution)/shard_map/blocks/ppermute | solution.py:25
  18.3 7.9 %collective-permute-start.5 = (bf16[400,128]{1,0:T(8,128)(2,1)S(1)}, bf16[400,128]{1,0:T(8,128)(2,1)S(1)}, u32[]{:S(2)}, u32[]{:S(2)}) collective-permute-start(bf16[400,128]{1,0:T(8,128)(2,1)S(1)} %concatenate.38), channel_id=1, source_target_pairs={{0,32},{8,104},{32,64},{40,8},{64,96},{72,40},{96,0},{104,72},{1,3... | collective-permute-start | bytes 307208 | tf_op jit(solution)/shard_map/blocks/ppermute | solution.py:25
  19.7 6.6 %collective-permute-start.6 = (bf16[400,128]{1,0:T(8,128)(2,1)S(1)}, bf16[400,128]{1,0:T(8,128)(2,1)S(1)}, u32[]{:S(2)}, u32[]{:S(2)}) collective-permute-start(bf16[400,128]{1,0:T(8,128)(2,1)S(1)} %concatenate.39), channel_id=1, source_target_pairs={{0,96},{8,40},{32,0},{40,72},{64,32},{72,104},{96,64},{104,8},{1,9... | collective-permute-start | bytes 307208 | tf_op jit(solution)/shard_map/blocks/ppermute | solution.py:25
  20.4 5.8 %collective-permute-start.2 = (bf16[128,1024]{1,0:T(8,128)(2,1)S(1)}, bf16[128,1024]{1,0:T(8,128)(2,1)S(1)}, u32[]{:S(2)}, u32[]{:S(2)}) collective-permute-start(bf16[128,1024]{1,0:T(8,128)(2,1)S(1)} %select_select_fusion.1), channel_id=1, source_target_pairs={{3,4},{6,5},{11,12},{14,13},{19,20},{22,21},{27,28},{30,29},{35,36... | collective-permute-start | bytes 786440 | tf_op jit(solution)/shard_map/panel_z/ppermute | solution.py:14
  21.1 5.2 %collective-permute-start.3 = (bf16[128,1024]{1,0:T(8,128)(2,1)S(1)}, bf16[128,1024]{1,0:T(8,128)(2,1)S(1)}, u32[]{:S(2)}, u32[]{:S(2)}) collective-permute-start(bf16[128,1024]{1,0:T(8,128)(2,1)S(1)} %select_select_fusion.1), channel_id=1, source_target_pairs={{3,2},{6,7},{11,10},{14,15},{19,18},{22,23},{27,26},{30,31},{35,34... | collective-permute-start | bytes 786440 | tf_op jit(solution)/shard_map/panel_z/ppermute | solution.py:14
  26.3 5.8 %collective-permute-start.8 = (bf16[128,1024]{1,0:T(8,128)(2,1)S(1)}, bf16[128,1024]{1,0:T(8,128)(2,1)S(1)}, u32[]{:S(2)}, u32[]{:S(2)}) collective-permute-start(bf16[128,1024]{1,0:T(8,128)(2,1)S(1)} %select_select_fusion), channel_id=1, source_target_pairs={{0,32},{8,104},{32,64},{40,8},{64,96},{72,40},{96,0},{104,72},{1,3... | collective-permute-start | bytes 786440 | tf_op jit(solution)/shard_map/panel_x/ppermute | solution.py:25
  28.8 9.2 %collective-permute-start.10 = (bf16[128,1024]{1,0:T(8,128)(2,1)S(1)}, bf16[128,1024]{1,0:T(8,128)(2,1)S(1)}, u32[]{:S(2)}, u32[]{:S(2)}) collective-permute-start(bf16[128,1024]{1,0:T(8,128)(2,1)S(1)} %select_select_fusion), channel_id=1, source_target_pairs={{0,96},{8,40},{32,0},{40,72},{64,32},{72,104},{96,64},{104,8},{1,9... | collective-permute-start | bytes 786440 | tf_op jit(solution)/shard_map/panel_x/ppermute | solution.py:25
  32.2 6.4 %collective-permute-start.9 = (bf16[128,1024]{1,0:T(8,128)(2,1)S(1)}, bf16[128,1024]{1,0:T(8,128)(2,1)S(1)}, u32[]{:S(2)}, u32[]{:S(2)}) collective-permute-start(bf16[128,1024]{1,0:T(8,128)(2,1)S(1)} %collective-permute-done.8), channel_id=1, source_target_pairs={{0,32},{8,104},{32,64},{40,8},{64,96},{72,40},{96,0},{104,72},{1,3... | collective-permute-start | bytes 786440 | tf_op jit(solution)/shard_map/panel_x/ppermute | solution.py:25
  39.4 9.8 %collective-permute-start.11 = (f32[4,48,1024]{2,1,0:T(8,128)S(1)}, f32[4,48,1024]{2,1,0:T(8,128)S(1)}, u32[]{:S(2)}, u32[]{:S(2)}) collective-permute-start(f32[4,48,1024]{2,1,0:T(8,128)S(1)} %dynamic-slice_bitcast_fusion), channel_id=1, source_target_pairs={{0,8},{8,0},{1,9},{9,1},{2,10},{10,2},{3,11},{11,3},{4,12},{12,4},... | collective-permute-start | bytes 2359304 | tf_op jit(solution)/shard_map/sum_core/ppermute | solution.py:29
  47.3 10.2 %copy-start = (bf16[1024,1024]{1,0:T(8,128)(2,1)S(1)}, bf16[1024,1024]{1,0:T(8,128)(2,1)}, u32[]{:S(2)}) copy-start(bf16[1024,1024]{1,0:T(8,128)(2,1)} %get-tuple-element.22) | copy-start | bytes 6291460
  49.3 5.7 %collective-permute-start.12 = (bf16[48,1024]{1,0:T(8,128)(2,1)S(1)}, bf16[48,1024]{1,0:T(8,128)(2,1)S(1)}, u32[]{:S(2)}, u32[]{:S(2)}) collective-permute-start(bf16[48,1024]{1,0:T(8,128)(2,1)S(1)} %get-tuple-element.34), channel_id=1, source_target_pairs={{0,128},{16,144},{128,0},{144,16},{1,129},{17,145},{129,1},{145,17... | collective-permute-start | bytes 294920 | tf_op jit(solution)/shard_map/sum_y/ppermute | solution.py:10
  52.3 4.7 %collective-permute-start.13 = (bf16[48,1024]{1,0:T(8,128)(2,1)S(1)}, bf16[48,1024]{1,0:T(8,128)(2,1)S(1)}, u32[]{:S(2)}, u32[]{:S(2)}) collective-permute-start(bf16[48,1024]{1,0:T(8,128)(2,1)S(1)} %get-tuple-element.36), channel_id=1, source_target_pairs={{0,16},{16,128},{128,144},{144,0},{1,17},{17,129},{129,145},{145,1... | collective-permute-start | bytes 294920 | tf_op jit(solution)/shard_map/sum_y/ppermute | solution.py:10
  52.7 4.6 %collective-permute-start.14 = (bf16[48,1024]{1,0:T(8,128)(2,1)S(1)}, bf16[48,1024]{1,0:T(8,128)(2,1)S(1)}, u32[]{:S(2)}, u32[]{:S(2)}) collective-permute-start(bf16[48,1024]{1,0:T(8,128)(2,1)S(1)} %get-tuple-element.35), channel_id=1, source_target_pairs={{0,144},{16,0},{128,16},{144,128},{1,145},{17,1},{129,17},{145,129... | collective-permute-start | bytes 294920 | tf_op jit(solution)/shard_map/sum_y/ppermute | solution.py:10
  59.1 5.0 %collective-permute-start.15 = (bf16[48,1024]{1,0:T(8,128)(2,1)S(1)}, bf16[48,1024]{1,0:T(8,128)(2,1)S(1)}, u32[]{:S(2)}, u32[]{:S(2)}) collective-permute-start(bf16[48,1024]{1,0:T(8,128)(2,1)S(1)} %get-tuple-element.27), channel_id=1, source_target_pairs={{0,128},{16,144},{128,0},{144,16},{1,129},{17,145},{129,1},{145,17... | collective-permute-start | bytes 294920 | tf_op jit(solution)/shard_map/gather_y/ppermute | solution.py:10
  60.6 5.6 %collective-permute-start.16 = (bf16[48,1024]{1,0:T(8,128)(2,1)S(1)}, bf16[48,1024]{1,0:T(8,128)(2,1)S(1)}, u32[]{:S(2)}, u32[]{:S(2)}) collective-permute-start(bf16[48,1024]{1,0:T(8,128)(2,1)S(1)} %get-tuple-element.27), channel_id=1, source_target_pairs={{0,16},{16,128},{128,144},{144,0},{1,17},{17,129},{129,145},{145,1... | collective-permute-start | bytes 294920 | tf_op jit(solution)/shard_map/gather_y/ppermute | solution.py:10
  62.1 4.1 %collective-permute-start.17 = (bf16[48,1024]{1,0:T(8,128)(2,1)S(1)}, bf16[48,1024]{1,0:T(8,128)(2,1)S(1)}, u32[]{:S(2)}, u32[]{:S(2)}) collective-permute-start(bf16[48,1024]{1,0:T(8,128)(2,1)S(1)} %get-tuple-element.27), channel_id=1, source_target_pairs={{0,144},{16,0},{128,16},{144,128},{1,145},{17,1},{129,17},{145,129... | collective-permute-start | bytes 294920 | tf_op jit(solution)/shard_map/gather_y/ppermute | solution.py:10
  66.2 4.5 %collective-permute-start.18 = (bf16[192,1024]{1,0:T(8,128)(2,1)S(1)}, bf16[192,1024]{1,0:T(8,128)(2,1)S(1)}, u32[]{:S(2)}, u32[]{:S(2)}) collective-permute-start(bf16[192,1024]{1,0:T(8,128)(2,1)S(1)} %pad_maximum_fusion.1), channel_id=1, source_target_pairs={{0,8},{8,0},{1,9},{9,1},{2,10},{10,2},{3,11},{11,3},{4,12},{12,4},... | collective-permute-start | bytes 1179656 | tf_op jit(solution)/shard_map/gather_y/ppermute | solution.py:29

commit v7 on v5

--- a/solution.py
+++ b/solution.py
@@ -12,6 +12,11 @@
 
 def along_z(value, *pairs):
     return lax.ppermute(value, Z, pairs)
+
+
+def along_x(value, size, step, columns):
+    pairs = [(i * 8 + z, (i + step) % size * 8 + z) for i in range(size) for z in columns]
+    return lax.ppermute(value, (X, Z), pairs)
 
 
 def swap(value):
@@ -66,16 +71,20 @@
         held = jnp.where(z == 3, far_a, jnp.where(z == 6, far_b, piece))
         near_a = along_z(held, (0, 1), (3, 4), (6, 5))
         near_b = along_z(held, (0, 7), (3, 2))
+        far_x = along_x(held, nx, 2, (0, 3, 6))
+        far_near_a = along_z(far_x, (0, 1), (3, 4), (6, 5))
+        far_near_b = along_z(far_x, (0, 7), (3, 2))
         inv_high, inv_rest = two_parts(block_inverse)
-        near_a, near_b, inv_high, inv_rest, *factors = lax.optimization_barrier(
-            (near_a, near_b, inv_high, inv_rest, *factors)
+        near_a, near_b, inv_high, inv_rest, _, *factors = lax.optimization_barrier(
+            (near_a, near_b, inv_high, inv_rest, far_x, *factors)
         )
-        held = jnp.where((z == 1) | (z == 4) | (z == 5), near_a, held)
-        held = jnp.where((z == 7) | (z == 2), near_b, held)
+        from_a, from_b = (z == 1) | (z == 4) | (z == 5), (z == 7) | (z == 2)
+        held = jnp.where(from_a, near_a, jnp.where(from_b, near_b, held))
 
     with jax.named_scope("panel_x"):
-        panels = [held] + [shift(held, X, nx, k) for k in steps[1:]]
-        panels = jnp.concatenate(panels, axis=0)
+        right, left = shift(held, X, nx, 1), shift(held, X, nx, 3)
+        far_x = jnp.where(from_a, far_near_a, jnp.where(from_b, far_near_b, far_x))
+        panels = jnp.concatenate([held, far_x, right, left], axis=0)
 
     with jax.named_scope("response"):
         factors = jnp.concatenate(factors, axis=1)

time: 82.2 us -> 84 us (1.022)
  starting transfers between devices: 34.3 us -> 41.9 us
  waiting for transfers between devices: 21.2 us -> 15.8 us
    ppermute x12 -> x11, waiting for transfers between devices: 17.3 us -> 5.28 us  [shift(): lax.ppermute(value, axis, [(i, (i + step) % size) for i in range(size)])]
    ppermute x0 -> x1, waiting for transfers between devices: none -> 4.31 us  [along_x(): return lax.ppermute(value, (X, Z), pairs)]
    ppermute x2, starting transfers between devices: 3.94 us -> 7.1 us  [swap(): return lax.ppermute(value, CORE, [(0, 1), (1, 0)])]
    ppermute x4 -> x6, starting transfers between devices: 12.1 us -> 14.7 us  [along_z(): return lax.ppermute(value, Z, pairs)]
    ppermute x4 -> x6, waiting for transfers between devices: 0.9 us -> 3.2 us  [along_z(): return lax.ppermute(value, Z, pairs)]
    ppermute x0 -> x1, starting transfers between devices: none -> 1.92 us  [along_x(): return lax.ppermute(value, (X, Z), pairs)]
    ppermute x12 -> x11, starting transfers between devices: 18.4 us -> 18.2 us  [shift(): lax.ppermute(value, axis, [(i, (i + step) % size) for i in range(size)])]
  transfers between devices with their start and end apart: 18 -> 20, of which waited for: 9 -> 9; matrix products, arithmetic and copies ran while one was open for 7% -> 7% of each run, Pallas kernels for 0% -> 0%
where the time goes in v7:
time: 84 us; the launch traced here: 83.6 us
  starting transfers between devices  41.9 us (50%)
  waiting for transfers between devices  15.8 us (19%)
  blocking collectives  13.5 us (16%)
  other arithmetic  4.85 us (6%)
  local copies, waits for them, and re-layouts  3.34 us (4%)
  matrix products  2.94 us (4%)
  between operations  1.17 us (1%)
    ppermute x11, starting transfers between devices, shift(): lax.ppermute(value, axis, [(i, (i + step) % size) for i in range(size)])  18.2 us
    ppermute x6, starting transfers between devices, along_z(): return lax.ppermute(value, Z, pairs)  14.7 us
    all_to_all x1, blocking collectives, body(): terms = lax.all_to_all(copies, (X, Z), 0, 0, tiled=True)  13.5 us
    ppermute x2, starting transfers between devices, swap(): return lax.ppermute(value, CORE, [(0, 1), (1, 0)])  7.1 us
    ppermute x11, waiting for transfers between devices, shift(): lax.ppermute(value, axis, [(i, (i + step) % size) for i in range(size)])  5.28 us
    ppermute x1, waiting for transfers between devices, along_x(): return lax.ppermute(value, (X, Z), pairs)  4.31 us
    convert_element_type x2, other arithmetic, two_parts(): return (high.astype(LOW), (value - high).astype(LOW))  3.22 us
    ppermute x6, waiting for transfers between devices, along_z(): return lax.ppermute(value, Z, pairs)  3.2 us
  transfers between devices with their start and end apart: 20, of which 9 were waited for; matrix products, arithmetic and copies ran while one was open for 7% of the time, Pallas kernels for 0%

profile of v7, /device:TPU:1, one launch (start us, length us, event | category | flops | bytes accessed | tf_op | source)
XLA Modules:
  0.0 83.6 jit_solution(7128255574690804086)
XLA Ops:
  0.6 1.0 %slice.31 = bf16[128,1024]{1,0:T(8,128)(2,1)S(1)} slice(bf16[128,1536]{1,0:T(8,128)(2,1)} %param.3), slice={[0:128], [0:1024]} | slice | bytes 524288 | tf_op jit(solution)/shard_map/panel_z/slice | solution.py:49
  1.7 7.1 %collective-permute-start = (bf16[128,1024]{1,0:T(8,128)(2,1)S(1)}, bf16[128,1024]{1,0:T(8,128)(2,1)S(1)}, u32[]{:S(2)}, u32[]{:S(2)}) collective-permute-start(bf16[128,1024]{1,0:T(8,128)(2,1)S(1)} %slice.31), channel_id=1, source_target_pairs={{0,3},{8,11},{16,19},{24,27},{32,35},{40,43},{48,51},{56,59},{64,6... | collective-permute-start | bytes 786440 | tf_op jit(solution)/shard_map/panel_z/ppermute | solution.py:14
  8.8 2.4 %collective-permute-start.1 = (bf16[128,1024]{1,0:T(8,128)(2,1)S(1)}, bf16[128,1024]{1,0:T(8,128)(2,1)S(1)}, u32[]{:S(2)}, u32[]{:S(2)}) collective-permute-start(bf16[128,1024]{1,0:T(8,128)(2,1)S(1)} %slice.31), channel_id=1, source_target_pairs={{0,6},{8,14},{16,22},{24,30},{32,38},{40,46},{48,54},{56,62},{64,7... | collective-permute-start | bytes 786440 | tf_op jit(solution)/shard_map/panel_z/ppermute | solution.py:14
  11.1 0.7 fusion.19
  11.9 1.2 %copy.18 = bf16[128,1536]{0,1:T(8,128)(2,1)S(1)} copy(bf16[128,1536]{1,0:T(8,128)(2,1)} %param.3) | data formatting | bytes 786432 | tf_op args[0]
  13.2 0.2 concatenate.37
  13.3 2.8 %collective-permute-start.5 = (bf16[400,128]{1,0:T(8,128)(2,1)S(1)}, bf16[400,128]{1,0:T(8,128)(2,1)S(1)}, u32[]{:S(2)}, u32[]{:S(2)}) collective-permute-start(bf16[400,128]{1,0:T(8,128)(2,1)S(1)} %concatenate.37), channel_id=1, source_target_pairs={{0,64},{32,96},{64,0},{96,32},{1,65},{33,97},{65,1},{97,33},{2,66}... | collective-permute-start | bytes 307208 | tf_op jit(solution)/shard_map/blocks/ppermute | solution.py:10
  16.2 0.2 concatenate.38
  16.3 0.4 collective-permute-start.6
  16.7 0.2 concatenate.39
  16.9 2.4 %collective-permute-start.7 = (bf16[400,128]{1,0:T(8,128)(2,1)S(1)}, bf16[400,128]{1,0:T(8,128)(2,1)S(1)}, u32[]{:S(2)}, u32[]{:S(2)}) collective-permute-start(bf16[400,128]{1,0:T(8,128)(2,1)S(1)} %concatenate.39), channel_id=1, source_target_pairs={{0,96},{32,0},{64,32},{96,64},{1,97},{33,1},{65,33},{97,65},{2,98}... | collective-permute-start | bytes 307208 | tf_op jit(solution)/shard_map/blocks/ppermute | solution.py:10
  19.3 0.2 concatenate.36
  19.7 1.3 %collective-permute-start.2 = (bf16[128,1024]{1,0:T(8,128)(2,1)S(1)}, bf16[128,1024]{1,0:T(8,128)(2,1)S(1)}, u32[]{:S(2)}, u32[]{:S(2)}) collective-permute-start(bf16[128,1024]{1,0:T(8,128)(2,1)S(1)} %select_select_fusion.2), channel_id=1, source_target_pairs={{0,1},{3,4},{6,5},{8,9},{11,12},{14,13},{16,17},{19,20},{22,21},{2... | collective-permute-start | bytes 786440 | tf_op jit(solution)/shard_map/panel_z/ppermute | solution.py:14
  21.0 1.3 %collective-permute-start.3 = (bf16[128,1024]{1,0:T(8,128)(2,1)S(1)}, bf16[128,1024]{1,0:T(8,128)(2,1)S(1)}, u32[]{:S(2)}, u32[]{:S(2)}) collective-permute-start(bf16[128,1024]{1,0:T(8,128)(2,1)S(1)} %select_select_fusion.2), channel_id=1, source_target_pairs={{0,7},{3,2},{8,15},{11,10},{16,23},{19,18},{24,31},{27,26},{32,39}... | collective-permute-start | bytes 786440 | tf_op jit(solution)/shard_map/panel_z/ppermute | solution.py:14
  22.3 1.9 %collective-permute-start.4 = (bf16[128,1024]{1,0:T(8,128)(2,1)S(1)}, bf16[128,1024]{1,0:T(8,128)(2,1)S(1)}, u32[]{:S(2)}, u32[]{:S(2)}) collective-permute-start(bf16[128,1024]{1,0:T(8,128)(2,1)S(1)} %select_select_fusion.2), channel_id=1, source_target_pairs={{0,64},{3,67},{6,70},{32,96},{35,99},{38,102},{64,0},{67,3},{70,6}... | collective-permute-start | bytes 786440 | tf_op jit(solution)/shard_map/panel_z/ppermute | solution.py:19
  24.2 3.1 %fusion = (bf16[1024,1024]{1,0:T(8,128)(2,1)S(1)}, bf16[1024,1024]{1,0:T(8,128)(2,1)S(1)}) fusion(f32[1024,1024]{1,0:T(8,128)} %param.5), kind=kLoop, calls=%fused_computation.2 | loop fusion | flops 4194304 | bytes 8388608 | tf_op jit(solution)/shard_map/panel_z/convert_element_type | solution.py:37
  27.4 4.3 %collective-permute-done.4 = bf16[128,1024]{1,0:T(8,128)(2,1)S(1)} collective-permute-done((bf16[128,1024]{1,0:T(8,128)(2,1)S(1)}, bf16[128,1024]{1,0:T(8,128)(2,1)S(1)}, u32[]{:S(2)}, u32[]{:S(2)}) %collective-permute-start.4) | collective-permute-done | bytes 262176 | tf_op jit(solution)/shard_map/panel_z/ppermute | solution.py:19
  31.8 0.1 collective-permute-start.10
  31.9 2.7 %collective-permute-start.11 = (bf16[128,1024]{1,0:T(8,128)(2,1)S(1)}, bf16[128,1024]{1,0:T(8,128)(2,1)S(1)}, u32[]{:S(2)}, u32[]{:S(2)}) collective-permute-start(bf16[128,1024]{1,0:T(8,128)(2,1)S(1)} %select_select_fusion.1), channel_id=1, source_target_pairs={{0,96},{32,0},{64,32},{96,64},{1,97},{33,1},{65,33},{97,65},{2,98}... | collective-permute-start | bytes 786440 | tf_op jit(solution)/shard_map/panel_x/ppermute | solution.py:10
  34.6 1.3 %collective-permute-start.8 = (bf16[128,1024]{1,0:T(8,128)(2,1)S(1)}, bf16[128,1024]{1,0:T(8,128)(2,1)S(1)}, u32[]{:S(2)}, u32[]{:S(2)}) collective-permute-start(bf16[128,1024]{1,0:T(8,128)(2,1)S(1)} %collective-permute-done.4), channel_id=1, source_target_pairs={{0,1},{3,4},{6,5},{8,9},{11,12},{14,13},{16,17},{19,20},{22,21},{2... | collective-permute-start | bytes 786440 | tf_op jit(solution)/shard_map/panel_z/ppermute | solution.py:14
  35.9 1.3 %collective-permute-start.9 = (bf16[128,1024]{1,0:T(8,128)(2,1)S(1)}, bf16[128,1024]{1,0:T(8,128)(2,1)S(1)}, u32[]{:S(2)}, u32[]{:S(2)}) collective-permute-start(bf16[128,1024]{1,0:T(8,128)(2,1)S(1)} %collective-permute-done.4), channel_id=1, source_target_pairs={{0,7},{3,2},{8,15},{11,10},{16,23},{19,18},{24,31},{27,26},{32,39}... | collective-permute-start | bytes 786440 | tf_op jit(solution)/shard_map/panel_z/ppermute | solution.py:14
  37.3 1.9 %collective-permute-done.8 = bf16[128,1024]{1,0:T(8,128)(2,1)S(1)} collective-permute-done((bf16[128,1024]{1,0:T(8,128)(2,1)S(1)}, bf16[128,1024]{1,0:T(8,128)(2,1)S(1)}, u32[]{:S(2)}, u32[]{:S(2)}) %collective-permute-start.8) | collective-permute-done | bytes 262176 | tf_op jit(solution)/shard_map/panel_z/ppermute | solution.py:14
  39.2 1.3 %collective-permute-done.9 = bf16[128,1024]{1,0:T(8,128)(2,1)S(1)} collective-permute-done((bf16[128,1024]{1,0:T(8,128)(2,1)S(1)}, bf16[128,1024]{1,0:T(8,128)(2,1)S(1)}, u32[]{:S(2)}, u32[]{:S(2)}) %collective-permute-start.9) | collective-permute-done | bytes 262176 | tf_op jit(solution)/shard_map/panel_z/ppermute | solution.py:14
  40.5 0.1 select_select_fusion
  40.6 0.7 fusion.2
  41.2 0.1 dynamic-slice_bitcast_fusion
  41.3 3.9 %collective-permute-start.12 = (f32[4,48,1024]{2,1,0:T(8,128)S(1)}, f32[4,48,1024]{2,1,0:T(8,128)S(1)}, u32[]{:S(2)}, u32[]{:S(2)}) collective-permute-start(f32[4,48,1024]{2,1,0:T(8,128)S(1)} %dynamic-slice_bitcast_fusion), channel_id=1, source_target_pairs={{0,8},{8,0},{1,9},{9,1},{2,10},{10,2},{3,11},{11,3},{4,12},{12,4},... | collective-permute-start | bytes 2359304 | tf_op jit(solution)/shard_map/sum_core/ppermute | solution.py:23
  45.4 1.7 %collective-permute-done.12 = f32[4,48,1024]{2,1,0:T(8,128)S(1)} collective-permute-done((f32[4,48,1024]{2,1,0:T(8,128)S(1)}, f32[4,48,1024]{2,1,0:T(8,128)S(1)}, u32[]{:S(2)}, u32[]{:S(2)}) %collective-permute-start.12) | collective-permute-done | bytes 786464 | tf_op jit(solution)/shard_map/sum_core/ppermute | solution.py:23
  47.2 0.1 bitcast_add_fusion
  47.3 3.0 %collective-permute-start.13 = (bf16[48,1024]{1,0:T(8,128)(2,1)S(1)}, bf16[48,1024]{1,0:T(8,128)(2,1)S(1)}, u32[]{:S(2)}, u32[]{:S(2)}) collective-permute-start(bf16[48,1024]{1,0:T(8,128)(2,1)S(1)} %get-tuple-element.32), channel_id=1, source_target_pairs={{0,128},{16,144},{128,0},{144,16},{1,129},{17,145},{129,1},{145,17... | collective-permute-start | bytes 294920 | tf_op jit(solution)/shard_map/sum_y/ppermute | solution.py:10
  50.3 0.4 collective-permute-start.14
  50.7 2.3 %collective-permute-start.15 = (bf16[48,1024]{1,0:T(8,128)(2,1)S(1)}, bf16[48,1024]{1,0:T(8,128)(2,1)S(1)}, u32[]{:S(2)}, u32[]{:S(2)}) collective-permute-start(bf16[48,1024]{1,0:T(8,128)(2,1)S(1)} %get-tuple-element.33), channel_id=1, source_target_pairs={{0,144},{16,0},{128,16},{144,128},{1,145},{17,1},{129,17},{145,129... | collective-permute-start | bytes 294920 | tf_op jit(solution)/shard_map/sum_y/ppermute | solution.py:10
  53.0 2.0 %collective-permute-done.14 = bf16[48,1024]{1,0:T(8,128)(2,1)S(1)} collective-permute-done((bf16[48,1024]{1,0:T(8,128)(2,1)S(1)}, bf16[48,1024]{1,0:T(8,128)(2,1)S(1)}, u32[]{:S(2)}, u32[]{:S(2)}) %collective-permute-start.14) | collective-permute-done | bytes 98336 | tf_op jit(solution)/shard_map/sum_y/ppermute | solution.py:10
  55.0 0.4 collective-permute-done.15
  55.4 0.1 fusion.4
  55.5 0.5 fusion.5
  56.0 1.2 %constant_dynamic-update-slice_fusion.8 = (bf16[384,1024]{1,0:T(8,128)(2,1)S(1)}, bf16[48,1024]{1,0:T(8,128)(2,1)S(1)}, f32[48,1024]{1,0:T(8,128)}) fusion(bf16[48,1024]{1,0:T(8,128)(2,1)S(1)} %get-tuple-element.31, bf16[1024,1024]{1,0:T(8,128)(2,1)S(1)} %get-tuple-element.23, f32[96,1024]{1,0:T(8,128)S(1)} %fusion.5), kind=kOutput, calls=%fused_computation.51 | convolution fusion | flops 100810752 | bytes 2981888 | tf_op jit(solution)/shard_map/screen/dot_general | solution.py:116
  57.1 1.5 %collective-permute-start.16 = (bf16[48,1024]{1,0:T(8,128)(2,1)S(1)}, bf16[48,1024]{1,0:T(8,128)(2,1)S(1)}, u32[]{:S(2)}, u32[]{:S(2)}) collective-permute-start(bf16[48,1024]{1,0:T(8,128)(2,1)S(1)} %get-tuple-element.25), channel_id=1, source_target_pairs={{0,128},{16,144},{128,0},{144,16},{1,129},{17,145},{129,1},{145,17... | collective-permute-start | bytes 294920 | tf_op jit(solution)/shard_map/gather_y/ppermute | solution.py:10
  58.6 1.5 %collective-permute-start.17 = (bf16[48,1024]{1,0:T(8,128)(2,1)S(1)}, bf16[48,1024]{1,0:T(8,128)(2,1)S(1)}, u32[]{:S(2)}, u32[]{:S(2)}) collective-permute-start(bf16[48,1024]{1,0:T(8,128)(2,1)S(1)} %get-tuple-element.25), channel_id=1, source_target_pairs={{0,16},{16,128},{128,144},{144,0},{1,17},{17,129},{129,145},{145,1... | collective-permute-start | bytes 294920 | tf_op jit(solution)/shard_map/gather_y/ppermute | solution.py:10
  60.2 1.2 %collective-permute-start.18 = (bf16[48,1024]{1,0:T(8,128)(2,1)S(1)}, bf16[48,1024]{1,0:T(8,128)(2,1)S(1)}, u32[]{:S(2)}, u32[]{:S(2)}) collective-permute-start(bf16[48,1024]{1,0:T(8,128)(2,1)S(1)} %get-tuple-element.25), channel_id=1, source_target_pairs={{0,144},{16,0},{128,16},{144,128},{1,145},{17,1},{129,17},{145,129... | collective-permute-start | bytes 294920 | tf_op jit(solution)/shard_map/gather_y/ppermute | solution.py:10
  61.3 0.8 collective-permute-done.16
  62.1 2.1 %collective-permute-done.17 = bf16[48,1024]{1,0:T(8,128)(2,1)S(1)} collective-permute-done((bf16[48,1024]{1,0:T(8,128)(2,1)S(1)}, bf16[48,1024]{1,0:T(8,128)(2,1)S(1)}, u32[]{:S(2)}, u32[]{:S(2)}) %collective-permute-start.17) | collective-permute-done | bytes 98336 | tf_op jit(solution)/shard_map/gather_y/ppermute | solution.py:10
  64.3 3.2 %collective-permute-start.19 = (bf16[192,1024]{1,0:T(8,128)(2,1)S(1)}, bf16[192,1024]{1,0:T(8,128)(2,1)S(1)}, u32[]{:S(2)}, u32[]{:S(2)}) collective-permute-start(bf16[192,1024]{1,0:T(8,128)(2,1)S(1)} %pad_maximum_fusion.1), channel_id=1, source_target_pairs={{0,8},{8,0},{1,9},{9,1},{2,10},{10,2},{3,11},{11,3},{4,12},{12,4},... | collective-permute-start | bytes 1179656 | tf_op jit(solution)/shard_map/gather_y/ppermute | solution.py:23
  67.5 1.3 %collective-permute-done.19 = bf16[192,1024]{1,0:T(8,128)(2,1)S(1)} collective-permute-done((bf16[192,1024]{1,0:T(8,128)(2,1)S(1)}, bf16[192,1024]{1,0:T(8,128)(2,1)S(1)}, u32[]{:S(2)}, u32[]{:S(2)}) %collective-permute-start.19) | collective-permute-done | bytes 393248 | tf_op jit(solution)/shard_map/gather_y/ppermute | solution.py:23
  68.8 0.6 fusion.1
  69.4 0.1 select_add_fusion
  69.5 13.5 %all_to_all.9 = f32[32,1,128]{2,1,0:T(1,128)S(1)} all-to-all(f32[32,1,128]{2,1,0:T(1,128)S(1)} %bitcast.61), channel_id=1, replica_groups=mesh['grp'=2,'x'=4,'ylo'=2,'core'=2,'col'=8] {'x','col'}, dimensions={0} | all-to-all | bytes 32768 | tf_op jit(solution)/shard_map/sigma/all_to_all | solution.py:141
  83.0 0.6 reduce_sum.29
  (44 shorter events, 0.6 us)
Async XLA Ops:
  0.6 19.0 %copy-start = (bf16[128,1536]{1,0:T(8,128)(2,1)S(1)}, bf16[128,1536]{1,0:T(8,128)(2,1)}, u32[]{:S(2)}) copy-start(bf16[128,1536]{1,0:T(8,128)(2,1)} %param.3) | copy-start | bytes 1179652
  1.7 17.9 %collective-permute-start = (bf16[128,1024]{1,0:T(8,128)(2,1)S(1)}, bf16[128,1024]{1,0:T(8,128)(2,1)S(1)}, u32[]{:S(2)}, u32[]{:S(2)}) collective-permute-start(bf16[128,1024]{1,0:T(8,128)(2,1)S(1)} %slice.31), channel_id=1, source_target_pairs={{0,3},{8,11},{16,19},{24,27},{32,35},{40,43},{48,51},{56,59},{64,6... | collective-permute-start | bytes 786440 | tf_op jit(solution)/shard_map/panel_z/ppermute | solution.py:14
  8.8 10.8 %collective-permute-start.1 = (bf16[128,1024]{1,0:T(8,128)(2,1)S(1)}, bf16[128,1024]{1,0:T(8,128)(2,1)S(1)}, u32[]{:S(2)}, u32[]{:S(2)}) collective-permute-start(bf16[128,1024]{1,0:T(8,128)(2,1)S(1)} %slice.31), channel_id=1, source_target_pairs={{0,6},{8,14},{16,22},{24,30},{32,38},{40,46},{48,54},{56,62},{64,7... | collective-permute-start | bytes 786440 | tf_op jit(solution)/shard_map/panel_z/ppermute | solution.py:14
  13.3 9.0 %collective-permute-start.5 = (bf16[400,128]{1,0:T(8,128)(2,1)S(1)}, bf16[400,128]{1,0:T(8,128)(2,1)S(1)}, u32[]{:S(2)}, u32[]{:S(2)}) collective-permute-start(bf16[400,128]{1,0:T(8,128)(2,1)S(1)} %concatenate.37), channel_id=1, source_target_pairs={{0,64},{32,96},{64,0},{96,32},{1,65},{33,97},{65,1},{97,33},{2,66}... | collective-permute-start | bytes 307208 | tf_op jit(solution)/shard_map/blocks/ppermute | solution.py:10
  16.3 11.0 %collective-permute-start.6 = (bf16[400,128]{1,0:T(8,128)(2,1)S(1)}, bf16[400,128]{1,0:T(8,128)(2,1)S(1)}, u32[]{:S(2)}, u32[]{:S(2)}) collective-permute-start(bf16[400,128]{1,0:T(8,128)(2,1)S(1)} %concatenate.38), channel_id=1, source_target_pairs={{0,32},{32,64},{64,96},{96,0},{1,33},{33,65},{65,97},{97,1},{2,34}... | collective-permute-start | bytes 307208 | tf_op jit(solution)/shard_map/blocks/ppermute | solution.py:10
  16.9 10.5 %collective-permute-start.7 = (bf16[400,128]{1,0:T(8,128)(2,1)S(1)}, bf16[400,128]{1,0:T(8,128)(2,1)S(1)}, u32[]{:S(2)}, u32[]{:S(2)}) collective-permute-start(bf16[400,128]{1,0:T(8,128)(2,1)S(1)} %concatenate.39), channel_id=1, source_target_pairs={{0,96},{32,0},{64,32},{96,64},{1,97},{33,1},{65,33},{97,65},{2,98}... | collective-permute-start | bytes 307208 | tf_op jit(solution)/shard_map/blocks/ppermute | solution.py:10
  19.7 7.7 %collective-permute-start.2 = (bf16[128,1024]{1,0:T(8,128)(2,1)S(1)}, bf16[128,1024]{1,0:T(8,128)(2,1)S(1)}, u32[]{:S(2)}, u32[]{:S(2)}) collective-permute-start(bf16[128,1024]{1,0:T(8,128)(2,1)S(1)} %select_select_fusion.2), channel_id=1, source_target_pairs={{0,1},{3,4},{6,5},{8,9},{11,12},{14,13},{16,17},{19,20},{22,21},{2... | collective-permute-start | bytes 786440 | tf_op jit(solution)/shard_map/panel_z/ppermute | solution.py:14
  21.0 6.4 %collective-permute-start.3 = (bf16[128,1024]{1,0:T(8,128)(2,1)S(1)}, bf16[128,1024]{1,0:T(8,128)(2,1)S(1)}, u32[]{:S(2)}, u32[]{:S(2)}) collective-permute-start(bf16[128,1024]{1,0:T(8,128)(2,1)S(1)} %select_select_fusion.2), channel_id=1, source_target_pairs={{0,7},{3,2},{8,15},{11,10},{16,23},{19,18},{24,31},{27,26},{32,39}... | collective-permute-start | bytes 786440 | tf_op jit(solution)/shard_map/panel_z/ppermute | solution.py:14
  22.3 9.4 %collective-permute-start.4 = (bf16[128,1024]{1,0:T(8,128)(2,1)S(1)}, bf16[128,1024]{1,0:T(8,128)(2,1)S(1)}, u32[]{:S(2)}, u32[]{:S(2)}) collective-permute-start(bf16[128,1024]{1,0:T(8,128)(2,1)S(1)} %select_select_fusion.2), channel_id=1, source_target_pairs={{0,64},{3,67},{6,70},{32,96},{35,99},{38,102},{64,0},{67,3},{70,6}... | collective-permute-start | bytes 786440 | tf_op jit(solution)/shard_map/panel_z/ppermute | solution.py:19
  31.8 8.8 %collective-permute-start.10 = (bf16[128,1024]{1,0:T(8,128)(2,1)S(1)}, bf16[128,1024]{1,0:T(8,128)(2,1)S(1)}, u32[]{:S(2)}, u32[]{:S(2)}) collective-permute-start(bf16[128,1024]{1,0:T(8,128)(2,1)S(1)} %select_select_fusion.1), channel_id=1, source_target_pairs={{0,32},{32,64},{64,96},{96,0},{1,33},{33,65},{65,97},{97,1},{2,34}... | collective-permute-start | bytes 786440 | tf_op jit(solution)/shard_map/panel_x/ppermute | solution.py:10
  31.9 8.7 %collective-permute-start.11 = (bf16[128,1024]{1,0:T(8,128)(2,1)S(1)}, bf16[128,1024]{1,0:T(8,128)(2,1)S(1)}, u32[]{:S(2)}, u32[]{:S(2)}) collective-permute-start(bf16[128,1024]{1,0:T(8,128)(2,1)S(1)} %select_select_fusion.1), channel_id=1, source_target_pairs={{0,96},{32,0},{64,32},{96,64},{1,97},{33,1},{65,33},{97,65},{2,98}... | collective-permute-start | bytes 786440 | tf_op jit(solution)/shard_map/panel_x/ppermute | solution.py:10
  34.6 4.6 %collective-permute-start.8 = (bf16[128,1024]{1,0:T(8,128)(2,1)S(1)}, bf16[128,1024]{1,0:T(8,128)(2,1)S(1)}, u32[]{:S(2)}, u32[]{:S(2)}) collective-permute-start(bf16[128,1024]{1,0:T(8,128)(2,1)S(1)} %collective-permute-done.4), channel_id=1, source_target_pairs={{0,1},{3,4},{6,5},{8,9},{11,12},{14,13},{16,17},{19,20},{22,21},{2... | collective-permute-start | bytes 786440 | tf_op jit(solution)/shard_map/panel_z/ppermute | solution.py:14
  35.9 4.6 %collective-permute-start.9 = (bf16[128,1024]{1,0:T(8,128)(2,1)S(1)}, bf16[128,1024]{1,0:T(8,128)(2,1)S(1)}, u32[]{:S(2)}, u32[]{:S(2)}) collective-permute-start(bf16[128,1024]{1,0:T(8,128)(2,1)S(1)} %collective-permute-done.4), channel_id=1, source_target_pairs={{0,7},{3,2},{8,15},{11,10},{16,23},{19,18},{24,31},{27,26},{32,39}... | collective-permute-start | bytes 786440 | tf_op jit(solution)/shard_map/panel_z/ppermute | solution.py:14
  41.3 5.9 %collective-permute-start.12 = (f32[4,48,1024]{2,1,0:T(8,128)S(1)}, f32[4,48,1024]{2,1,0:T(8,128)S(1)}, u32[]{:S(2)}, u32[]{:S(2)}) collective-permute-start(f32[4,48,1024]{2,1,0:T(8,128)S(1)} %dynamic-slice_bitcast_fusion), channel_id=1, source_target_pairs={{0,8},{8,0},{1,9},{9,1},{2,10},{10,2},{3,11},{11,3},{4,12},{12,4},... | collective-permute-start | bytes 2359304 | tf_op jit(solution)/shard_map/sum_core/ppermute | solution.py:23
  47.3 5.7 %collective-permute-start.13 = (bf16[48,1024]{1,0:T(8,128)(2,1)S(1)}, bf16[48,1024]{1,0:T(8,128)(2,1)S(1)}, u32[]{:S(2)}, u32[]{:S(2)}) collective-permute-start(bf16[48,1024]{1,0:T(8,128)(2,1)S(1)} %get-tuple-element.32), channel_id=1, source_target_pairs={{0,128},{16,144},{128,0},{144,16},{1,129},{17,145},{129,1},{145,17... | collective-permute-start | bytes 294920 | tf_op jit(solution)/shard_map/sum_y/ppermute | solution.py:10
  50.3 4.7 %collective-permute-start.14 = (bf16[48,1024]{1,0:T(8,128)(2,1)S(1)}, bf16[48,1024]{1,0:T(8,128)(2,1)S(1)}, u32[]{:S(2)}, u32[]{:S(2)}) collective-permute-start(bf16[48,1024]{1,0:T(8,128)(2,1)S(1)} %get-tuple-element.34), channel_id=1, source_target_pairs={{0,16},{16,128},{128,144},{144,0},{1,17},{17,129},{129,145},{145,1... | collective-permute-start | bytes 294920 | tf_op jit(solution)/shard_map/sum_y/ppermute | solution.py:10
  50.7 4.6 %collective-permute-start.15 = (bf16[48,1024]{1,0:T(8,128)(2,1)S(1)}, bf16[48,1024]{1,0:T(8,128)(2,1)S(1)}, u32[]{:S(2)}, u32[]{:S(2)}) collective-permute-start(bf16[48,1024]{1,0:T(8,128)(2,1)S(1)} %get-tuple-element.33), channel_id=1, source_target_pairs={{0,144},{16,0},{128,16},{144,128},{1,145},{17,1},{129,17},{145,129... | collective-permute-start | bytes 294920 | tf_op jit(solution)/shard_map/sum_y/ppermute | solution.py:10
  57.1 5.0 %collective-permute-start.16 = (bf16[48,1024]{1,0:T(8,128)(2,1)S(1)}, bf16[48,1024]{1,0:T(8,128)(2,1)S(1)}, u32[]{:S(2)}, u32[]{:S(2)}) collective-permute-start(bf16[48,1024]{1,0:T(8,128)(2,1)S(1)} %get-tuple-element.25), channel_id=1, source_target_pairs={{0,128},{16,144},{128,0},{144,16},{1,129},{17,145},{129,1},{145,17... | collective-permute-start | bytes 294920 | tf_op jit(solution)/shard_map/gather_y/ppermute | solution.py:10
  58.6 5.6 %collective-permute-start.17 = (bf16[48,1024]{1,0:T(8,128)(2,1)S(1)}, bf16[48,1024]{1,0:T(8,128)(2,1)S(1)}, u32[]{:S(2)}, u32[]{:S(2)}) collective-permute-start(bf16[48,1024]{1,0:T(8,128)(2,1)S(1)} %get-tuple-element.25), channel_id=1, source_target_pairs={{0,16},{16,128},{128,144},{144,0},{1,17},{17,129},{129,145},{145,1... | collective-permute-start | bytes 294920 | tf_op jit(solution)/shard_map/gather_y/ppermute | solution.py:10
  60.2 4.1 %collective-permute-start.18 = (bf16[48,1024]{1,0:T(8,128)(2,1)S(1)}, bf16[48,1024]{1,0:T(8,128)(2,1)S(1)}, u32[]{:S(2)}, u32[]{:S(2)}) collective-permute-start(bf16[48,1024]{1,0:T(8,128)(2,1)S(1)} %get-tuple-element.25), channel_id=1, source_target_pairs={{0,144},{16,0},{128,16},{144,128},{1,145},{17,1},{129,17},{145,129... | collective-permute-start | bytes 294920 | tf_op jit(solution)/shard_map/gather_y/ppermute | solution.py:10
  64.3 4.5 %collective-permute-start.19 = (bf16[192,1024]{1,0:T(8,128)(2,1)S(1)}, bf16[192,1024]{1,0:T(8,128)(2,1)S(1)}, u32[]{:S(2)}, u32[]{:S(2)}) collective-permute-start(bf16[192,1024]{1,0:T(8,128)(2,1)S(1)} %pad_maximum_fusion.1), channel_id=1, source_target_pairs={{0,8},{8,0},{1,9},{9,1},{2,10},{10,2},{3,11},{11,3},{4,12},{12,4},... | collective-permute-start | bytes 1179656 | tf_op jit(solution)/shard_map/gather_y/ppermute | solution.py:23

commit v8 on v5

v8 whole, which is shorter than its diff:
```python
import jax
import jax.numpy as jnp
from jax import lax
from jax.sharding import Mesh, PartitionSpec as P

X, Y, Z, CORE = "x", ("grp", "ylo"), "col", "core"
PLANE = ("grp", "x", "ylo", "core")
LOW, F32 = jnp.bfloat16, jnp.float32
def shift(value, axis, size, step):
    return lax.ppermute(value, axis, [(i, (i + step) % size) for i in range(size)])


def along_z(value, *pairs):
    return lax.ppermute(value, Z, pairs)


def along_x(value, size, step, columns):
    pairs = [(i * 8 + z, (i + step) % size * 8 + z) for i in range(size) for z in columns]
    return lax.ppermute(value, (X, Z), pairs)


def swap(value):
    return lax.ppermute(value, CORE, [(0, 1), (1, 0)])


def parts_of(value):
    out = []
    for _ in range(3):
        part = lax.reduce_precision(value, 8, 7)
        out.append(part.astype(LOW))
        value = value - part
    return out


def two_parts(value):
    high = lax.reduce_precision(value, 8, 7)
    return high.astype(LOW), (value - high).astype(LOW)


def body(orbital_b, gaps, block_inverse):
    own, width = orbital_b.shape
    panel = block_inverse.shape[0]
    nx, ny, nz = lax.axis_size(X), lax.axis_size(Y), lax.axis_size(Z)
    x, y, z, core = (lax.axis_index(a) for a in (X, Y, Z, CORE))
    count = width // lax.axis_size(PLANE)
    quarter = panel // nx
    steps = (0, 2, 1, 3)

    def by_place(values):
        return [
            sum(
                jnp.where((x - k) % nx == q, value, jnp.zeros_like(value))
                for k, value in zip(steps, values)
            )
            for q in range(nx)
        ]

    with jax.named_scope("quarters"):
        def quarter_of(i):
            return lax.dynamic_slice(orbital_b, (0, i * quarter), (own, quarter))

        got = [quarter_of(x)]
        got += [along_x(quarter_of((x + k) % nx), nx, k, (0,)) for k in steps[1:]]
        piece = jnp.concatenate(got, axis=0)

    with jax.named_scope("panel_z"):
        far_a = along_z(piece, (0, 3))
        far_b = along_z(piece, (0, 6))

    with jax.named_scope("blocks"):
        weight = 2.0 * gaps / (gaps * gaps + 1.0)
        rows, piece = lax.optimization_barrier((orbital_b, piece))
        rows = jnp.concatenate(
            [rows.T, jnp.stack(parts_of(weight)), jnp.zeros((13, own), LOW)], axis=0
        )
        factors = [rows] + [shift(rows, X, nx, k) for k in steps[1:]]

    with jax.named_scope("panel_z"):
        far_a, far_b, block_inverse, _ = lax.optimization_barrier(
            (far_a, far_b, block_inverse, rows)
        )
        held = jnp.where(z == 3, far_a, jnp.where(z == 6, far_b, piece))
        near_a = along_z(held, (0, 1), (3, 4), (6, 5))
        near_b = along_z(held, (0, 7), (3, 2))
        inv_high, inv_rest = two_parts(block_inverse)
        near_a, near_b, inv_high, inv_rest = lax.optimization_barrier(
            (near_a, near_b, inv_high, inv_rest)
        )
        held = jnp.where((z == 1) | (z == 4) | (z == 5), near_a, held)
        held = jnp.where((z == 7) | (z == 2), near_b, held)

    with jax.named_scope("response"):
        factors = jnp.concatenate(factors, axis=1)
        weight = jnp.sum(factors[width : width + 3].astype(F32), axis=0)
        factors = factors[:width]
        weighted = (weight[:, None] * held.astype(F32)).astype(LOW)
        part = jnp.dot(factors, weighted, preferred_element_type=F32)

    with jax.named_scope("sum_core"):
        part = part.reshape(2, nx, 2, 2, count, quarter)
        sent = lax.dynamic_index_in_dim(part, 1 - core, 3, False)
        kept = lax.dynamic_index_in_dim(part, core, 3, False) + swap(sent)

    with jax.named_scope("sum_y"):

        def rows_at(i):
            block = lax.dynamic_slice(
                kept, (i // 2, 0, i % 2, 0, 0), (1, nx, 1, count, quarter)
            )
            return block.reshape(nx * count, quarter)

        total = rows_at(y)
        for k in steps[1:]:
            total = total + shift(rows_at((y + k) % ny).astype(LOW), Y, ny, k).astype(F32)

    with jax.named_scope("exchange_x"):
        total = total.reshape(nx, count, quarter)
        held, total = lax.optimization_barrier((held, total))
        panels = [held] + [shift(held, X, nx, k) for k in steps[1:]]
        own_rows = [lax.dynamic_index_in_dim(total, x, 0, False)]
        for k in steps[1:]:
            own_rows.append(
                shift(lax.dynamic_index_in_dim(total, (x + k) % nx, 0, False), X, nx, k)
            )
        total = jnp.concatenate(by_place(own_rows), axis=1)

    with jax.named_scope("screen"):
        place = z * width + lax.axis_index(PLANE) * count
        unit = (lax.iota(jnp.int32, count)[:, None] + place) == lax.iota(jnp.int32, panel)[None, :]
        total = unit.astype(F32) + total
        high, rest = two_parts(total)
        screened = jnp.dot(
            jnp.concatenate([high, rest], axis=0), inv_high, preferred_element_type=F32
        )
        screened = screened[:count] + screened[count:]
        screened = screened + jnp.dot(high, inv_rest, preferred_element_type=F32)

    with jax.named_scope("gather_y"):
        low = screened.astype(LOW)
        gathered = jnp.concatenate([low] + [shift(low, Y, ny, k) for k in steps[1:]], axis=0)
        gathered, *panels = lax.optimization_barrier((gathered, *panels))
        gathered = jnp.concatenate([gathered, swap(gathered)], axis=0)
        for i, k in enumerate(steps):
            block = panels[i].reshape(nx, own, quarter)
            panels[i] = jnp.concatenate(
                [block[steps.index((m - k) % nx)] for m in steps], axis=0
            )
        panels = jnp.concatenate(by_place(panels), axis=1)


        block = factors.reshape(2, nx, 2, 2, count, nx * own)
        ordered = jnp.concatenate(
            [
                lax.dynamic_slice(
                    block,
                    ((y - k) % ny // 2, x, (y - k) % ny % 2, c, 0, 0),
                    (1, 1, 1, 1, count, nx * own),
                ).reshape(count, nx * own)
                for c in (core, 1 - core)
                for k in steps
            ],
            axis=0,
        )

    with jax.named_scope("sigma"):
        products = lax.dot_general(
            gathered, panels, (((1,), (1,)), ((), ())), preferred_element_type=F32
        )
        local = -jnp.sum(products * ordered.astype(F32), axis=0).reshape(nx, own)
        local = jnp.stack(by_place(list(local)))
        copies = jnp.broadcast_to(local[:, None], (nx, nz, own)).reshape(-1, own)
        terms = lax.all_to_all(copies, (X, Z), 0, 0, tiled=True)
        sigma = jnp.sum(terms, axis=0)
    return sigma, screened[None]


def solution(mesh):
    split = Mesh(mesh.devices.reshape(2, 4, 2, 2, 8), ("grp", "x", "ylo", "core", "col"))
    return jax.shard_map(
        body,
        mesh=split,
        in_specs=(P(PLANE, Z), P(PLANE), P()),
        out_specs=(P(PLANE), P(Z, PLANE, None)),
        check_vma=False,
    )
```

time: 82.2 us -> 97.4 us (1.18); the launches traced: 81.9 us -> 96.1 us
  starting transfers between devices: 34.3 us -> 46.6 us
  other arithmetic: 4.79 us -> 9.01 us
  blocking collectives: 14.1 us -> 12.3 us
    ppermute x0 -> x3, starting transfers between devices: none -> 12 us  [along_x(): return lax.ppermute(value, (X, Z), pairs)]
    ppermute x4, starting transfers between devices: 12.1 us -> 5.22 us  [along_z(): return lax.ppermute(value, Z, pairs)]
    ppermute x12 -> x15, starting transfers between devices: 18.4 us -> 22.9 us  [shift(): lax.ppermute(value, axis, [(i, (i + step) % size) for i in range(size)])]
    ppermute x2, starting transfers between devices: 3.94 us -> 6.46 us  [swap(): return lax.ppermute(value, CORE, [(0, 1), (1, 0)])]
    add x2 -> x10, other arithmetic: 0.18 us -> 2.19 us  [the longest x1 1.24 us: body(): kept = lax.dynamic_index_in_dim(part, core, 3, False) + swap(sent)]
    convert_element_type x2, other arithmetic: 3.22 us -> 5.23 us  [two_parts(): return (high.astype(LOW), (value - high).astype(LOW))]
    all_to_all x1, blocking collectives: 14.1 us -> 12.3 us  [body(): terms = lax.all_to_all(copies, (X, Z), 0, 0, tiled=True)]
    ppermute x0 -> x3, waiting for transfers between devices: none -> 1.29 us  [along_x(): return lax.ppermute(value, (X, Z), pairs)]
  transfers between devices with their start and end apart: 18 -> 24, of which waited for: 9 -> 8; matrix products, arithmetic and copies ran while one was open for 7% -> 10% of each run, Pallas kernels for 0% -> 0%
where the time goes in v8:
time: 97.4 us; the launch traced here: 96.1 us
  starting transfers between devices  46.6 us (48%)
  waiting for transfers between devices  20.4 us (21%)
  blocking collectives  12.3 us (13%)
  other arithmetic  9.01 us (9%)
  local copies, waits for them, and re-layouts  3.83 us (4%)
  matrix products  2.93 us (3%)
  between operations  1.08 us (1%)
    ppermute x15, starting transfers between devices, shift(): lax.ppermute(value, axis, [(i, (i + step) % size) for i in range(size)])  22.9 us
    ppermute x15, waiting for transfers between devices, shift(): lax.ppermute(value, axis, [(i, (i + step) % size) for i in range(size)])  16.2 us
    all_to_all x1, blocking collectives, body(): terms = lax.all_to_all(copies, (X, Z), 0, 0, tiled=True)  12.3 us
    ppermute x3, starting transfers between devices, along_x(): return lax.ppermute(value, (X, Z), pairs)  12 us
    ppermute x2, starting transfers between devices, swap(): return lax.ppermute(value, CORE, [(0, 1), (1, 0)])  6.46 us
    convert_element_type x2, other arithmetic, two_parts(): return (high.astype(LOW), (value - high).astype(LOW))  5.23 us
    ppermute x4, starting transfers between devices, along_z(): return lax.ppermute(value, Z, pairs)  5.22 us
    ppermute x2, waiting for transfers between devices, swap(): return lax.ppermute(value, CORE, [(0, 1), (1, 0)])  2.95 us
  transfers between devices with their start and end apart: 24, of which 8 were waited for; matrix products, arithmetic and copies ran while one was open for 10% of the time, Pallas kernels for 0%

profile of v8, /device:TPU:1, one launch (start us, length us, event | category | flops | bytes accessed | tf_op | source)
XLA Modules:
  0.0 96.1 jit_solution(6283434271604701168)
XLA Ops:
  0.7 1.0 %constant_dynamic-slice_fusion.4 = (bf16[128,256]{1,0:T(8,128)(2,1)S(1)}, bf16[128,256]{1,0:T(8,128)(2,1)S(1)}, bf16[128,256]{1,0:T(8,128)(2,1)S(1)}, bf16[128,256]{1,0:T(8,128)(2,1)S(1)}) fusion(bf16[128,1536]{1,0:T(8,128)(2,1)} %param.3, s32[]{:T(128)S(6)} %select_n.725, s32[]{:T(128)S(6)} %select_n.729, s32[]{:T(128)S(6)} %select_n.727, s32[]{:T(128)S(6)} %select_n.731), kind=kLoop, calls=%fused_computation.77 | loop fusion | bytes 524304 | tf_op jit(solution)/shard_map/quarters/dynamic_slice | solution.py:60
  1.6 5.5 %collective-permute-start = (bf16[128,256]{1,0:T(8,128)(2,1)S(1)}, bf16[128,256]{1,0:T(8,128)(2,1)S(1)}, u32[]{:S(2)}, u32[]{:S(2)}) collective-permute-start(bf16[128,256]{1,0:T(8,128)(2,1)S(1)} %get-tuple-element.43), channel_id=1, source_target_pairs={{0,64},{32,96},{64,0},{96,32},{8,72},{40,104},{72,8},{104,40},{16,... | collective-permute-start | bytes 196616 | tf_op jit(solution)/shard_map/quarters/ppermute | solution.py:19
  7.1 2.2 %collective-permute-start.1 = (bf16[128,256]{1,0:T(8,128)(2,1)S(1)}, bf16[128,256]{1,0:T(8,128)(2,1)S(1)}, u32[]{:S(2)}, u32[]{:S(2)}) collective-permute-start(bf16[128,256]{1,0:T(8,128)(2,1)S(1)} %get-tuple-element.42), channel_id=1, source_target_pairs={{0,32},{32,64},{64,96},{96,0},{8,40},{40,72},{72,104},{104,8},{16,... | collective-permute-start | bytes 196616 | tf_op jit(solution)/shard_map/quarters/ppermute | solution.py:19
  9.4 4.3 %collective-permute-start.2 = (bf16[128,256]{1,0:T(8,128)(2,1)S(1)}, bf16[128,256]{1,0:T(8,128)(2,1)S(1)}, u32[]{:S(2)}, u32[]{:S(2)}) collective-permute-start(bf16[128,256]{1,0:T(8,128)(2,1)S(1)} %get-tuple-element.44), channel_id=1, source_target_pairs={{0,96},{32,0},{64,32},{96,64},{8,104},{40,8},{72,40},{104,72},{16,... | collective-permute-start | bytes 196616 | tf_op jit(solution)/shard_map/quarters/ppermute | solution.py:19
  13.7 1.3 %collective-permute-done.2 = bf16[128,256]{1,0:T(8,128)(2,1)S(1)} collective-permute-done((bf16[128,256]{1,0:T(8,128)(2,1)S(1)}, bf16[128,256]{1,0:T(8,128)(2,1)S(1)}, u32[]{:S(2)}, u32[]{:S(2)}) %collective-permute-start.2) | collective-permute-done | bytes 65568 | tf_op jit(solution)/shard_map/quarters/ppermute | solution.py:19
  15.0 1.3 %collective-permute-start.3 = (bf16[512,256]{1,0:T(8,128)(2,1)S(1)}, bf16[512,256]{1,0:T(8,128)(2,1)S(1)}, u32[]{:S(2)}, u32[]{:S(2)}) collective-permute-start(bf16[512,256]{1,0:T(8,128)(2,1)S(1)} %pad_maximum_fusion.2), channel_id=1, source_target_pairs={{0,3},{8,11},{16,19},{24,27},{32,35},{40,43},{48,51},{56,59},{64,6... | collective-permute-start | bytes 786440 | tf_op jit(solution)/shard_map/panel_z/ppermute | solution.py:14
  16.3 1.3 %collective-permute-start.4 = (bf16[512,256]{1,0:T(8,128)(2,1)S(1)}, bf16[512,256]{1,0:T(8,128)(2,1)S(1)}, u32[]{:S(2)}, u32[]{:S(2)}) collective-permute-start(bf16[512,256]{1,0:T(8,128)(2,1)S(1)} %pad_maximum_fusion.2), channel_id=1, source_target_pairs={{0,6},{8,14},{16,22},{24,30},{32,38},{40,46},{48,54},{56,62},{64,7... | collective-permute-start | bytes 786440 | tf_op jit(solution)/shard_map/panel_z/ppermute | solution.py:14
  17.6 0.7 fusion.33
  18.3 1.2 %copy.17 = bf16[128,1536]{0,1:T(8,128)(2,1)S(1)} copy(bf16[128,1536]{1,0:T(8,128)(2,1)} %param.3) | data formatting | bytes 786432 | tf_op jit(solution)/shard_map/blocks/optimization_barrier | solution.py:72
  19.5 0.3 concatenate.41
  19.8 1.6 %collective-permute-start.7 = (bf16[1552,128]{1,0:T(8,128)(2,1)S(1)}, bf16[1552,128]{1,0:T(8,128)(2,1)S(1)}, u32[]{:S(2)}, u32[]{:S(2)}) collective-permute-start(bf16[1552,128]{1,0:T(8,128)(2,1)S(1)} %concatenate.41), channel_id=1, source_target_pairs={{0,64},{32,96},{64,0},{96,32},{1,65},{33,97},{65,1},{97,33},{2,66}... | collective-permute-start | bytes 1191944 | tf_op jit(solution)/shard_map/blocks/ppermute | solution.py:10
  21.4 2.1 %collective-permute-start.8 = (bf16[1552,128]{1,0:T(8,128)(2,1)S(1)}, bf16[1552,128]{1,0:T(8,128)(2,1)S(1)}, u32[]{:S(2)}, u32[]{:S(2)}) collective-permute-start(bf16[1552,128]{1,0:T(8,128)(2,1)S(1)} %concatenate.41), channel_id=1, source_target_pairs={{0,32},{32,64},{64,96},{96,0},{1,33},{33,65},{65,97},{97,1},{2,34}... | collective-permute-start | bytes 1191944 | tf_op jit(solution)/shard_map/blocks/ppermute | solution.py:10
  23.5 0.6 collective-permute-start.9
  24.1 1.3 %collective-permute-start.5 = (bf16[512,256]{1,0:T(8,128)(2,1)S(1)}, bf16[512,256]{1,0:T(8,128)(2,1)S(1)}, u32[]{:S(2)}, u32[]{:S(2)}) collective-permute-start(bf16[512,256]{1,0:T(8,128)(2,1)S(1)} %select_select_fusion.1), channel_id=1, source_target_pairs={{0,1},{3,4},{6,5},{8,9},{11,12},{14,13},{16,17},{19,20},{22,21},{2... | collective-permute-start | bytes 786440 | tf_op jit(solution)/shard_map/panel_z/ppermute | solution.py:14
  25.5 1.3 %collective-permute-start.6 = (bf16[512,256]{1,0:T(8,128)(2,1)S(1)}, bf16[512,256]{1,0:T(8,128)(2,1)S(1)}, u32[]{:S(2)}, u32[]{:S(2)}) collective-permute-start(bf16[512,256]{1,0:T(8,128)(2,1)S(1)} %select_select_fusion.1), channel_id=1, source_target_pairs={{0,7},{3,2},{8,15},{11,10},{16,23},{19,18},{24,31},{27,26},{32,39}... | collective-permute-start | bytes 786440 | tf_op jit(solution)/shard_map/panel_z/ppermute | solution.py:14
  26.8 5.1 %fusion = (bf16[1024,1024]{1,0:T(8,128)(2,1)}, bf16[1024,1024]{1,0:T(8,128)(2,1)}) fusion(f32[1024,1024]{1,0:T(8,128)} %param.5), kind=kLoop, calls=%fused_computation.2 | loop fusion | flops 4194304 | bytes 8388608 | tf_op jit(solution)/shard_map/panel_z/convert_element_type | solution.py:37
  31.9 9.2 %collective-permute-done.8 = bf16[1552,128]{1,0:T(8,128)(2,1)S(1)} collective-permute-done((bf16[1552,128]{1,0:T(8,128)(2,1)S(1)}, bf16[1552,128]{1,0:T(8,128)(2,1)S(1)}, u32[]{:S(2)}, u32[]{:S(2)}) %collective-permute-start.8) | collective-permute-done | bytes 397344 | tf_op jit(solution)/shard_map/blocks/ppermute | solution.py:10
  41.3 0.7 fusion.12
  42.0 1.0 %dynamic-slice_bitcast_fusion = f32[2,4,2,48,256]{4,3,2,1,0:T(8,128)} fusion(f32[2,4,2,2,48,256]{5,4,3,2,1,0:T(8,128)S(1)} %bitcast.82, s32[]{:T(128)S(6)} %select_n.739), kind=kLoop, calls=%fused_computation.18 | loop fusion | bytes 1572868 | tf_op jit(solution)/shard_map/sum_core/jit(dynamic_index_in_dim)/squeeze | solution.py:101
  43.0 1.1 %collective-permute-start.10 = (f32[2,4,2,48,256]{4,3,2,1,0:T(8,128)}, f32[2,4,2,48,256]{4,3,2,1,0:T(8,128)}, u32[]{:S(2)}, u32[]{:S(2)}) collective-permute-start(f32[2,4,2,48,256]{4,3,2,1,0:T(8,128)} %dynamic-slice_bitcast_fusion), channel_id=1, source_target_pairs={{0,8},{8,0},{1,9},{9,1},{2,10},{10,2},{3,11},{11,3},{4,12},{12,4},... | collective-permute-start | bytes 2359304 | tf_op jit(solution)/shard_map/sum_core/ppermute | solution.py:23
  44.4 2.0 %collective-permute-done.10 = f32[2,4,2,48,256]{4,3,2,1,0:T(8,128)} collective-permute-done((f32[2,4,2,48,256]{4,3,2,1,0:T(8,128)}, f32[2,4,2,48,256]{4,3,2,1,0:T(8,128)}, u32[]{:S(2)}, u32[]{:S(2)}) %collective-permute-start.10) | collective-permute-done | bytes 786464 | tf_op jit(solution)/shard_map/sum_core/ppermute | solution.py:23
  46.4 1.2 %bitcast_add_fusion = f32[2,4,2,48,256]{4,3,2,1,0:T(8,128)S(1)} fusion(f32[2,4,2,48,256]{4,3,2,1,0:T(8,128)} %collective-permute-done.10, f32[2,4,2,2,48,256]{5,4,3,2,1,0:T(8,128)S(1)} %bitcast.83, s32[]{:T(128)S(6)} %select_n.738), kind=kLoop, calls=%fused_computation.17 | loop fusion | flops 196608 | bytes 2359300 | tf_op jit(solution)/shard_map/sum_core/add | solution.py:102
  47.7 3.0 %collective-permute-start.11 = (bf16[192,256]{1,0:T(8,128)(2,1)S(1)}, bf16[192,256]{1,0:T(8,128)(2,1)S(1)}, u32[]{:S(2)}, u32[]{:S(2)}) collective-permute-start(bf16[192,256]{1,0:T(8,128)(2,1)S(1)} %bitcast.99), channel_id=1, source_target_pairs={{0,128},{16,144},{128,0},{144,16},{1,129},{17,145},{129,1},{145,17... | collective-permute-start | bytes 294920 | tf_op jit(solution)/shard_map/sum_y/ppermute | solution.py:10
  50.7 0.4 collective-permute-start.12
  51.1 2.3 %collective-permute-start.13 = (bf16[192,256]{1,0:T(8,128)(2,1)S(1)}, bf16[192,256]{1,0:T(8,128)(2,1)S(1)}, u32[]{:S(2)}, u32[]{:S(2)}) collective-permute-start(bf16[192,256]{1,0:T(8,128)(2,1)S(1)} %bitcast.97), channel_id=1, source_target_pairs={{0,144},{16,0},{128,16},{144,128},{1,145},{17,1},{129,17},{145,129... | collective-permute-start | bytes 294920 | tf_op jit(solution)/shard_map/sum_y/ppermute | solution.py:10
  53.4 2.0 %collective-permute-done.12 = bf16[192,256]{1,0:T(8,128)(2,1)S(1)} collective-permute-done((bf16[192,256]{1,0:T(8,128)(2,1)S(1)}, bf16[192,256]{1,0:T(8,128)(2,1)S(1)}, u32[]{:S(2)}, u32[]{:S(2)}) %collective-permute-start.12) | collective-permute-done | bytes 98336 | tf_op jit(solution)/shard_map/sum_y/ppermute | solution.py:10
  55.4 0.4 collective-permute-done.13
  55.8 1.0 collective-permute-start.14
  56.7 2.1 %collective-permute-start.15 = (f32[48,256]{1,0:T(8,128)S(1)}, f32[48,256]{1,0:T(8,128)S(1)}, u32[]{:S(2)}, u32[]{:S(2)}) collective-permute-start(f32[48,256]{1,0:T(8,128)S(1)} %get-tuple-element.60), channel_id=1, source_target_pairs={{0,32},{32,64},{64,96},{96,0},{1,33},{33,65},{65,97},{97,1},{2,34}... | collective-permute-start | bytes 147464 | tf_op jit(solution)/shard_map/exchange_x/ppermute | solution.py:10
  58.8 0.6 collective-permute-start.16
  59.4 1.2 %collective-permute-start.20 = (bf16[512,256]{1,0:T(8,128)(2,1)S(1)}, bf16[512,256]{1,0:T(8,128)(2,1)S(1)}, u32[]{:S(2)}, u32[]{:S(2)}) collective-permute-start(bf16[512,256]{1,0:T(8,128)(2,1)S(1)} %select_select_fusion), channel_id=1, source_target_pairs={{0,64},{32,96},{64,0},{96,32},{1,65},{33,97},{65,1},{97,33},{2,66}... | collective-permute-start | bytes 786440 | tf_op jit(solution)/shard_map/exchange_x/ppermute | solution.py:10
  60.6 2.7 %collective-permute-start.22 = (bf16[512,256]{1,0:T(8,128)(2,1)S(1)}, bf16[512,256]{1,0:T(8,128)(2,1)S(1)}, u32[]{:S(2)}, u32[]{:S(2)}) collective-permute-start(bf16[512,256]{1,0:T(8,128)(2,1)S(1)} %select_select_fusion), channel_id=1, source_target_pairs={{0,96},{32,0},{64,32},{96,64},{1,97},{33,1},{65,33},{97,65},{2,98}... | collective-permute-start | bytes 786440 | tf_op jit(solution)/shard_map/exchange_x/ppermute | solution.py:10
  63.5 0.5 fusion.15
  64.0 1.2 %fusion.56 = (bf16[48,1024]{1,0:T(8,128)(2,1)S(1)}, f32[48,1024]{1,0:T(8,128)}) fusion(bf16[48,1024]{1,0:T(8,128)(2,1)S(1)} %get-tuple-element.57, bf16[1024,1024]{1,0:T(8,128)(2,1)S(1)} %copy-done, f32[96,1024]{1,0:T(8,128)S(1)} %fusion.15), kind=kOutput, calls=%fused_computation.128 | convolution fusion | flops 100810752 | bytes 2883584 | tf_op jit(solution)/shard_map/screen/dot_general | solution.py:136
  65.1 1.4 %collective-permute-start.17 = (bf16[48,1024]{1,0:T(8,128)(2,1)S(1)}, bf16[48,1024]{1,0:T(8,128)(2,1)S(1)}, u32[]{:S(2)}, u32[]{:S(2)}) collective-permute-start(bf16[48,1024]{1,0:T(8,128)(2,1)S(1)} %get-tuple-element.67), channel_id=1, source_target_pairs={{0,128},{16,144},{128,0},{144,16},{1,129},{17,145},{129,1},{145,17... | collective-permute-start | bytes 294920 | tf_op jit(solution)/shard_map/gather_y/ppermute | solution.py:10
  66.6 1.6 %collective-permute-start.18 = (bf16[48,1024]{1,0:T(8,128)(2,1)S(1)}, bf16[48,1024]{1,0:T(8,128)(2,1)S(1)}, u32[]{:S(2)}, u32[]{:S(2)}) collective-permute-start(bf16[48,1024]{1,0:T(8,128)(2,1)S(1)} %get-tuple-element.67), channel_id=1, source_target_pairs={{0,16},{16,128},{128,144},{144,0},{1,17},{17,129},{129,145},{145,1... | collective-permute-start | bytes 294920 | tf_op jit(solution)/shard_map/gather_y/ppermute | solution.py:10
  68.2 2.2 %collective-permute-done.17 = bf16[48,1024]{1,0:T(8,128)(2,1)S(1)} collective-permute-done((bf16[48,1024]{1,0:T(8,128)(2,1)S(1)}, bf16[48,1024]{1,0:T(8,128)(2,1)S(1)}, u32[]{:S(2)}, u32[]{:S(2)}) %collective-permute-start.17) | collective-permute-done | bytes 98336 | tf_op jit(solution)/shard_map/gather_y/ppermute | solution.py:10
  70.4 2.4 %collective-permute-start.19 = (bf16[48,1024]{1,0:T(8,128)(2,1)S(1)}, bf16[48,1024]{1,0:T(8,128)(2,1)S(1)}, u32[]{:S(2)}, u32[]{:S(2)}) collective-permute-start(bf16[48,1024]{1,0:T(8,128)(2,1)S(1)} %get-tuple-element.67), channel_id=1, source_target_pairs={{0,144},{16,0},{128,16},{144,128},{1,145},{17,1},{129,17},{145,129... | collective-permute-start | bytes 294920 | tf_op jit(solution)/shard_map/gather_y/ppermute | solution.py:10
  72.9 2.4 %collective-permute-done.19 = bf16[48,1024]{1,0:T(8,128)(2,1)S(1)} collective-permute-done((bf16[48,1024]{1,0:T(8,128)(2,1)S(1)}, bf16[48,1024]{1,0:T(8,128)(2,1)S(1)}, u32[]{:S(2)}, u32[]{:S(2)}) %collective-permute-start.19) | collective-permute-done | bytes 98336 | tf_op jit(solution)/shard_map/gather_y/ppermute | solution.py:10
  75.4 0.2 select_add_fusion.3
  75.6 0.2 select_add_fusion.2
  75.8 5.4 %collective-permute-start.23 = (bf16[192,1024]{1,0:T(8,128)(2,1)S(1)}, bf16[192,1024]{1,0:T(8,128)(2,1)S(1)}, u32[]{:S(2)}, u32[]{:S(2)}) collective-permute-start(bf16[192,1024]{1,0:T(8,128)(2,1)S(1)} %pad_maximum_fusion.1), channel_id=1, source_target_pairs={{0,8},{8,0},{1,9},{9,1},{2,10},{10,2},{3,11},{11,3},{4,12},{12,4},... | collective-permute-start | bytes 1179656 | tf_op jit(solution)/shard_map/gather_y/ppermute | solution.py:23
  81.2 0.2 select_add_fusion.1
  81.4 0.2 select_add_fusion
  81.6 0.9 collective-permute-done.23
  82.6 0.6 fusion.1
  83.3 12.3 %all_to_all.9 = f32[32,1,128]{2,1,0:T(1,128)S(1)} all-to-all(f32[32,1,128]{2,1,0:T(1,128)S(1)} %bitcast.100), channel_id=1, replica_groups=mesh['grp'=2,'x'=4,'ylo'=2,'core'=2,'col'=8] {'x','col'}, dimensions={0} | all-to-all | bytes 32768 | tf_op jit(solution)/shard_map/sigma/all_to_all | solution.py:172
  95.5 0.6 reduce_sum.29
  (55 shorter events, 1.0 us)
Async XLA Ops:
  1.6 12.0 %collective-permute-start = (bf16[128,256]{1,0:T(8,128)(2,1)S(1)}, bf16[128,256]{1,0:T(8,128)(2,1)S(1)}, u32[]{:S(2)}, u32[]{:S(2)}) collective-permute-start(bf16[128,256]{1,0:T(8,128)(2,1)S(1)} %get-tuple-element.43), channel_id=1, source_target_pairs={{0,64},{32,96},{64,0},{96,32},{8,72},{40,104},{72,8},{104,40},{16,... | collective-permute-start | bytes 196616 | tf_op jit(solution)/shard_map/quarters/ppermute | solution.py:19
  7.1 6.5 %collective-permute-start.1 = (bf16[128,256]{1,0:T(8,128)(2,1)S(1)}, bf16[128,256]{1,0:T(8,128)(2,1)S(1)}, u32[]{:S(2)}, u32[]{:S(2)}) collective-permute-start(bf16[128,256]{1,0:T(8,128)(2,1)S(1)} %get-tuple-element.42), channel_id=1, source_target_pairs={{0,32},{32,64},{64,96},{96,0},{8,40},{40,72},{72,104},{104,8},{16,... | collective-permute-start | bytes 196616 | tf_op jit(solution)/shard_map/quarters/ppermute | solution.py:19
  9.4 5.6 %collective-permute-start.2 = (bf16[128,256]{1,0:T(8,128)(2,1)S(1)}, bf16[128,256]{1,0:T(8,128)(2,1)S(1)}, u32[]{:S(2)}, u32[]{:S(2)}) collective-permute-start(bf16[128,256]{1,0:T(8,128)(2,1)S(1)} %get-tuple-element.44), channel_id=1, source_target_pairs={{0,96},{32,0},{64,32},{96,64},{8,104},{40,8},{72,40},{104,72},{16,... | collective-permute-start | bytes 196616 | tf_op jit(solution)/shard_map/quarters/ppermute | solution.py:19
  15.0 9.1 %collective-permute-start.3 = (bf16[512,256]{1,0:T(8,128)(2,1)S(1)}, bf16[512,256]{1,0:T(8,128)(2,1)S(1)}, u32[]{:S(2)}, u32[]{:S(2)}) collective-permute-start(bf16[512,256]{1,0:T(8,128)(2,1)S(1)} %pad_maximum_fusion.2), channel_id=1, source_target_pairs={{0,3},{8,11},{16,19},{24,27},{32,35},{40,43},{48,51},{56,59},{64,6... | collective-permute-start | bytes 786440 | tf_op jit(solution)/shard_map/panel_z/ppermute | solution.py:14
  16.3 7.8 %collective-permute-start.4 = (bf16[512,256]{1,0:T(8,128)(2,1)S(1)}, bf16[512,256]{1,0:T(8,128)(2,1)S(1)}, u32[]{:S(2)}, u32[]{:S(2)}) collective-permute-start(bf16[512,256]{1,0:T(8,128)(2,1)S(1)} %pad_maximum_fusion.2), channel_id=1, source_target_pairs={{0,6},{8,14},{16,22},{24,30},{32,38},{40,46},{48,54},{56,62},{64,7... | collective-permute-start | bytes 786440 | tf_op jit(solution)/shard_map/panel_z/ppermute | solution.py:14
  19.8 12.1 %collective-permute-start.7 = (bf16[1552,128]{1,0:T(8,128)(2,1)S(1)}, bf16[1552,128]{1,0:T(8,128)(2,1)S(1)}, u32[]{:S(2)}, u32[]{:S(2)}) collective-permute-start(bf16[1552,128]{1,0:T(8,128)(2,1)S(1)} %concatenate.41), channel_id=1, source_target_pairs={{0,64},{32,96},{64,0},{96,32},{1,65},{33,97},{65,1},{97,33},{2,66}... | collective-permute-start | bytes 1191944 | tf_op jit(solution)/shard_map/blocks/ppermute | solution.py:10
  21.4 19.6 %collective-permute-start.8 = (bf16[1552,128]{1,0:T(8,128)(2,1)S(1)}, bf16[1552,128]{1,0:T(8,128)(2,1)S(1)}, u32[]{:S(2)}, u32[]{:S(2)}) collective-permute-start(bf16[1552,128]{1,0:T(8,128)(2,1)S(1)} %concatenate.41), channel_id=1, source_target_pairs={{0,32},{32,64},{64,96},{96,0},{1,33},{33,65},{65,97},{97,1},{2,34}... | collective-permute-start | bytes 1191944 | tf_op jit(solution)/shard_map/blocks/ppermute | solution.py:10
  23.5 17.6 %collective-permute-start.9 = (bf16[1552,128]{1,0:T(8,128)(2,1)S(1)}, bf16[1552,128]{1,0:T(8,128)(2,1)S(1)}, u32[]{:S(2)}, u32[]{:S(2)}) collective-permute-start(bf16[1552,128]{1,0:T(8,128)(2,1)S(1)} %concatenate.41), channel_id=1, source_target_pairs={{0,96},{32,0},{64,32},{96,64},{1,97},{33,1},{65,33},{97,65},{2,98}... | collective-permute-start | bytes 1191944 | tf_op jit(solution)/shard_map/blocks/ppermute | solution.py:10
  24.1 17.1 %collective-permute-start.5 = (bf16[512,256]{1,0:T(8,128)(2,1)S(1)}, bf16[512,256]{1,0:T(8,128)(2,1)S(1)}, u32[]{:S(2)}, u32[]{:S(2)}) collective-permute-start(bf16[512,256]{1,0:T(8,128)(2,1)S(1)} %select_select_fusion.1), channel_id=1, source_target_pairs={{0,1},{3,4},{6,5},{8,9},{11,12},{14,13},{16,17},{19,20},{22,21},{2... | collective-permute-start | bytes 786440 | tf_op jit(solution)/shard_map/panel_z/ppermute | solution.py:14
  25.5 15.8 %collective-permute-start.6 = (bf16[512,256]{1,0:T(8,128)(2,1)S(1)}, bf16[512,256]{1,0:T(8,128)(2,1)S(1)}, u32[]{:S(2)}, u32[]{:S(2)}) collective-permute-start(bf16[512,256]{1,0:T(8,128)(2,1)S(1)} %select_select_fusion.1), channel_id=1, source_target_pairs={{0,7},{3,2},{8,15},{11,10},{16,23},{19,18},{24,31},{27,26},{32,39}... | collective-permute-start | bytes 786440 | tf_op jit(solution)/shard_map/panel_z/ppermute | solution.py:14
  43.0 3.4 %collective-permute-start.10 = (f32[2,4,2,48,256]{4,3,2,1,0:T(8,128)}, f32[2,4,2,48,256]{4,3,2,1,0:T(8,128)}, u32[]{:S(2)}, u32[]{:S(2)}) collective-permute-start(f32[2,4,2,48,256]{4,3,2,1,0:T(8,128)} %dynamic-slice_bitcast_fusion), channel_id=1, source_target_pairs={{0,8},{8,0},{1,9},{9,1},{2,10},{10,2},{3,11},{11,3},{4,12},{12,4},... | collective-permute-start | bytes 2359304 | tf_op jit(solution)/shard_map/sum_core/ppermute | solution.py:23
  47.6 15.9 %copy-start.1 = (bf16[1024,1024]{1,0:T(8,128)(2,1)S(1)}, bf16[1024,1024]{1,0:T(8,128)(2,1)}, u32[]{:S(2)}) copy-start(bf16[1024,1024]{1,0:T(8,128)(2,1)} %get-tuple-element.26) | copy-start | bytes 6291460
  47.7 5.7 %collective-permute-start.11 = (bf16[192,256]{1,0:T(8,128)(2,1)S(1)}, bf16[192,256]{1,0:T(8,128)(2,1)S(1)}, u32[]{:S(2)}, u32[]{:S(2)}) collective-permute-start(bf16[192,256]{1,0:T(8,128)(2,1)S(1)} %bitcast.99), channel_id=1, source_target_pairs={{0,128},{16,144},{128,0},{144,16},{1,129},{17,145},{129,1},{145,17... | collective-permute-start | bytes 294920 | tf_op jit(solution)/shard_map/sum_y/ppermute | solution.py:10
  50.7 4.7 %collective-permute-start.12 = (bf16[192,256]{1,0:T(8,128)(2,1)S(1)}, bf16[192,256]{1,0:T(8,128)(2,1)S(1)}, u32[]{:S(2)}, u32[]{:S(2)}) collective-permute-start(bf16[192,256]{1,0:T(8,128)(2,1)S(1)} %bitcast.98), channel_id=1, source_target_pairs={{0,16},{16,128},{128,144},{144,0},{1,17},{17,129},{129,145},{145,1... | collective-permute-start | bytes 294920 | tf_op jit(solution)/shard_map/sum_y/ppermute | solution.py:10
  51.1 4.6 %collective-permute-start.13 = (bf16[192,256]{1,0:T(8,128)(2,1)S(1)}, bf16[192,256]{1,0:T(8,128)(2,1)S(1)}, u32[]{:S(2)}, u32[]{:S(2)}) collective-permute-start(bf16[192,256]{1,0:T(8,128)(2,1)S(1)} %bitcast.97), channel_id=1, source_target_pairs={{0,144},{16,0},{128,16},{144,128},{1,145},{17,1},{129,17},{145,129... | collective-permute-start | bytes 294920 | tf_op jit(solution)/shard_map/sum_y/ppermute | solution.py:10
  55.7 8.2 %copy-start = (bf16[1024,1024]{1,0:T(8,128)(2,1)S(1)}, bf16[1024,1024]{1,0:T(8,128)(2,1)}, u32[]{:S(2)}) copy-start(bf16[1024,1024]{1,0:T(8,128)(2,1)} %get-tuple-element.27) | copy-start | bytes 6291460
  55.8 4.8 %collective-permute-start.14 = (f32[48,256]{1,0:T(8,128)S(1)}, f32[48,256]{1,0:T(8,128)S(1)}, u32[]{:S(2)}, u32[]{:S(2)}) collective-permute-start(f32[48,256]{1,0:T(8,128)S(1)} %get-tuple-element.58), channel_id=1, source_target_pairs={{0,64},{32,96},{64,0},{96,32},{1,65},{33,97},{65,1},{97,33},{2,66}... | collective-permute-start | bytes 147464 | tf_op jit(solution)/shard_map/exchange_x/ppermute | solution.py:10
  56.7 6.5 %collective-permute-start.15 = (f32[48,256]{1,0:T(8,128)S(1)}, f32[48,256]{1,0:T(8,128)S(1)}, u32[]{:S(2)}, u32[]{:S(2)}) collective-permute-start(f32[48,256]{1,0:T(8,128)S(1)} %get-tuple-element.60), channel_id=1, source_target_pairs={{0,32},{32,64},{64,96},{96,0},{1,33},{33,65},{65,97},{97,1},{2,34}... | collective-permute-start | bytes 147464 | tf_op jit(solution)/shard_map/exchange_x/ppermute | solution.py:10
  58.8 4.5 %collective-permute-start.16 = (f32[48,256]{1,0:T(8,128)S(1)}, f32[48,256]{1,0:T(8,128)S(1)}, u32[]{:S(2)}, u32[]{:S(2)}) collective-permute-start(f32[48,256]{1,0:T(8,128)S(1)} %get-tuple-element.59), channel_id=1, source_target_pairs={{0,96},{32,0},{64,32},{96,64},{1,97},{33,1},{65,33},{97,65},{2,98}... | collective-permute-start | bytes 147464 | tf_op jit(solution)/shard_map/exchange_x/ppermute | solution.py:10
  59.4 15.9 %collective-permute-start.20 = (bf16[512,256]{1,0:T(8,128)(2,1)S(1)}, bf16[512,256]{1,0:T(8,128)(2,1)S(1)}, u32[]{:S(2)}, u32[]{:S(2)}) collective-permute-start(bf16[512,256]{1,0:T(8,128)(2,1)S(1)} %select_select_fusion), channel_id=1, source_target_pairs={{0,64},{32,96},{64,0},{96,32},{1,65},{33,97},{65,1},{97,33},{2,66}... | collective-permute-start | bytes 786440 | tf_op jit(solution)/shard_map/exchange_x/ppermute | solution.py:10
  60.6 14.7 %collective-permute-start.21 = (bf16[512,256]{1,0:T(8,128)(2,1)S(1)}, bf16[512,256]{1,0:T(8,128)(2,1)S(1)}, u32[]{:S(2)}, u32[]{:S(2)}) collective-permute-start(bf16[512,256]{1,0:T(8,128)(2,1)S(1)} %select_select_fusion), channel_id=1, source_target_pairs={{0,32},{32,64},{64,96},{96,0},{1,33},{33,65},{65,97},{97,1},{2,34}... | collective-permute-start | bytes 786440 | tf_op jit(solution)/shard_map/exchange_x/ppermute | solution.py:10
  60.6 14.7 %collective-permute-start.22 = (bf16[512,256]{1,0:T(8,128)(2,1)S(1)}, bf16[512,256]{1,0:T(8,128)(2,1)S(1)}, u32[]{:S(2)}, u32[]{:S(2)}) collective-permute-start(bf16[512,256]{1,0:T(8,128)(2,1)S(1)} %select_select_fusion), channel_id=1, source_target_pairs={{0,96},{32,0},{64,32},{96,64},{1,97},{33,1},{65,33},{97,65},{2,98}... | collective-permute-start | bytes 786440 | tf_op jit(solution)/shard_map/exchange_x/ppermute | solution.py:10
  65.1 5.3 %collective-permute-start.17 = (bf16[48,1024]{1,0:T(8,128)(2,1)S(1)}, bf16[48,1024]{1,0:T(8,128)(2,1)S(1)}, u32[]{:S(2)}, u32[]{:S(2)}) collective-permute-start(bf16[48,1024]{1,0:T(8,128)(2,1)S(1)} %get-tuple-element.67), channel_id=1, source_target_pairs={{0,128},{16,144},{128,0},{144,16},{1,129},{17,145},{129,1},{145,17... | collective-permute-start | bytes 294920 | tf_op jit(solution)/shard_map/gather_y/ppermute | solution.py:10
  66.6 6.3 %collective-permute-start.18 = (bf16[48,1024]{1,0:T(8,128)(2,1)S(1)}, bf16[48,1024]{1,0:T(8,128)(2,1)S(1)}, u32[]{:S(2)}, u32[]{:S(2)}) collective-permute-start(bf16[48,1024]{1,0:T(8,128)(2,1)S(1)} %get-tuple-element.67), channel_id=1, source_target_pairs={{0,16},{16,128},{128,144},{144,0},{1,17},{17,129},{129,145},{145,1... | collective-permute-start | bytes 294920 | tf_op jit(solution)/shard_map/gather_y/ppermute | solution.py:10
  70.4 4.9 %collective-permute-start.19 = (bf16[48,1024]{1,0:T(8,128)(2,1)S(1)}, bf16[48,1024]{1,0:T(8,128)(2,1)S(1)}, u32[]{:S(2)}, u32[]{:S(2)}) collective-permute-start(bf16[48,1024]{1,0:T(8,128)(2,1)S(1)} %get-tuple-element.67), channel_id=1, source_target_pairs={{0,144},{16,0},{128,16},{144,128},{1,145},{17,1},{129,17},{145,129... | collective-permute-start | bytes 294920 | tf_op jit(solution)/shard_map/gather_y/ppermute | solution.py:10
  75.8 6.7 %collective-permute-start.23 = (bf16[192,1024]{1,0:T(8,128)(2,1)S(1)}, bf16[192,1024]{1,0:T(8,128)(2,1)S(1)}, u32[]{:S(2)}, u32[]{:S(2)}) collective-permute-start(bf16[192,1024]{1,0:T(8,128)(2,1)S(1)} %pad_maximum_fusion.1), channel_id=1, source_target_pairs={{0,8},{8,0},{1,9},{9,1},{2,10},{10,2},{3,11},{11,3},{4,12},{12,4},... | collective-permute-start | bytes 1179656 | tf_op jit(solution)/shard_map/gather_y/ppermute | solution.py:23

commit v9 on v5

--- a/solution.py
+++ b/solution.py
@@ -12,6 +12,11 @@
 
 def along_z(value, *pairs):
     return lax.ppermute(value, Z, pairs)
+
+
+def cross(value, size, step, *columns):
+    pairs = [(i * 8 + a, (i + step) % size * 8 + b) for i in range(size) for a, b in columns]
+    return lax.ppermute(value, (X, Z), pairs)
 
 
 def swap(value):
@@ -66,16 +71,20 @@
         held = jnp.where(z == 3, far_a, jnp.where(z == 6, far_b, piece))
         near_a = along_z(held, (0, 1), (3, 4), (6, 5))
         near_b = along_z(held, (0, 7), (3, 2))
+        cross_a = cross(held, nx, 2, (0, 1), (3, 4), (6, 5))
+        cross_b = cross(held, nx, 2, (0, 7), (3, 2))
+        cross_c = cross(held, nx, 2, (0, 0), (3, 3), (6, 6))
         inv_high, inv_rest = two_parts(block_inverse)
         near_a, near_b, inv_high, inv_rest, *factors = lax.optimization_barrier(
             (near_a, near_b, inv_high, inv_rest, *factors)
         )
-        held = jnp.where((z == 1) | (z == 4) | (z == 5), near_a, held)
-        held = jnp.where((z == 7) | (z == 2), near_b, held)
+        from_a, from_b = (z == 1) | (z == 4) | (z == 5), (z == 7) | (z == 2)
+        held = jnp.where(from_a, near_a, jnp.where(from_b, near_b, held))
 
     with jax.named_scope("panel_x"):
-        panels = [held] + [shift(held, X, nx, k) for k in steps[1:]]
-        panels = jnp.concatenate(panels, axis=0)
+        right, left = shift(held, X, nx, 1), shift(held, X, nx, 3)
+        far = jnp.where(from_a, cross_a, jnp.where(from_b, cross_b, cross_c))
+        panels = jnp.concatenate([held, far, right, left], axis=0)
 
     with jax.named_scope("response"):
         factors = jnp.concatenate(factors, axis=1)

time: 82.2 us -> 83.8 us (1.019)
  starting transfers between devices: 34.3 us -> 38.9 us
  blocking collectives: 14.1 us -> 12 us
  waiting for transfers between devices: 21.2 us -> 20.3 us
    ppermute x0 -> x3, starting transfers between devices: none -> 4.86 us  [cross(): return lax.ppermute(value, (X, Z), pairs)]
    ppermute x12 -> x11, waiting for transfers between devices: 17.3 us -> 13 us  [shift(): lax.ppermute(value, axis, [(i, (i + step) % size) for i in range(size)])]
    ppermute x0 -> x3, waiting for transfers between devices: none -> 4.24 us  [cross(): return lax.ppermute(value, (X, Z), pairs)]
    all_to_all x1, blocking collectives: 14.1 us -> 12 us  [body(): terms = lax.all_to_all(copies, (X, Z), 0, 0, tiled=True)]
    ppermute x4, waiting for transfers between devices: 0.9 us -> 0.01 us  [along_z(): return lax.ppermute(value, Z, pairs)]
    ppermute x12 -> x11, starting transfers between devices: 18.4 us -> 18.3 us  [shift(): lax.ppermute(value, axis, [(i, (i + step) % size) for i in range(size)])]
  transfers between devices with their start and end apart: 18 -> 20, of which waited for: 9 -> 8; matrix products, arithmetic and copies ran while one was open for 7% -> 7% of each run, Pallas kernels for 0% -> 0%
where the time goes in v9:
time: 83.8 us; the launch traced here: 83.5 us
  starting transfers between devices  38.9 us (46%)
  waiting for transfers between devices  20.3 us (24%)
  blocking collectives  12 us (14%)
  other arithmetic  4.83 us (6%)
  local copies, waits for them, and re-layouts  3.34 us (4%)
  matrix products  2.94 us (4%)
  between operations  1.18 us (1%)
    ppermute x11, starting transfers between devices, shift(): lax.ppermute(value, axis, [(i, (i + step) % size) for i in range(size)])  18.3 us
    ppermute x11, waiting for transfers between devices, shift(): lax.ppermute(value, axis, [(i, (i + step) % size) for i in range(size)])  13 us
    ppermute x4, starting transfers between devices, along_z(): return lax.ppermute(value, Z, pairs)  12.1 us
    all_to_all x1, blocking collectives, body(): terms = lax.all_to_all(copies, (X, Z), 0, 0, tiled=True)  12 us
    ppermute x3, starting transfers between devices, cross(): return lax.ppermute(value, (X, Z), pairs)  4.86 us
    ppermute x3, waiting for transfers between devices, cross(): return lax.ppermute(value, (X, Z), pairs)  4.24 us
    ppermute x2, starting transfers between devices, swap(): return lax.ppermute(value, CORE, [(0, 1), (1, 0)])  3.74 us
    convert_element_type x2, other arithmetic, two_parts(): return (high.astype(LOW), (value - high).astype(LOW))  3.22 us
  transfers between devices with their start and end apart: 20, of which 8 were waited for; matrix products, arithmetic and copies ran while one was open for 7% of the time, Pallas kernels for 0%

profile of v9, /device:TPU:1, one launch (start us, length us, event | category | flops | bytes accessed | tf_op | source)
XLA Modules:
  0.0 83.5 jit_solution(16321804724349924216)
XLA Ops:
  0.6 0.0 copy-start
  0.6 1.0 %slice.31 = bf16[128,1024]{1,0:T(8,128)(2,1)S(1)} slice(bf16[128,1536]{1,0:T(8,128)(2,1)} %param.3), slice={[0:128], [0:1024]} | slice | bytes 524288 | tf_op jit(solution)/shard_map/panel_z/slice | solution.py:49
  1.7 7.1 %collective-permute-start = (bf16[128,1024]{1,0:T(8,128)(2,1)S(1)}, bf16[128,1024]{1,0:T(8,128)(2,1)S(1)}, u32[]{:S(2)}, u32[]{:S(2)}) collective-permute-start(bf16[128,1024]{1,0:T(8,128)(2,1)S(1)} %slice.31), channel_id=1, source_target_pairs={{0,3},{8,11},{16,19},{24,27},{32,35},{40,43},{48,51},{56,59},{64,6... | collective-permute-start | bytes 786440 | tf_op jit(solution)/shard_map/panel_z/ppermute | solution.py:14
  8.8 2.4 %collective-permute-start.1 = (bf16[128,1024]{1,0:T(8,128)(2,1)S(1)}, bf16[128,1024]{1,0:T(8,128)(2,1)S(1)}, u32[]{:S(2)}, u32[]{:S(2)}) collective-permute-start(bf16[128,1024]{1,0:T(8,128)(2,1)S(1)} %slice.31), channel_id=1, source_target_pairs={{0,6},{8,14},{16,22},{24,30},{32,38},{40,46},{48,54},{56,62},{64,7... | collective-permute-start | bytes 786440 | tf_op jit(solution)/shard_map/panel_z/ppermute | solution.py:14
  11.1 0.7 fusion.19
  11.9 1.2 %copy.18 = bf16[128,1536]{0,1:T(8,128)(2,1)S(1)} copy(bf16[128,1536]{1,0:T(8,128)(2,1)} %param.3) | data formatting | bytes 786432 | tf_op args[0]
  13.2 0.2 concatenate.37
  13.3 2.8 %collective-permute-start.4 = (bf16[400,128]{1,0:T(8,128)(2,1)S(1)}, bf16[400,128]{1,0:T(8,128)(2,1)S(1)}, u32[]{:S(2)}, u32[]{:S(2)}) collective-permute-start(bf16[400,128]{1,0:T(8,128)(2,1)S(1)} %concatenate.37), channel_id=1, source_target_pairs={{0,64},{32,96},{64,0},{96,32},{1,65},{33,97},{65,1},{97,33},{2,66}... | collective-permute-start | bytes 307208 | tf_op jit(solution)/shard_map/blocks/ppermute | solution.py:10
  16.2 0.2 concatenate.38
  16.3 0.4 collective-permute-start.5
  16.7 0.2 concatenate.39
  16.9 2.4 %collective-permute-start.6 = (bf16[400,128]{1,0:T(8,128)(2,1)S(1)}, bf16[400,128]{1,0:T(8,128)(2,1)S(1)}, u32[]{:S(2)}, u32[]{:S(2)}) collective-permute-start(bf16[400,128]{1,0:T(8,128)(2,1)S(1)} %concatenate.39), channel_id=1, source_target_pairs={{0,96},{32,0},{64,32},{96,64},{1,97},{33,1},{65,33},{97,65},{2,98}... | collective-permute-start | bytes 307208 | tf_op jit(solution)/shard_map/blocks/ppermute | solution.py:10
  19.3 0.2 concatenate.36
  19.6 0.0 collective-permute-done.1
  19.7 1.3 %collective-permute-start.2 = (bf16[128,1024]{1,0:T(8,128)(2,1)S(1)}, bf16[128,1024]{1,0:T(8,128)(2,1)S(1)}, u32[]{:S(2)}, u32[]{:S(2)}) collective-permute-start(bf16[128,1024]{1,0:T(8,128)(2,1)S(1)} %select_select_fusion.2), channel_id=1, source_target_pairs={{0,1},{3,4},{6,5},{8,9},{11,12},{14,13},{16,17},{19,20},{22,21},{2... | collective-permute-start | bytes 786440 | tf_op jit(solution)/shard_map/panel_z/ppermute | solution.py:14
  21.0 1.3 %collective-permute-start.3 = (bf16[128,1024]{1,0:T(8,128)(2,1)S(1)}, bf16[128,1024]{1,0:T(8,128)(2,1)S(1)}, u32[]{:S(2)}, u32[]{:S(2)}) collective-permute-start(bf16[128,1024]{1,0:T(8,128)(2,1)S(1)} %select_select_fusion.2), channel_id=1, source_target_pairs={{0,7},{3,2},{8,15},{11,10},{16,23},{19,18},{24,31},{27,26},{32,39}... | collective-permute-start | bytes 786440 | tf_op jit(solution)/shard_map/panel_z/ppermute | solution.py:14
  22.3 3.1 %fusion = (bf16[1024,1024]{1,0:T(8,128)(2,1)S(1)}, bf16[1024,1024]{1,0:T(8,128)(2,1)S(1)}) fusion(f32[1024,1024]{1,0:T(8,128)} %param.5), kind=kLoop, calls=%fused_computation.2 | loop fusion | flops 4194304 | bytes 8388608 | tf_op jit(solution)/shard_map/panel_z/convert_element_type | solution.py:37
  25.4 1.3 %collective-permute-start.7 = (bf16[128,1024]{1,0:T(8,128)(2,1)S(1)}, bf16[128,1024]{1,0:T(8,128)(2,1)S(1)}, u32[]{:S(2)}, u32[]{:S(2)}) collective-permute-start(bf16[128,1024]{1,0:T(8,128)(2,1)S(1)} %select_select_fusion.2), channel_id=1, source_target_pairs={{0,65},{3,68},{6,69},{32,97},{35,100},{38,101},{64,1},{67,4},{70,5... | collective-permute-start | bytes 786440 | tf_op jit(solution)/shard_map/panel_z/ppermute | solution.py:19
  26.8 1.3 %collective-permute-start.8 = (bf16[128,1024]{1,0:T(8,128)(2,1)S(1)}, bf16[128,1024]{1,0:T(8,128)(2,1)S(1)}, u32[]{:S(2)}, u32[]{:S(2)}) collective-permute-start(bf16[128,1024]{1,0:T(8,128)(2,1)S(1)} %select_select_fusion.2), channel_id=1, source_target_pairs={{0,71},{3,66},{32,103},{35,98},{64,7},{67,2},{96,39},{99,34},{8,79... | collective-permute-start | bytes 786440 | tf_op jit(solution)/shard_map/panel_z/ppermute | solution.py:19
  28.1 2.3 %collective-permute-start.9 = (bf16[128,1024]{1,0:T(8,128)(2,1)S(1)}, bf16[128,1024]{1,0:T(8,128)(2,1)S(1)}, u32[]{:S(2)}, u32[]{:S(2)}) collective-permute-start(bf16[128,1024]{1,0:T(8,128)(2,1)S(1)} %select_select_fusion.2), channel_id=1, source_target_pairs={{0,64},{3,67},{6,70},{32,96},{35,99},{38,102},{64,0},{67,3},{70,6}... | collective-permute-start | bytes 786440 | tf_op jit(solution)/shard_map/panel_z/ppermute | solution.py:19
  30.4 0.5 collective-permute-start.10
  30.9 2.3 %collective-permute-start.11 = (bf16[128,1024]{1,0:T(8,128)(2,1)S(1)}, bf16[128,1024]{1,0:T(8,128)(2,1)S(1)}, u32[]{:S(2)}, u32[]{:S(2)}) collective-permute-start(bf16[128,1024]{1,0:T(8,128)(2,1)S(1)} %select_select_fusion.1), channel_id=1, source_target_pairs={{0,96},{32,0},{64,32},{96,64},{1,97},{33,1},{65,33},{97,65},{2,98}... | collective-permute-start | bytes 786440 | tf_op jit(solution)/shard_map/panel_x/ppermute | solution.py:10
  33.3 4.2 %collective-permute-done.9 = bf16[128,1024]{1,0:T(8,128)(2,1)S(1)} collective-permute-done((bf16[128,1024]{1,0:T(8,128)(2,1)S(1)}, bf16[128,1024]{1,0:T(8,128)(2,1)S(1)}, u32[]{:S(2)}, u32[]{:S(2)}) %collective-permute-start.9) | collective-permute-done | bytes 262176 | tf_op jit(solution)/shard_map/panel_z/ppermute | solution.py:19
  37.6 7.7 %collective-permute-done.10 = bf16[128,1024]{1,0:T(8,128)(2,1)S(1)} collective-permute-done((bf16[128,1024]{1,0:T(8,128)(2,1)S(1)}, bf16[128,1024]{1,0:T(8,128)(2,1)S(1)}, u32[]{:S(2)}, u32[]{:S(2)}) %collective-permute-start.10) | collective-permute-done | bytes 262176 | tf_op jit(solution)/shard_map/panel_x/ppermute | solution.py:10
  45.3 0.7 fusion.2
  46.0 0.1 dynamic-slice_bitcast_fusion
  46.1 0.6 collective-permute-start.12
  46.8 1.7 %collective-permute-done.12 = f32[4,48,1024]{2,1,0:T(8,128)S(1)} collective-permute-done((f32[4,48,1024]{2,1,0:T(8,128)S(1)}, f32[4,48,1024]{2,1,0:T(8,128)S(1)}, u32[]{:S(2)}, u32[]{:S(2)}) %collective-permute-start.12) | collective-permute-done | bytes 786464 | tf_op jit(solution)/shard_map/sum_core/ppermute | solution.py:23
  48.6 0.1 bitcast_add_fusion
  48.7 3.0 %collective-permute-start.13 = (bf16[48,1024]{1,0:T(8,128)(2,1)S(1)}, bf16[48,1024]{1,0:T(8,128)(2,1)S(1)}, u32[]{:S(2)}, u32[]{:S(2)}) collective-permute-start(bf16[48,1024]{1,0:T(8,128)(2,1)S(1)} %get-tuple-element.32), channel_id=1, source_target_pairs={{0,128},{16,144},{128,0},{144,16},{1,129},{17,145},{129,1},{145,17... | collective-permute-start | bytes 294920 | tf_op jit(solution)/shard_map/sum_y/ppermute | solution.py:10
  51.7 0.4 collective-permute-start.14
  52.1 2.3 %collective-permute-start.15 = (bf16[48,1024]{1,0:T(8,128)(2,1)S(1)}, bf16[48,1024]{1,0:T(8,128)(2,1)S(1)}, u32[]{:S(2)}, u32[]{:S(2)}) collective-permute-start(bf16[48,1024]{1,0:T(8,128)(2,1)S(1)} %get-tuple-element.33), channel_id=1, source_target_pairs={{0,144},{16,0},{128,16},{144,128},{1,145},{17,1},{129,17},{145,129... | collective-permute-start | bytes 294920 | tf_op jit(solution)/shard_map/sum_y/ppermute | solution.py:10
  54.4 2.0 %collective-permute-done.14 = bf16[48,1024]{1,0:T(8,128)(2,1)S(1)} collective-permute-done((bf16[48,1024]{1,0:T(8,128)(2,1)S(1)}, bf16[48,1024]{1,0:T(8,128)(2,1)S(1)}, u32[]{:S(2)}, u32[]{:S(2)}) %collective-permute-start.14) | collective-permute-done | bytes 98336 | tf_op jit(solution)/shard_map/sum_y/ppermute | solution.py:10
  56.4 0.4 collective-permute-done.15
  56.8 0.1 fusion.4
  56.9 0.5 fusion.5
  57.4 1.2 %constant_dynamic-update-slice_fusion.8 = (bf16[384,1024]{1,0:T(8,128)(2,1)S(1)}, bf16[48,1024]{1,0:T(8,128)(2,1)S(1)}, f32[48,1024]{1,0:T(8,128)}) fusion(bf16[48,1024]{1,0:T(8,128)(2,1)S(1)} %get-tuple-element.31, bf16[1024,1024]{1,0:T(8,128)(2,1)S(1)} %get-tuple-element.23, f32[96,1024]{1,0:T(8,128)S(1)} %fusion.5), kind=kOutput, calls=%fused_computation.51 | convolution fusion | flops 100810752 | bytes 2981888 | tf_op jit(solution)/shard_map/screen/dot_general | solution.py:116
  58.5 1.5 %collective-permute-start.16 = (bf16[48,1024]{1,0:T(8,128)(2,1)S(1)}, bf16[48,1024]{1,0:T(8,128)(2,1)S(1)}, u32[]{:S(2)}, u32[]{:S(2)}) collective-permute-start(bf16[48,1024]{1,0:T(8,128)(2,1)S(1)} %get-tuple-element.25), channel_id=1, source_target_pairs={{0,128},{16,144},{128,0},{144,16},{1,129},{17,145},{129,1},{145,17... | collective-permute-start | bytes 294920 | tf_op jit(solution)/shard_map/gather_y/ppermute | solution.py:10
  60.0 1.5 %collective-permute-start.17 = (bf16[48,1024]{1,0:T(8,128)(2,1)S(1)}, bf16[48,1024]{1,0:T(8,128)(2,1)S(1)}, u32[]{:S(2)}, u32[]{:S(2)}) collective-permute-start(bf16[48,1024]{1,0:T(8,128)(2,1)S(1)} %get-tuple-element.25), channel_id=1, source_target_pairs={{0,16},{16,128},{128,144},{144,0},{1,17},{17,129},{129,145},{145,1... | collective-permute-start | bytes 294920 | tf_op jit(solution)/shard_map/gather_y/ppermute | solution.py:10
  61.6 1.2 %collective-permute-start.18 = (bf16[48,1024]{1,0:T(8,128)(2,1)S(1)}, bf16[48,1024]{1,0:T(8,128)(2,1)S(1)}, u32[]{:S(2)}, u32[]{:S(2)}) collective-permute-start(bf16[48,1024]{1,0:T(8,128)(2,1)S(1)} %get-tuple-element.25), channel_id=1, source_target_pairs={{0,144},{16,0},{128,16},{144,128},{1,145},{17,1},{129,17},{145,129... | collective-permute-start | bytes 294920 | tf_op jit(solution)/shard_map/gather_y/ppermute | solution.py:10
  62.7 0.8 collective-permute-done.16
  63.5 2.1 %collective-permute-done.17 = bf16[48,1024]{1,0:T(8,128)(2,1)S(1)} collective-permute-done((bf16[48,1024]{1,0:T(8,128)(2,1)S(1)}, bf16[48,1024]{1,0:T(8,128)(2,1)S(1)}, u32[]{:S(2)}, u32[]{:S(2)}) %collective-permute-start.17) | collective-permute-done | bytes 98336 | tf_op jit(solution)/shard_map/gather_y/ppermute | solution.py:10
  65.7 3.2 %collective-permute-start.19 = (bf16[192,1024]{1,0:T(8,128)(2,1)S(1)}, bf16[192,1024]{1,0:T(8,128)(2,1)S(1)}, u32[]{:S(2)}, u32[]{:S(2)}) collective-permute-start(bf16[192,1024]{1,0:T(8,128)(2,1)S(1)} %pad_maximum_fusion.1), channel_id=1, source_target_pairs={{0,8},{8,0},{1,9},{9,1},{2,10},{10,2},{3,11},{11,3},{4,12},{12,4},... | collective-permute-start | bytes 1179656 | tf_op jit(solution)/shard_map/gather_y/ppermute | solution.py:23
  68.9 1.3 %collective-permute-done.19 = bf16[192,1024]{1,0:T(8,128)(2,1)S(1)} collective-permute-done((bf16[192,1024]{1,0:T(8,128)(2,1)S(1)}, bf16[192,1024]{1,0:T(8,128)(2,1)S(1)}, u32[]{:S(2)}, u32[]{:S(2)}) %collective-permute-start.19) | collective-permute-done | bytes 393248 | tf_op jit(solution)/shard_map/gather_y/ppermute | solution.py:23
  70.2 0.6 fusion.1
  70.8 0.1 select_add_fusion
  70.9 12.0 %all_to_all.9 = f32[32,1,128]{2,1,0:T(1,128)S(1)} all-to-all(f32[32,1,128]{2,1,0:T(1,128)S(1)} %bitcast.61), channel_id=1, replica_groups=mesh['grp'=2,'x'=4,'ylo'=2,'core'=2,'col'=8] {'x','col'}, dimensions={0} | all-to-all | bytes 32768 | tf_op jit(solution)/shard_map/sigma/all_to_all | solution.py:141
  82.9 0.6 reduce_sum.29
  (44 shorter events, 0.6 us)
Async XLA Ops:
  0.6 19.0 %copy-start = (bf16[128,1536]{1,0:T(8,128)(2,1)S(1)}, bf16[128,1536]{1,0:T(8,128)(2,1)}, u32[]{:S(2)}) copy-start(bf16[128,1536]{1,0:T(8,128)(2,1)} %param.3) | copy-start | bytes 1179652
  1.7 17.9 %collective-permute-start = (bf16[128,1024]{1,0:T(8,128)(2,1)S(1)}, bf16[128,1024]{1,0:T(8,128)(2,1)S(1)}, u32[]{:S(2)}, u32[]{:S(2)}) collective-permute-start(bf16[128,1024]{1,0:T(8,128)(2,1)S(1)} %slice.31), channel_id=1, source_target_pairs={{0,3},{8,11},{16,19},{24,27},{32,35},{40,43},{48,51},{56,59},{64,6... | collective-permute-start | bytes 786440 | tf_op jit(solution)/shard_map/panel_z/ppermute | solution.py:14
  8.8 10.8 %collective-permute-start.1 = (bf16[128,1024]{1,0:T(8,128)(2,1)S(1)}, bf16[128,1024]{1,0:T(8,128)(2,1)S(1)}, u32[]{:S(2)}, u32[]{:S(2)}) collective-permute-start(bf16[128,1024]{1,0:T(8,128)(2,1)S(1)} %slice.31), channel_id=1, source_target_pairs={{0,6},{8,14},{16,22},{24,30},{32,38},{40,46},{48,54},{56,62},{64,7... | collective-permute-start | bytes 786440 | tf_op jit(solution)/shard_map/panel_z/ppermute | solution.py:14
  13.3 12.1 %collective-permute-start.4 = (bf16[400,128]{1,0:T(8,128)(2,1)S(1)}, bf16[400,128]{1,0:T(8,128)(2,1)S(1)}, u32[]{:S(2)}, u32[]{:S(2)}) collective-permute-start(bf16[400,128]{1,0:T(8,128)(2,1)S(1)} %concatenate.37), channel_id=1, source_target_pairs={{0,64},{32,96},{64,0},{96,32},{1,65},{33,97},{65,1},{97,33},{2,66}... | collective-permute-start | bytes 307208 | tf_op jit(solution)/shard_map/blocks/ppermute | solution.py:10
  16.3 10.4 %collective-permute-start.5 = (bf16[400,128]{1,0:T(8,128)(2,1)S(1)}, bf16[400,128]{1,0:T(8,128)(2,1)S(1)}, u32[]{:S(2)}, u32[]{:S(2)}) collective-permute-start(bf16[400,128]{1,0:T(8,128)(2,1)S(1)} %concatenate.38), channel_id=1, source_target_pairs={{0,32},{32,64},{64,96},{96,0},{1,33},{33,65},{65,97},{97,1},{2,34}... | collective-permute-start | bytes 307208 | tf_op jit(solution)/shard_map/blocks/ppermute | solution.py:10
  16.9 11.2 %collective-permute-start.6 = (bf16[400,128]{1,0:T(8,128)(2,1)S(1)}, bf16[400,128]{1,0:T(8,128)(2,1)S(1)}, u32[]{:S(2)}, u32[]{:S(2)}) collective-permute-start(bf16[400,128]{1,0:T(8,128)(2,1)S(1)} %concatenate.39), channel_id=1, source_target_pairs={{0,96},{32,0},{64,32},{96,64},{1,97},{33,1},{65,33},{97,65},{2,98}... | collective-permute-start | bytes 307208 | tf_op jit(solution)/shard_map/blocks/ppermute | solution.py:10
  19.7 10.7 %collective-permute-start.2 = (bf16[128,1024]{1,0:T(8,128)(2,1)S(1)}, bf16[128,1024]{1,0:T(8,128)(2,1)S(1)}, u32[]{:S(2)}, u32[]{:S(2)}) collective-permute-start(bf16[128,1024]{1,0:T(8,128)(2,1)S(1)} %select_select_fusion.2), channel_id=1, source_target_pairs={{0,1},{3,4},{6,5},{8,9},{11,12},{14,13},{16,17},{19,20},{22,21},{2... | collective-permute-start | bytes 786440 | tf_op jit(solution)/shard_map/panel_z/ppermute | solution.py:14
  21.0 9.4 %collective-permute-start.3 = (bf16[128,1024]{1,0:T(8,128)(2,1)S(1)}, bf16[128,1024]{1,0:T(8,128)(2,1)S(1)}, u32[]{:S(2)}, u32[]{:S(2)}) collective-permute-start(bf16[128,1024]{1,0:T(8,128)(2,1)S(1)} %select_select_fusion.2), channel_id=1, source_target_pairs={{0,7},{3,2},{8,15},{11,10},{16,23},{19,18},{24,31},{27,26},{32,39}... | collective-permute-start | bytes 786440 | tf_op jit(solution)/shard_map/panel_z/ppermute | solution.py:14
  25.4 7.9 %collective-permute-start.7 = (bf16[128,1024]{1,0:T(8,128)(2,1)S(1)}, bf16[128,1024]{1,0:T(8,128)(2,1)S(1)}, u32[]{:S(2)}, u32[]{:S(2)}) collective-permute-start(bf16[128,1024]{1,0:T(8,128)(2,1)S(1)} %select_select_fusion.2), channel_id=1, source_target_pairs={{0,65},{3,68},{6,69},{32,97},{35,100},{38,101},{64,1},{67,4},{70,5... | collective-permute-start | bytes 786440 | tf_op jit(solution)/shard_map/panel_z/ppermute | solution.py:19
  26.8 6.6 %collective-permute-start.8 = (bf16[128,1024]{1,0:T(8,128)(2,1)S(1)}, bf16[128,1024]{1,0:T(8,128)(2,1)S(1)}, u32[]{:S(2)}, u32[]{:S(2)}) collective-permute-start(bf16[128,1024]{1,0:T(8,128)(2,1)S(1)} %select_select_fusion.2), channel_id=1, source_target_pairs={{0,71},{3,66},{32,103},{35,98},{64,7},{67,2},{96,39},{99,34},{8,79... | collective-permute-start | bytes 786440 | tf_op jit(solution)/shard_map/panel_z/ppermute | solution.py:19
  28.1 9.5 %collective-permute-start.9 = (bf16[128,1024]{1,0:T(8,128)(2,1)S(1)}, bf16[128,1024]{1,0:T(8,128)(2,1)S(1)}, u32[]{:S(2)}, u32[]{:S(2)}) collective-permute-start(bf16[128,1024]{1,0:T(8,128)(2,1)S(1)} %select_select_fusion.2), channel_id=1, source_target_pairs={{0,64},{3,67},{6,70},{32,96},{35,99},{38,102},{64,0},{67,3},{70,6}... | collective-permute-start | bytes 786440 | tf_op jit(solution)/shard_map/panel_z/ppermute | solution.py:19
  30.4 14.9 %collective-permute-start.10 = (bf16[128,1024]{1,0:T(8,128)(2,1)S(1)}, bf16[128,1024]{1,0:T(8,128)(2,1)S(1)}, u32[]{:S(2)}, u32[]{:S(2)}) collective-permute-start(bf16[128,1024]{1,0:T(8,128)(2,1)S(1)} %select_select_fusion.1), channel_id=1, source_target_pairs={{0,32},{32,64},{64,96},{96,0},{1,33},{33,65},{65,97},{97,1},{2,34}... | collective-permute-start | bytes 786440 | tf_op jit(solution)/shard_map/panel_x/ppermute | solution.py:10
  30.9 14.5 %collective-permute-start.11 = (bf16[128,1024]{1,0:T(8,128)(2,1)S(1)}, bf16[128,1024]{1,0:T(8,128)(2,1)S(1)}, u32[]{:S(2)}, u32[]{:S(2)}) collective-permute-start(bf16[128,1024]{1,0:T(8,128)(2,1)S(1)} %select_select_fusion.1), channel_id=1, source_target_pairs={{0,96},{32,0},{64,32},{96,64},{1,97},{33,1},{65,33},{97,65},{2,98}... | collective-permute-start | bytes 786440 | tf_op jit(solution)/shard_map/panel_x/ppermute | solution.py:10
  46.1 2.5 %collective-permute-start.12 = (f32[4,48,1024]{2,1,0:T(8,128)S(1)}, f32[4,48,1024]{2,1,0:T(8,128)S(1)}, u32[]{:S(2)}, u32[]{:S(2)}) collective-permute-start(f32[4,48,1024]{2,1,0:T(8,128)S(1)} %dynamic-slice_bitcast_fusion), channel_id=1, source_target_pairs={{0,8},{8,0},{1,9},{9,1},{2,10},{10,2},{3,11},{11,3},{4,12},{12,4},... | collective-permute-start | bytes 2359304 | tf_op jit(solution)/shard_map/sum_core/ppermute | solution.py:23
  48.7 5.7 %collective-permute-start.13 = (bf16[48,1024]{1,0:T(8,128)(2,1)S(1)}, bf16[48,1024]{1,0:T(8,128)(2,1)S(1)}, u32[]{:S(2)}, u32[]{:S(2)}) collective-permute-start(bf16[48,1024]{1,0:T(8,128)(2,1)S(1)} %get-tuple-element.32), channel_id=1, source_target_pairs={{0,128},{16,144},{128,0},{144,16},{1,129},{17,145},{129,1},{145,17... | collective-permute-start | bytes 294920 | tf_op jit(solution)/shard_map/sum_y/ppermute | solution.py:10
  51.7 4.7 %collective-permute-start.14 = (bf16[48,1024]{1,0:T(8,128)(2,1)S(1)}, bf16[48,1024]{1,0:T(8,128)(2,1)S(1)}, u32[]{:S(2)}, u32[]{:S(2)}) collective-permute-start(bf16[48,1024]{1,0:T(8,128)(2,1)S(1)} %get-tuple-element.34), channel_id=1, source_target_pairs={{0,16},{16,128},{128,144},{144,0},{1,17},{17,129},{129,145},{145,1... | collective-permute-start | bytes 294920 | tf_op jit(solution)/shard_map/sum_y/ppermute | solution.py:10
  52.1 4.6 %collective-permute-start.15 = (bf16[48,1024]{1,0:T(8,128)(2,1)S(1)}, bf16[48,1024]{1,0:T(8,128)(2,1)S(1)}, u32[]{:S(2)}, u32[]{:S(2)}) collective-permute-start(bf16[48,1024]{1,0:T(8,128)(2,1)S(1)} %get-tuple-element.33), channel_id=1, source_target_pairs={{0,144},{16,0},{128,16},{144,128},{1,145},{17,1},{129,17},{145,129... | collective-permute-start | bytes 294920 | tf_op jit(solution)/shard_map/sum_y/ppermute | solution.py:10
  58.5 5.0 %collective-permute-start.16 = (bf16[48,1024]{1,0:T(8,128)(2,1)S(1)}, bf16[48,1024]{1,0:T(8,128)(2,1)S(1)}, u32[]{:S(2)}, u32[]{:S(2)}) collective-permute-start(bf16[48,1024]{1,0:T(8,128)(2,1)S(1)} %get-tuple-element.25), channel_id=1, source_target_pairs={{0,128},{16,144},{128,0},{144,16},{1,129},{17,145},{129,1},{145,17... | collective-permute-start | bytes 294920 | tf_op jit(solution)/shard_map/gather_y/ppermute | solution.py:10
  60.0 5.6 %collective-permute-start.17 = (bf16[48,1024]{1,0:T(8,128)(2,1)S(1)}, bf16[48,1024]{1,0:T(8,128)(2,1)S(1)}, u32[]{:S(2)}, u32[]{:S(2)}) collective-permute-start(bf16[48,1024]{1,0:T(8,128)(2,1)S(1)} %get-tuple-element.25), channel_id=1, source_target_pairs={{0,16},{16,128},{128,144},{144,0},{1,17},{17,129},{129,145},{145,1... | collective-permute-start | bytes 294920 | tf_op jit(solution)/shard_map/gather_y/ppermute | solution.py:10
  61.6 4.1 %collective-permute-start.18 = (bf16[48,1024]{1,0:T(8,128)(2,1)S(1)}, bf16[48,1024]{1,0:T(8,128)(2,1)S(1)}, u32[]{:S(2)}, u32[]{:S(2)}) collective-permute-start(bf16[48,1024]{1,0:T(8,128)(2,1)S(1)} %get-tuple-element.25), channel_id=1, source_target_pairs={{0,144},{16,0},{128,16},{144,128},{1,145},{17,1},{129,17},{145,129... | collective-permute-start | bytes 294920 | tf_op jit(solution)/shard_map/gather_y/ppermute | solution.py:10
  65.7 4.5 %collective-permute-start.19 = (bf16[192,1024]{1,0:T(8,128)(2,1)S(1)}, bf16[192,1024]{1,0:T(8,128)(2,1)S(1)}, u32[]{:S(2)}, u32[]{:S(2)}) collective-permute-start(bf16[192,1024]{1,0:T(8,128)(2,1)S(1)} %pad_maximum_fusion.1), channel_id=1, source_target_pairs={{0,8},{8,0},{1,9},{9,1},{2,10},{10,2},{3,11},{11,3},{4,12},{12,4},... | collective-permute-start | bytes 1179656 | tf_op jit(solution)/shard_map/gather_y/ppermute | solution.py:23

commit v10 on v5

--- a/solution.py
+++ b/solution.py
@@ -42,8 +42,10 @@
 
     with jax.named_scope("panel_z"):
         piece = orbital_b[:, :panel]
-        far_a = along_z(piece, (0, 3))
-        far_b = along_z(piece, (0, 6))
+        one = along_z(piece, (0, 1))
+        first, one = lax.optimization_barrier((piece, one))
+        far_b = along_z(first, (0, 6))
+        far_a = along_z(first, (0, 3))
 
     with jax.named_scope("blocks"):
         weight = 2.0 * gaps / (gaps * gaps + 1.0)
@@ -63,15 +65,17 @@
         far_a, far_b, block_inverse, *_ = lax.optimization_barrier(
             (far_a, far_b, block_inverse, *rows)
         )
-        held = jnp.where(z == 3, far_a, jnp.where(z == 6, far_b, piece))
-        near_a = along_z(held, (0, 1), (3, 4), (6, 5))
-        near_b = along_z(held, (0, 7), (3, 2))
+        two = along_z(one, (1, 2))
+        first, far_b = lax.optimization_barrier((first, far_b))
+        seven = along_z(first, (0, 7))
+        held = jnp.where(z == 6, far_b, jnp.where(z == 3, far_a, piece))
+        near = along_z(held, (3, 4), (6, 5))
         inv_high, inv_rest = two_parts(block_inverse)
-        near_a, near_b, inv_high, inv_rest, *factors = lax.optimization_barrier(
-            (near_a, near_b, inv_high, inv_rest, *factors)
+        near, inv_high, inv_rest, *factors = lax.optimization_barrier(
+            (near, inv_high, inv_rest, *factors)
         )
-        held = jnp.where((z == 1) | (z == 4) | (z == 5), near_a, held)
-        held = jnp.where((z == 7) | (z == 2), near_b, held)
+        held = jnp.where(z == 1, one, jnp.where(z == 2, two, jnp.where(z == 7, seven, held)))
+        held = jnp.where((z == 4) | (z == 5), near, held)
 
     with jax.named_scope("panel_x"):
         panels = [held] + [shift(held, X, nx, k) for k in steps[1:]]

time: 82.2 us -> 85.3 us (1.038)
  blocking collectives: 14.1 us -> 15.7 us
    ppermute x4 -> x6, waiting for transfers between devices: 0.9 us -> 4.41 us  [along_z(): return lax.ppermute(value, Z, pairs)]
    ppermute x2, starting transfers between devices: 3.94 us -> 7.23 us  [swap(): return lax.ppermute(value, CORE, [(0, 1), (1, 0)])]
    ppermute x12, waiting for transfers between devices: 17.3 us -> 14.4 us  [shift(): lax.ppermute(value, axis, [(i, (i + step) % size) for i in range(size)])]
    ppermute x4 -> x6, starting transfers between devices: 12.1 us -> 9.65 us  [along_z(): return lax.ppermute(value, Z, pairs)]
    all_to_all x1, blocking collectives: 14.1 us -> 15.7 us  [body(): terms = lax.all_to_all(copies, (X, Z), 0, 0, tiled=True)]
  transfers between devices with their start and end apart: 18 -> 20, of which waited for: 9 -> 11; matrix products, arithmetic and copies ran while one was open for 7% -> 7% of each run, Pallas kernels for 0% -> 0%
where the time goes in v10:
time: 85.3 us; the launch traced here: 85 us
  starting transfers between devices  35.1 us (41%)
  waiting for transfers between devices  21.8 us (26%)
  blocking collectives  15.7 us (18%)
  other arithmetic  4.83 us (6%)
  local copies, waits for them, and re-layouts  3.34 us (4%)
  matrix products  2.97 us (3%)
  between operations  1.15 us (1%)
    ppermute x12, starting transfers between devices, shift(): lax.ppermute(value, axis, [(i, (i + step) % size) for i in range(size)])  18.2 us
    all_to_all x1, blocking collectives, body(): terms = lax.all_to_all(copies, (X, Z), 0, 0, tiled=True)  15.7 us
    ppermute x12, waiting for transfers between devices, shift(): lax.ppermute(value, axis, [(i, (i + step) % size) for i in range(size)])  14.4 us
    ppermute x6, starting transfers between devices, along_z(): return lax.ppermute(value, Z, pairs)  9.65 us
    ppermute x2, starting transfers between devices, swap(): return lax.ppermute(value, CORE, [(0, 1), (1, 0)])  7.23 us
    ppermute x6, waiting for transfers between devices, along_z(): return lax.ppermute(value, Z, pairs)  4.41 us
    convert_element_type x2, other arithmetic, two_parts(): return (high.astype(LOW), (value - high).astype(LOW))  3.22 us
    ppermute x2, waiting for transfers between devices, swap(): return lax.ppermute(value, CORE, [(0, 1), (1, 0)])  3.05 us
  transfers between devices with their start and end apart: 20, of which 11 were waited for; matrix products, arithmetic and copies ran while one was open for 7% of the time, Pallas kernels for 0%

profile of v10, /device:TPU:1, one launch (start us, length us, event | category | flops | bytes accessed | tf_op | source)
XLA Modules:
  0.0 85.0 jit_solution(2568678563655269422)
XLA Ops:
  0.6 1.0 %slice.31 = bf16[128,1024]{1,0:T(8,128)(2,1)S(1)} slice(bf16[128,1536]{1,0:T(8,128)(2,1)} %param.3), slice={[0:128], [0:1024]} | slice | bytes 524288 | tf_op jit(solution)/shard_map/panel_z/slice | solution.py:44
  1.7 4.4 %collective-permute-start = (bf16[128,1024]{1,0:T(8,128)(2,1)S(1)}, bf16[128,1024]{1,0:T(8,128)(2,1)S(1)}, u32[]{:S(2)}, u32[]{:S(2)}) collective-permute-start(bf16[128,1024]{1,0:T(8,128)(2,1)S(1)} %slice.31), channel_id=1, source_target_pairs={{0,1},{8,9},{16,17},{24,25},{32,33},{40,41},{48,49},{56,57},{64,65... | collective-permute-start | bytes 786440 | tf_op jit(solution)/shard_map/panel_z/ppermute | solution.py:14
  6.1 0.7 fusion.19
  6.7 4.3 %collective-permute-done = bf16[128,1024]{1,0:T(8,128)(2,1)S(1)} collective-permute-done((bf16[128,1024]{1,0:T(8,128)(2,1)S(1)}, bf16[128,1024]{1,0:T(8,128)(2,1)S(1)}, u32[]{:S(2)}, u32[]{:S(2)}) %collective-permute-start) | collective-permute-done | bytes 262176 | tf_op jit(solution)/shard_map/panel_z/ppermute | solution.py:14
  11.0 1.3 %collective-permute-start.1 = (bf16[128,1024]{1,0:T(8,128)(2,1)S(1)}, bf16[128,1024]{1,0:T(8,128)(2,1)S(1)}, u32[]{:S(2)}, u32[]{:S(2)}) collective-permute-start(bf16[128,1024]{1,0:T(8,128)(2,1)S(1)} %slice.31), channel_id=1, source_target_pairs={{0,3},{8,11},{16,19},{24,27},{32,35},{40,43},{48,51},{56,59},{64,6... | collective-permute-start | bytes 786440 | tf_op jit(solution)/shard_map/panel_z/ppermute | solution.py:14
  12.3 1.3 %collective-permute-start.2 = (bf16[128,1024]{1,0:T(8,128)(2,1)S(1)}, bf16[128,1024]{1,0:T(8,128)(2,1)S(1)}, u32[]{:S(2)}, u32[]{:S(2)}) collective-permute-start(bf16[128,1024]{1,0:T(8,128)(2,1)S(1)} %slice.31), channel_id=1, source_target_pairs={{0,6},{8,14},{16,22},{24,30},{32,38},{40,46},{48,54},{56,62},{64,7... | collective-permute-start | bytes 786440 | tf_op jit(solution)/shard_map/panel_z/ppermute | solution.py:14
  13.7 1.2 %copy.18 = bf16[128,1536]{0,1:T(8,128)(2,1)S(1)} copy(bf16[128,1536]{1,0:T(8,128)(2,1)} %param.3) | data formatting | bytes 786432 | tf_op args[0]
  15.0 0.2 concatenate.37
  15.2 2.8 %collective-permute-start.4 = (bf16[400,128]{1,0:T(8,128)(2,1)S(1)}, bf16[400,128]{1,0:T(8,128)(2,1)S(1)}, u32[]{:S(2)}, u32[]{:S(2)}) collective-permute-start(bf16[400,128]{1,0:T(8,128)(2,1)S(1)} %concatenate.37), channel_id=1, source_target_pairs={{0,64},{32,96},{64,0},{96,32},{1,65},{33,97},{65,1},{97,33},{2,66}... | collective-permute-start | bytes 307208 | tf_op jit(solution)/shard_map/blocks/ppermute | solution.py:10
  18.0 0.2 concatenate.38
  18.2 0.4 collective-permute-start.5
  18.6 0.2 concatenate.39
  18.7 2.4 %collective-permute-start.6 = (bf16[400,128]{1,0:T(8,128)(2,1)S(1)}, bf16[400,128]{1,0:T(8,128)(2,1)S(1)}, u32[]{:S(2)}, u32[]{:S(2)}) collective-permute-start(bf16[400,128]{1,0:T(8,128)(2,1)S(1)} %concatenate.39), channel_id=1, source_target_pairs={{0,96},{32,0},{64,32},{96,64},{1,97},{33,1},{65,33},{97,65},{2,98}... | collective-permute-start | bytes 307208 | tf_op jit(solution)/shard_map/blocks/ppermute | solution.py:10
  21.2 0.2 concatenate.36
  21.4 0.7 collective-permute-start.7
  22.2 0.7 collective-permute-start.3
  22.9 1.3 %collective-permute-start.8 = (bf16[128,1024]{1,0:T(8,128)(2,1)S(1)}, bf16[128,1024]{1,0:T(8,128)(2,1)S(1)}, u32[]{:S(2)}, u32[]{:S(2)}) collective-permute-start(bf16[128,1024]{1,0:T(8,128)(2,1)S(1)} %slice.31), channel_id=1, source_target_pairs={{0,7},{8,15},{16,23},{24,31},{32,39},{40,47},{48,55},{56,63},{64,7... | collective-permute-start | bytes 786440 | tf_op jit(solution)/shard_map/panel_z/ppermute | solution.py:14
  24.2 3.1 %fusion = (bf16[1024,1024]{1,0:T(8,128)(2,1)S(1)}, bf16[1024,1024]{1,0:T(8,128)(2,1)S(1)}) fusion(f32[1024,1024]{1,0:T(8,128)} %param.5), kind=kLoop, calls=%fused_computation.2 | loop fusion | flops 4194304 | bytes 8388608 | tf_op jit(solution)/shard_map/panel_z/convert_element_type | solution.py:32
  27.4 0.1 collective-permute-done.8
  27.5 0.1 select_select_fusion
  27.6 0.1 collective-permute-start.10
  27.7 2.7 %collective-permute-start.11 = (bf16[128,1024]{1,0:T(8,128)(2,1)S(1)}, bf16[128,1024]{1,0:T(8,128)(2,1)S(1)}, u32[]{:S(2)}, u32[]{:S(2)}) collective-permute-start(bf16[128,1024]{1,0:T(8,128)(2,1)S(1)} %select_select_fusion), channel_id=1, source_target_pairs={{0,96},{32,0},{64,32},{96,64},{1,97},{33,1},{65,33},{97,65},{2,98}... | collective-permute-start | bytes 786440 | tf_op jit(solution)/shard_map/panel_x/ppermute | solution.py:10
  30.5 3.6 %collective-permute-done.10 = bf16[128,1024]{1,0:T(8,128)(2,1)S(1)} collective-permute-done((bf16[128,1024]{1,0:T(8,128)(2,1)S(1)}, bf16[128,1024]{1,0:T(8,128)(2,1)S(1)}, u32[]{:S(2)}, u32[]{:S(2)}) %collective-permute-start.10) | collective-permute-done | bytes 262176 | tf_op jit(solution)/shard_map/panel_x/ppermute | solution.py:10
  34.1 2.4 %collective-permute-done.11 = bf16[128,1024]{1,0:T(8,128)(2,1)S(1)} collective-permute-done((bf16[128,1024]{1,0:T(8,128)(2,1)S(1)}, bf16[128,1024]{1,0:T(8,128)(2,1)S(1)}, u32[]{:S(2)}, u32[]{:S(2)}) %collective-permute-start.11) | collective-permute-done | bytes 262176 | tf_op jit(solution)/shard_map/panel_x/ppermute | solution.py:10
  36.5 3.1 %collective-permute-done.9 = bf16[128,1024]{1,0:T(8,128)(2,1)S(1)} collective-permute-done((bf16[128,1024]{1,0:T(8,128)(2,1)S(1)}, bf16[128,1024]{1,0:T(8,128)(2,1)S(1)}, u32[]{:S(2)}, u32[]{:S(2)}) %collective-permute-start.9) | collective-permute-done | bytes 262176 | tf_op jit(solution)/shard_map/panel_x/ppermute | solution.py:10
  39.6 0.7 fusion.2
  40.4 4.1 %collective-permute-start.12 = (f32[4,48,1024]{2,1,0:T(8,128)S(1)}, f32[4,48,1024]{2,1,0:T(8,128)S(1)}, u32[]{:S(2)}, u32[]{:S(2)}) collective-permute-start(f32[4,48,1024]{2,1,0:T(8,128)S(1)} %dynamic-slice_bitcast_fusion), channel_id=1, source_target_pairs={{0,8},{8,0},{1,9},{9,1},{2,10},{10,2},{3,11},{11,3},{4,12},{12,4},... | collective-permute-start | bytes 2359304 | tf_op jit(solution)/shard_map/sum_core/ppermute | solution.py:18
  44.6 1.7 %collective-permute-done.12 = f32[4,48,1024]{2,1,0:T(8,128)S(1)} collective-permute-done((f32[4,48,1024]{2,1,0:T(8,128)S(1)}, f32[4,48,1024]{2,1,0:T(8,128)S(1)}, u32[]{:S(2)}, u32[]{:S(2)}) %collective-permute-start.12) | collective-permute-done | bytes 786464 | tf_op jit(solution)/shard_map/sum_core/ppermute | solution.py:18
  46.4 0.1 bitcast_add_fusion
  46.5 3.0 %collective-permute-start.13 = (bf16[48,1024]{1,0:T(8,128)(2,1)S(1)}, bf16[48,1024]{1,0:T(8,128)(2,1)S(1)}, u32[]{:S(2)}, u32[]{:S(2)}) collective-permute-start(bf16[48,1024]{1,0:T(8,128)(2,1)S(1)} %get-tuple-element.38), channel_id=1, source_target_pairs={{0,128},{16,144},{128,0},{144,16},{1,129},{17,145},{129,1},{145,17... | collective-permute-start | bytes 294920 | tf_op jit(solution)/shard_map/sum_y/ppermute | solution.py:10
  49.5 0.4 collective-permute-start.14
  49.9 2.3 %collective-permute-start.15 = (bf16[48,1024]{1,0:T(8,128)(2,1)S(1)}, bf16[48,1024]{1,0:T(8,128)(2,1)S(1)}, u32[]{:S(2)}, u32[]{:S(2)}) collective-permute-start(bf16[48,1024]{1,0:T(8,128)(2,1)S(1)} %get-tuple-element.39), channel_id=1, source_target_pairs={{0,144},{16,0},{128,16},{144,128},{1,145},{17,1},{129,17},{145,129... | collective-permute-start | bytes 294920 | tf_op jit(solution)/shard_map/sum_y/ppermute | solution.py:10
  52.2 2.0 %collective-permute-done.14 = bf16[48,1024]{1,0:T(8,128)(2,1)S(1)} collective-permute-done((bf16[48,1024]{1,0:T(8,128)(2,1)S(1)}, bf16[48,1024]{1,0:T(8,128)(2,1)S(1)}, u32[]{:S(2)}, u32[]{:S(2)}) %collective-permute-start.14) | collective-permute-done | bytes 98336 | tf_op jit(solution)/shard_map/sum_y/ppermute | solution.py:10
  54.2 0.4 collective-permute-done.15
  54.5 0.1 fusion.4
  54.7 0.5 fusion.5
  55.1 1.2 %constant_dynamic-update-slice_fusion.8 = (bf16[384,1024]{1,0:T(8,128)(2,1)S(1)}, bf16[48,1024]{1,0:T(8,128)(2,1)S(1)}, f32[48,1024]{1,0:T(8,128)}) fusion(bf16[48,1024]{1,0:T(8,128)(2,1)S(1)} %get-tuple-element.37, bf16[1024,1024]{1,0:T(8,128)(2,1)S(1)} %get-tuple-element.29, f32[96,1024]{1,0:T(8,128)S(1)} %fusion.5), kind=kOutput, calls=%fused_computation.50 | convolution fusion | flops 100810752 | bytes 2981888 | tf_op jit(solution)/shard_map/screen/dot_general | solution.py:111
  56.3 1.5 %collective-permute-start.16 = (bf16[48,1024]{1,0:T(8,128)(2,1)S(1)}, bf16[48,1024]{1,0:T(8,128)(2,1)S(1)}, u32[]{:S(2)}, u32[]{:S(2)}) collective-permute-start(bf16[48,1024]{1,0:T(8,128)(2,1)S(1)} %get-tuple-element.31), channel_id=1, source_target_pairs={{0,128},{16,144},{128,0},{144,16},{1,129},{17,145},{129,1},{145,17... | collective-permute-start | bytes 294920 | tf_op jit(solution)/shard_map/gather_y/ppermute | solution.py:10
  57.8 1.5 %collective-permute-start.17 = (bf16[48,1024]{1,0:T(8,128)(2,1)S(1)}, bf16[48,1024]{1,0:T(8,128)(2,1)S(1)}, u32[]{:S(2)}, u32[]{:S(2)}) collective-permute-start(bf16[48,1024]{1,0:T(8,128)(2,1)S(1)} %get-tuple-element.31), channel_id=1, source_target_pairs={{0,16},{16,128},{128,144},{144,0},{1,17},{17,129},{129,145},{145,1... | collective-permute-start | bytes 294920 | tf_op jit(solution)/shard_map/gather_y/ppermute | solution.py:10
  59.3 1.2 %collective-permute-start.18 = (bf16[48,1024]{1,0:T(8,128)(2,1)S(1)}, bf16[48,1024]{1,0:T(8,128)(2,1)S(1)}, u32[]{:S(2)}, u32[]{:S(2)}) collective-permute-start(bf16[48,1024]{1,0:T(8,128)(2,1)S(1)} %get-tuple-element.31), channel_id=1, source_target_pairs={{0,144},{16,0},{128,16},{144,128},{1,145},{17,1},{129,17},{145,129... | collective-permute-start | bytes 294920 | tf_op jit(solution)/shard_map/gather_y/ppermute | solution.py:10
  60.5 0.8 collective-permute-done.16
  61.3 2.1 %collective-permute-done.17 = bf16[48,1024]{1,0:T(8,128)(2,1)S(1)} collective-permute-done((bf16[48,1024]{1,0:T(8,128)(2,1)S(1)}, bf16[48,1024]{1,0:T(8,128)(2,1)S(1)}, u32[]{:S(2)}, u32[]{:S(2)}) %collective-permute-start.17) | collective-permute-done | bytes 98336 | tf_op jit(solution)/shard_map/gather_y/ppermute | solution.py:10
  63.4 3.2 %collective-permute-start.19 = (bf16[192,1024]{1,0:T(8,128)(2,1)S(1)}, bf16[192,1024]{1,0:T(8,128)(2,1)S(1)}, u32[]{:S(2)}, u32[]{:S(2)}) collective-permute-start(bf16[192,1024]{1,0:T(8,128)(2,1)S(1)} %pad_maximum_fusion.1), channel_id=1, source_target_pairs={{0,8},{8,0},{1,9},{9,1},{2,10},{10,2},{3,11},{11,3},{4,12},{12,4},... | collective-permute-start | bytes 1179656 | tf_op jit(solution)/shard_map/gather_y/ppermute | solution.py:18
  66.6 1.3 %collective-permute-done.19 = bf16[192,1024]{1,0:T(8,128)(2,1)S(1)} collective-permute-done((bf16[192,1024]{1,0:T(8,128)(2,1)S(1)}, bf16[192,1024]{1,0:T(8,128)(2,1)S(1)}, u32[]{:S(2)}, u32[]{:S(2)}) %collective-permute-start.19) | collective-permute-done | bytes 393248 | tf_op jit(solution)/shard_map/gather_y/ppermute | solution.py:18
  68.0 0.6 fusion.1
  68.6 0.1 select_add_fusion
  68.7 15.7 %all_to_all.9 = f32[32,1,128]{2,1,0:T(1,128)S(1)} all-to-all(f32[32,1,128]{2,1,0:T(1,128)S(1)} %bitcast.61), channel_id=1, replica_groups=mesh['grp'=2,'x'=4,'ylo'=2,'core'=2,'col'=8] {'x','col'}, dimensions={0} | all-to-all | bytes 32768 | tf_op jit(solution)/shard_map/sigma/all_to_all | solution.py:136
  84.4 0.6 reduce_sum.29
  (43 shorter events, 0.6 us)
Async XLA Ops:
  0.6 21.5 %copy-start = (bf16[128,1536]{1,0:T(8,128)(2,1)S(1)}, bf16[128,1536]{1,0:T(8,128)(2,1)}, u32[]{:S(2)}) copy-start(bf16[128,1536]{1,0:T(8,128)(2,1)} %param.3) | copy-start | bytes 1179652
  1.7 9.3 %collective-permute-start = (bf16[128,1024]{1,0:T(8,128)(2,1)S(1)}, bf16[128,1024]{1,0:T(8,128)(2,1)S(1)}, u32[]{:S(2)}, u32[]{:S(2)}) collective-permute-start(bf16[128,1024]{1,0:T(8,128)(2,1)S(1)} %slice.31), channel_id=1, source_target_pairs={{0,1},{8,9},{16,17},{24,25},{32,33},{40,41},{48,49},{56,57},{64,65... | collective-permute-start | bytes 786440 | tf_op jit(solution)/shard_map/panel_z/ppermute | solution.py:14
  11.0 10.4 %collective-permute-start.1 = (bf16[128,1024]{1,0:T(8,128)(2,1)S(1)}, bf16[128,1024]{1,0:T(8,128)(2,1)S(1)}, u32[]{:S(2)}, u32[]{:S(2)}) collective-permute-start(bf16[128,1024]{1,0:T(8,128)(2,1)S(1)} %slice.31), channel_id=1, source_target_pairs={{0,3},{8,11},{16,19},{24,27},{32,35},{40,43},{48,51},{56,59},{64,6... | collective-permute-start | bytes 786440 | tf_op jit(solution)/shard_map/panel_z/ppermute | solution.py:14
  12.3 9.8 %collective-permute-start.2 = (bf16[128,1024]{1,0:T(8,128)(2,1)S(1)}, bf16[128,1024]{1,0:T(8,128)(2,1)S(1)}, u32[]{:S(2)}, u32[]{:S(2)}) collective-permute-start(bf16[128,1024]{1,0:T(8,128)(2,1)S(1)} %slice.31), channel_id=1, source_target_pairs={{0,6},{8,14},{16,22},{24,30},{32,38},{40,46},{48,54},{56,62},{64,7... | collective-permute-start | bytes 786440 | tf_op jit(solution)/shard_map/panel_z/ppermute | solution.py:14
  15.2 7.7 %collective-permute-start.4 = (bf16[400,128]{1,0:T(8,128)(2,1)S(1)}, bf16[400,128]{1,0:T(8,128)(2,1)S(1)}, u32[]{:S(2)}, u32[]{:S(2)}) collective-permute-start(bf16[400,128]{1,0:T(8,128)(2,1)S(1)} %concatenate.37), channel_id=1, source_target_pairs={{0,64},{32,96},{64,0},{96,32},{1,65},{33,97},{65,1},{97,33},{2,66}... | collective-permute-start | bytes 307208 | tf_op jit(solution)/shard_map/blocks/ppermute | solution.py:10
  18.2 9.2 %collective-permute-start.5 = (bf16[400,128]{1,0:T(8,128)(2,1)S(1)}, bf16[400,128]{1,0:T(8,128)(2,1)S(1)}, u32[]{:S(2)}, u32[]{:S(2)}) collective-permute-start(bf16[400,128]{1,0:T(8,128)(2,1)S(1)} %concatenate.38), channel_id=1, source_target_pairs={{0,32},{32,64},{64,96},{96,0},{1,33},{33,65},{65,97},{97,1},{2,34}... | collective-permute-start | bytes 307208 | tf_op jit(solution)/shard_map/blocks/ppermute | solution.py:10
  18.7 8.6 %collective-permute-start.6 = (bf16[400,128]{1,0:T(8,128)(2,1)S(1)}, bf16[400,128]{1,0:T(8,128)(2,1)S(1)}, u32[]{:S(2)}, u32[]{:S(2)}) collective-permute-start(bf16[400,128]{1,0:T(8,128)(2,1)S(1)} %concatenate.39), channel_id=1, source_target_pairs={{0,96},{32,0},{64,32},{96,64},{1,97},{33,1},{65,33},{97,65},{2,98}... | collective-permute-start | bytes 307208 | tf_op jit(solution)/shard_map/blocks/ppermute | solution.py:10
  21.4 5.9 %collective-permute-start.7 = (bf16[128,1024]{1,0:T(8,128)(2,1)S(1)}, bf16[128,1024]{1,0:T(8,128)(2,1)S(1)}, u32[]{:S(2)}, u32[]{:S(2)}) collective-permute-start(bf16[128,1024]{1,0:T(8,128)(2,1)S(1)} %collective-permute-done), channel_id=1, source_target_pairs={{1,2},{9,10},{17,18},{25,26},{33,34},{41,42},{49,50},{57,58},{65,6... | collective-permute-start | bytes 786440 | tf_op jit(solution)/shard_map/panel_z/ppermute | solution.py:14
  22.2 5.2 %collective-permute-start.3 = (bf16[128,1024]{1,0:T(8,128)(2,1)S(1)}, bf16[128,1024]{1,0:T(8,128)(2,1)S(1)}, u32[]{:S(2)}, u32[]{:S(2)}) collective-permute-start(bf16[128,1024]{1,0:T(8,128)(2,1)S(1)} %select_select_fusion.1), channel_id=1, source_target_pairs={{3,4},{6,5},{11,12},{14,13},{19,20},{22,21},{27,28},{30,29},{35,36... | collective-permute-start | bytes 786440 | tf_op jit(solution)/shard_map/panel_z/ppermute | solution.py:14
  22.9 4.6 %collective-permute-start.8 = (bf16[128,1024]{1,0:T(8,128)(2,1)S(1)}, bf16[128,1024]{1,0:T(8,128)(2,1)S(1)}, u32[]{:S(2)}, u32[]{:S(2)}) collective-permute-start(bf16[128,1024]{1,0:T(8,128)(2,1)S(1)} %slice.31), channel_id=1, source_target_pairs={{0,7},{8,15},{16,23},{24,31},{32,39},{40,47},{48,55},{56,63},{64,7... | collective-permute-start | bytes 786440 | tf_op jit(solution)/shard_map/panel_z/ppermute | solution.py:14
  27.6 6.5 %collective-permute-start.10 = (bf16[128,1024]{1,0:T(8,128)(2,1)S(1)}, bf16[128,1024]{1,0:T(8,128)(2,1)S(1)}, u32[]{:S(2)}, u32[]{:S(2)}) collective-permute-start(bf16[128,1024]{1,0:T(8,128)(2,1)S(1)} %select_select_fusion), channel_id=1, source_target_pairs={{0,32},{32,64},{64,96},{96,0},{1,33},{33,65},{65,97},{97,1},{2,34}... | collective-permute-start | bytes 786440 | tf_op jit(solution)/shard_map/panel_x/ppermute | solution.py:10
  27.7 8.9 %collective-permute-start.11 = (bf16[128,1024]{1,0:T(8,128)(2,1)S(1)}, bf16[128,1024]{1,0:T(8,128)(2,1)S(1)}, u32[]{:S(2)}, u32[]{:S(2)}) collective-permute-start(bf16[128,1024]{1,0:T(8,128)(2,1)S(1)} %select_select_fusion), channel_id=1, source_target_pairs={{0,96},{32,0},{64,32},{96,64},{1,97},{33,1},{65,33},{97,65},{2,98}... | collective-permute-start | bytes 786440 | tf_op jit(solution)/shard_map/panel_x/ppermute | solution.py:10
  30.3 9.3 %collective-permute-start.9 = (bf16[128,1024]{1,0:T(8,128)(2,1)S(1)}, bf16[128,1024]{1,0:T(8,128)(2,1)S(1)}, u32[]{:S(2)}, u32[]{:S(2)}) collective-permute-start(bf16[128,1024]{1,0:T(8,128)(2,1)S(1)} %select_select_fusion), channel_id=1, source_target_pairs={{0,64},{32,96},{64,0},{96,32},{1,65},{33,97},{65,1},{97,33},{2,66}... | collective-permute-start | bytes 786440 | tf_op jit(solution)/shard_map/panel_x/ppermute | solution.py:10
  40.4 6.0 %collective-permute-start.12 = (f32[4,48,1024]{2,1,0:T(8,128)S(1)}, f32[4,48,1024]{2,1,0:T(8,128)S(1)}, u32[]{:S(2)}, u32[]{:S(2)}) collective-permute-start(f32[4,48,1024]{2,1,0:T(8,128)S(1)} %dynamic-slice_bitcast_fusion), channel_id=1, source_target_pairs={{0,8},{8,0},{1,9},{9,1},{2,10},{10,2},{3,11},{11,3},{4,12},{12,4},... | collective-permute-start | bytes 2359304 | tf_op jit(solution)/shard_map/sum_core/ppermute | solution.py:18
  46.5 5.7 %collective-permute-start.13 = (bf16[48,1024]{1,0:T(8,128)(2,1)S(1)}, bf16[48,1024]{1,0:T(8,128)(2,1)S(1)}, u32[]{:S(2)}, u32[]{:S(2)}) collective-permute-start(bf16[48,1024]{1,0:T(8,128)(2,1)S(1)} %get-tuple-element.38), channel_id=1, source_target_pairs={{0,128},{16,144},{128,0},{144,16},{1,129},{17,145},{129,1},{145,17... | collective-permute-start | bytes 294920 | tf_op jit(solution)/shard_map/sum_y/ppermute | solution.py:10
  49.5 4.7 %collective-permute-start.14 = (bf16[48,1024]{1,0:T(8,128)(2,1)S(1)}, bf16[48,1024]{1,0:T(8,128)(2,1)S(1)}, u32[]{:S(2)}, u32[]{:S(2)}) collective-permute-start(bf16[48,1024]{1,0:T(8,128)(2,1)S(1)} %get-tuple-element.40), channel_id=1, source_target_pairs={{0,16},{16,128},{128,144},{144,0},{1,17},{17,129},{129,145},{145,1... | collective-permute-start | bytes 294920 | tf_op jit(solution)/shard_map/sum_y/ppermute | solution.py:10
  49.9 4.6 %collective-permute-start.15 = (bf16[48,1024]{1,0:T(8,128)(2,1)S(1)}, bf16[48,1024]{1,0:T(8,128)(2,1)S(1)}, u32[]{:S(2)}, u32[]{:S(2)}) collective-permute-start(bf16[48,1024]{1,0:T(8,128)(2,1)S(1)} %get-tuple-element.39), channel_id=1, source_target_pairs={{0,144},{16,0},{128,16},{144,128},{1,145},{17,1},{129,17},{145,129... | collective-permute-start | bytes 294920 | tf_op jit(solution)/shard_map/sum_y/ppermute | solution.py:10
  56.3 5.0 %collective-permute-start.16 = (bf16[48,1024]{1,0:T(8,128)(2,1)S(1)}, bf16[48,1024]{1,0:T(8,128)(2,1)S(1)}, u32[]{:S(2)}, u32[]{:S(2)}) collective-permute-start(bf16[48,1024]{1,0:T(8,128)(2,1)S(1)} %get-tuple-element.31), channel_id=1, source_target_pairs={{0,128},{16,144},{128,0},{144,16},{1,129},{17,145},{129,1},{145,17... | collective-permute-start | bytes 294920 | tf_op jit(solution)/shard_map/gather_y/ppermute | solution.py:10
  57.8 5.6 %collective-permute-start.17 = (bf16[48,1024]{1,0:T(8,128)(2,1)S(1)}, bf16[48,1024]{1,0:T(8,128)(2,1)S(1)}, u32[]{:S(2)}, u32[]{:S(2)}) collective-permute-start(bf16[48,1024]{1,0:T(8,128)(2,1)S(1)} %get-tuple-element.31), channel_id=1, source_target_pairs={{0,16},{16,128},{128,144},{144,0},{1,17},{17,129},{129,145},{145,1... | collective-permute-start | bytes 294920 | tf_op jit(solution)/shard_map/gather_y/ppermute | solution.py:10
  59.3 4.1 %collective-permute-start.18 = (bf16[48,1024]{1,0:T(8,128)(2,1)S(1)}, bf16[48,1024]{1,0:T(8,128)(2,1)S(1)}, u32[]{:S(2)}, u32[]{:S(2)}) collective-permute-start(bf16[48,1024]{1,0:T(8,128)(2,1)S(1)} %get-tuple-element.31), channel_id=1, source_target_pairs={{0,144},{16,0},{128,16},{144,128},{1,145},{17,1},{129,17},{145,129... | collective-permute-start | bytes 294920 | tf_op jit(solution)/shard_map/gather_y/ppermute | solution.py:10
  63.4 4.5 %collective-permute-start.19 = (bf16[192,1024]{1,0:T(8,128)(2,1)S(1)}, bf16[192,1024]{1,0:T(8,128)(2,1)S(1)}, u32[]{:S(2)}, u32[]{:S(2)}) collective-permute-start(bf16[192,1024]{1,0:T(8,128)(2,1)S(1)} %pad_maximum_fusion.1), channel_id=1, source_target_pairs={{0,8},{8,0},{1,9},{9,1},{2,10},{10,2},{3,11},{11,3},{4,12},{12,4},... | collective-permute-start | bytes 1179656 | tf_op jit(solution)/shard_map/gather_y/ppermute | solution.py:18

commit v11 on v5

--- a/solution.py
+++ b/solution.py
@@ -64,14 +64,14 @@
             (far_a, far_b, block_inverse, *rows)
         )
         held = jnp.where(z == 3, far_a, jnp.where(z == 6, far_b, piece))
-        near_a = along_z(held, (0, 1), (3, 4), (6, 5))
-        near_b = along_z(held, (0, 7), (3, 2))
+        near_a = along_z(held, (0, 7), (3, 4), (6, 5))
+        near_b = along_z(held, (0, 1), (3, 2))
         inv_high, inv_rest = two_parts(block_inverse)
         near_a, near_b, inv_high, inv_rest, *factors = lax.optimization_barrier(
             (near_a, near_b, inv_high, inv_rest, *factors)
         )
-        held = jnp.where((z == 1) | (z == 4) | (z == 5), near_a, held)
-        held = jnp.where((z == 7) | (z == 2), near_b, held)
+        held = jnp.where((z == 7) | (z == 4) | (z == 5), near_a, held)
+        held = jnp.where((z == 1) | (z == 2), near_b, held)
 
     with jax.named_scope("panel_x"):
         panels = [held] + [shift(held, X, nx, k) for k in steps[1:]]
@@ -86,8 +86,8 @@
 
     with jax.named_scope("sum_core"):
         part = part.reshape(ny, 2, count, panel)
-        sent = lax.dynamic_index_in_dim(part, 1 - core, 1, False)
-        kept = lax.dynamic_index_in_dim(part, core, 1, False) + swap(sent)
+        sent = lax.dynamic_index_in_dim(part, 1 - core, 1, False).astype(LOW)
+        kept = lax.dynamic_index_in_dim(part, core, 1, False) + swap(sent).astype(F32)
 
     with jax.named_scope("sum_y"):
         total = lax.dynamic_index_in_dim(kept, y, 0, False)

time: 82.2 us -> 81.6 us (level)
  no operation moved by 1% of the time
where the time goes in v11:
time: 81.6 us; the launch traced here: 81.3 us
  starting transfers between devices  34.4 us (42%)
  waiting for transfers between devices  20.7 us (25%)
  blocking collectives  14.1 us (17%)
  other arithmetic  4.78 us (6%)
  local copies, waits for them, and re-layouts  3.3 us (4%)
  matrix products  2.97 us (4%)
  between operations  1.11 us (1%)
    ppermute x12, starting transfers between devices, shift(): lax.ppermute(value, axis, [(i, (i + step) % size) for i in range(size)])  18.3 us
    ppermute x12, waiting for transfers between devices, shift(): lax.ppermute(value, axis, [(i, (i + step) % size) for i in range(size)])  17.2 us
    all_to_all x1, blocking collectives, body(): terms = lax.all_to_all(copies, (X, Z), 0, 0, tiled=True)  14.1 us
    ppermute x4, starting transfers between devices, along_z(): return lax.ppermute(value, Z, pairs)  12.1 us
    ppermute x2, starting transfers between devices, swap(): return lax.ppermute(value, CORE, [(0, 1), (1, 0)])  3.95 us
    convert_element_type x2, other arithmetic, two_parts(): return (high.astype(LOW), (value - high).astype(LOW))  3.22 us
    ppermute x2, waiting for transfers between devices, swap(): return lax.ppermute(value, CORE, [(0, 1), (1, 0)])  2.59 us
  transfers between devices with their start and end apart: 18, of which 9 were waited for; matrix products, arithmetic and copies ran while one was open for 7% of the time, Pallas kernels for 0%

profile of v11, /device:TPU:1, one launch (start us, length us, event | category | flops | bytes accessed | tf_op | source)
XLA Modules:
  0.0 81.3 jit_solution(8561380435672665160)
XLA Ops:
  0.6 0.0 copy-start
  0.6 1.0 %slice.31 = bf16[128,1024]{1,0:T(8,128)(2,1)S(1)} slice(bf16[128,1536]{1,0:T(8,128)(2,1)} %param.3), slice={[0:128], [0:1024]} | slice | bytes 524288 | tf_op jit(solution)/shard_map/panel_z/slice | solution.py:44
  1.7 7.1 %collective-permute-start = (bf16[128,1024]{1,0:T(8,128)(2,1)S(1)}, bf16[128,1024]{1,0:T(8,128)(2,1)S(1)}, u32[]{:S(2)}, u32[]{:S(2)}) collective-permute-start(bf16[128,1024]{1,0:T(8,128)(2,1)S(1)} %slice.31), channel_id=1, source_target_pairs={{0,3},{8,11},{16,19},{24,27},{32,35},{40,43},{48,51},{56,59},{64,6... | collective-permute-start | bytes 786440 | tf_op jit(solution)/shard_map/panel_z/ppermute | solution.py:14
  8.8 2.4 %collective-permute-start.1 = (bf16[128,1024]{1,0:T(8,128)(2,1)S(1)}, bf16[128,1024]{1,0:T(8,128)(2,1)S(1)}, u32[]{:S(2)}, u32[]{:S(2)}) collective-permute-start(bf16[128,1024]{1,0:T(8,128)(2,1)S(1)} %slice.31), channel_id=1, source_target_pairs={{0,6},{8,14},{16,22},{24,30},{32,38},{40,46},{48,54},{56,62},{64,7... | collective-permute-start | bytes 786440 | tf_op jit(solution)/shard_map/panel_z/ppermute | solution.py:14
  11.2 1.2 %copy.18 = bf16[128,1536]{0,1:T(8,128)(2,1)S(1)} copy(bf16[128,1536]{1,0:T(8,128)(2,1)} %param.3) | data formatting | bytes 786432 | tf_op args[0]
  12.4 0.7 fusion.20
  13.2 0.2 concatenate.37
  13.3 2.8 %collective-permute-start.4 = (bf16[400,128]{1,0:T(8,128)(2,1)S(1)}, bf16[400,128]{1,0:T(8,128)(2,1)S(1)}, u32[]{:S(2)}, u32[]{:S(2)}) collective-permute-start(bf16[400,128]{1,0:T(8,128)(2,1)S(1)} %concatenate.37), channel_id=1, source_target_pairs={{0,64},{32,96},{64,0},{96,32},{1,65},{33,97},{65,1},{97,33},{2,66}... | collective-permute-start | bytes 307208 | tf_op jit(solution)/shard_map/blocks/ppermute | solution.py:10
  16.2 0.2 concatenate.38
  16.3 0.4 collective-permute-start.5
  16.7 0.2 concatenate.39
  16.9 2.4 %collective-permute-start.6 = (bf16[400,128]{1,0:T(8,128)(2,1)S(1)}, bf16[400,128]{1,0:T(8,128)(2,1)S(1)}, u32[]{:S(2)}, u32[]{:S(2)}) collective-permute-start(bf16[400,128]{1,0:T(8,128)(2,1)S(1)} %concatenate.39), channel_id=1, source_target_pairs={{0,96},{32,0},{64,32},{96,64},{1,97},{33,1},{65,33},{97,65},{2,98}... | collective-permute-start | bytes 307208 | tf_op jit(solution)/shard_map/blocks/ppermute | solution.py:10
  19.3 0.2 concatenate.36
  19.6 0.0 collective-permute-done
  19.7 1.3 %collective-permute-start.2 = (bf16[128,1024]{1,0:T(8,128)(2,1)S(1)}, bf16[128,1024]{1,0:T(8,128)(2,1)S(1)}, u32[]{:S(2)}, u32[]{:S(2)}) collective-permute-start(bf16[128,1024]{1,0:T(8,128)(2,1)S(1)} %select_select_fusion.1), channel_id=1, source_target_pairs={{0,7},{3,4},{6,5},{8,15},{11,12},{14,13},{16,23},{19,20},{22,21},{... | collective-permute-start | bytes 786440 | tf_op jit(solution)/shard_map/panel_z/ppermute | solution.py:14
  21.0 1.3 %collective-permute-start.3 = (bf16[128,1024]{1,0:T(8,128)(2,1)S(1)}, bf16[128,1024]{1,0:T(8,128)(2,1)S(1)}, u32[]{:S(2)}, u32[]{:S(2)}) collective-permute-start(bf16[128,1024]{1,0:T(8,128)(2,1)S(1)} %select_select_fusion.1), channel_id=1, source_target_pairs={{0,1},{3,2},{8,9},{11,10},{16,17},{19,18},{24,25},{27,26},{32,33},... | collective-permute-start | bytes 786440 | tf_op jit(solution)/shard_map/panel_z/ppermute | solution.py:14
  22.3 3.1 %fusion = (bf16[1024,1024]{1,0:T(8,128)(2,1)S(1)}, bf16[1024,1024]{1,0:T(8,128)(2,1)S(1)}) fusion(f32[1024,1024]{1,0:T(8,128)} %param.5), kind=kLoop, calls=%fused_computation.2 | loop fusion | flops 4194304 | bytes 8388608 | tf_op jit(solution)/shard_map/panel_z/convert_element_type | solution.py:32
  25.4 0.0 collective-permute-done.4
  25.5 0.9 %collective-permute-done.3 = bf16[128,1024]{1,0:T(8,128)(2,1)S(1)} collective-permute-done((bf16[128,1024]{1,0:T(8,128)(2,1)S(1)}, bf16[128,1024]{1,0:T(8,128)(2,1)S(1)}, u32[]{:S(2)}, u32[]{:S(2)}) %collective-permute-start.3) | collective-permute-done | bytes 262176 | tf_op jit(solution)/shard_map/panel_z/ppermute | solution.py:14
  26.4 0.1 collective-permute-start.7
  26.5 1.0 %collective-permute-start.8 = (bf16[128,1024]{1,0:T(8,128)(2,1)S(1)}, bf16[128,1024]{1,0:T(8,128)(2,1)S(1)}, u32[]{:S(2)}, u32[]{:S(2)}) collective-permute-start(bf16[128,1024]{1,0:T(8,128)(2,1)S(1)} %select_select_fusion), channel_id=1, source_target_pairs={{0,32},{32,64},{64,96},{96,0},{1,33},{33,65},{65,97},{97,1},{2,34}... | collective-permute-start | bytes 786440 | tf_op jit(solution)/shard_map/panel_x/ppermute | solution.py:10
  27.5 1.7 %collective-permute-start.9 = (bf16[128,1024]{1,0:T(8,128)(2,1)S(1)}, bf16[128,1024]{1,0:T(8,128)(2,1)S(1)}, u32[]{:S(2)}, u32[]{:S(2)}) collective-permute-start(bf16[128,1024]{1,0:T(8,128)(2,1)S(1)} %select_select_fusion), channel_id=1, source_target_pairs={{0,96},{32,0},{64,32},{96,64},{1,97},{33,1},{65,33},{97,65},{2,98}... | collective-permute-start | bytes 786440 | tf_op jit(solution)/shard_map/panel_x/ppermute | solution.py:10
  29.5 3.9 %collective-permute-done.7 = bf16[128,1024]{1,0:T(8,128)(2,1)S(1)} collective-permute-done((bf16[128,1024]{1,0:T(8,128)(2,1)S(1)}, bf16[128,1024]{1,0:T(8,128)(2,1)S(1)}, u32[]{:S(2)}, u32[]{:S(2)}) %collective-permute-start.7) | collective-permute-done | bytes 262176 | tf_op jit(solution)/shard_map/panel_x/ppermute | solution.py:10
  33.3 8.1 %collective-permute-done.8 = bf16[128,1024]{1,0:T(8,128)(2,1)S(1)} collective-permute-done((bf16[128,1024]{1,0:T(8,128)(2,1)S(1)}, bf16[128,1024]{1,0:T(8,128)(2,1)S(1)}, u32[]{:S(2)}, u32[]{:S(2)}) %collective-permute-start.8) | collective-permute-done | bytes 262176 | tf_op jit(solution)/shard_map/panel_x/ppermute | solution.py:10
  41.4 0.7 fusion.2
  42.1 0.1 fusion.4
  42.2 0.8 collective-permute-start.10
  43.0 1.3 %collective-permute-done.10 = bf16[4,48,1024]{2,1,0:T(8,128)(2,1)S(1)} collective-permute-done((bf16[4,48,1024]{2,1,0:T(8,128)(2,1)S(1)}, bf16[4,48,1024]{2,1,0:T(8,128)(2,1)S(1)}, u32[]{:S(2)}, u32[]{:S(2)}) %collective-permute-start.10) | collective-permute-done | bytes 393248 | tf_op jit(solution)/shard_map/sum_core/ppermute | solution.py:18
  44.3 0.1 bitcast_add_fusion
  44.5 3.0 %collective-permute-start.11 = (bf16[48,1024]{1,0:T(8,128)(2,1)S(1)}, bf16[48,1024]{1,0:T(8,128)(2,1)S(1)}, u32[]{:S(2)}, u32[]{:S(2)}) collective-permute-start(bf16[48,1024]{1,0:T(8,128)(2,1)S(1)} %get-tuple-element.32), channel_id=1, source_target_pairs={{0,128},{16,144},{128,0},{144,16},{1,129},{17,145},{129,1},{145,17... | collective-permute-start | bytes 294920 | tf_op jit(solution)/shard_map/sum_y/ppermute | solution.py:10
  47.5 0.4 collective-permute-start.12
  47.9 2.3 %collective-permute-start.13 = (bf16[48,1024]{1,0:T(8,128)(2,1)S(1)}, bf16[48,1024]{1,0:T(8,128)(2,1)S(1)}, u32[]{:S(2)}, u32[]{:S(2)}) collective-permute-start(bf16[48,1024]{1,0:T(8,128)(2,1)S(1)} %get-tuple-element.33), channel_id=1, source_target_pairs={{0,144},{16,0},{128,16},{144,128},{1,145},{17,1},{129,17},{145,129... | collective-permute-start | bytes 294920 | tf_op jit(solution)/shard_map/sum_y/ppermute | solution.py:10
  50.2 2.0 %collective-permute-done.12 = bf16[48,1024]{1,0:T(8,128)(2,1)S(1)} collective-permute-done((bf16[48,1024]{1,0:T(8,128)(2,1)S(1)}, bf16[48,1024]{1,0:T(8,128)(2,1)S(1)}, u32[]{:S(2)}, u32[]{:S(2)}) %collective-permute-start.12) | collective-permute-done | bytes 98336 | tf_op jit(solution)/shard_map/sum_y/ppermute | solution.py:10
  52.2 0.4 collective-permute-done.13
  52.5 0.1 fusion.5
  52.6 0.5 fusion.6
  53.1 1.2 %constant_dynamic-update-slice_fusion.8 = (bf16[384,1024]{1,0:T(8,128)(2,1)S(1)}, bf16[48,1024]{1,0:T(8,128)(2,1)S(1)}, f32[48,1024]{1,0:T(8,128)}) fusion(bf16[48,1024]{1,0:T(8,128)(2,1)S(1)} %get-tuple-element.31, bf16[1024,1024]{1,0:T(8,128)(2,1)S(1)} %get-tuple-element.23, f32[96,1024]{1,0:T(8,128)S(1)} %fusion.6), kind=kOutput, calls=%fused_computation.51 | convolution fusion | flops 100810752 | bytes 2981888 | tf_op jit(solution)/shard_map/screen/dot_general | solution.py:107
  54.3 1.5 %collective-permute-start.14 = (bf16[48,1024]{1,0:T(8,128)(2,1)S(1)}, bf16[48,1024]{1,0:T(8,128)(2,1)S(1)}, u32[]{:S(2)}, u32[]{:S(2)}) collective-permute-start(bf16[48,1024]{1,0:T(8,128)(2,1)S(1)} %get-tuple-element.25), channel_id=1, source_target_pairs={{0,128},{16,144},{128,0},{144,16},{1,129},{17,145},{129,1},{145,17... | collective-permute-start | bytes 294920 | tf_op jit(solution)/shard_map/gather_y/ppermute | solution.py:10
  55.8 1.5 %collective-permute-start.15 = (bf16[48,1024]{1,0:T(8,128)(2,1)S(1)}, bf16[48,1024]{1,0:T(8,128)(2,1)S(1)}, u32[]{:S(2)}, u32[]{:S(2)}) collective-permute-start(bf16[48,1024]{1,0:T(8,128)(2,1)S(1)} %get-tuple-element.25), channel_id=1, source_target_pairs={{0,16},{16,128},{128,144},{144,0},{1,17},{17,129},{129,145},{145,1... | collective-permute-start | bytes 294920 | tf_op jit(solution)/shard_map/gather_y/ppermute | solution.py:10
  57.3 1.2 %collective-permute-start.16 = (bf16[48,1024]{1,0:T(8,128)(2,1)S(1)}, bf16[48,1024]{1,0:T(8,128)(2,1)S(1)}, u32[]{:S(2)}, u32[]{:S(2)}) collective-permute-start(bf16[48,1024]{1,0:T(8,128)(2,1)S(1)} %get-tuple-element.25), channel_id=1, source_target_pairs={{0,144},{16,0},{128,16},{144,128},{1,145},{17,1},{129,17},{145,129... | collective-permute-start | bytes 294920 | tf_op jit(solution)/shard_map/gather_y/ppermute | solution.py:10
  58.5 0.8 collective-permute-done.14
  59.3 2.1 %collective-permute-done.15 = bf16[48,1024]{1,0:T(8,128)(2,1)S(1)} collective-permute-done((bf16[48,1024]{1,0:T(8,128)(2,1)S(1)}, bf16[48,1024]{1,0:T(8,128)(2,1)S(1)}, u32[]{:S(2)}, u32[]{:S(2)}) %collective-permute-start.15) | collective-permute-done | bytes 98336 | tf_op jit(solution)/shard_map/gather_y/ppermute | solution.py:10
  61.4 3.2 %collective-permute-start.17 = (bf16[192,1024]{1,0:T(8,128)(2,1)S(1)}, bf16[192,1024]{1,0:T(8,128)(2,1)S(1)}, u32[]{:S(2)}, u32[]{:S(2)}) collective-permute-start(bf16[192,1024]{1,0:T(8,128)(2,1)S(1)} %pad_maximum_fusion.1), channel_id=1, source_target_pairs={{0,8},{8,0},{1,9},{9,1},{2,10},{10,2},{3,11},{11,3},{4,12},{12,4},... | collective-permute-start | bytes 1179656 | tf_op jit(solution)/shard_map/gather_y/ppermute | solution.py:18
  64.6 1.3 %collective-permute-done.17 = bf16[192,1024]{1,0:T(8,128)(2,1)S(1)} collective-permute-done((bf16[192,1024]{1,0:T(8,128)(2,1)S(1)}, bf16[192,1024]{1,0:T(8,128)(2,1)S(1)}, u32[]{:S(2)}, u32[]{:S(2)}) %collective-permute-start.17) | collective-permute-done | bytes 393248 | tf_op jit(solution)/shard_map/gather_y/ppermute | solution.py:18
  65.9 0.6 fusion.1
  66.6 0.1 select_add_fusion
  66.7 14.1 %all_to_all.9 = f32[32,1,128]{2,1,0:T(1,128)S(1)} all-to-all(f32[32,1,128]{2,1,0:T(1,128)S(1)} %bitcast.61), channel_id=1, replica_groups=mesh['grp'=2,'x'=4,'ylo'=2,'core'=2,'col'=8] {'x','col'}, dimensions={0} | all-to-all | bytes 32768 | tf_op jit(solution)/shard_map/sigma/all_to_all | solution.py:132
  80.8 0.6 reduce_sum.29
  (39 shorter events, 0.5 us)
Async XLA Ops:
  0.6 19.0 %copy-start = (bf16[128,1536]{1,0:T(8,128)(2,1)S(1)}, bf16[128,1536]{1,0:T(8,128)(2,1)}, u32[]{:S(2)}) copy-start(bf16[128,1536]{1,0:T(8,128)(2,1)} %param.3) | copy-start | bytes 1179652
  1.7 17.9 %collective-permute-start = (bf16[128,1024]{1,0:T(8,128)(2,1)S(1)}, bf16[128,1024]{1,0:T(8,128)(2,1)S(1)}, u32[]{:S(2)}, u32[]{:S(2)}) collective-permute-start(bf16[128,1024]{1,0:T(8,128)(2,1)S(1)} %slice.31), channel_id=1, source_target_pairs={{0,3},{8,11},{16,19},{24,27},{32,35},{40,43},{48,51},{56,59},{64,6... | collective-permute-start | bytes 786440 | tf_op jit(solution)/shard_map/panel_z/ppermute | solution.py:14
  8.8 10.8 %collective-permute-start.1 = (bf16[128,1024]{1,0:T(8,128)(2,1)S(1)}, bf16[128,1024]{1,0:T(8,128)(2,1)S(1)}, u32[]{:S(2)}, u32[]{:S(2)}) collective-permute-start(bf16[128,1024]{1,0:T(8,128)(2,1)S(1)} %slice.31), channel_id=1, source_target_pairs={{0,6},{8,14},{16,22},{24,30},{32,38},{40,46},{48,54},{56,62},{64,7... | collective-permute-start | bytes 786440 | tf_op jit(solution)/shard_map/panel_z/ppermute | solution.py:14
  13.3 12.1 %collective-permute-start.4 = (bf16[400,128]{1,0:T(8,128)(2,1)S(1)}, bf16[400,128]{1,0:T(8,128)(2,1)S(1)}, u32[]{:S(2)}, u32[]{:S(2)}) collective-permute-start(bf16[400,128]{1,0:T(8,128)(2,1)S(1)} %concatenate.37), channel_id=1, source_target_pairs={{0,64},{32,96},{64,0},{96,32},{1,65},{33,97},{65,1},{97,33},{2,66}... | collective-permute-start | bytes 307208 | tf_op jit(solution)/shard_map/blocks/ppermute | solution.py:10
  16.3 9.1 %collective-permute-start.5 = (bf16[400,128]{1,0:T(8,128)(2,1)S(1)}, bf16[400,128]{1,0:T(8,128)(2,1)S(1)}, u32[]{:S(2)}, u32[]{:S(2)}) collective-permute-start(bf16[400,128]{1,0:T(8,128)(2,1)S(1)} %concatenate.38), channel_id=1, source_target_pairs={{0,32},{32,64},{64,96},{96,0},{1,33},{33,65},{65,97},{97,1},{2,34}... | collective-permute-start | bytes 307208 | tf_op jit(solution)/shard_map/blocks/ppermute | solution.py:10
  16.9 8.6 %collective-permute-start.6 = (bf16[400,128]{1,0:T(8,128)(2,1)S(1)}, bf16[400,128]{1,0:T(8,128)(2,1)S(1)}, u32[]{:S(2)}, u32[]{:S(2)}) collective-permute-start(bf16[400,128]{1,0:T(8,128)(2,1)S(1)} %concatenate.39), channel_id=1, source_target_pairs={{0,96},{32,0},{64,32},{96,64},{1,97},{33,1},{65,33},{97,65},{2,98}... | collective-permute-start | bytes 307208 | tf_op jit(solution)/shard_map/blocks/ppermute | solution.py:10
  19.7 5.8 %collective-permute-start.2 = (bf16[128,1024]{1,0:T(8,128)(2,1)S(1)}, bf16[128,1024]{1,0:T(8,128)(2,1)S(1)}, u32[]{:S(2)}, u32[]{:S(2)}) collective-permute-start(bf16[128,1024]{1,0:T(8,128)(2,1)S(1)} %select_select_fusion.1), channel_id=1, source_target_pairs={{0,7},{3,4},{6,5},{8,15},{11,12},{14,13},{16,23},{19,20},{22,21},{... | collective-permute-start | bytes 786440 | tf_op jit(solution)/shard_map/panel_z/ppermute | solution.py:14
  21.0 5.4 %collective-permute-start.3 = (bf16[128,1024]{1,0:T(8,128)(2,1)S(1)}, bf16[128,1024]{1,0:T(8,128)(2,1)S(1)}, u32[]{:S(2)}, u32[]{:S(2)}) collective-permute-start(bf16[128,1024]{1,0:T(8,128)(2,1)S(1)} %select_select_fusion.1), channel_id=1, source_target_pairs={{0,1},{3,2},{8,9},{11,10},{16,17},{19,18},{24,25},{27,26},{32,33},... | collective-permute-start | bytes 786440 | tf_op jit(solution)/shard_map/panel_z/ppermute | solution.py:14
  26.4 6.9 %collective-permute-start.7 = (bf16[128,1024]{1,0:T(8,128)(2,1)S(1)}, bf16[128,1024]{1,0:T(8,128)(2,1)S(1)}, u32[]{:S(2)}, u32[]{:S(2)}) collective-permute-start(bf16[128,1024]{1,0:T(8,128)(2,1)S(1)} %select_select_fusion), channel_id=1, source_target_pairs={{0,64},{32,96},{64,0},{96,32},{1,65},{33,97},{65,1},{97,33},{2,66}... | collective-permute-start | bytes 786440 | tf_op jit(solution)/shard_map/panel_x/ppermute | solution.py:10
  26.5 14.9 %collective-permute-start.8 = (bf16[128,1024]{1,0:T(8,128)(2,1)S(1)}, bf16[128,1024]{1,0:T(8,128)(2,1)S(1)}, u32[]{:S(2)}, u32[]{:S(2)}) collective-permute-start(bf16[128,1024]{1,0:T(8,128)(2,1)S(1)} %select_select_fusion), channel_id=1, source_target_pairs={{0,32},{32,64},{64,96},{96,0},{1,33},{33,65},{65,97},{97,1},{2,34}... | collective-permute-start | bytes 786440 | tf_op jit(solution)/shard_map/panel_x/ppermute | solution.py:10
  27.5 13.9 %collective-permute-start.9 = (bf16[128,1024]{1,0:T(8,128)(2,1)S(1)}, bf16[128,1024]{1,0:T(8,128)(2,1)S(1)}, u32[]{:S(2)}, u32[]{:S(2)}) collective-permute-start(bf16[128,1024]{1,0:T(8,128)(2,1)S(1)} %select_select_fusion), channel_id=1, source_target_pairs={{0,96},{32,0},{64,32},{96,64},{1,97},{33,1},{65,33},{97,65},{2,98}... | collective-permute-start | bytes 786440 | tf_op jit(solution)/shard_map/panel_x/ppermute | solution.py:10
  42.2 2.1 %collective-permute-start.10 = (bf16[4,48,1024]{2,1,0:T(8,128)(2,1)S(1)}, bf16[4,48,1024]{2,1,0:T(8,128)(2,1)S(1)}, u32[]{:S(2)}, u32[]{:S(2)}) collective-permute-start(bf16[4,48,1024]{2,1,0:T(8,128)(2,1)S(1)} %fusion.4), channel_id=1, source_target_pairs={{0,8},{8,0},{1,9},{9,1},{2,10},{10,2},{3,11},{11,3},{4,12},{12,4},... | collective-permute-start | bytes 1179656 | tf_op jit(solution)/shard_map/sum_core/ppermute | solution.py:18
  44.5 5.7 %collective-permute-start.11 = (bf16[48,1024]{1,0:T(8,128)(2,1)S(1)}, bf16[48,1024]{1,0:T(8,128)(2,1)S(1)}, u32[]{:S(2)}, u32[]{:S(2)}) collective-permute-start(bf16[48,1024]{1,0:T(8,128)(2,1)S(1)} %get-tuple-element.32), channel_id=1, source_target_pairs={{0,128},{16,144},{128,0},{144,16},{1,129},{17,145},{129,1},{145,17... | collective-permute-start | bytes 294920 | tf_op jit(solution)/shard_map/sum_y/ppermute | solution.py:10
  47.5 4.7 %collective-permute-start.12 = (bf16[48,1024]{1,0:T(8,128)(2,1)S(1)}, bf16[48,1024]{1,0:T(8,128)(2,1)S(1)}, u32[]{:S(2)}, u32[]{:S(2)}) collective-permute-start(bf16[48,1024]{1,0:T(8,128)(2,1)S(1)} %get-tuple-element.34), channel_id=1, source_target_pairs={{0,16},{16,128},{128,144},{144,0},{1,17},{17,129},{129,145},{145,1... | collective-permute-start | bytes 294920 | tf_op jit(solution)/shard_map/sum_y/ppermute | solution.py:10
  47.9 4.6 %collective-permute-start.13 = (bf16[48,1024]{1,0:T(8,128)(2,1)S(1)}, bf16[48,1024]{1,0:T(8,128)(2,1)S(1)}, u32[]{:S(2)}, u32[]{:S(2)}) collective-permute-start(bf16[48,1024]{1,0:T(8,128)(2,1)S(1)} %get-tuple-element.33), channel_id=1, source_target_pairs={{0,144},{16,0},{128,16},{144,128},{1,145},{17,1},{129,17},{145,129... | collective-permute-start | bytes 294920 | tf_op jit(solution)/shard_map/sum_y/ppermute | solution.py:10
  54.3 5.0 %collective-permute-start.14 = (bf16[48,1024]{1,0:T(8,128)(2,1)S(1)}, bf16[48,1024]{1,0:T(8,128)(2,1)S(1)}, u32[]{:S(2)}, u32[]{:S(2)}) collective-permute-start(bf16[48,1024]{1,0:T(8,128)(2,1)S(1)} %get-tuple-element.25), channel_id=1, source_target_pairs={{0,128},{16,144},{128,0},{144,16},{1,129},{17,145},{129,1},{145,17... | collective-permute-start | bytes 294920 | tf_op jit(solution)/shard_map/gather_y/ppermute | solution.py:10
  55.8 5.6 %collective-permute-start.15 = (bf16[48,1024]{1,0:T(8,128)(2,1)S(1)}, bf16[48,1024]{1,0:T(8,128)(2,1)S(1)}, u32[]{:S(2)}, u32[]{:S(2)}) collective-permute-start(bf16[48,1024]{1,0:T(8,128)(2,1)S(1)} %get-tuple-element.25), channel_id=1, source_target_pairs={{0,16},{16,128},{128,144},{144,0},{1,17},{17,129},{129,145},{145,1... | collective-permute-start | bytes 294920 | tf_op jit(solution)/shard_map/gather_y/ppermute | solution.py:10
  57.3 4.1 %collective-permute-start.16 = (bf16[48,1024]{1,0:T(8,128)(2,1)S(1)}, bf16[48,1024]{1,0:T(8,128)(2,1)S(1)}, u32[]{:S(2)}, u32[]{:S(2)}) collective-permute-start(bf16[48,1024]{1,0:T(8,128)(2,1)S(1)} %get-tuple-element.25), channel_id=1, source_target_pairs={{0,144},{16,0},{128,16},{144,128},{1,145},{17,1},{129,17},{145,129... | collective-permute-start | bytes 294920 | tf_op jit(solution)/shard_map/gather_y/ppermute | solution.py:10
  61.4 4.5 %collective-permute-start.17 = (bf16[192,1024]{1,0:T(8,128)(2,1)S(1)}, bf16[192,1024]{1,0:T(8,128)(2,1)S(1)}, u32[]{:S(2)}, u32[]{:S(2)}) collective-permute-start(bf16[192,1024]{1,0:T(8,128)(2,1)S(1)} %pad_maximum_fusion.1), channel_id=1, source_target_pairs={{0,8},{8,0},{1,9},{9,1},{2,10},{10,2},{3,11},{11,3},{4,12},{12,4},... | collective-permute-start | bytes 1179656 | tf_op jit(solution)/shard_map/gather_y/ppermute | solution.py:18

commit v12 on v11

--- a/solution.py
+++ b/solution.py
@@ -95,6 +95,12 @@
             piece = lax.dynamic_index_in_dim(kept, (y + k) % ny, 0, False).astype(LOW)
             total = total + shift(piece, Y, ny, k).astype(F32)
 
+    with jax.named_scope("inverse_factors"):
+        inverse_factors = sum(
+            lax.dot_general(panels, part, (((1,), (1,)), ((), ())), preferred_element_type=F32)
+            for part in (inv_high, inv_rest)
+        ).astype(LOW)
+
     with jax.named_scope("screen"):
         place = z * width + lax.axis_index(PLANE) * count
         unit = (lax.iota(jnp.int32, count)[:, None] + place) == lax.iota(jnp.int32, panel)[None, :]
@@ -107,8 +113,8 @@
         screened = screened + jnp.dot(high, inv_rest, preferred_element_type=F32)
 
     with jax.named_scope("gather_y"):
-        low = screened.astype(LOW)
-        gathered = jnp.concatenate([low] + [shift(low, Y, ny, k) for k in steps[1:]], axis=0)
+        gathered = jnp.concatenate([high] + [shift(high, Y, ny, k) for k in steps[1:]], axis=0)
+        gathered, inverse_factors = lax.optimization_barrier((gathered, inverse_factors))
         gathered = jnp.concatenate([gathered, swap(gathered)], axis=0)
         by_y = factors.reshape(ny, 2, count, -1)
         ordered = jnp.concatenate(
@@ -121,7 +127,7 @@
 
     with jax.named_scope("sigma"):
         products = lax.dot_general(
-            gathered, panels, (((1,), (1,)), ((), ())), preferred_element_type=F32
+            gathered, inverse_factors, (((1,), (1,)), ((), ())), preferred_element_type=F32
         )
         local = -jnp.sum(products * ordered.astype(F32), axis=0).reshape(nx, own)
         back = (x - lax.iota(jnp.int32, nx)) % nx

time: 81.6 us -> 85.1 us (1.043)
  blocking collectives: 14.1 us -> 0 us
  starting transfers between devices: 34.4 us -> 44 us
  waiting for transfers between devices: 20.7 us -> 25.7 us
  matrix products: 2.97 us -> 5.54 us
    all_to_all x1 -> x0, blocking collectives: 14.1 us -> none  [body(): terms = lax.all_to_all(copies, (X, Z), 0, 0, tiled=True)]
    all_to_all x0 -> x1, waiting for transfers between devices: none -> 7.47 us  [body(): terms = lax.all_to_all(copies, (X, Z), 0, 0, tiled=True)]
    all_to_all x0 -> x1, starting transfers between devices: none -> 7.11 us  [body(): terms = lax.all_to_all(copies, (X, Z), 0, 0, tiled=True)]
    ppermute x2, starting transfers between devices: 3.95 us -> 7.63 us  [swap(): return lax.ppermute(value, CORE, [(0, 1), (1, 0)])]
    dot_general x1 -> x3, matrix products: 0.63 us -> 3.23 us  [the longest x2 2.6 us: body(): lax.dot_general(panels, part, (((1,), (1,)), ((), ())), preferred_element...]
    ppermute x12, waiting for transfers between devices: 17.2 us -> 14.9 us  [shift(): lax.ppermute(value, axis, [(i, (i + step) % size) for i in range(size)])]
    ppermute x12, starting transfers between devices: 18.3 us -> 16.5 us  [shift(): lax.ppermute(value, axis, [(i, (i + step) % size) for i in range(size)])]
  transfers between devices with their start and end apart: 18 -> 19, of which waited for: 9 -> 10; matrix products, arithmetic and copies ran while one was open for 7% -> 12% of each run, Pallas kernels for 0% -> 0%
where the time goes in v12:
time: 85.1 us; the launch traced here: 84.8 us
  starting transfers between devices  44 us (52%)
  waiting for transfers between devices  25.7 us (30%)
  matrix products  5.54 us (7%)
  other arithmetic  4.62 us (5%)
  local copies, waits for them, and re-layouts  3.87 us (5%)
  between operations  1.13 us (1%)
    ppermute x12, starting transfers between devices, shift(): lax.ppermute(value, axis, [(i, (i + step) % size) for i in range(size)])  16.5 us
    ppermute x12, waiting for transfers between devices, shift(): lax.ppermute(value, axis, [(i, (i + step) % size) for i in range(size)])  14.9 us
    ppermute x4, starting transfers between devices, along_z(): return lax.ppermute(value, Z, pairs)  12.7 us
    ppermute x2, starting transfers between devices, swap(): return lax.ppermute(value, CORE, [(0, 1), (1, 0)])  7.63 us
    all_to_all x1, waiting for transfers between devices, body(): terms = lax.all_to_all(copies, (X, Z), 0, 0, tiled=True)  7.47 us
    all_to_all x1, starting transfers between devices, body(): terms = lax.all_to_all(copies, (X, Z), 0, 0, tiled=True)  7.11 us
    convert_element_type x2, other arithmetic, two_parts(): return (high.astype(LOW), (value - high).astype(LOW))  3.03 us
    dot_general x2, matrix products, body(): lax.dot_general(panels, part, (((1,), (1,)), ((), ())), preferred_element...  2.6 us
  transfers between devices with their start and end apart: 19, of which 10 were waited for; matrix products, arithmetic and copies ran while one was open for 12% of the time, Pallas kernels for 0%

profile of v12, /device:TPU:1, one launch (start us, length us, event | category | flops | bytes accessed | tf_op | source)
XLA Modules:
  0.0 84.8 jit_solution(9136313408550706694)
XLA Ops:
  0.6 0.0 copy-start
  0.6 1.0 %slice.31 = bf16[128,1024]{1,0:T(8,128)(2,1)S(1)} slice(bf16[128,1536]{1,0:T(8,128)(2,1)} %param.3), slice={[0:128], [0:1024]} | slice | bytes 524288 | tf_op jit(solution)/shard_map/panel_z/slice | solution.py:44
  1.7 8.8 %collective-permute-start.1 = (bf16[128,1024]{1,0:T(8,128)(2,1)S(1)}, bf16[128,1024]{1,0:T(8,128)(2,1)S(1)}, u32[]{:S(2)}, u32[]{:S(2)}) collective-permute-start(bf16[128,1024]{1,0:T(8,128)(2,1)S(1)} %slice.31), channel_id=1, source_target_pairs={{0,6},{8,14},{16,22},{24,30},{32,38},{40,46},{48,54},{56,62},{64,7... | collective-permute-start | bytes 786440 | tf_op jit(solution)/shard_map/panel_z/ppermute | solution.py:14
  10.5 1.3 %collective-permute-start = (bf16[128,1024]{1,0:T(8,128)(2,1)S(1)}, bf16[128,1024]{1,0:T(8,128)(2,1)S(1)}, u32[]{:S(2)}, u32[]{:S(2)}) collective-permute-start(bf16[128,1024]{1,0:T(8,128)(2,1)S(1)} %slice.31), channel_id=1, source_target_pairs={{0,3},{8,11},{16,19},{24,27},{32,35},{40,43},{48,51},{56,59},{64,6... | collective-permute-start | bytes 786440 | tf_op jit(solution)/shard_map/panel_z/ppermute | solution.py:14
  11.8 1.2 %copy.18 = bf16[128,1536]{0,1:T(8,128)(2,1)S(1)} copy(bf16[128,1536]{1,0:T(8,128)(2,1)} %param.3) | data formatting | bytes 786432 | tf_op args[0]
  13.0 0.7 fusion.24
  13.8 0.2 concatenate.36
  14.0 2.8 %collective-permute-start.4 = (bf16[400,128]{1,0:T(8,128)(2,1)S(1)}, bf16[400,128]{1,0:T(8,128)(2,1)S(1)}, u32[]{:S(2)}, u32[]{:S(2)}) collective-permute-start(bf16[400,128]{1,0:T(8,128)(2,1)S(1)} %concatenate.36), channel_id=1, source_target_pairs={{0,64},{32,96},{64,0},{96,32},{1,65},{33,97},{65,1},{97,33},{2,66}... | collective-permute-start | bytes 307208 | tf_op jit(solution)/shard_map/blocks/ppermute | solution.py:10
  16.8 0.2 concatenate.38
  17.0 0.9 %collective-permute-start.6 = (bf16[400,128]{1,0:T(8,128)(2,1)S(1)}, bf16[400,128]{1,0:T(8,128)(2,1)S(1)}, u32[]{:S(2)}, u32[]{:S(2)}) collective-permute-start(bf16[400,128]{1,0:T(8,128)(2,1)S(1)} %concatenate.38), channel_id=1, source_target_pairs={{0,96},{32,0},{64,32},{96,64},{1,97},{33,1},{65,33},{97,65},{2,98}... | collective-permute-start | bytes 307208 | tf_op jit(solution)/shard_map/blocks/ppermute | solution.py:10
  17.9 0.2 concatenate.37
  18.1 0.7 collective-permute-start.5
  18.8 0.2 concatenate.35
  19.1 1.3 %collective-permute-start.3 = (bf16[128,1024]{1,0:T(8,128)(2,1)S(1)}, bf16[128,1024]{1,0:T(8,128)(2,1)S(1)}, u32[]{:S(2)}, u32[]{:S(2)}) collective-permute-start(bf16[128,1024]{1,0:T(8,128)(2,1)S(1)} %select_select_fusion.1), channel_id=1, source_target_pairs={{0,1},{3,2},{8,9},{11,10},{16,17},{19,18},{24,25},{27,26},{32,33},... | collective-permute-start | bytes 786440 | tf_op jit(solution)/shard_map/panel_z/ppermute | solution.py:14
  20.4 1.3 %collective-permute-start.2 = (bf16[128,1024]{1,0:T(8,128)(2,1)S(1)}, bf16[128,1024]{1,0:T(8,128)(2,1)S(1)}, u32[]{:S(2)}, u32[]{:S(2)}) collective-permute-start(bf16[128,1024]{1,0:T(8,128)(2,1)S(1)} %select_select_fusion.1), channel_id=1, source_target_pairs={{0,7},{3,4},{6,5},{8,15},{11,12},{14,13},{16,23},{19,20},{22,21},{... | collective-permute-start | bytes 786440 | tf_op jit(solution)/shard_map/panel_z/ppermute | solution.py:14
  21.7 2.9 %fusion = (bf16[1024,1024]{1,0:T(8,128)(2,1)S(1)}, bf16[1024,1024]{1,0:T(8,128)(2,1)S(1)}) fusion(f32[1024,1024]{1,0:T(8,128)} %param.5), kind=kLoop, calls=%fused_computation.2 | loop fusion | flops 4194304 | bytes 8388608 | tf_op jit(solution)/shard_map/panel_z/convert_element_type | solution.py:32
  24.7 1.1 %collective-permute-done.2 = bf16[128,1024]{1,0:T(8,128)(2,1)S(1)} collective-permute-done((bf16[128,1024]{1,0:T(8,128)(2,1)S(1)}, bf16[128,1024]{1,0:T(8,128)(2,1)S(1)}, u32[]{:S(2)}, u32[]{:S(2)}) %collective-permute-start.2) | collective-permute-done | bytes 262176 | tf_op jit(solution)/shard_map/panel_z/ppermute | solution.py:14
  25.8 2.1 %collective-permute-start.9 = (bf16[128,1024]{1,0:T(8,128)(2,1)S(1)}, bf16[128,1024]{1,0:T(8,128)(2,1)S(1)}, u32[]{:S(2)}, u32[]{:S(2)}) collective-permute-start(bf16[128,1024]{1,0:T(8,128)(2,1)S(1)} %select_select_fusion), channel_id=1, source_target_pairs={{0,96},{32,0},{64,32},{96,64},{1,97},{33,1},{65,33},{97,65},{2,98}... | collective-permute-start | bytes 786440 | tf_op jit(solution)/shard_map/panel_x/ppermute | solution.py:10
  28.0 1.3 %collective-permute-start.7 = (bf16[128,1024]{1,0:T(8,128)(2,1)S(1)}, bf16[128,1024]{1,0:T(8,128)(2,1)S(1)}, u32[]{:S(2)}, u32[]{:S(2)}) collective-permute-start(bf16[128,1024]{1,0:T(8,128)(2,1)S(1)} %select_select_fusion), channel_id=1, source_target_pairs={{0,64},{32,96},{64,0},{96,32},{1,65},{33,97},{65,1},{97,33},{2,66}... | collective-permute-start | bytes 786440 | tf_op jit(solution)/shard_map/panel_x/ppermute | solution.py:10
  29.5 1.8 %collective-permute-done.9 = bf16[128,1024]{1,0:T(8,128)(2,1)S(1)} collective-permute-done((bf16[128,1024]{1,0:T(8,128)(2,1)S(1)}, bf16[128,1024]{1,0:T(8,128)(2,1)S(1)}, u32[]{:S(2)}, u32[]{:S(2)}) %collective-permute-start.9) | collective-permute-done | bytes 262176 | tf_op jit(solution)/shard_map/panel_x/ppermute | solution.py:10
  31.3 6.0 %collective-permute-done.8 = bf16[128,1024]{1,0:T(8,128)(2,1)S(1)} collective-permute-done((bf16[128,1024]{1,0:T(8,128)(2,1)S(1)}, bf16[128,1024]{1,0:T(8,128)(2,1)S(1)}, u32[]{:S(2)}, u32[]{:S(2)}) %collective-permute-start.8) | collective-permute-done | bytes 262176 | tf_op jit(solution)/shard_map/panel_x/ppermute | solution.py:10
  37.3 1.2 %collective-permute-done.7 = bf16[128,1024]{1,0:T(8,128)(2,1)S(1)} collective-permute-done((bf16[128,1024]{1,0:T(8,128)(2,1)S(1)}, bf16[128,1024]{1,0:T(8,128)(2,1)S(1)}, u32[]{:S(2)}, u32[]{:S(2)}) %collective-permute-start.7) | collective-permute-done | bytes 262176 | tf_op jit(solution)/shard_map/panel_x/ppermute | solution.py:10
  38.5 0.7 fusion.3
  39.1 0.1 fusion.8
  39.2 5.1 %collective-permute-start.10 = (bf16[4,48,1024]{2,1,0:T(8,128)(2,1)S(1)}, bf16[4,48,1024]{2,1,0:T(8,128)(2,1)S(1)}, u32[]{:S(2)}, u32[]{:S(2)}) collective-permute-start(bf16[4,48,1024]{2,1,0:T(8,128)(2,1)S(1)} %fusion.8), channel_id=1, source_target_pairs={{0,8},{8,0},{1,9},{9,1},{2,10},{10,2},{3,11},{11,3},{4,12},{12,4},... | collective-permute-start | bytes 1179656 | tf_op jit(solution)/shard_map/sum_core/ppermute | solution.py:18
  44.4 1.3 %collective-permute-done.10 = bf16[4,48,1024]{2,1,0:T(8,128)(2,1)S(1)} collective-permute-done((bf16[4,48,1024]{2,1,0:T(8,128)(2,1)S(1)}, bf16[4,48,1024]{2,1,0:T(8,128)(2,1)S(1)}, u32[]{:S(2)}, u32[]{:S(2)}) %collective-permute-start.10) | collective-permute-done | bytes 393248 | tf_op jit(solution)/shard_map/sum_core/ppermute | solution.py:18
  45.7 0.1 bitcast_add_fusion
  45.9 3.0 %collective-permute-start.11 = (bf16[48,1024]{1,0:T(8,128)(2,1)S(1)}, bf16[48,1024]{1,0:T(8,128)(2,1)S(1)}, u32[]{:S(2)}, u32[]{:S(2)}) collective-permute-start(bf16[48,1024]{1,0:T(8,128)(2,1)S(1)} %get-tuple-element.34), channel_id=1, source_target_pairs={{0,128},{16,144},{128,0},{144,16},{1,129},{17,145},{129,1},{145,17... | collective-permute-start | bytes 294920 | tf_op jit(solution)/shard_map/sum_y/ppermute | solution.py:10
  48.9 0.8 collective-permute-start.13
  49.7 0.7 collective-permute-start.12
  50.4 1.3 %fusion.29 = f32[512,1024]{1,0:T(8,128)S(1)} fusion(bf16[1024,1024]{1,0:T(8,128)(2,1)S(1)} %get-tuple-element.25, bf16[128,1024]{1,0:T(8,128)(2,1)S(1)} %collective-permute-done.9, bf16[128,1024]{1,0:T(8,128)(2,1)S(1)} %collective-permute-done.8, bf16[128,1024]{1,0:T(8,128)(2,1)S(1)} %collective-permute-done.7, bf16[128,1024]{1,0:T(8,128)(2,1)S(1)} %select_select_fusion), kind=kOutput, calls=%fused_computation.80 | convolution fusion | flops 1077936128 | bytes 5242880 | tf_op jit(solution)/shard_map/inverse_factors/dot_general | solution.py:100
  51.7 2.3 %collective-permute-done.13 = bf16[48,1024]{1,0:T(8,128)(2,1)S(1)} collective-permute-done((bf16[48,1024]{1,0:T(8,128)(2,1)S(1)}, bf16[48,1024]{1,0:T(8,128)(2,1)S(1)}, u32[]{:S(2)}, u32[]{:S(2)}) %collective-permute-start.13) | collective-permute-done | bytes 98336 | tf_op jit(solution)/shard_map/sum_y/ppermute | solution.py:10
  53.9 0.4 collective-permute-done.12
  54.3 0.1 fusion.9
  54.5 2.6 %collective-permute-start.16 = (bf16[48,1024]{1,0:T(8,128)(2,1)S(1)}, bf16[48,1024]{1,0:T(8,128)(2,1)S(1)}, u32[]{:S(2)}, u32[]{:S(2)}) collective-permute-start(bf16[48,1024]{1,0:T(8,128)(2,1)S(1)} %get-tuple-element.33), channel_id=1, source_target_pairs={{0,144},{16,0},{128,16},{144,128},{1,145},{17,1},{129,17},{145,129... | collective-permute-start | bytes 294920 | tf_op jit(solution)/shard_map/gather_y/ppermute | solution.py:10
  57.1 1.5 %collective-permute-start.14 = (bf16[48,1024]{1,0:T(8,128)(2,1)S(1)}, bf16[48,1024]{1,0:T(8,128)(2,1)S(1)}, u32[]{:S(2)}, u32[]{:S(2)}) collective-permute-start(bf16[48,1024]{1,0:T(8,128)(2,1)S(1)} %get-tuple-element.33), channel_id=1, source_target_pairs={{0,128},{16,144},{128,0},{144,16},{1,129},{17,145},{129,1},{145,17... | collective-permute-start | bytes 294920 | tf_op jit(solution)/shard_map/gather_y/ppermute | solution.py:10
  58.6 1.3 %add_convert_fusion = bf16[512,1024]{1,0:T(8,128)(2,1)S(1)} fusion(f32[512,1024]{1,0:T(8,128)S(1)} %fusion.29, bf16[1024,1024]{1,0:T(8,128)(2,1)S(1)} %get-tuple-element.24, bf16[128,1024]{1,0:T(8,128)(2,1)S(1)} %collective-permute-done.9, bf16[128,1024]{1,0:T(8,128)(2,1)S(1)} %collective-permute-done.8, bf16[128,1024]{1,0:T(8,128)(2,1)S(1)} %collective-permute-done.7, ...), kind=kOutput, calls=%fused_computation.3 | convolution fusion | flops 1078984704 | bytes 6291456 | tf_op jit(solution)/shard_map/inverse_factors/dot_general | solution.py:100
  60.0 3.3 %collective-permute-done.15 = bf16[48,1024]{1,0:T(8,128)(2,1)S(1)} collective-permute-done((bf16[48,1024]{1,0:T(8,128)(2,1)S(1)}, bf16[48,1024]{1,0:T(8,128)(2,1)S(1)}, u32[]{:S(2)}, u32[]{:S(2)}) %collective-permute-start.15) | collective-permute-done | bytes 98336 | tf_op jit(solution)/shard_map/gather_y/ppermute | solution.py:10
  63.3 2.5 %collective-permute-start.17 = (bf16[192,1024]{1,0:T(8,128)(2,1)S(1)}, bf16[192,1024]{1,0:T(8,128)(2,1)S(1)}, u32[]{:S(2)}, u32[]{:S(2)}) collective-permute-start(bf16[192,1024]{1,0:T(8,128)(2,1)S(1)} %pad_maximum_fusion.1), channel_id=1, source_target_pairs={{0,8},{8,0},{1,9},{9,1},{2,10},{10,2},{3,11},{11,3},{4,12},{12,4},... | collective-permute-start | bytes 1179656 | tf_op jit(solution)/shard_map/gather_y/ppermute | solution.py:18
  65.8 0.5 fusion.10
  66.2 0.9 %collective-permute-done.17 = bf16[192,1024]{1,0:T(8,128)(2,1)S(1)} collective-permute-done((bf16[192,1024]{1,0:T(8,128)(2,1)S(1)}, bf16[192,1024]{1,0:T(8,128)(2,1)S(1)}, u32[]{:S(2)}, u32[]{:S(2)}) %collective-permute-start.17) | collective-permute-done | bytes 393248 | tf_op jit(solution)/shard_map/gather_y/ppermute | solution.py:18
  67.1 0.6 fusion.1
  67.8 0.1 select_add_fusion
  67.8 0.6 broadcast_in_dim.82
  68.5 7.1 %all-to-all-start = ((f32[32,1,128]{2,1,0:T(1,128)}), f32[32,1,128]{2,1,0:T(1,128)S(1)}, u32[]{:S(2)}, u32[]{:S(2)}) async-start(f32[32,1,128]{2,1,0:T(1,128)} %bitcast.19), calls=%async_computation | async-start | bytes 32768 | tf_op jit(solution)/shard_map/sigma/all_to_all | solution.py:138
  75.6 1.2 %fusion.2 = f32[1,48,1024]{2,1,0:T(8,128)} fusion(bf16[48,1024]{1,0:T(8,128)(2,1)S(1)} %get-tuple-element.33, bf16[1024,1024]{1,0:T(8,128)(2,1)S(1)} %get-tuple-element.25, f32[96,1024]{1,0:T(8,128)S(1)} %fusion.10), kind=kOutput, calls=%fused_computation.8 | convolution fusion | flops 100761600 | bytes 2785280 | tf_op jit(solution)/shard_map/screen/dot_general | solution.py:113
  76.7 7.5 %all-to-all-done = f32[32,1,128]{2,1,0:T(1,128)S(1)} async-done(((f32[32,1,128]{2,1,0:T(1,128)}), f32[32,1,128]{2,1,0:T(1,128)S(1)}, u32[]{:S(2)}, u32[]{:S(2)}) %all-to-all-start) | async-done | bytes 16416 | tf_op jit(solution)/shard_map/sigma/all_to_all | solution.py:138
  84.2 0.6 reduce_sum.29
  (38 shorter events, 0.5 us)
Async XLA Ops:
  0.6 18.4 %copy-start = (bf16[128,1536]{1,0:T(8,128)(2,1)S(1)}, bf16[128,1536]{1,0:T(8,128)(2,1)}, u32[]{:S(2)}) copy-start(bf16[128,1536]{1,0:T(8,128)(2,1)} %param.3) | copy-start | bytes 1179652
  1.7 17.4 %collective-permute-start.1 = (bf16[128,1024]{1,0:T(8,128)(2,1)S(1)}, bf16[128,1024]{1,0:T(8,128)(2,1)S(1)}, u32[]{:S(2)}, u32[]{:S(2)}) collective-permute-start(bf16[128,1024]{1,0:T(8,128)(2,1)S(1)} %slice.31), channel_id=1, source_target_pairs={{0,6},{8,14},{16,22},{24,30},{32,38},{40,46},{48,54},{56,62},{64,7... | collective-permute-start | bytes 786440 | tf_op jit(solution)/shard_map/panel_z/ppermute | solution.py:14
  10.5 8.6 %collective-permute-start = (bf16[128,1024]{1,0:T(8,128)(2,1)S(1)}, bf16[128,1024]{1,0:T(8,128)(2,1)S(1)}, u32[]{:S(2)}, u32[]{:S(2)}) collective-permute-start(bf16[128,1024]{1,0:T(8,128)(2,1)S(1)} %slice.31), channel_id=1, source_target_pairs={{0,3},{8,11},{16,19},{24,27},{32,35},{40,43},{48,51},{56,59},{64,6... | collective-permute-start | bytes 786440 | tf_op jit(solution)/shard_map/panel_z/ppermute | solution.py:14
  14.0 10.7 %collective-permute-start.4 = (bf16[400,128]{1,0:T(8,128)(2,1)S(1)}, bf16[400,128]{1,0:T(8,128)(2,1)S(1)}, u32[]{:S(2)}, u32[]{:S(2)}) collective-permute-start(bf16[400,128]{1,0:T(8,128)(2,1)S(1)} %concatenate.36), channel_id=1, source_target_pairs={{0,64},{32,96},{64,0},{96,32},{1,65},{33,97},{65,1},{97,33},{2,66}... | collective-permute-start | bytes 307208 | tf_op jit(solution)/shard_map/blocks/ppermute | solution.py:10
  17.0 7.7 %collective-permute-start.6 = (bf16[400,128]{1,0:T(8,128)(2,1)S(1)}, bf16[400,128]{1,0:T(8,128)(2,1)S(1)}, u32[]{:S(2)}, u32[]{:S(2)}) collective-permute-start(bf16[400,128]{1,0:T(8,128)(2,1)S(1)} %concatenate.38), channel_id=1, source_target_pairs={{0,96},{32,0},{64,32},{96,64},{1,97},{33,1},{65,33},{97,65},{2,98}... | collective-permute-start | bytes 307208 | tf_op jit(solution)/shard_map/blocks/ppermute | solution.py:10
  18.1 6.6 %collective-permute-start.5 = (bf16[400,128]{1,0:T(8,128)(2,1)S(1)}, bf16[400,128]{1,0:T(8,128)(2,1)S(1)}, u32[]{:S(2)}, u32[]{:S(2)}) collective-permute-start(bf16[400,128]{1,0:T(8,128)(2,1)S(1)} %concatenate.37), channel_id=1, source_target_pairs={{0,32},{32,64},{64,96},{96,0},{1,33},{33,65},{65,97},{97,1},{2,34}... | collective-permute-start | bytes 307208 | tf_op jit(solution)/shard_map/blocks/ppermute | solution.py:10
  19.1 5.6 %collective-permute-start.3 = (bf16[128,1024]{1,0:T(8,128)(2,1)S(1)}, bf16[128,1024]{1,0:T(8,128)(2,1)S(1)}, u32[]{:S(2)}, u32[]{:S(2)}) collective-permute-start(bf16[128,1024]{1,0:T(8,128)(2,1)S(1)} %select_select_fusion.1), channel_id=1, source_target_pairs={{0,1},{3,2},{8,9},{11,10},{16,17},{19,18},{24,25},{27,26},{32,33},... | collective-permute-start | bytes 786440 | tf_op jit(solution)/shard_map/panel_z/ppermute | solution.py:14
  20.4 5.4 %collective-permute-start.2 = (bf16[128,1024]{1,0:T(8,128)(2,1)S(1)}, bf16[128,1024]{1,0:T(8,128)(2,1)S(1)}, u32[]{:S(2)}, u32[]{:S(2)}) collective-permute-start(bf16[128,1024]{1,0:T(8,128)(2,1)S(1)} %select_select_fusion.1), channel_id=1, source_target_pairs={{0,7},{3,4},{6,5},{8,15},{11,12},{14,13},{16,23},{19,20},{22,21},{... | collective-permute-start | bytes 786440 | tf_op jit(solution)/shard_map/panel_z/ppermute | solution.py:14
  25.8 5.5 %collective-permute-start.9 = (bf16[128,1024]{1,0:T(8,128)(2,1)S(1)}, bf16[128,1024]{1,0:T(8,128)(2,1)S(1)}, u32[]{:S(2)}, u32[]{:S(2)}) collective-permute-start(bf16[128,1024]{1,0:T(8,128)(2,1)S(1)} %select_select_fusion), channel_id=1, source_target_pairs={{0,96},{32,0},{64,32},{96,64},{1,97},{33,1},{65,33},{97,65},{2,98}... | collective-permute-start | bytes 786440 | tf_op jit(solution)/shard_map/panel_x/ppermute | solution.py:10
  28.0 9.3 %collective-permute-start.8 = (bf16[128,1024]{1,0:T(8,128)(2,1)S(1)}, bf16[128,1024]{1,0:T(8,128)(2,1)S(1)}, u32[]{:S(2)}, u32[]{:S(2)}) collective-permute-start(bf16[128,1024]{1,0:T(8,128)(2,1)S(1)} %select_select_fusion), channel_id=1, source_target_pairs={{0,32},{32,64},{64,96},{96,0},{1,33},{33,65},{65,97},{97,1},{2,34}... | collective-permute-start | bytes 786440 | tf_op jit(solution)/shard_map/panel_x/ppermute | solution.py:10
  28.0 10.5 %collective-permute-start.7 = (bf16[128,1024]{1,0:T(8,128)(2,1)S(1)}, bf16[128,1024]{1,0:T(8,128)(2,1)S(1)}, u32[]{:S(2)}, u32[]{:S(2)}) collective-permute-start(bf16[128,1024]{1,0:T(8,128)(2,1)S(1)} %select_select_fusion), channel_id=1, source_target_pairs={{0,64},{32,96},{64,0},{96,32},{1,65},{33,97},{65,1},{97,33},{2,66}... | collective-permute-start | bytes 786440 | tf_op jit(solution)/shard_map/panel_x/ppermute | solution.py:10
  39.2 6.5 %collective-permute-start.10 = (bf16[4,48,1024]{2,1,0:T(8,128)(2,1)S(1)}, bf16[4,48,1024]{2,1,0:T(8,128)(2,1)S(1)}, u32[]{:S(2)}, u32[]{:S(2)}) collective-permute-start(bf16[4,48,1024]{2,1,0:T(8,128)(2,1)S(1)} %fusion.8), channel_id=1, source_target_pairs={{0,8},{8,0},{1,9},{9,1},{2,10},{10,2},{3,11},{11,3},{4,12},{12,4},... | collective-permute-start | bytes 1179656 | tf_op jit(solution)/shard_map/sum_core/ppermute | solution.py:18
  45.9 5.8 %collective-permute-start.11 = (bf16[48,1024]{1,0:T(8,128)(2,1)S(1)}, bf16[48,1024]{1,0:T(8,128)(2,1)S(1)}, u32[]{:S(2)}, u32[]{:S(2)}) collective-permute-start(bf16[48,1024]{1,0:T(8,128)(2,1)S(1)} %get-tuple-element.34), channel_id=1, source_target_pairs={{0,128},{16,144},{128,0},{144,16},{1,129},{17,145},{129,1},{145,17... | collective-permute-start | bytes 294920 | tf_op jit(solution)/shard_map/sum_y/ppermute | solution.py:10
  48.9 5.0 %collective-permute-start.13 = (bf16[48,1024]{1,0:T(8,128)(2,1)S(1)}, bf16[48,1024]{1,0:T(8,128)(2,1)S(1)}, u32[]{:S(2)}, u32[]{:S(2)}) collective-permute-start(bf16[48,1024]{1,0:T(8,128)(2,1)S(1)} %get-tuple-element.35), channel_id=1, source_target_pairs={{0,144},{16,0},{128,16},{144,128},{1,145},{17,1},{129,17},{145,129... | collective-permute-start | bytes 294920 | tf_op jit(solution)/shard_map/sum_y/ppermute | solution.py:10
  49.7 4.7 %collective-permute-start.12 = (bf16[48,1024]{1,0:T(8,128)(2,1)S(1)}, bf16[48,1024]{1,0:T(8,128)(2,1)S(1)}, u32[]{:S(2)}, u32[]{:S(2)}) collective-permute-start(bf16[48,1024]{1,0:T(8,128)(2,1)S(1)} %get-tuple-element.36), channel_id=1, source_target_pairs={{0,16},{16,128},{128,144},{144,0},{1,17},{17,129},{129,145},{145,1... | collective-permute-start | bytes 294920 | tf_op jit(solution)/shard_map/sum_y/ppermute | solution.py:10
  54.5 5.5 %collective-permute-start.16 = (bf16[48,1024]{1,0:T(8,128)(2,1)S(1)}, bf16[48,1024]{1,0:T(8,128)(2,1)S(1)}, u32[]{:S(2)}, u32[]{:S(2)}) collective-permute-start(bf16[48,1024]{1,0:T(8,128)(2,1)S(1)} %get-tuple-element.33), channel_id=1, source_target_pairs={{0,144},{16,0},{128,16},{144,128},{1,145},{17,1},{129,17},{145,129... | collective-permute-start | bytes 294920 | tf_op jit(solution)/shard_map/gather_y/ppermute | solution.py:10
  57.1 6.1 %collective-permute-start.15 = (bf16[48,1024]{1,0:T(8,128)(2,1)S(1)}, bf16[48,1024]{1,0:T(8,128)(2,1)S(1)}, u32[]{:S(2)}, u32[]{:S(2)}) collective-permute-start(bf16[48,1024]{1,0:T(8,128)(2,1)S(1)} %get-tuple-element.33), channel_id=1, source_target_pairs={{0,16},{16,128},{128,144},{144,0},{1,17},{17,129},{129,145},{145,1... | collective-permute-start | bytes 294920 | tf_op jit(solution)/shard_map/gather_y/ppermute | solution.py:10
  57.1 6.1 %collective-permute-start.14 = (bf16[48,1024]{1,0:T(8,128)(2,1)S(1)}, bf16[48,1024]{1,0:T(8,128)(2,1)S(1)}, u32[]{:S(2)}, u32[]{:S(2)}) collective-permute-start(bf16[48,1024]{1,0:T(8,128)(2,1)S(1)} %get-tuple-element.33), channel_id=1, source_target_pairs={{0,128},{16,144},{128,0},{144,16},{1,129},{17,145},{129,1},{145,17... | collective-permute-start | bytes 294920 | tf_op jit(solution)/shard_map/gather_y/ppermute | solution.py:10
  63.3 3.8 %collective-permute-start.17 = (bf16[192,1024]{1,0:T(8,128)(2,1)S(1)}, bf16[192,1024]{1,0:T(8,128)(2,1)S(1)}, u32[]{:S(2)}, u32[]{:S(2)}) collective-permute-start(bf16[192,1024]{1,0:T(8,128)(2,1)S(1)} %pad_maximum_fusion.1), channel_id=1, source_target_pairs={{0,8},{8,0},{1,9},{9,1},{2,10},{10,2},{3,11},{11,3},{4,12},{12,4},... | collective-permute-start | bytes 1179656 | tf_op jit(solution)/shard_map/gather_y/ppermute | solution.py:18
  68.5 15.8 %all-to-all-start = ((f32[32,1,128]{2,1,0:T(1,128)}), f32[32,1,128]{2,1,0:T(1,128)S(1)}, u32[]{:S(2)}, u32[]{:S(2)}) async-start(f32[32,1,128]{2,1,0:T(1,128)} %bitcast.19), calls=%async_computation | async-start | bytes 32768 | tf_op jit(solution)/shard_map/sigma/all_to_all | solution.py:138

commit v13 on v11

--- a/solution.py
+++ b/solution.py
@@ -95,6 +95,14 @@
             piece = lax.dynamic_index_in_dim(kept, (y + k) % ny, 0, False).astype(LOW)
             total = total + shift(piece, Y, ny, k).astype(F32)
 
+    with jax.named_scope("inverse_factors"):
+        inverse_factors = two_parts(
+            sum(
+                lax.dot_general(panels, part, (((1,), (1,)), ((), ())), preferred_element_type=F32)
+                for part in (inv_high, inv_rest)
+            )
+        )
+
     with jax.named_scope("screen"):
         place = z * width + lax.axis_index(PLANE) * count
         unit = (lax.iota(jnp.int32, count)[:, None] + place) == lax.iota(jnp.int32, panel)[None, :]
@@ -107,8 +115,10 @@
         screened = screened + jnp.dot(high, inv_rest, preferred_element_type=F32)
 
     with jax.named_scope("gather_y"):
-        low = screened.astype(LOW)
-        gathered = jnp.concatenate([low] + [shift(low, Y, ny, k) for k in steps[1:]], axis=0)
+        gathered = jnp.concatenate([high] + [shift(high, Y, ny, k) for k in steps[1:]], axis=0)
+        gathered, inverse_factors, screened = lax.optimization_barrier(
+            (gathered, inverse_factors, screened)
+        )
         gathered = jnp.concatenate([gathered, swap(gathered)], axis=0)
         by_y = factors.reshape(ny, 2, count, -1)
         ordered = jnp.concatenate(
@@ -120,8 +130,9 @@
         ).reshape(-1, nx * own)
 
     with jax.named_scope("sigma"):
-        products = lax.dot_general(
-            gathered, panels, (((1,), (1,)), ((), ())), preferred_element_type=F32
+        products = sum(
+            lax.dot_general(gathered, part, (((1,), (1,)), ((), ())), preferred_element_type=F32)
+            for part in inverse_factors
         )
         local = -jnp.sum(products * ordered.astype(F32), axis=0).reshape(nx, own)
         back = (x - lax.iota(jnp.int32, nx)) % nx

time: 81.6 us -> 80.7 us (0.989)
  waiting for transfers between devices: 20.7 us -> 16.4 us
  matrix products: 2.97 us -> 6.26 us
    dot_general x1 -> x4, matrix products: 0.63 us -> 3.94 us  [the longest x2 2.66 us: body(): lax.dot_general(panels, part, (((1,), (1,)), ((), ())), preferred_element...]
    ppermute x12, waiting for transfers between devices: 17.2 us -> 14.2 us  [shift(): lax.ppermute(value, axis, [(i, (i + step) % size) for i in range(size)])]
    ppermute x2, waiting for transfers between devices: 2.59 us -> 1.31 us  [swap(): return lax.ppermute(value, CORE, [(0, 1), (1, 0)])]
  transfers between devices with their start and end apart: 18 -> 18, of which waited for: 9 -> 7; matrix products, arithmetic and copies ran while one was open for 7% -> 13% of each run, Pallas kernels for 0% -> 0%
where the time goes in v13:
time: 80.7 us; the launch traced here: 80.4 us
  starting transfers between devices  34.4 us (43%)
  waiting for transfers between devices  16.4 us (20%)
  blocking collectives  14.1 us (17%)
  matrix products  6.26 us (8%)
  other arithmetic  4.81 us (6%)
  local copies, waits for them, and re-layouts  3.32 us (4%)
  between operations  1.14 us (1%)
    ppermute x12, starting transfers between devices, shift(): lax.ppermute(value, axis, [(i, (i + step) % size) for i in range(size)])  18.4 us
    ppermute x12, waiting for transfers between devices, shift(): lax.ppermute(value, axis, [(i, (i + step) % size) for i in range(size)])  14.2 us
    all_to_all x1, blocking collectives, body(): terms = lax.all_to_all(copies, (X, Z), 0, 0, tiled=True)  14.1 us
    ppermute x4, starting transfers between devices, along_z(): return lax.ppermute(value, Z, pairs)  12.1 us
    ppermute x2, starting transfers between devices, swap(): return lax.ppermute(value, CORE, [(0, 1), (1, 0)])  3.94 us
    convert_element_type x2, other arithmetic, two_parts(): return (high.astype(LOW), (value - high).astype(LOW))  3.22 us
    dot_general x2, matrix products, body(): lax.dot_general(panels, part, (((1,), (1,)), ((), ())), preferred_element...  2.66 us
  transfers between devices with their start and end apart: 18, of which 7 were waited for; matrix products, arithmetic and copies ran while one was open for 13% of the time, Pallas kernels for 0%

profile of v13, /device:TPU:1, one launch (start us, length us, event | category | flops | bytes accessed | tf_op | source)
XLA Modules:
  0.0 80.4 jit_solution(13137726354552927563)
XLA Ops:
  0.6 0.0 copy-start
  0.6 1.0 %slice.31 = bf16[128,1024]{1,0:T(8,128)(2,1)S(1)} slice(bf16[128,1536]{1,0:T(8,128)(2,1)} %param.3), slice={[0:128], [0:1024]} | slice | bytes 524288 | tf_op jit(solution)/shard_map/panel_z/slice | solution.py:44
  1.7 7.1 %collective-permute-start = (bf16[128,1024]{1,0:T(8,128)(2,1)S(1)}, bf16[128,1024]{1,0:T(8,128)(2,1)S(1)}, u32[]{:S(2)}, u32[]{:S(2)}) collective-permute-start(bf16[128,1024]{1,0:T(8,128)(2,1)S(1)} %slice.31), channel_id=1, source_target_pairs={{0,3},{8,11},{16,19},{24,27},{32,35},{40,43},{48,51},{56,59},{64,6... | collective-permute-start | bytes 786440 | tf_op jit(solution)/shard_map/panel_z/ppermute | solution.py:14
  8.8 2.4 %collective-permute-start.1 = (bf16[128,1024]{1,0:T(8,128)(2,1)S(1)}, bf16[128,1024]{1,0:T(8,128)(2,1)S(1)}, u32[]{:S(2)}, u32[]{:S(2)}) collective-permute-start(bf16[128,1024]{1,0:T(8,128)(2,1)S(1)} %slice.31), channel_id=1, source_target_pairs={{0,6},{8,14},{16,22},{24,30},{32,38},{40,46},{48,54},{56,62},{64,7... | collective-permute-start | bytes 786440 | tf_op jit(solution)/shard_map/panel_z/ppermute | solution.py:14
  11.2 1.2 %copy.18 = bf16[128,1536]{0,1:T(8,128)(2,1)S(1)} copy(bf16[128,1536]{1,0:T(8,128)(2,1)} %param.3) | data formatting | bytes 786432 | tf_op args[0]
  12.4 0.7 fusion.22
  13.2 0.2 concatenate.36
  13.3 2.8 %collective-permute-start.4 = (bf16[400,128]{1,0:T(8,128)(2,1)S(1)}, bf16[400,128]{1,0:T(8,128)(2,1)S(1)}, u32[]{:S(2)}, u32[]{:S(2)}) collective-permute-start(bf16[400,128]{1,0:T(8,128)(2,1)S(1)} %concatenate.36), channel_id=1, source_target_pairs={{0,64},{32,96},{64,0},{96,32},{1,65},{33,97},{65,1},{97,33},{2,66}... | collective-permute-start | bytes 307208 | tf_op jit(solution)/shard_map/blocks/ppermute | solution.py:10
  16.2 0.2 concatenate.37
  16.3 0.4 collective-permute-start.5
  16.7 0.2 concatenate.38
  16.9 2.4 %collective-permute-start.6 = (bf16[400,128]{1,0:T(8,128)(2,1)S(1)}, bf16[400,128]{1,0:T(8,128)(2,1)S(1)}, u32[]{:S(2)}, u32[]{:S(2)}) collective-permute-start(bf16[400,128]{1,0:T(8,128)(2,1)S(1)} %concatenate.38), channel_id=1, source_target_pairs={{0,96},{32,0},{64,32},{96,64},{1,97},{33,1},{65,33},{97,65},{2,98}... | collective-permute-start | bytes 307208 | tf_op jit(solution)/shard_map/blocks/ppermute | solution.py:10
  19.3 0.2 concatenate.35
  19.7 1.3 %collective-permute-start.2 = (bf16[128,1024]{1,0:T(8,128)(2,1)S(1)}, bf16[128,1024]{1,0:T(8,128)(2,1)S(1)}, u32[]{:S(2)}, u32[]{:S(2)}) collective-permute-start(bf16[128,1024]{1,0:T(8,128)(2,1)S(1)} %select_select_fusion.1), channel_id=1, source_target_pairs={{0,7},{3,4},{6,5},{8,15},{11,12},{14,13},{16,23},{19,20},{22,21},{... | collective-permute-start | bytes 786440 | tf_op jit(solution)/shard_map/panel_z/ppermute | solution.py:14
  21.0 1.3 %collective-permute-start.3 = (bf16[128,1024]{1,0:T(8,128)(2,1)S(1)}, bf16[128,1024]{1,0:T(8,128)(2,1)S(1)}, u32[]{:S(2)}, u32[]{:S(2)}) collective-permute-start(bf16[128,1024]{1,0:T(8,128)(2,1)S(1)} %select_select_fusion.1), channel_id=1, source_target_pairs={{0,1},{3,2},{8,9},{11,10},{16,17},{19,18},{24,25},{27,26},{32,33},... | collective-permute-start | bytes 786440 | tf_op jit(solution)/shard_map/panel_z/ppermute | solution.py:14
  22.3 3.1 %fusion = (bf16[1024,1024]{1,0:T(8,128)(2,1)S(1)}, bf16[1024,1024]{1,0:T(8,128)(2,1)S(1)}) fusion(f32[1024,1024]{1,0:T(8,128)} %param.5), kind=kLoop, calls=%fused_computation.2 | loop fusion | flops 4194304 | bytes 8388608 | tf_op jit(solution)/shard_map/panel_z/convert_element_type | solution.py:32
  25.5 0.9 %collective-permute-done.3 = bf16[128,1024]{1,0:T(8,128)(2,1)S(1)} collective-permute-done((bf16[128,1024]{1,0:T(8,128)(2,1)S(1)}, bf16[128,1024]{1,0:T(8,128)(2,1)S(1)}, u32[]{:S(2)}, u32[]{:S(2)}) %collective-permute-start.3) | collective-permute-done | bytes 262176 | tf_op jit(solution)/shard_map/panel_z/ppermute | solution.py:14
  26.4 0.1 collective-permute-start.7
  26.5 1.0 %collective-permute-start.8 = (bf16[128,1024]{1,0:T(8,128)(2,1)S(1)}, bf16[128,1024]{1,0:T(8,128)(2,1)S(1)}, u32[]{:S(2)}, u32[]{:S(2)}) collective-permute-start(bf16[128,1024]{1,0:T(8,128)(2,1)S(1)} %select_select_fusion), channel_id=1, source_target_pairs={{0,32},{32,64},{64,96},{96,0},{1,33},{33,65},{65,97},{97,1},{2,34}... | collective-permute-start | bytes 786440 | tf_op jit(solution)/shard_map/panel_x/ppermute | solution.py:10
  27.5 1.7 %collective-permute-start.9 = (bf16[128,1024]{1,0:T(8,128)(2,1)S(1)}, bf16[128,1024]{1,0:T(8,128)(2,1)S(1)}, u32[]{:S(2)}, u32[]{:S(2)}) collective-permute-start(bf16[128,1024]{1,0:T(8,128)(2,1)S(1)} %select_select_fusion), channel_id=1, source_target_pairs={{0,96},{32,0},{64,32},{96,64},{1,97},{33,1},{65,33},{97,65},{2,98}... | collective-permute-start | bytes 786440 | tf_op jit(solution)/shard_map/panel_x/ppermute | solution.py:10
  29.5 3.8 %collective-permute-done.7 = bf16[128,1024]{1,0:T(8,128)(2,1)S(1)} collective-permute-done((bf16[128,1024]{1,0:T(8,128)(2,1)S(1)}, bf16[128,1024]{1,0:T(8,128)(2,1)S(1)}, u32[]{:S(2)}, u32[]{:S(2)}) %collective-permute-start.7) | collective-permute-done | bytes 262176 | tf_op jit(solution)/shard_map/panel_x/ppermute | solution.py:10
  33.3 8.1 %collective-permute-done.8 = bf16[128,1024]{1,0:T(8,128)(2,1)S(1)} collective-permute-done((bf16[128,1024]{1,0:T(8,128)(2,1)S(1)}, bf16[128,1024]{1,0:T(8,128)(2,1)S(1)}, u32[]{:S(2)}, u32[]{:S(2)}) %collective-permute-start.8) | collective-permute-done | bytes 262176 | tf_op jit(solution)/shard_map/panel_x/ppermute | solution.py:10
  41.4 0.7 fusion.4
  42.1 0.1 fusion.6
  42.2 0.8 collective-permute-start.10
  43.0 1.3 %fusion.26 = f32[512,1024]{1,0:T(8,128)S(1)} fusion(bf16[1024,1024]{1,0:T(8,128)(2,1)S(1)} %get-tuple-element.27, bf16[128,1024]{1,0:T(8,128)(2,1)S(1)} %collective-permute-done.9, bf16[128,1024]{1,0:T(8,128)(2,1)S(1)} %collective-permute-done.8, bf16[128,1024]{1,0:T(8,128)(2,1)S(1)} %collective-permute-done.7, bf16[128,1024]{1,0:T(8,128)(2,1)S(1)} %select_select_fusion), kind=kOutput, calls=%fused_computation.81 | convolution fusion | flops 1077936128 | bytes 5242880 | tf_op jit(solution)/shard_map/inverse_factors/dot_general | solution.py:101
  44.3 0.0 collective-permute-done.10
  44.3 0.1 bitcast_add_fusion
  44.5 3.0 %collective-permute-start.11 = (bf16[48,1024]{1,0:T(8,128)(2,1)S(1)}, bf16[48,1024]{1,0:T(8,128)(2,1)S(1)}, u32[]{:S(2)}, u32[]{:S(2)}) collective-permute-start(bf16[48,1024]{1,0:T(8,128)(2,1)S(1)} %get-tuple-element.40), channel_id=1, source_target_pairs={{0,128},{16,144},{128,0},{144,16},{1,129},{17,145},{129,1},{145,17... | collective-permute-start | bytes 294920 | tf_op jit(solution)/shard_map/sum_y/ppermute | solution.py:10
  47.5 0.4 collective-permute-start.12
  47.9 2.3 %collective-permute-start.13 = (bf16[48,1024]{1,0:T(8,128)(2,1)S(1)}, bf16[48,1024]{1,0:T(8,128)(2,1)S(1)}, u32[]{:S(2)}, u32[]{:S(2)}) collective-permute-start(bf16[48,1024]{1,0:T(8,128)(2,1)S(1)} %get-tuple-element.41), channel_id=1, source_target_pairs={{0,144},{16,0},{128,16},{144,128},{1,145},{17,1},{129,17},{145,129... | collective-permute-start | bytes 294920 | tf_op jit(solution)/shard_map/sum_y/ppermute | solution.py:10
  50.2 1.4 %fusion.1 = (bf16[512,1024]{1,0:T(8,128)(2,1)S(1)}, bf16[512,1024]{1,0:T(8,128)(2,1)S(1)}) fusion(f32[512,1024]{1,0:T(8,128)S(1)} %fusion.26, bf16[1024,1024]{1,0:T(8,128)(2,1)S(1)} %get-tuple-element.26, bf16[128,1024]{1,0:T(8,128)(2,1)S(1)} %collective-permute-done.9, bf16[128,1024]{1,0:T(8,128)(2,1)S(1)} %collective-permute-done.8, ...), kind=kOutput, calls=%fused_computation.5 | convolution fusion | flops 1080557568 | bytes 7340032 | tf_op jit(solution)/shard_map/inverse_factors/dot_general | solution.py:101
  51.5 0.6 collective-permute-done.12
  52.2 0.4 collective-permute-done.13
  52.5 0.1 fusion.7
  52.7 1.6 %collective-permute-start.14 = (bf16[48,1024]{1,0:T(8,128)(2,1)S(1)}, bf16[48,1024]{1,0:T(8,128)(2,1)S(1)}, u32[]{:S(2)}, u32[]{:S(2)}) collective-permute-start(bf16[48,1024]{1,0:T(8,128)(2,1)S(1)} %get-tuple-element.39), channel_id=1, source_target_pairs={{0,128},{16,144},{128,0},{144,16},{1,129},{17,145},{129,1},{145,17... | collective-permute-start | bytes 294920 | tf_op jit(solution)/shard_map/gather_y/ppermute | solution.py:10
  54.2 1.5 %collective-permute-start.15 = (bf16[48,1024]{1,0:T(8,128)(2,1)S(1)}, bf16[48,1024]{1,0:T(8,128)(2,1)S(1)}, u32[]{:S(2)}, u32[]{:S(2)}) collective-permute-start(bf16[48,1024]{1,0:T(8,128)(2,1)S(1)} %get-tuple-element.39), channel_id=1, source_target_pairs={{0,16},{16,128},{128,144},{144,0},{1,17},{17,129},{129,145},{145,1... | collective-permute-start | bytes 294920 | tf_op jit(solution)/shard_map/gather_y/ppermute | solution.py:10
  55.8 1.2 %collective-permute-start.16 = (bf16[48,1024]{1,0:T(8,128)(2,1)S(1)}, bf16[48,1024]{1,0:T(8,128)(2,1)S(1)}, u32[]{:S(2)}, u32[]{:S(2)}) collective-permute-start(bf16[48,1024]{1,0:T(8,128)(2,1)S(1)} %get-tuple-element.39), channel_id=1, source_target_pairs={{0,144},{16,0},{128,16},{144,128},{1,145},{17,1},{129,17},{145,129... | collective-permute-start | bytes 294920 | tf_op jit(solution)/shard_map/gather_y/ppermute | solution.py:10
  56.9 0.5 fusion.8
  57.4 1.2 %convolution_add_fusion.2 = f32[48,1024]{1,0:T(8,128)} fusion(bf16[48,1024]{1,0:T(8,128)(2,1)S(1)} %get-tuple-element.39, bf16[1024,1024]{1,0:T(8,128)(2,1)S(1)} %get-tuple-element.27, f32[96,1024]{1,0:T(8,128)S(1)} %fusion.8), kind=kOutput, calls=%fused_computation.11 | convolution fusion | flops 100761600 | bytes 2785280 | tf_op jit(solution)/shard_map/screen/dot_general | solution.py:115
  58.6 1.3 %collective-permute-done.15 = bf16[48,1024]{1,0:T(8,128)(2,1)S(1)} collective-permute-done((bf16[48,1024]{1,0:T(8,128)(2,1)S(1)}, bf16[48,1024]{1,0:T(8,128)(2,1)S(1)}, u32[]{:S(2)}, u32[]{:S(2)}) %collective-permute-start.15) | collective-permute-done | bytes 98336 | tf_op jit(solution)/shard_map/gather_y/ppermute | solution.py:10
  59.9 3.2 %collective-permute-start.17 = (bf16[192,1024]{1,0:T(8,128)(2,1)S(1)}, bf16[192,1024]{1,0:T(8,128)(2,1)S(1)}, u32[]{:S(2)}, u32[]{:S(2)}) collective-permute-start(bf16[192,1024]{1,0:T(8,128)(2,1)S(1)} %pad_maximum_fusion.1), channel_id=1, source_target_pairs={{0,8},{8,0},{1,9},{9,1},{2,10},{10,2},{3,11},{11,3},{4,12},{12,4},... | collective-permute-start | bytes 1179656 | tf_op jit(solution)/shard_map/gather_y/ppermute | solution.py:18
  63.1 1.3 %collective-permute-done.17 = bf16[192,1024]{1,0:T(8,128)(2,1)S(1)} collective-permute-done((bf16[192,1024]{1,0:T(8,128)(2,1)S(1)}, bf16[192,1024]{1,0:T(8,128)(2,1)S(1)}, u32[]{:S(2)}, u32[]{:S(2)}) %collective-permute-start.17) | collective-permute-done | bytes 393248 | tf_op jit(solution)/shard_map/gather_y/ppermute | solution.py:18
  64.4 0.6 fusion.28
  65.0 0.7 fusion.3
  65.7 0.1 select_add_fusion
  65.8 14.1 %all_to_all.9 = f32[32,1,128]{2,1,0:T(1,128)S(1)} all-to-all(f32[32,1,128]{2,1,0:T(1,128)S(1)} %bitcast.66), channel_id=1, replica_groups=mesh['grp'=2,'x'=4,'ylo'=2,'core'=2,'col'=8] {'x','col'}, dimensions={0} | all-to-all | bytes 32768 | tf_op jit(solution)/shard_map/sigma/all_to_all | solution.py:143
  79.9 0.6 reduce_sum.29
  (40 shorter events, 0.6 us)
Async XLA Ops:
  0.6 19.0 %copy-start = (bf16[128,1536]{1,0:T(8,128)(2,1)S(1)}, bf16[128,1536]{1,0:T(8,128)(2,1)}, u32[]{:S(2)}) copy-start(bf16[128,1536]{1,0:T(8,128)(2,1)} %param.3) | copy-start | bytes 1179652
  1.7 17.9 %collective-permute-start = (bf16[128,1024]{1,0:T(8,128)(2,1)S(1)}, bf16[128,1024]{1,0:T(8,128)(2,1)S(1)}, u32[]{:S(2)}, u32[]{:S(2)}) collective-permute-start(bf16[128,1024]{1,0:T(8,128)(2,1)S(1)} %slice.31), channel_id=1, source_target_pairs={{0,3},{8,11},{16,19},{24,27},{32,35},{40,43},{48,51},{56,59},{64,6... | collective-permute-start | bytes 786440 | tf_op jit(solution)/shard_map/panel_z/ppermute | solution.py:14
  8.8 10.8 %collective-permute-start.1 = (bf16[128,1024]{1,0:T(8,128)(2,1)S(1)}, bf16[128,1024]{1,0:T(8,128)(2,1)S(1)}, u32[]{:S(2)}, u32[]{:S(2)}) collective-permute-start(bf16[128,1024]{1,0:T(8,128)(2,1)S(1)} %slice.31), channel_id=1, source_target_pairs={{0,6},{8,14},{16,22},{24,30},{32,38},{40,46},{48,54},{56,62},{64,7... | collective-permute-start | bytes 786440 | tf_op jit(solution)/shard_map/panel_z/ppermute | solution.py:14
  13.3 12.1 %collective-permute-start.4 = (bf16[400,128]{1,0:T(8,128)(2,1)S(1)}, bf16[400,128]{1,0:T(8,128)(2,1)S(1)}, u32[]{:S(2)}, u32[]{:S(2)}) collective-permute-start(bf16[400,128]{1,0:T(8,128)(2,1)S(1)} %concatenate.36), channel_id=1, source_target_pairs={{0,64},{32,96},{64,0},{96,32},{1,65},{33,97},{65,1},{97,33},{2,66}... | collective-permute-start | bytes 307208 | tf_op jit(solution)/shard_map/blocks/ppermute | solution.py:10
  16.3 9.1 %collective-permute-start.5 = (bf16[400,128]{1,0:T(8,128)(2,1)S(1)}, bf16[400,128]{1,0:T(8,128)(2,1)S(1)}, u32[]{:S(2)}, u32[]{:S(2)}) collective-permute-start(bf16[400,128]{1,0:T(8,128)(2,1)S(1)} %concatenate.37), channel_id=1, source_target_pairs={{0,32},{32,64},{64,96},{96,0},{1,33},{33,65},{65,97},{97,1},{2,34}... | collective-permute-start | bytes 307208 | tf_op jit(solution)/shard_map/blocks/ppermute | solution.py:10
  16.9 8.6 %collective-permute-start.6 = (bf16[400,128]{1,0:T(8,128)(2,1)S(1)}, bf16[400,128]{1,0:T(8,128)(2,1)S(1)}, u32[]{:S(2)}, u32[]{:S(2)}) collective-permute-start(bf16[400,128]{1,0:T(8,128)(2,1)S(1)} %concatenate.38), channel_id=1, source_target_pairs={{0,96},{32,0},{64,32},{96,64},{1,97},{33,1},{65,33},{97,65},{2,98}... | collective-permute-start | bytes 307208 | tf_op jit(solution)/shard_map/blocks/ppermute | solution.py:10
  19.7 5.8 %collective-permute-start.2 = (bf16[128,1024]{1,0:T(8,128)(2,1)S(1)}, bf16[128,1024]{1,0:T(8,128)(2,1)S(1)}, u32[]{:S(2)}, u32[]{:S(2)}) collective-permute-start(bf16[128,1024]{1,0:T(8,128)(2,1)S(1)} %select_select_fusion.1), channel_id=1, source_target_pairs={{0,7},{3,4},{6,5},{8,15},{11,12},{14,13},{16,23},{19,20},{22,21},{... | collective-permute-start | bytes 786440 | tf_op jit(solution)/shard_map/panel_z/ppermute | solution.py:14
  21.0 5.4 %collective-permute-start.3 = (bf16[128,1024]{1,0:T(8,128)(2,1)S(1)}, bf16[128,1024]{1,0:T(8,128)(2,1)S(1)}, u32[]{:S(2)}, u32[]{:S(2)}) collective-permute-start(bf16[128,1024]{1,0:T(8,128)(2,1)S(1)} %select_select_fusion.1), channel_id=1, source_target_pairs={{0,1},{3,2},{8,9},{11,10},{16,17},{19,18},{24,25},{27,26},{32,33},... | collective-permute-start | bytes 786440 | tf_op jit(solution)/shard_map/panel_z/ppermute | solution.py:14
  26.4 6.9 %collective-permute-start.7 = (bf16[128,1024]{1,0:T(8,128)(2,1)S(1)}, bf16[128,1024]{1,0:T(8,128)(2,1)S(1)}, u32[]{:S(2)}, u32[]{:S(2)}) collective-permute-start(bf16[128,1024]{1,0:T(8,128)(2,1)S(1)} %select_select_fusion), channel_id=1, source_target_pairs={{0,64},{32,96},{64,0},{96,32},{1,65},{33,97},{65,1},{97,33},{2,66}... | collective-permute-start | bytes 786440 | tf_op jit(solution)/shard_map/panel_x/ppermute | solution.py:10
  26.5 14.9 %collective-permute-start.8 = (bf16[128,1024]{1,0:T(8,128)(2,1)S(1)}, bf16[128,1024]{1,0:T(8,128)(2,1)S(1)}, u32[]{:S(2)}, u32[]{:S(2)}) collective-permute-start(bf16[128,1024]{1,0:T(8,128)(2,1)S(1)} %select_select_fusion), channel_id=1, source_target_pairs={{0,32},{32,64},{64,96},{96,0},{1,33},{33,65},{65,97},{97,1},{2,34}... | collective-permute-start | bytes 786440 | tf_op jit(solution)/shard_map/panel_x/ppermute | solution.py:10
  27.5 13.9 %collective-permute-start.9 = (bf16[128,1024]{1,0:T(8,128)(2,1)S(1)}, bf16[128,1024]{1,0:T(8,128)(2,1)S(1)}, u32[]{:S(2)}, u32[]{:S(2)}) collective-permute-start(bf16[128,1024]{1,0:T(8,128)(2,1)S(1)} %select_select_fusion), channel_id=1, source_target_pairs={{0,96},{32,0},{64,32},{96,64},{1,97},{33,1},{65,33},{97,65},{2,98}... | collective-permute-start | bytes 786440 | tf_op jit(solution)/shard_map/panel_x/ppermute | solution.py:10
  42.2 2.1 %collective-permute-start.10 = (bf16[4,48,1024]{2,1,0:T(8,128)(2,1)S(1)}, bf16[4,48,1024]{2,1,0:T(8,128)(2,1)S(1)}, u32[]{:S(2)}, u32[]{:S(2)}) collective-permute-start(bf16[4,48,1024]{2,1,0:T(8,128)(2,1)S(1)} %fusion.6), channel_id=1, source_target_pairs={{0,8},{8,0},{1,9},{9,1},{2,10},{10,2},{3,11},{11,3},{4,12},{12,4},... | collective-permute-start | bytes 1179656 | tf_op jit(solution)/shard_map/sum_core/ppermute | solution.py:18
  44.5 7.0 %collective-permute-start.11 = (bf16[48,1024]{1,0:T(8,128)(2,1)S(1)}, bf16[48,1024]{1,0:T(8,128)(2,1)S(1)}, u32[]{:S(2)}, u32[]{:S(2)}) collective-permute-start(bf16[48,1024]{1,0:T(8,128)(2,1)S(1)} %get-tuple-element.40), channel_id=1, source_target_pairs={{0,128},{16,144},{128,0},{144,16},{1,129},{17,145},{129,1},{145,17... | collective-permute-start | bytes 294920 | tf_op jit(solution)/shard_map/sum_y/ppermute | solution.py:10
  47.5 4.7 %collective-permute-start.12 = (bf16[48,1024]{1,0:T(8,128)(2,1)S(1)}, bf16[48,1024]{1,0:T(8,128)(2,1)S(1)}, u32[]{:S(2)}, u32[]{:S(2)}) collective-permute-start(bf16[48,1024]{1,0:T(8,128)(2,1)S(1)} %get-tuple-element.42), channel_id=1, source_target_pairs={{0,16},{16,128},{128,144},{144,0},{1,17},{17,129},{129,145},{145,1... | collective-permute-start | bytes 294920 | tf_op jit(solution)/shard_map/sum_y/ppermute | solution.py:10
  47.9 4.6 %collective-permute-start.13 = (bf16[48,1024]{1,0:T(8,128)(2,1)S(1)}, bf16[48,1024]{1,0:T(8,128)(2,1)S(1)}, u32[]{:S(2)}, u32[]{:S(2)}) collective-permute-start(bf16[48,1024]{1,0:T(8,128)(2,1)S(1)} %get-tuple-element.41), channel_id=1, source_target_pairs={{0,144},{16,0},{128,16},{144,128},{1,145},{17,1},{129,17},{145,129... | collective-permute-start | bytes 294920 | tf_op jit(solution)/shard_map/sum_y/ppermute | solution.py:10
  52.7 5.9 %collective-permute-start.14 = (bf16[48,1024]{1,0:T(8,128)(2,1)S(1)}, bf16[48,1024]{1,0:T(8,128)(2,1)S(1)}, u32[]{:S(2)}, u32[]{:S(2)}) collective-permute-start(bf16[48,1024]{1,0:T(8,128)(2,1)S(1)} %get-tuple-element.39), channel_id=1, source_target_pairs={{0,128},{16,144},{128,0},{144,16},{1,129},{17,145},{129,1},{145,17... | collective-permute-start | bytes 294920 | tf_op jit(solution)/shard_map/gather_y/ppermute | solution.py:10
  54.2 5.6 %collective-permute-start.15 = (bf16[48,1024]{1,0:T(8,128)(2,1)S(1)}, bf16[48,1024]{1,0:T(8,128)(2,1)S(1)}, u32[]{:S(2)}, u32[]{:S(2)}) collective-permute-start(bf16[48,1024]{1,0:T(8,128)(2,1)S(1)} %get-tuple-element.39), channel_id=1, source_target_pairs={{0,16},{16,128},{128,144},{144,0},{1,17},{17,129},{129,145},{145,1... | collective-permute-start | bytes 294920 | tf_op jit(solution)/shard_map/gather_y/ppermute | solution.py:10
  55.8 4.1 %collective-permute-start.16 = (bf16[48,1024]{1,0:T(8,128)(2,1)S(1)}, bf16[48,1024]{1,0:T(8,128)(2,1)S(1)}, u32[]{:S(2)}, u32[]{:S(2)}) collective-permute-start(bf16[48,1024]{1,0:T(8,128)(2,1)S(1)} %get-tuple-element.39), channel_id=1, source_target_pairs={{0,144},{16,0},{128,16},{144,128},{1,145},{17,1},{129,17},{145,129... | collective-permute-start | bytes 294920 | tf_op jit(solution)/shard_map/gather_y/ppermute | solution.py:10
  59.9 4.5 %collective-permute-start.17 = (bf16[192,1024]{1,0:T(8,128)(2,1)S(1)}, bf16[192,1024]{1,0:T(8,128)(2,1)S(1)}, u32[]{:S(2)}, u32[]{:S(2)}) collective-permute-start(bf16[192,1024]{1,0:T(8,128)(2,1)S(1)} %pad_maximum_fusion.1), channel_id=1, source_target_pairs={{0,8},{8,0},{1,9},{9,1},{2,10},{10,2},{3,11},{11,3},{4,12},{12,4},... | collective-permute-start | bytes 1179656 | tf_op jit(solution)/shard_map/gather_y/ppermute | solution.py:18

commit v14 on v12

--- a/solution.py
+++ b/solution.py
@@ -74,20 +74,24 @@
         held = jnp.where((z == 1) | (z == 2), near_b, held)
 
     with jax.named_scope("panel_x"):
-        panels = [held] + [shift(held, X, nx, k) for k in steps[1:]]
-        panels = jnp.concatenate(panels, axis=0)
+        blocks = [held] + [shift(held, X, nx, k) for k in steps[1:]]
+        panels = jnp.concatenate(blocks, axis=0)
 
     with jax.named_scope("response"):
         factors = jnp.concatenate(factors, axis=1)
         weight = jnp.sum(factors[-16:-13].astype(F32), axis=0)
         factors = factors[:-16]
         weighted = (weight[:, None] * panels.astype(F32)).astype(LOW)
-        part = jnp.dot(factors, weighted, preferred_element_type=F32)
-
-    with jax.named_scope("sum_core"):
-        part = part.reshape(ny, 2, count, panel)
-        sent = lax.dynamic_index_in_dim(part, 1 - core, 1, False).astype(LOW)
-        kept = lax.dynamic_index_in_dim(part, core, 1, False) + swap(sent).astype(F32)
+        by_core = factors.reshape(ny, 2, count, -1)
+        theirs, mine = (
+            lax.dynamic_index_in_dim(by_core, c, 1, False).reshape(ny * count, -1)
+            for c in (1 - core, core)
+        )
+        sent = jnp.dot(theirs, weighted, preferred_element_type=F32).astype(LOW)
+        kept = jnp.dot(mine, weighted, preferred_element_type=F32)
+        kept, sent = lax.optimization_barrier((kept, swap(sent)))
+        kept = (kept + sent.astype(F32)).reshape(ny, count, panel)
+        kept, *blocks = lax.optimization_barrier((kept, *blocks))
 
     with jax.named_scope("sum_y"):
         total = lax.dynamic_index_in_dim(kept, y, 0, False)
@@ -96,10 +100,12 @@
             total = total + shift(piece, Y, ny, k).astype(F32)
 
     with jax.named_scope("inverse_factors"):
+        panels = jnp.concatenate(blocks, axis=0)
         inverse_factors = sum(
             lax.dot_general(panels, part, (((1,), (1,)), ((), ())), preferred_element_type=F32)
             for part in (inv_high, inv_rest)
-        ).astype(LOW)
+        )
+        inverse_factors = jnp.concatenate(two_parts(inverse_factors), axis=0)
 
     with jax.named_scope("screen"):
         place = z * width + lax.axis_index(PLANE) * count
@@ -114,7 +120,9 @@
 
     with jax.named_scope("gather_y"):
         gathered = jnp.concatenate([high] + [shift(high, Y, ny, k) for k in steps[1:]], axis=0)
-        gathered, inverse_factors = lax.optimization_barrier((gathered, inverse_factors))
+        gathered, inverse_factors, screened = lax.optimization_barrier(
+            (gathered, inverse_factors, screened)
+        )
         gathered = jnp.concatenate([gathered, swap(gathered)], axis=0)
         by_y = factors.reshape(ny, 2, count, -1)
         ordered = jnp.concatenate(
@@ -129,7 +137,9 @@
         products = lax.dot_general(
             gathered, inverse_factors, (((1,), (1,)), ((), ())), preferred_element_type=F32
         )
-        local = -jnp.sum(products * ordered.astype(F32), axis=0).reshape(nx, own)
+        ordered = jnp.concatenate([ordered, ordered], axis=1).astype(F32)
+        local = -jnp.sum(products * ordered, axis=0).reshape(2, nx, own)
+        local = local[0] + local[1]
         back = (x - lax.iota(jnp.int32, nx)) % nx
         by_x = sum(
             jnp.where((back == k)[:, None], local[i][None], 0.0) for i, k in enumerate(steps)

time: 85.1 us -> 80.3 us (0.944)
  blocking collectives: 0 us -> 14.1 us
  starting transfers between devices: 44 us -> 33.6 us
  waiting for transfers between devices: 25.7 us -> 16.6 us
    all_to_all x0 -> x1, blocking collectives: none -> 14.1 us  [body(): terms = lax.all_to_all(copies, (X, Z), 0, 0, tiled=True)]
    all_to_all x1 -> x0, waiting for transfers between devices: 7.47 us -> none  [body(): terms = lax.all_to_all(copies, (X, Z), 0, 0, tiled=True)]
    all_to_all x1 -> x0, starting transfers between devices: 7.11 us -> none  [body(): terms = lax.all_to_all(copies, (X, Z), 0, 0, tiled=True)]
    ppermute x2, starting transfers between devices: 7.63 us -> 3.67 us  [swap(): return lax.ppermute(value, CORE, [(0, 1), (1, 0)])]
    ppermute x12, waiting for transfers between devices: 14.9 us -> 13.5 us  [shift(): lax.ppermute(value, axis, [(i, (i + step) % size) for i in range(size)])]
    ppermute x12, starting transfers between devices: 16.5 us -> 17.8 us  [shift(): lax.ppermute(value, axis, [(i, (i + step) % size) for i in range(size)])]
  transfers between devices with their start and end apart: 19 -> 18, of which waited for: 10 -> 6; matrix products, arithmetic and copies ran while one was open for 12% -> 14% of each run, Pallas kernels for 0% -> 0%
where the time goes in v14:
time: 80.3 us; the launch traced here: 80 us
  starting transfers between devices  33.6 us (42%)
  waiting for transfers between devices  16.6 us (21%)
  blocking collectives  14.1 us (18%)
  matrix products  6.08 us (8%)
  other arithmetic  5.21 us (6%)
  local copies, waits for them, and re-layouts  3.31 us (4%)
  between operations  1.19 us (1%)
    ppermute x12, starting transfers between devices, shift(): lax.ppermute(value, axis, [(i, (i + step) % size) for i in range(size)])  17.8 us
    all_to_all x1, blocking collectives, body(): terms = lax.all_to_all(copies, (X, Z), 0, 0, tiled=True)  14.1 us
    ppermute x12, waiting for transfers between devices, shift(): lax.ppermute(value, axis, [(i, (i + step) % size) for i in range(size)])  13.5 us
    ppermute x4, starting transfers between devices, along_z(): return lax.ppermute(value, Z, pairs)  12.1 us
    ppermute x2, starting transfers between devices, swap(): return lax.ppermute(value, CORE, [(0, 1), (1, 0)])  3.67 us
    convert_element_type x2, other arithmetic, two_parts(): return (high.astype(LOW), (value - high).astype(LOW))  3.22 us
    dot_general x2, matrix products, body(): lax.dot_general(panels, part, (((1,), (1,)), ((), ())), preferred_element...  2.63 us
    ppermute x2, waiting for transfers between devices, swap(): return lax.ppermute(value, CORE, [(0, 1), (1, 0)])  2.25 us
  transfers between devices with their start and end apart: 18, of which 6 were waited for; matrix products, arithmetic and copies ran while one was open for 14% of the time, Pallas kernels for 0%

profile of v14, /device:TPU:1, one launch (start us, length us, event | category | flops | bytes accessed | tf_op | source)
XLA Modules:
  0.0 80.0 jit_solution(13516735700096703111)
XLA Ops:
  0.6 0.0 copy-start
  0.6 1.0 %slice.39 = bf16[128,1024]{1,0:T(8,128)(2,1)S(1)} slice(bf16[128,1536]{1,0:T(8,128)(2,1)} %param.3), slice={[0:128], [0:1024]} | slice | bytes 524288 | tf_op jit(solution)/shard_map/panel_z/slice | solution.py:44
  1.7 7.1 %collective-permute-start = (bf16[128,1024]{1,0:T(8,128)(2,1)S(1)}, bf16[128,1024]{1,0:T(8,128)(2,1)S(1)}, u32[]{:S(2)}, u32[]{:S(2)}) collective-permute-start(bf16[128,1024]{1,0:T(8,128)(2,1)S(1)} %slice.39), channel_id=1, source_target_pairs={{0,3},{8,11},{16,19},{24,27},{32,35},{40,43},{48,51},{56,59},{64,6... | collective-permute-start | bytes 786440 | tf_op jit(solution)/shard_map/panel_z/ppermute | solution.py:14
  8.8 2.4 %collective-permute-start.1 = (bf16[128,1024]{1,0:T(8,128)(2,1)S(1)}, bf16[128,1024]{1,0:T(8,128)(2,1)S(1)}, u32[]{:S(2)}, u32[]{:S(2)}) collective-permute-start(bf16[128,1024]{1,0:T(8,128)(2,1)S(1)} %slice.39), channel_id=1, source_target_pairs={{0,6},{8,14},{16,22},{24,30},{32,38},{40,46},{48,54},{56,62},{64,7... | collective-permute-start | bytes 786440 | tf_op jit(solution)/shard_map/panel_z/ppermute | solution.py:14
  11.2 1.2 %copy.18 = bf16[128,1536]{0,1:T(8,128)(2,1)S(1)} copy(bf16[128,1536]{1,0:T(8,128)(2,1)} %param.3) | data formatting | bytes 786432 | tf_op args[0]
  12.4 0.7 fusion.20
  13.2 0.2 concatenate.45
  13.3 2.8 %collective-permute-start.4 = (bf16[400,128]{1,0:T(8,128)(2,1)S(1)}, bf16[400,128]{1,0:T(8,128)(2,1)S(1)}, u32[]{:S(2)}, u32[]{:S(2)}) collective-permute-start(bf16[400,128]{1,0:T(8,128)(2,1)S(1)} %concatenate.45), channel_id=1, source_target_pairs={{0,64},{32,96},{64,0},{96,32},{1,65},{33,97},{65,1},{97,33},{2,66}... | collective-permute-start | bytes 307208 | tf_op jit(solution)/shard_map/blocks/ppermute | solution.py:10
  16.2 0.2 concatenate.46
  16.3 0.4 collective-permute-start.5
  16.7 0.2 concatenate.47
  16.9 2.4 %collective-permute-start.6 = (bf16[400,128]{1,0:T(8,128)(2,1)S(1)}, bf16[400,128]{1,0:T(8,128)(2,1)S(1)}, u32[]{:S(2)}, u32[]{:S(2)}) collective-permute-start(bf16[400,128]{1,0:T(8,128)(2,1)S(1)} %concatenate.47), channel_id=1, source_target_pairs={{0,96},{32,0},{64,32},{96,64},{1,97},{33,1},{65,33},{97,65},{2,98}... | collective-permute-start | bytes 307208 | tf_op jit(solution)/shard_map/blocks/ppermute | solution.py:10
  19.3 0.2 concatenate.44
  19.6 0.0 collective-permute-done.1
  19.7 1.3 %collective-permute-start.2 = (bf16[128,1024]{1,0:T(8,128)(2,1)S(1)}, bf16[128,1024]{1,0:T(8,128)(2,1)S(1)}, u32[]{:S(2)}, u32[]{:S(2)}) collective-permute-start(bf16[128,1024]{1,0:T(8,128)(2,1)S(1)} %select_select_fusion.1), channel_id=1, source_target_pairs={{0,7},{3,4},{6,5},{8,15},{11,12},{14,13},{16,23},{19,20},{22,21},{... | collective-permute-start | bytes 786440 | tf_op jit(solution)/shard_map/panel_z/ppermute | solution.py:14
  21.0 1.3 %collective-permute-start.3 = (bf16[128,1024]{1,0:T(8,128)(2,1)S(1)}, bf16[128,1024]{1,0:T(8,128)(2,1)S(1)}, u32[]{:S(2)}, u32[]{:S(2)}) collective-permute-start(bf16[128,1024]{1,0:T(8,128)(2,1)S(1)} %select_select_fusion.1), channel_id=1, source_target_pairs={{0,1},{3,2},{8,9},{11,10},{16,17},{19,18},{24,25},{27,26},{32,33},... | collective-permute-start | bytes 786440 | tf_op jit(solution)/shard_map/panel_z/ppermute | solution.py:14
  22.3 3.1 %fusion = (bf16[1024,1024]{1,0:T(8,128)(2,1)S(1)}, bf16[1024,1024]{1,0:T(8,128)(2,1)S(1)}) fusion(f32[1024,1024]{1,0:T(8,128)} %param.5), kind=kLoop, calls=%fused_computation.2 | loop fusion | flops 4194304 | bytes 8388608 | tf_op jit(solution)/shard_map/panel_z/convert_element_type | solution.py:32
  25.5 0.9 %collective-permute-done.3 = bf16[128,1024]{1,0:T(8,128)(2,1)S(1)} collective-permute-done((bf16[128,1024]{1,0:T(8,128)(2,1)S(1)}, bf16[128,1024]{1,0:T(8,128)(2,1)S(1)}, u32[]{:S(2)}, u32[]{:S(2)}) %collective-permute-start.3) | collective-permute-done | bytes 262176 | tf_op jit(solution)/shard_map/panel_z/ppermute | solution.py:14
  26.4 0.1 collective-permute-start.7
  26.5 1.0 %collective-permute-start.8 = (bf16[128,1024]{1,0:T(8,128)(2,1)S(1)}, bf16[128,1024]{1,0:T(8,128)(2,1)S(1)}, u32[]{:S(2)}, u32[]{:S(2)}) collective-permute-start(bf16[128,1024]{1,0:T(8,128)(2,1)S(1)} %select_select_fusion), channel_id=1, source_target_pairs={{0,32},{32,64},{64,96},{96,0},{1,33},{33,65},{65,97},{97,1},{2,34}... | collective-permute-start | bytes 786440 | tf_op jit(solution)/shard_map/panel_x/ppermute | solution.py:10
  27.5 1.7 %collective-permute-start.9 = (bf16[128,1024]{1,0:T(8,128)(2,1)S(1)}, bf16[128,1024]{1,0:T(8,128)(2,1)S(1)}, u32[]{:S(2)}, u32[]{:S(2)}) collective-permute-start(bf16[128,1024]{1,0:T(8,128)(2,1)S(1)} %select_select_fusion), channel_id=1, source_target_pairs={{0,96},{32,0},{64,32},{96,64},{1,97},{33,1},{65,33},{97,65},{2,98}... | collective-permute-start | bytes 786440 | tf_op jit(solution)/shard_map/panel_x/ppermute | solution.py:10
  29.5 3.8 %collective-permute-done.7 = bf16[128,1024]{1,0:T(8,128)(2,1)S(1)} collective-permute-done((bf16[128,1024]{1,0:T(8,128)(2,1)S(1)}, bf16[128,1024]{1,0:T(8,128)(2,1)S(1)}, u32[]{:S(2)}, u32[]{:S(2)}) %collective-permute-start.7) | collective-permute-done | bytes 262176 | tf_op jit(solution)/shard_map/panel_x/ppermute | solution.py:10
  33.3 8.1 %collective-permute-done.8 = bf16[128,1024]{1,0:T(8,128)(2,1)S(1)} collective-permute-done((bf16[128,1024]{1,0:T(8,128)(2,1)S(1)}, bf16[128,1024]{1,0:T(8,128)(2,1)S(1)}, u32[]{:S(2)}, u32[]{:S(2)}) %collective-permute-start.8) | collective-permute-done | bytes 262176 | tf_op jit(solution)/shard_map/panel_x/ppermute | solution.py:10
  41.4 0.2 multiply_convert_fusion
  41.7 0.4 convolution_convert_fusion
  42.1 0.8 collective-permute-start.10
  42.9 0.4 fusion.24
  43.2 1.0 %collective-permute-done.10 = bf16[192,1024]{1,0:T(8,128)(2,1)S(1)} collective-permute-done((bf16[192,1024]{1,0:T(8,128)(2,1)S(1)}, bf16[192,1024]{1,0:T(8,128)(2,1)S(1)}, u32[]{:S(2)}, u32[]{:S(2)}) %collective-permute-start.10) | collective-permute-done | bytes 393248 | tf_op jit(solution)/shard_map/response/ppermute | solution.py:18
  44.2 0.1 convert_add_fusion
  44.4 3.0 %collective-permute-start.11 = (bf16[48,1024]{1,0:T(8,128)(2,1)S(1)}, bf16[48,1024]{1,0:T(8,128)(2,1)S(1)}, u32[]{:S(2)}, u32[]{:S(2)}) collective-permute-start(bf16[48,1024]{1,0:T(8,128)(2,1)S(1)} %get-tuple-element.52), channel_id=1, source_target_pairs={{0,128},{16,144},{128,0},{144,16},{1,129},{17,145},{129,1},{145,17... | collective-permute-start | bytes 294920 | tf_op jit(solution)/shard_map/sum_y/ppermute | solution.py:10
  47.4 0.4 collective-permute-start.12
  47.8 2.3 %collective-permute-start.13 = (bf16[48,1024]{1,0:T(8,128)(2,1)S(1)}, bf16[48,1024]{1,0:T(8,128)(2,1)S(1)}, u32[]{:S(2)}, u32[]{:S(2)}) collective-permute-start(bf16[48,1024]{1,0:T(8,128)(2,1)S(1)} %get-tuple-element.53), channel_id=1, source_target_pairs={{0,144},{16,0},{128,16},{144,128},{1,145},{17,1},{129,17},{145,129... | collective-permute-start | bytes 294920 | tf_op jit(solution)/shard_map/sum_y/ppermute | solution.py:10
  50.1 1.3 %fusion.25 = f32[512,1024]{1,0:T(8,128)S(1)} fusion(bf16[512,1024]{1,0:T(8,128)(2,1)S(1)} %constant_dynamic-update-slice_fusion.4, bf16[1024,1024]{1,0:T(8,128)(2,1)S(1)} %get-tuple-element.40), kind=kOutput, calls=%fused_computation.89 | convolution fusion | flops 1073741824 | bytes 5242880 | tf_op jit(solution)/shard_map/inverse_factors/dot_general | solution.py:105
  51.4 1.3 %reduce-precision_convert_fusion.1 = (bf16[512,1024]{1,0:T(8,128)(2,1)S(1)}, bf16[512,1024]{1,0:T(8,128)(2,1)S(1)}) fusion(f32[512,1024]{1,0:T(8,128)S(1)} %fusion.25, bf16[512,1024]{1,0:T(8,128)(2,1)S(1)} %constant_dynamic-update-slice_fusion.4, bf16[1024,1024]{1,0:T(8,128)(2,1)S(1)} %get-tuple-element.39), kind=kOutput, calls=%fused_computation.4 | convolution fusion | flops 1076363264 | bytes 7340032 | tf_op jit(solution)/shard_map/inverse_factors/dot_general | solution.py:105
  52.8 0.2 pad_maximum_fusion
  53.0 0.1 fusion.5
  53.1 1.0 %collective-permute-start.14 = (bf16[48,1024]{1,0:T(8,128)(2,1)S(1)}, bf16[48,1024]{1,0:T(8,128)(2,1)S(1)}, u32[]{:S(2)}, u32[]{:S(2)}) collective-permute-start(bf16[48,1024]{1,0:T(8,128)(2,1)S(1)} %get-tuple-element.51), channel_id=1, source_target_pairs={{0,128},{16,144},{128,0},{144,16},{1,129},{17,145},{129,1},{145,17... | collective-permute-start | bytes 294920 | tf_op jit(solution)/shard_map/gather_y/ppermute | solution.py:10
  54.1 1.5 %collective-permute-start.15 = (bf16[48,1024]{1,0:T(8,128)(2,1)S(1)}, bf16[48,1024]{1,0:T(8,128)(2,1)S(1)}, u32[]{:S(2)}, u32[]{:S(2)}) collective-permute-start(bf16[48,1024]{1,0:T(8,128)(2,1)S(1)} %get-tuple-element.51), channel_id=1, source_target_pairs={{0,16},{16,128},{128,144},{144,0},{1,17},{17,129},{129,145},{145,1... | collective-permute-start | bytes 294920 | tf_op jit(solution)/shard_map/gather_y/ppermute | solution.py:10
  55.6 1.2 %collective-permute-start.16 = (bf16[48,1024]{1,0:T(8,128)(2,1)S(1)}, bf16[48,1024]{1,0:T(8,128)(2,1)S(1)}, u32[]{:S(2)}, u32[]{:S(2)}) collective-permute-start(bf16[48,1024]{1,0:T(8,128)(2,1)S(1)} %get-tuple-element.51), channel_id=1, source_target_pairs={{0,144},{16,0},{128,16},{144,128},{1,145},{17,1},{129,17},{145,129... | collective-permute-start | bytes 294920 | tf_op jit(solution)/shard_map/gather_y/ppermute | solution.py:10
  56.8 0.5 fusion.6
  57.2 1.2 %convolution_add_fusion.1 = f32[48,1024]{1,0:T(8,128)} fusion(bf16[48,1024]{1,0:T(8,128)(2,1)S(1)} %get-tuple-element.51, bf16[1024,1024]{1,0:T(8,128)(2,1)S(1)} %get-tuple-element.40, f32[96,1024]{1,0:T(8,128)S(1)} %fusion.6), kind=kOutput, calls=%fused_computation.11 | convolution fusion | flops 100761600 | bytes 2785280 | tf_op jit(solution)/shard_map/screen/dot_general | solution.py:119
  58.4 1.5 %collective-permute-done.15 = bf16[48,1024]{1,0:T(8,128)(2,1)S(1)} collective-permute-done((bf16[48,1024]{1,0:T(8,128)(2,1)S(1)}, bf16[48,1024]{1,0:T(8,128)(2,1)S(1)}, u32[]{:S(2)}, u32[]{:S(2)}) %collective-permute-start.15) | collective-permute-done | bytes 98336 | tf_op jit(solution)/shard_map/gather_y/ppermute | solution.py:10
  60.0 2.9 %collective-permute-start.17 = (bf16[192,1024]{1,0:T(8,128)(2,1)S(1)}, bf16[192,1024]{1,0:T(8,128)(2,1)S(1)}, u32[]{:S(2)}, u32[]{:S(2)}) collective-permute-start(bf16[192,1024]{1,0:T(8,128)(2,1)S(1)} %pad_maximum_fusion.1), channel_id=1, source_target_pairs={{0,8},{8,0},{1,9},{9,1},{2,10},{10,2},{3,11},{11,3},{4,12},{12,4},... | collective-permute-start | bytes 1179656 | tf_op jit(solution)/shard_map/gather_y/ppermute | solution.py:18
  62.9 1.3 %collective-permute-done.17 = bf16[192,1024]{1,0:T(8,128)(2,1)S(1)} collective-permute-done((bf16[192,1024]{1,0:T(8,128)(2,1)S(1)}, bf16[192,1024]{1,0:T(8,128)(2,1)S(1)}, u32[]{:S(2)}, u32[]{:S(2)}) %collective-permute-start.17) | collective-permute-done | bytes 393248 | tf_op jit(solution)/shard_map/gather_y/ppermute | solution.py:18
  64.2 1.0 %multiply_reduce_fusion = f32[1024]{0:T(1024)S(1)} fusion(bf16[1024,1024]{1,0:T(8,128)(2,1)S(1)} %pad_maximum_fusion, bf16[192,1024]{1,0:T(8,128)(2,1)S(1)} %collective-permute-done.17, bf16[192,1024]{1,0:T(8,128)(2,1)S(1)} %pad_maximum_fusion.1, bf16[384,512]{1,0:T(8,128)(2,1)S(1)} %bitcast.80), kind=kOutput, calls=%fused_computation.8 | convolution fusion | flops 809237504 | bytes 3280896 | tf_op jit(solution)/shard_map/sigma/dot_general | solution.py:137
  65.3 0.1 select_add_fusion
  65.4 14.1 %all_to_all.9 = f32[32,1,128]{2,1,0:T(1,128)S(1)} all-to-all(f32[32,1,128]{2,1,0:T(1,128)S(1)} %bitcast.79), channel_id=1, replica_groups=mesh['grp'=2,'x'=4,'ylo'=2,'core'=2,'col'=8] {'x','col'}, dimensions={0} | all-to-all | bytes 32768 | tf_op jit(solution)/shard_map/sigma/all_to_all | solution.py:148
  79.5 0.6 reduce_sum.29
  (45 shorter events, 0.6 us)
Async XLA Ops:
  0.6 19.0 %copy-start = (bf16[128,1536]{1,0:T(8,128)(2,1)S(1)}, bf16[128,1536]{1,0:T(8,128)(2,1)}, u32[]{:S(2)}) copy-start(bf16[128,1536]{1,0:T(8,128)(2,1)} %param.3) | copy-start | bytes 1179652
  1.7 17.9 %collective-permute-start = (bf16[128,1024]{1,0:T(8,128)(2,1)S(1)}, bf16[128,1024]{1,0:T(8,128)(2,1)S(1)}, u32[]{:S(2)}, u32[]{:S(2)}) collective-permute-start(bf16[128,1024]{1,0:T(8,128)(2,1)S(1)} %slice.39), channel_id=1, source_target_pairs={{0,3},{8,11},{16,19},{24,27},{32,35},{40,43},{48,51},{56,59},{64,6... | collective-permute-start | bytes 786440 | tf_op jit(solution)/shard_map/panel_z/ppermute | solution.py:14
  8.8 10.8 %collective-permute-start.1 = (bf16[128,1024]{1,0:T(8,128)(2,1)S(1)}, bf16[128,1024]{1,0:T(8,128)(2,1)S(1)}, u32[]{:S(2)}, u32[]{:S(2)}) collective-permute-start(bf16[128,1024]{1,0:T(8,128)(2,1)S(1)} %slice.39), channel_id=1, source_target_pairs={{0,6},{8,14},{16,22},{24,30},{32,38},{40,46},{48,54},{56,62},{64,7... | collective-permute-start | bytes 786440 | tf_op jit(solution)/shard_map/panel_z/ppermute | solution.py:14
  13.3 12.1 %collective-permute-start.4 = (bf16[400,128]{1,0:T(8,128)(2,1)S(1)}, bf16[400,128]{1,0:T(8,128)(2,1)S(1)}, u32[]{:S(2)}, u32[]{:S(2)}) collective-permute-start(bf16[400,128]{1,0:T(8,128)(2,1)S(1)} %concatenate.45), channel_id=1, source_target_pairs={{0,64},{32,96},{64,0},{96,32},{1,65},{33,97},{65,1},{97,33},{2,66}... | collective-permute-start | bytes 307208 | tf_op jit(solution)/shard_map/blocks/ppermute | solution.py:10
  16.3 9.1 %collective-permute-start.5 = (bf16[400,128]{1,0:T(8,128)(2,1)S(1)}, bf16[400,128]{1,0:T(8,128)(2,1)S(1)}, u32[]{:S(2)}, u32[]{:S(2)}) collective-permute-start(bf16[400,128]{1,0:T(8,128)(2,1)S(1)} %concatenate.46), channel_id=1, source_target_pairs={{0,32},{32,64},{64,96},{96,0},{1,33},{33,65},{65,97},{97,1},{2,34}... | collective-permute-start | bytes 307208 | tf_op jit(solution)/shard_map/blocks/ppermute | solution.py:10
  16.9 8.6 %collective-permute-start.6 = (bf16[400,128]{1,0:T(8,128)(2,1)S(1)}, bf16[400,128]{1,0:T(8,128)(2,1)S(1)}, u32[]{:S(2)}, u32[]{:S(2)}) collective-permute-start(bf16[400,128]{1,0:T(8,128)(2,1)S(1)} %concatenate.47), channel_id=1, source_target_pairs={{0,96},{32,0},{64,32},{96,64},{1,97},{33,1},{65,33},{97,65},{2,98}... | collective-permute-start | bytes 307208 | tf_op jit(solution)/shard_map/blocks/ppermute | solution.py:10
  19.7 5.8 %collective-permute-start.2 = (bf16[128,1024]{1,0:T(8,128)(2,1)S(1)}, bf16[128,1024]{1,0:T(8,128)(2,1)S(1)}, u32[]{:S(2)}, u32[]{:S(2)}) collective-permute-start(bf16[128,1024]{1,0:T(8,128)(2,1)S(1)} %select_select_fusion.1), channel_id=1, source_target_pairs={{0,7},{3,4},{6,5},{8,15},{11,12},{14,13},{16,23},{19,20},{22,21},{... | collective-permute-start | bytes 786440 | tf_op jit(solution)/shard_map/panel_z/ppermute | solution.py:14
  21.0 5.4 %collective-permute-start.3 = (bf16[128,1024]{1,0:T(8,128)(2,1)S(1)}, bf16[128,1024]{1,0:T(8,128)(2,1)S(1)}, u32[]{:S(2)}, u32[]{:S(2)}) collective-permute-start(bf16[128,1024]{1,0:T(8,128)(2,1)S(1)} %select_select_fusion.1), channel_id=1, source_target_pairs={{0,1},{3,2},{8,9},{11,10},{16,17},{19,18},{24,25},{27,26},{32,33},... | collective-permute-start | bytes 786440 | tf_op jit(solution)/shard_map/panel_z/ppermute | solution.py:14
  26.4 6.9 %collective-permute-start.7 = (bf16[128,1024]{1,0:T(8,128)(2,1)S(1)}, bf16[128,1024]{1,0:T(8,128)(2,1)S(1)}, u32[]{:S(2)}, u32[]{:S(2)}) collective-permute-start(bf16[128,1024]{1,0:T(8,128)(2,1)S(1)} %select_select_fusion), channel_id=1, source_target_pairs={{0,64},{32,96},{64,0},{96,32},{1,65},{33,97},{65,1},{97,33},{2,66}... | collective-permute-start | bytes 786440 | tf_op jit(solution)/shard_map/panel_x/ppermute | solution.py:10
  26.5 14.9 %collective-permute-start.8 = (bf16[128,1024]{1,0:T(8,128)(2,1)S(1)}, bf16[128,1024]{1,0:T(8,128)(2,1)S(1)}, u32[]{:S(2)}, u32[]{:S(2)}) collective-permute-start(bf16[128,1024]{1,0:T(8,128)(2,1)S(1)} %select_select_fusion), channel_id=1, source_target_pairs={{0,32},{32,64},{64,96},{96,0},{1,33},{33,65},{65,97},{97,1},{2,34}... | collective-permute-start | bytes 786440 | tf_op jit(solution)/shard_map/panel_x/ppermute | solution.py:10
  27.5 13.9 %collective-permute-start.9 = (bf16[128,1024]{1,0:T(8,128)(2,1)S(1)}, bf16[128,1024]{1,0:T(8,128)(2,1)S(1)}, u32[]{:S(2)}, u32[]{:S(2)}) collective-permute-start(bf16[128,1024]{1,0:T(8,128)(2,1)S(1)} %select_select_fusion), channel_id=1, source_target_pairs={{0,96},{32,0},{64,32},{96,64},{1,97},{33,1},{65,33},{97,65},{2,98}... | collective-permute-start | bytes 786440 | tf_op jit(solution)/shard_map/panel_x/ppermute | solution.py:10
  42.1 2.1 %collective-permute-start.10 = (bf16[192,1024]{1,0:T(8,128)(2,1)S(1)}, bf16[192,1024]{1,0:T(8,128)(2,1)S(1)}, u32[]{:S(2)}, u32[]{:S(2)}) collective-permute-start(bf16[192,1024]{1,0:T(8,128)(2,1)S(1)} %convolution_convert_fusion), channel_id=1, source_target_pairs={{0,8},{8,0},{1,9},{9,1},{2,10},{10,2},{3,11},{11,3},{4,12},{12,4},... | collective-permute-start | bytes 1179656 | tf_op jit(solution)/shard_map/response/ppermute | solution.py:18
  44.4 8.6 %collective-permute-start.11 = (bf16[48,1024]{1,0:T(8,128)(2,1)S(1)}, bf16[48,1024]{1,0:T(8,128)(2,1)S(1)}, u32[]{:S(2)}, u32[]{:S(2)}) collective-permute-start(bf16[48,1024]{1,0:T(8,128)(2,1)S(1)} %get-tuple-element.52), channel_id=1, source_target_pairs={{0,128},{16,144},{128,0},{144,16},{1,129},{17,145},{129,1},{145,17... | collective-permute-start | bytes 294920 | tf_op jit(solution)/shard_map/sum_y/ppermute | solution.py:10
  47.4 5.6 %collective-permute-start.12 = (bf16[48,1024]{1,0:T(8,128)(2,1)S(1)}, bf16[48,1024]{1,0:T(8,128)(2,1)S(1)}, u32[]{:S(2)}, u32[]{:S(2)}) collective-permute-start(bf16[48,1024]{1,0:T(8,128)(2,1)S(1)} %get-tuple-element.54), channel_id=1, source_target_pairs={{0,16},{16,128},{128,144},{144,0},{1,17},{17,129},{129,145},{145,1... | collective-permute-start | bytes 294920 | tf_op jit(solution)/shard_map/sum_y/ppermute | solution.py:10
  47.8 5.2 %collective-permute-start.13 = (bf16[48,1024]{1,0:T(8,128)(2,1)S(1)}, bf16[48,1024]{1,0:T(8,128)(2,1)S(1)}, u32[]{:S(2)}, u32[]{:S(2)}) collective-permute-start(bf16[48,1024]{1,0:T(8,128)(2,1)S(1)} %get-tuple-element.53), channel_id=1, source_target_pairs={{0,144},{16,0},{128,16},{144,128},{1,145},{17,1},{129,17},{145,129... | collective-permute-start | bytes 294920 | tf_op jit(solution)/shard_map/sum_y/ppermute | solution.py:10
  53.1 5.3 %collective-permute-start.14 = (bf16[48,1024]{1,0:T(8,128)(2,1)S(1)}, bf16[48,1024]{1,0:T(8,128)(2,1)S(1)}, u32[]{:S(2)}, u32[]{:S(2)}) collective-permute-start(bf16[48,1024]{1,0:T(8,128)(2,1)S(1)} %get-tuple-element.51), channel_id=1, source_target_pairs={{0,128},{16,144},{128,0},{144,16},{1,129},{17,145},{129,1},{145,17... | collective-permute-start | bytes 294920 | tf_op jit(solution)/shard_map/gather_y/ppermute | solution.py:10
  54.1 5.9 %collective-permute-start.15 = (bf16[48,1024]{1,0:T(8,128)(2,1)S(1)}, bf16[48,1024]{1,0:T(8,128)(2,1)S(1)}, u32[]{:S(2)}, u32[]{:S(2)}) collective-permute-start(bf16[48,1024]{1,0:T(8,128)(2,1)S(1)} %get-tuple-element.51), channel_id=1, source_target_pairs={{0,16},{16,128},{128,144},{144,0},{1,17},{17,129},{129,145},{145,1... | collective-permute-start | bytes 294920 | tf_op jit(solution)/shard_map/gather_y/ppermute | solution.py:10
  55.6 4.3 %collective-permute-start.16 = (bf16[48,1024]{1,0:T(8,128)(2,1)S(1)}, bf16[48,1024]{1,0:T(8,128)(2,1)S(1)}, u32[]{:S(2)}, u32[]{:S(2)}) collective-permute-start(bf16[48,1024]{1,0:T(8,128)(2,1)S(1)} %get-tuple-element.51), channel_id=1, source_target_pairs={{0,144},{16,0},{128,16},{144,128},{1,145},{17,1},{129,17},{145,129... | collective-permute-start | bytes 294920 | tf_op jit(solution)/shard_map/gather_y/ppermute | solution.py:10
  60.0 4.2 %collective-permute-start.17 = (bf16[192,1024]{1,0:T(8,128)(2,1)S(1)}, bf16[192,1024]{1,0:T(8,128)(2,1)S(1)}, u32[]{:S(2)}, u32[]{:S(2)}) collective-permute-start(bf16[192,1024]{1,0:T(8,128)(2,1)S(1)} %pad_maximum_fusion.1), channel_id=1, source_target_pairs={{0,8},{8,0},{1,9},{9,1},{2,10},{10,2},{3,11},{11,3},{4,12},{12,4},... | collective-permute-start | bytes 1179656 | tf_op jit(solution)/shard_map/gather_y/ppermute | solution.py:18

commit v15 on v14

--- a/solution.py
+++ b/solution.py
@@ -123,22 +123,28 @@
         gathered, inverse_factors, screened = lax.optimization_barrier(
             (gathered, inverse_factors, screened)
         )
-        gathered = jnp.concatenate([gathered, swap(gathered)], axis=0)
         by_y = factors.reshape(ny, 2, count, -1)
-        ordered = jnp.concatenate(
-            [
-                lax.dynamic_slice(by_y, ((y - k) % ny, c, 0, 0), (1, 1, count, nx * own))
-                for c in (core, 1 - core)
-                for k in steps
-            ]
-        ).reshape(-1, nx * own)
+        ordered = [
+            jnp.concatenate(
+                [
+                    lax.dynamic_slice(by_y, ((y - k) % ny, c, 0, 0), (1, 1, count, nx * own))
+                    for k in steps
+                ]
+            ).reshape(-1, nx * own)
+            for c in (core, 1 - core)
+        ]
 
     with jax.named_scope("sigma"):
-        products = lax.dot_general(
-            gathered, inverse_factors, (((1,), (1,)), ((), ())), preferred_element_type=F32
-        )
-        ordered = jnp.concatenate([ordered, ordered], axis=1).astype(F32)
-        local = -jnp.sum(products * ordered, axis=0).reshape(2, nx, own)
+
+        def terms_of(rows, weights):
+            products = lax.dot_general(
+                rows, inverse_factors, (((1,), (1,)), ((), ())), preferred_element_type=F32
+            )
+            weights = jnp.concatenate([weights, weights], axis=1).astype(F32)
+            return jnp.sum(products * weights, axis=0)
+
+        local, other = lax.optimization_barrier((terms_of(gathered, ordered[0]), swap(gathered)))
+        local = -(local + terms_of(other, ordered[1])).reshape(2, nx, own)
         local = local[0] + local[1]
         back = (x - lax.iota(jnp.int32, nx)) % nx
         by_x = sum(

time: 80.3 us -> 80.2 us (level)
    ppermute x2, waiting for transfers between devices: 2.25 us -> 1.35 us  [swap(): return lax.ppermute(value, CORE, [(0, 1), (1, 0)])]
    dot_general x1 -> x2, matrix products: 1.04 us -> 1.73 us  [terms_of(): lax.dot_general(rows, inverse_factors, (((1,), (1,)), ((), ())), preferre...]
  transfers between devices with their start and end apart: 18 -> 18, of which waited for: 6 -> 6; matrix products, arithmetic and copies ran while one was open for 14% -> 15% of each run, Pallas kernels for 0% -> 0%
where the time goes in v15:
time: 80.2 us; the launch traced here: 79.9 us
  starting transfers between devices  33.5 us (42%)
  waiting for transfers between devices  15.8 us (20%)
  blocking collectives  14.1 us (18%)
  matrix products  6.79 us (8%)
  other arithmetic  5.29 us (7%)
  local copies, waits for them, and re-layouts  3.27 us (4%)
  between operations  1.17 us (1%)
    ppermute x12, starting transfers between devices, shift(): lax.ppermute(value, axis, [(i, (i + step) % size) for i in range(size)])  17.8 us
    all_to_all x1, blocking collectives, body(): terms = lax.all_to_all(copies, (X, Z), 0, 0, tiled=True)  14.1 us
    ppermute x12, waiting for transfers between devices, shift(): lax.ppermute(value, axis, [(i, (i + step) % size) for i in range(size)])  13.5 us
    ppermute x4, starting transfers between devices, along_z(): return lax.ppermute(value, Z, pairs)  12.1 us
    ppermute x2, starting transfers between devices, swap(): return lax.ppermute(value, CORE, [(0, 1), (1, 0)])  3.66 us
    convert_element_type x2, other arithmetic, two_parts(): return (high.astype(LOW), (value - high).astype(LOW))  3.22 us
    dot_general x2, matrix products, body(): lax.dot_general(panels, part, (((1,), (1,)), ((), ())), preferred_element...  2.64 us
    dot_general x2, matrix products, terms_of(): lax.dot_general(rows, inverse_factors, (((1,), (1,)), ((), ())), preferre...  1.73 us
  transfers between devices with their start and end apart: 18, of which 6 were waited for; matrix products, arithmetic and copies ran while one was open for 15% of the time, Pallas kernels for 0%

profile of v15, /device:TPU:1, one launch (start us, length us, event | category | flops | bytes accessed | tf_op | source)
XLA Modules:
  0.0 79.9 jit_solution(16247328681882262315)
XLA Ops:
  0.6 0.0 copy-start
  0.6 1.0 %slice.39 = bf16[128,1024]{1,0:T(8,128)(2,1)S(1)} slice(bf16[128,1536]{1,0:T(8,128)(2,1)} %param.3), slice={[0:128], [0:1024]} | slice | bytes 524288 | tf_op jit(solution)/shard_map/panel_z/slice | solution.py:44
  1.7 7.1 %collective-permute-start = (bf16[128,1024]{1,0:T(8,128)(2,1)S(1)}, bf16[128,1024]{1,0:T(8,128)(2,1)S(1)}, u32[]{:S(2)}, u32[]{:S(2)}) collective-permute-start(bf16[128,1024]{1,0:T(8,128)(2,1)S(1)} %slice.39), channel_id=1, source_target_pairs={{0,3},{8,11},{16,19},{24,27},{32,35},{40,43},{48,51},{56,59},{64,6... | collective-permute-start | bytes 786440 | tf_op jit(solution)/shard_map/panel_z/ppermute | solution.py:14
  8.8 2.4 %collective-permute-start.1 = (bf16[128,1024]{1,0:T(8,128)(2,1)S(1)}, bf16[128,1024]{1,0:T(8,128)(2,1)S(1)}, u32[]{:S(2)}, u32[]{:S(2)}) collective-permute-start(bf16[128,1024]{1,0:T(8,128)(2,1)S(1)} %slice.39), channel_id=1, source_target_pairs={{0,6},{8,14},{16,22},{24,30},{32,38},{40,46},{48,54},{56,62},{64,7... | collective-permute-start | bytes 786440 | tf_op jit(solution)/shard_map/panel_z/ppermute | solution.py:14
  11.2 1.2 %copy.18 = bf16[128,1536]{0,1:T(8,128)(2,1)S(1)} copy(bf16[128,1536]{1,0:T(8,128)(2,1)} %param.3) | data formatting | bytes 786432 | tf_op args[0]
  12.4 0.7 fusion.19
  13.2 0.2 concatenate.48
  13.3 2.8 %collective-permute-start.4 = (bf16[400,128]{1,0:T(8,128)(2,1)S(1)}, bf16[400,128]{1,0:T(8,128)(2,1)S(1)}, u32[]{:S(2)}, u32[]{:S(2)}) collective-permute-start(bf16[400,128]{1,0:T(8,128)(2,1)S(1)} %concatenate.48), channel_id=1, source_target_pairs={{0,64},{32,96},{64,0},{96,32},{1,65},{33,97},{65,1},{97,33},{2,66}... | collective-permute-start | bytes 307208 | tf_op jit(solution)/shard_map/blocks/ppermute | solution.py:10
  16.2 0.2 concatenate.49
  16.3 0.4 collective-permute-start.5
  16.7 0.2 concatenate.50
  16.9 2.4 %collective-permute-start.6 = (bf16[400,128]{1,0:T(8,128)(2,1)S(1)}, bf16[400,128]{1,0:T(8,128)(2,1)S(1)}, u32[]{:S(2)}, u32[]{:S(2)}) collective-permute-start(bf16[400,128]{1,0:T(8,128)(2,1)S(1)} %concatenate.50), channel_id=1, source_target_pairs={{0,96},{32,0},{64,32},{96,64},{1,97},{33,1},{65,33},{97,65},{2,98}... | collective-permute-start | bytes 307208 | tf_op jit(solution)/shard_map/blocks/ppermute | solution.py:10
  19.3 0.2 concatenate.47
  19.7 1.3 %collective-permute-start.2 = (bf16[128,1024]{1,0:T(8,128)(2,1)S(1)}, bf16[128,1024]{1,0:T(8,128)(2,1)S(1)}, u32[]{:S(2)}, u32[]{:S(2)}) collective-permute-start(bf16[128,1024]{1,0:T(8,128)(2,1)S(1)} %select_select_fusion.1), channel_id=1, source_target_pairs={{0,7},{3,4},{6,5},{8,15},{11,12},{14,13},{16,23},{19,20},{22,21},{... | collective-permute-start | bytes 786440 | tf_op jit(solution)/shard_map/panel_z/ppermute | solution.py:14
  21.0 1.3 %collective-permute-start.3 = (bf16[128,1024]{1,0:T(8,128)(2,1)S(1)}, bf16[128,1024]{1,0:T(8,128)(2,1)S(1)}, u32[]{:S(2)}, u32[]{:S(2)}) collective-permute-start(bf16[128,1024]{1,0:T(8,128)(2,1)S(1)} %select_select_fusion.1), channel_id=1, source_target_pairs={{0,1},{3,2},{8,9},{11,10},{16,17},{19,18},{24,25},{27,26},{32,33},... | collective-permute-start | bytes 786440 | tf_op jit(solution)/shard_map/panel_z/ppermute | solution.py:14
  22.3 3.1 %fusion = (bf16[1024,1024]{1,0:T(8,128)(2,1)S(1)}, bf16[1024,1024]{1,0:T(8,128)(2,1)S(1)}) fusion(f32[1024,1024]{1,0:T(8,128)} %param.5), kind=kLoop, calls=%fused_computation.2 | loop fusion | flops 4194304 | bytes 8388608 | tf_op jit(solution)/shard_map/panel_z/convert_element_type | solution.py:32
  25.5 0.9 %collective-permute-done.3 = bf16[128,1024]{1,0:T(8,128)(2,1)S(1)} collective-permute-done((bf16[128,1024]{1,0:T(8,128)(2,1)S(1)}, bf16[128,1024]{1,0:T(8,128)(2,1)S(1)}, u32[]{:S(2)}, u32[]{:S(2)}) %collective-permute-start.3) | collective-permute-done | bytes 262176 | tf_op jit(solution)/shard_map/panel_z/ppermute | solution.py:14
  26.4 0.1 collective-permute-start.7
  26.5 1.0 %collective-permute-start.8 = (bf16[128,1024]{1,0:T(8,128)(2,1)S(1)}, bf16[128,1024]{1,0:T(8,128)(2,1)S(1)}, u32[]{:S(2)}, u32[]{:S(2)}) collective-permute-start(bf16[128,1024]{1,0:T(8,128)(2,1)S(1)} %select_select_fusion), channel_id=1, source_target_pairs={{0,32},{32,64},{64,96},{96,0},{1,33},{33,65},{65,97},{97,1},{2,34}... | collective-permute-start | bytes 786440 | tf_op jit(solution)/shard_map/panel_x/ppermute | solution.py:10
  27.5 1.7 %collective-permute-start.9 = (bf16[128,1024]{1,0:T(8,128)(2,1)S(1)}, bf16[128,1024]{1,0:T(8,128)(2,1)S(1)}, u32[]{:S(2)}, u32[]{:S(2)}) collective-permute-start(bf16[128,1024]{1,0:T(8,128)(2,1)S(1)} %select_select_fusion), channel_id=1, source_target_pairs={{0,96},{32,0},{64,32},{96,64},{1,97},{33,1},{65,33},{97,65},{2,98}... | collective-permute-start | bytes 786440 | tf_op jit(solution)/shard_map/panel_x/ppermute | solution.py:10
  29.5 3.8 %collective-permute-done.7 = bf16[128,1024]{1,0:T(8,128)(2,1)S(1)} collective-permute-done((bf16[128,1024]{1,0:T(8,128)(2,1)S(1)}, bf16[128,1024]{1,0:T(8,128)(2,1)S(1)}, u32[]{:S(2)}, u32[]{:S(2)}) %collective-permute-start.7) | collective-permute-done | bytes 262176 | tf_op jit(solution)/shard_map/panel_x/ppermute | solution.py:10
  33.3 8.1 %collective-permute-done.8 = bf16[128,1024]{1,0:T(8,128)(2,1)S(1)} collective-permute-done((bf16[128,1024]{1,0:T(8,128)(2,1)S(1)}, bf16[128,1024]{1,0:T(8,128)(2,1)S(1)}, u32[]{:S(2)}, u32[]{:S(2)}) %collective-permute-start.8) | collective-permute-done | bytes 262176 | tf_op jit(solution)/shard_map/panel_x/ppermute | solution.py:10
  41.4 0.2 multiply_convert_fusion
  41.7 0.4 convolution_convert_fusion
  42.1 0.8 collective-permute-start.10
  42.9 0.4 fusion.22
  43.3 0.9 %collective-permute-done.10 = bf16[192,1024]{1,0:T(8,128)(2,1)S(1)} collective-permute-done((bf16[192,1024]{1,0:T(8,128)(2,1)S(1)}, bf16[192,1024]{1,0:T(8,128)(2,1)S(1)}, u32[]{:S(2)}, u32[]{:S(2)}) %collective-permute-start.10) | collective-permute-done | bytes 393248 | tf_op jit(solution)/shard_map/response/ppermute | solution.py:18
  44.2 0.1 convert_add_fusion
  44.4 3.0 %collective-permute-start.11 = (bf16[48,1024]{1,0:T(8,128)(2,1)S(1)}, bf16[48,1024]{1,0:T(8,128)(2,1)S(1)}, u32[]{:S(2)}, u32[]{:S(2)}) collective-permute-start(bf16[48,1024]{1,0:T(8,128)(2,1)S(1)} %get-tuple-element.56), channel_id=1, source_target_pairs={{0,128},{16,144},{128,0},{144,16},{1,129},{17,145},{129,1},{145,17... | collective-permute-start | bytes 294920 | tf_op jit(solution)/shard_map/sum_y/ppermute | solution.py:10
  47.4 0.4 collective-permute-start.12
  47.8 2.3 %collective-permute-start.13 = (bf16[48,1024]{1,0:T(8,128)(2,1)S(1)}, bf16[48,1024]{1,0:T(8,128)(2,1)S(1)}, u32[]{:S(2)}, u32[]{:S(2)}) collective-permute-start(bf16[48,1024]{1,0:T(8,128)(2,1)S(1)} %get-tuple-element.57), channel_id=1, source_target_pairs={{0,144},{16,0},{128,16},{144,128},{1,145},{17,1},{129,17},{145,129... | collective-permute-start | bytes 294920 | tf_op jit(solution)/shard_map/sum_y/ppermute | solution.py:10
  50.2 1.3 %fusion.23 = f32[512,1024]{1,0:T(8,128)S(1)} fusion(bf16[512,1024]{1,0:T(8,128)(2,1)S(1)} %constant_dynamic-update-slice_fusion.4, bf16[1024,1024]{1,0:T(8,128)(2,1)S(1)} %get-tuple-element.42), kind=kOutput, calls=%fused_computation.91 | convolution fusion | flops 1073741824 | bytes 5242880 | tf_op jit(solution)/shard_map/inverse_factors/dot_general | solution.py:105
  51.5 1.3 %reduce-precision_convert_fusion.1 = (bf16[512,1024]{1,0:T(8,128)(2,1)S(1)}, bf16[512,1024]{1,0:T(8,128)(2,1)S(1)}) fusion(f32[512,1024]{1,0:T(8,128)S(1)} %fusion.23, bf16[512,1024]{1,0:T(8,128)(2,1)S(1)} %constant_dynamic-update-slice_fusion.4, bf16[1024,1024]{1,0:T(8,128)(2,1)S(1)} %get-tuple-element.41), kind=kOutput, calls=%fused_computation.4 | convolution fusion | flops 1076363264 | bytes 7340032 | tf_op jit(solution)/shard_map/inverse_factors/dot_general | solution.py:105
  52.8 0.2 pad_maximum_fusion
  53.0 0.1 fusion.4
  53.2 1.0 %collective-permute-start.14 = (bf16[48,1024]{1,0:T(8,128)(2,1)S(1)}, bf16[48,1024]{1,0:T(8,128)(2,1)S(1)}, u32[]{:S(2)}, u32[]{:S(2)}) collective-permute-start(bf16[48,1024]{1,0:T(8,128)(2,1)S(1)} %get-tuple-element.55), channel_id=1, source_target_pairs={{0,128},{16,144},{128,0},{144,16},{1,129},{17,145},{129,1},{145,17... | collective-permute-start | bytes 294920 | tf_op jit(solution)/shard_map/gather_y/ppermute | solution.py:10
  54.1 1.5 %collective-permute-start.15 = (bf16[48,1024]{1,0:T(8,128)(2,1)S(1)}, bf16[48,1024]{1,0:T(8,128)(2,1)S(1)}, u32[]{:S(2)}, u32[]{:S(2)}) collective-permute-start(bf16[48,1024]{1,0:T(8,128)(2,1)S(1)} %get-tuple-element.55), channel_id=1, source_target_pairs={{0,16},{16,128},{128,144},{144,0},{1,17},{17,129},{129,145},{145,1... | collective-permute-start | bytes 294920 | tf_op jit(solution)/shard_map/gather_y/ppermute | solution.py:10
  55.7 1.2 %collective-permute-start.16 = (bf16[48,1024]{1,0:T(8,128)(2,1)S(1)}, bf16[48,1024]{1,0:T(8,128)(2,1)S(1)}, u32[]{:S(2)}, u32[]{:S(2)}) collective-permute-start(bf16[48,1024]{1,0:T(8,128)(2,1)S(1)} %get-tuple-element.55), channel_id=1, source_target_pairs={{0,144},{16,0},{128,16},{144,128},{1,145},{17,1},{129,17},{145,129... | collective-permute-start | bytes 294920 | tf_op jit(solution)/shard_map/gather_y/ppermute | solution.py:10
  56.8 0.5 fusion.5
  57.3 1.2 %convolution_add_fusion.1 = f32[48,1024]{1,0:T(8,128)} fusion(bf16[48,1024]{1,0:T(8,128)(2,1)S(1)} %get-tuple-element.55, bf16[1024,1024]{1,0:T(8,128)(2,1)S(1)} %get-tuple-element.42, f32[96,1024]{1,0:T(8,128)S(1)} %fusion.5), kind=kOutput, calls=%fused_computation.14 | convolution fusion | flops 100761600 | bytes 2785280 | tf_op jit(solution)/shard_map/screen/dot_general | solution.py:119
  58.5 1.5 %collective-permute-done.15 = bf16[48,1024]{1,0:T(8,128)(2,1)S(1)} collective-permute-done((bf16[48,1024]{1,0:T(8,128)(2,1)S(1)}, bf16[48,1024]{1,0:T(8,128)(2,1)S(1)}, u32[]{:S(2)}, u32[]{:S(2)}) %collective-permute-start.15) | collective-permute-done | bytes 98336 | tf_op jit(solution)/shard_map/gather_y/ppermute | solution.py:10
  60.0 2.9 %collective-permute-start.17 = (bf16[192,1024]{1,0:T(8,128)(2,1)S(1)}, bf16[192,1024]{1,0:T(8,128)(2,1)S(1)}, u32[]{:S(2)}, u32[]{:S(2)}) collective-permute-start(bf16[192,1024]{1,0:T(8,128)(2,1)S(1)} %pad_maximum_fusion.1), channel_id=1, source_target_pairs={{0,8},{8,0},{1,9},{9,1},{2,10},{10,2},{3,11},{11,3},{4,12},{12,4},... | collective-permute-start | bytes 1179656 | tf_op jit(solution)/shard_map/sigma/ppermute | solution.py:18
  63.0 0.9 %fusion.2 = f32[1024]{0:T(1024)S(1)} fusion(bf16[192,1024]{1,0:T(8,128)(2,1)S(1)} %pad_maximum_fusion.1, bf16[1024,1024]{1,0:T(8,128)(2,1)S(1)} %pad_maximum_fusion, bf16[192,512]{1,0:T(8,128)(2,1)S(1)} %bitcast.77), kind=kOutput, calls=%fused_computation.12 | convolution fusion | flops 403831808 | bytes 2691072 | tf_op jit(solution)/shard_map/sigma/dot_general | solution.py:140
  63.8 0.4 collective-permute-done.17
  64.3 0.9 %fusion.3 = f32[1024]{0:T(1024)S(1)} fusion(bf16[192,1024]{1,0:T(8,128)(2,1)S(1)} %collective-permute-done.17, bf16[1024,1024]{1,0:T(8,128)(2,1)S(1)} %pad_maximum_fusion, bf16[192,512]{1,0:T(8,128)(2,1)S(1)} %bitcast.76), kind=kOutput, calls=%fused_computation.13 | convolution fusion | flops 403831808 | bytes 2691072 | tf_op jit(solution)/shard_map/sigma/dot_general | solution.py:140
  65.2 0.1 select_add_fusion
  65.3 14.1 %all_to_all.9 = f32[32,1,128]{2,1,0:T(1,128)S(1)} all-to-all(f32[32,1,128]{2,1,0:T(1,128)S(1)} %bitcast.78), channel_id=1, replica_groups=mesh['grp'=2,'x'=4,'ylo'=2,'core'=2,'col'=8] {'x','col'}, dimensions={0} | all-to-all | bytes 32768 | tf_op jit(solution)/shard_map/sigma/all_to_all | solution.py:154
  79.4 0.6 reduce_sum.39
  (41 shorter events, 0.6 us)
Async XLA Ops:
  0.6 19.0 %copy-start = (bf16[128,1536]{1,0:T(8,128)(2,1)S(1)}, bf16[128,1536]{1,0:T(8,128)(2,1)}, u32[]{:S(2)}) copy-start(bf16[128,1536]{1,0:T(8,128)(2,1)} %param.3) | copy-start | bytes 1179652
  1.7 17.9 %collective-permute-start = (bf16[128,1024]{1,0:T(8,128)(2,1)S(1)}, bf16[128,1024]{1,0:T(8,128)(2,1)S(1)}, u32[]{:S(2)}, u32[]{:S(2)}) collective-permute-start(bf16[128,1024]{1,0:T(8,128)(2,1)S(1)} %slice.39), channel_id=1, source_target_pairs={{0,3},{8,11},{16,19},{24,27},{32,35},{40,43},{48,51},{56,59},{64,6... | collective-permute-start | bytes 786440 | tf_op jit(solution)/shard_map/panel_z/ppermute | solution.py:14
  8.8 10.8 %collective-permute-start.1 = (bf16[128,1024]{1,0:T(8,128)(2,1)S(1)}, bf16[128,1024]{1,0:T(8,128)(2,1)S(1)}, u32[]{:S(2)}, u32[]{:S(2)}) collective-permute-start(bf16[128,1024]{1,0:T(8,128)(2,1)S(1)} %slice.39), channel_id=1, source_target_pairs={{0,6},{8,14},{16,22},{24,30},{32,38},{40,46},{48,54},{56,62},{64,7... | collective-permute-start | bytes 786440 | tf_op jit(solution)/shard_map/panel_z/ppermute | solution.py:14
  13.3 12.1 %collective-permute-start.4 = (bf16[400,128]{1,0:T(8,128)(2,1)S(1)}, bf16[400,128]{1,0:T(8,128)(2,1)S(1)}, u32[]{:S(2)}, u32[]{:S(2)}) collective-permute-start(bf16[400,128]{1,0:T(8,128)(2,1)S(1)} %concatenate.48), channel_id=1, source_target_pairs={{0,64},{32,96},{64,0},{96,32},{1,65},{33,97},{65,1},{97,33},{2,66}... | collective-permute-start | bytes 307208 | tf_op jit(solution)/shard_map/blocks/ppermute | solution.py:10
  16.3 9.1 %collective-permute-start.5 = (bf16[400,128]{1,0:T(8,128)(2,1)S(1)}, bf16[400,128]{1,0:T(8,128)(2,1)S(1)}, u32[]{:S(2)}, u32[]{:S(2)}) collective-permute-start(bf16[400,128]{1,0:T(8,128)(2,1)S(1)} %concatenate.49), channel_id=1, source_target_pairs={{0,32},{32,64},{64,96},{96,0},{1,33},{33,65},{65,97},{97,1},{2,34}... | collective-permute-start | bytes 307208 | tf_op jit(solution)/shard_map/blocks/ppermute | solution.py:10
  16.9 8.6 %collective-permute-start.6 = (bf16[400,128]{1,0:T(8,128)(2,1)S(1)}, bf16[400,128]{1,0:T(8,128)(2,1)S(1)}, u32[]{:S(2)}, u32[]{:S(2)}) collective-permute-start(bf16[400,128]{1,0:T(8,128)(2,1)S(1)} %concatenate.50), channel_id=1, source_target_pairs={{0,96},{32,0},{64,32},{96,64},{1,97},{33,1},{65,33},{97,65},{2,98}... | collective-permute-start | bytes 307208 | tf_op jit(solution)/shard_map/blocks/ppermute | solution.py:10
  19.7 5.8 %collective-permute-start.2 = (bf16[128,1024]{1,0:T(8,128)(2,1)S(1)}, bf16[128,1024]{1,0:T(8,128)(2,1)S(1)}, u32[]{:S(2)}, u32[]{:S(2)}) collective-permute-start(bf16[128,1024]{1,0:T(8,128)(2,1)S(1)} %select_select_fusion.1), channel_id=1, source_target_pairs={{0,7},{3,4},{6,5},{8,15},{11,12},{14,13},{16,23},{19,20},{22,21},{... | collective-permute-start | bytes 786440 | tf_op jit(solution)/shard_map/panel_z/ppermute | solution.py:14
  21.0 5.4 %collective-permute-start.3 = (bf16[128,1024]{1,0:T(8,128)(2,1)S(1)}, bf16[128,1024]{1,0:T(8,128)(2,1)S(1)}, u32[]{:S(2)}, u32[]{:S(2)}) collective-permute-start(bf16[128,1024]{1,0:T(8,128)(2,1)S(1)} %select_select_fusion.1), channel_id=1, source_target_pairs={{0,1},{3,2},{8,9},{11,10},{16,17},{19,18},{24,25},{27,26},{32,33},... | collective-permute-start | bytes 786440 | tf_op jit(solution)/shard_map/panel_z/ppermute | solution.py:14
  26.4 6.9 %collective-permute-start.7 = (bf16[128,1024]{1,0:T(8,128)(2,1)S(1)}, bf16[128,1024]{1,0:T(8,128)(2,1)S(1)}, u32[]{:S(2)}, u32[]{:S(2)}) collective-permute-start(bf16[128,1024]{1,0:T(8,128)(2,1)S(1)} %select_select_fusion), channel_id=1, source_target_pairs={{0,64},{32,96},{64,0},{96,32},{1,65},{33,97},{65,1},{97,33},{2,66}... | collective-permute-start | bytes 786440 | tf_op jit(solution)/shard_map/panel_x/ppermute | solution.py:10
  26.5 14.9 %collective-permute-start.8 = (bf16[128,1024]{1,0:T(8,128)(2,1)S(1)}, bf16[128,1024]{1,0:T(8,128)(2,1)S(1)}, u32[]{:S(2)}, u32[]{:S(2)}) collective-permute-start(bf16[128,1024]{1,0:T(8,128)(2,1)S(1)} %select_select_fusion), channel_id=1, source_target_pairs={{0,32},{32,64},{64,96},{96,0},{1,33},{33,65},{65,97},{97,1},{2,34}... | collective-permute-start | bytes 786440 | tf_op jit(solution)/shard_map/panel_x/ppermute | solution.py:10
  27.5 13.9 %collective-permute-start.9 = (bf16[128,1024]{1,0:T(8,128)(2,1)S(1)}, bf16[128,1024]{1,0:T(8,128)(2,1)S(1)}, u32[]{:S(2)}, u32[]{:S(2)}) collective-permute-start(bf16[128,1024]{1,0:T(8,128)(2,1)S(1)} %select_select_fusion), channel_id=1, source_target_pairs={{0,96},{32,0},{64,32},{96,64},{1,97},{33,1},{65,33},{97,65},{2,98}... | collective-permute-start | bytes 786440 | tf_op jit(solution)/shard_map/panel_x/ppermute | solution.py:10
  42.1 2.1 %collective-permute-start.10 = (bf16[192,1024]{1,0:T(8,128)(2,1)S(1)}, bf16[192,1024]{1,0:T(8,128)(2,1)S(1)}, u32[]{:S(2)}, u32[]{:S(2)}) collective-permute-start(bf16[192,1024]{1,0:T(8,128)(2,1)S(1)} %convolution_convert_fusion), channel_id=1, source_target_pairs={{0,8},{8,0},{1,9},{9,1},{2,10},{10,2},{3,11},{11,3},{4,12},{12,4},... | collective-permute-start | bytes 1179656 | tf_op jit(solution)/shard_map/response/ppermute | solution.py:18
  44.4 8.6 %collective-permute-start.11 = (bf16[48,1024]{1,0:T(8,128)(2,1)S(1)}, bf16[48,1024]{1,0:T(8,128)(2,1)S(1)}, u32[]{:S(2)}, u32[]{:S(2)}) collective-permute-start(bf16[48,1024]{1,0:T(8,128)(2,1)S(1)} %get-tuple-element.56), channel_id=1, source_target_pairs={{0,128},{16,144},{128,0},{144,16},{1,129},{17,145},{129,1},{145,17... | collective-permute-start | bytes 294920 | tf_op jit(solution)/shard_map/sum_y/ppermute | solution.py:10
  47.4 5.6 %collective-permute-start.12 = (bf16[48,1024]{1,0:T(8,128)(2,1)S(1)}, bf16[48,1024]{1,0:T(8,128)(2,1)S(1)}, u32[]{:S(2)}, u32[]{:S(2)}) collective-permute-start(bf16[48,1024]{1,0:T(8,128)(2,1)S(1)} %get-tuple-element.58), channel_id=1, source_target_pairs={{0,16},{16,128},{128,144},{144,0},{1,17},{17,129},{129,145},{145,1... | collective-permute-start | bytes 294920 | tf_op jit(solution)/shard_map/sum_y/ppermute | solution.py:10
  47.8 5.2 %collective-permute-start.13 = (bf16[48,1024]{1,0:T(8,128)(2,1)S(1)}, bf16[48,1024]{1,0:T(8,128)(2,1)S(1)}, u32[]{:S(2)}, u32[]{:S(2)}) collective-permute-start(bf16[48,1024]{1,0:T(8,128)(2,1)S(1)} %get-tuple-element.57), channel_id=1, source_target_pairs={{0,144},{16,0},{128,16},{144,128},{1,145},{17,1},{129,17},{145,129... | collective-permute-start | bytes 294920 | tf_op jit(solution)/shard_map/sum_y/ppermute | solution.py:10
  53.2 5.3 %collective-permute-start.14 = (bf16[48,1024]{1,0:T(8,128)(2,1)S(1)}, bf16[48,1024]{1,0:T(8,128)(2,1)S(1)}, u32[]{:S(2)}, u32[]{:S(2)}) collective-permute-start(bf16[48,1024]{1,0:T(8,128)(2,1)S(1)} %get-tuple-element.55), channel_id=1, source_target_pairs={{0,128},{16,144},{128,0},{144,16},{1,129},{17,145},{129,1},{145,17... | collective-permute-start | bytes 294920 | tf_op jit(solution)/shard_map/gather_y/ppermute | solution.py:10
  54.1 5.9 %collective-permute-start.15 = (bf16[48,1024]{1,0:T(8,128)(2,1)S(1)}, bf16[48,1024]{1,0:T(8,128)(2,1)S(1)}, u32[]{:S(2)}, u32[]{:S(2)}) collective-permute-start(bf16[48,1024]{1,0:T(8,128)(2,1)S(1)} %get-tuple-element.55), channel_id=1, source_target_pairs={{0,16},{16,128},{128,144},{144,0},{1,17},{17,129},{129,145},{145,1... | collective-permute-start | bytes 294920 | tf_op jit(solution)/shard_map/gather_y/ppermute | solution.py:10
  55.7 4.3 %collective-permute-start.16 = (bf16[48,1024]{1,0:T(8,128)(2,1)S(1)}, bf16[48,1024]{1,0:T(8,128)(2,1)S(1)}, u32[]{:S(2)}, u32[]{:S(2)}) collective-permute-start(bf16[48,1024]{1,0:T(8,128)(2,1)S(1)} %get-tuple-element.55), channel_id=1, source_target_pairs={{0,144},{16,0},{128,16},{144,128},{1,145},{17,1},{129,17},{145,129... | collective-permute-start | bytes 294920 | tf_op jit(solution)/shard_map/gather_y/ppermute | solution.py:10
  60.0 4.2 %collective-permute-start.17 = (bf16[192,1024]{1,0:T(8,128)(2,1)S(1)}, bf16[192,1024]{1,0:T(8,128)(2,1)S(1)}, u32[]{:S(2)}, u32[]{:S(2)}) collective-permute-start(bf16[192,1024]{1,0:T(8,128)(2,1)S(1)} %pad_maximum_fusion.1), channel_id=1, source_target_pairs={{0,8},{8,0},{1,9},{9,1},{2,10},{10,2},{3,11},{11,3},{4,12},{12,4},... | collective-permute-start | bytes 1179656 | tf_op jit(solution)/shard_map/sigma/ppermute | solution.py:18

commit v16 on v14

--- a/solution.py
+++ b/solution.py
@@ -12,6 +12,13 @@
 
 def along_z(value, *pairs):
     return lax.ppermute(value, Z, pairs)
+
+
+def turn(value, size, step):
+    pairs = []
+    for x in range(size):
+        pairs += [(x * 2, (x + step) % size * 2), (x * 2 + 1, (x - step) % size * 2 + 1)]
+    return lax.ppermute(value, (X, CORE), pairs)
 
 
 def swap(value):
@@ -39,6 +46,7 @@
     x, y, z, core = (lax.axis_index(a) for a in (X, Y, Z, CORE))
     count = width // lax.axis_size(PLANE)
     steps = (0, 2, 1, 3)
+    way = 1 - 2 * core
 
     with jax.named_scope("panel_z"):
         piece = orbital_b[:, :panel]
@@ -56,8 +64,8 @@
             block = lax.dynamic_index_in_dim(blocks, i, 1, False).reshape(-1, own)
             return jnp.concatenate([block, extra], axis=0)
 
-        rows = [rows_of((x + k) % nx) for k in steps]
-        factors = [rows[0]] + [shift(row, X, nx, k) for row, k in zip(rows[1:], steps[1:])]
+        rows = [rows_of((x + way * k) % nx) for k in steps]
+        factors = [rows[0]] + [turn(row, nx, k) for row, k in zip(rows[1:], steps[1:])]
 
     with jax.named_scope("panel_z"):
         far_a, far_b, block_inverse, *_ = lax.optimization_barrier(
@@ -74,7 +82,7 @@
         held = jnp.where((z == 1) | (z == 2), near_b, held)
 
     with jax.named_scope("panel_x"):
-        blocks = [held] + [shift(held, X, nx, k) for k in steps[1:]]
+        blocks = [held] + [turn(held, nx, k) for k in steps[1:]]
         panels = jnp.concatenate(blocks, axis=0)
 
     with jax.named_scope("response"):
@@ -140,7 +148,7 @@
         ordered = jnp.concatenate([ordered, ordered], axis=1).astype(F32)
         local = -jnp.sum(products * ordered, axis=0).reshape(2, nx, own)
         local = local[0] + local[1]
-        back = (x - lax.iota(jnp.int32, nx)) % nx
+        back = way * (x - lax.iota(jnp.int32, nx)) % nx
         by_x = sum(
             jnp.where((back == k)[:, None], local[i][None], 0.0) for i, k in enumerate(steps)
         )

time: 80.3 us -> 80.7 us (level)
  waiting for transfers between devices: 16.6 us -> 15.2 us
  starting transfers between devices: 33.6 us -> 34.8 us
    ppermute x12 -> x6, waiting for transfers between devices: 13.5 us -> 1.55 us  [shift(): lax.ppermute(value, axis, [(i, (i + step) % size) for i in range(size)])]
    ppermute x0 -> x6, waiting for transfers between devices: none -> 11.3 us  [turn(): return lax.ppermute(value, (X, CORE), pairs)]
    ppermute x0 -> x6, starting transfers between devices: none -> 9.13 us  [turn(): return lax.ppermute(value, (X, CORE), pairs)]
    ppermute x12 -> x6, starting transfers between devices: 17.8 us -> 9.32 us  [shift(): lax.ppermute(value, axis, [(i, (i + step) % size) for i in range(size)])]
  transfers between devices with their start and end apart: 18 -> 18, of which waited for: 6 -> 7; matrix products, arithmetic and copies ran while one was open for 14% -> 14% of each run, Pallas kernels for 0% -> 0%
where the time goes in v16:
time: 80.7 us; the launch traced here: 80.4 us
  starting transfers between devices  34.8 us (43%)
  waiting for transfers between devices  15.2 us (19%)
  blocking collectives  14.4 us (18%)
  matrix products  6.07 us (8%)
  other arithmetic  5.2 us (6%)
  local copies, waits for them, and re-layouts  3.32 us (4%)
  between operations  1.36 us (2%)
    all_to_all x1, blocking collectives, body(): terms = lax.all_to_all(copies, (X, Z), 0, 0, tiled=True)  14.4 us
    ppermute x4, starting transfers between devices, along_z(): return lax.ppermute(value, Z, pairs)  12.1 us
    ppermute x6, waiting for transfers between devices, turn(): return lax.ppermute(value, (X, CORE), pairs)  11.3 us
    ppermute x6, starting transfers between devices, shift(): lax.ppermute(value, axis, [(i, (i + step) % size) for i in range(size)])  9.32 us
    ppermute x6, starting transfers between devices, turn(): return lax.ppermute(value, (X, CORE), pairs)  9.13 us
    ppermute x2, starting transfers between devices, swap(): return lax.ppermute(value, CORE, [(0, 1), (1, 0)])  4.31 us
    convert_element_type x2, other arithmetic, two_parts(): return (high.astype(LOW), (value - high).astype(LOW))  3.23 us
    dot_general x2, matrix products, body(): lax.dot_general(panels, part, (((1,), (1,)), ((), ())), preferred_element...  2.63 us
  transfers between devices with their start and end apart: 18, of which 7 were waited for; matrix products, arithmetic and copies ran while one was open for 14% of the time, Pallas kernels for 0%

profile of v16, /device:TPU:1, one launch (start us, length us, event | category | flops | bytes accessed | tf_op | source)
XLA Modules:
  0.0 80.4 jit_solution(16259826033120892588)
XLA Ops:
  0.6 0.0 copy-start
  0.6 1.0 %slice.39 = bf16[128,1024]{1,0:T(8,128)(2,1)S(1)} slice(bf16[128,1536]{1,0:T(8,128)(2,1)} %param.3), slice={[0:128], [0:1024]} | slice | bytes 524288 | tf_op jit(solution)/shard_map/panel_z/slice | solution.py:52
  1.7 7.1 %collective-permute-start = (bf16[128,1024]{1,0:T(8,128)(2,1)S(1)}, bf16[128,1024]{1,0:T(8,128)(2,1)S(1)}, u32[]{:S(2)}, u32[]{:S(2)}) collective-permute-start(bf16[128,1024]{1,0:T(8,128)(2,1)S(1)} %slice.39), channel_id=1, source_target_pairs={{0,3},{8,11},{16,19},{24,27},{32,35},{40,43},{48,51},{56,59},{64,6... | collective-permute-start | bytes 786440 | tf_op jit(solution)/shard_map/panel_z/ppermute | solution.py:14
  8.8 2.4 %collective-permute-start.1 = (bf16[128,1024]{1,0:T(8,128)(2,1)S(1)}, bf16[128,1024]{1,0:T(8,128)(2,1)S(1)}, u32[]{:S(2)}, u32[]{:S(2)}) collective-permute-start(bf16[128,1024]{1,0:T(8,128)(2,1)S(1)} %slice.39), channel_id=1, source_target_pairs={{0,6},{8,14},{16,22},{24,30},{32,38},{40,46},{48,54},{56,62},{64,7... | collective-permute-start | bytes 786440 | tf_op jit(solution)/shard_map/panel_z/ppermute | solution.py:14
  11.2 1.2 %copy.18 = bf16[128,1536]{0,1:T(8,128)(2,1)S(1)} copy(bf16[128,1536]{1,0:T(8,128)(2,1)} %param.3) | data formatting | bytes 786432 | tf_op args[0]
  12.4 0.7 fusion.20
  13.2 0.2 concatenate.45
  13.4 2.8 %collective-permute-start.4 = (bf16[400,128]{1,0:T(8,128)(2,1)S(1)}, bf16[400,128]{1,0:T(8,128)(2,1)S(1)}, u32[]{:S(2)}, u32[]{:S(2)}) collective-permute-start(bf16[400,128]{1,0:T(8,128)(2,1)S(1)} %concatenate.45), channel_id=1, source_target_pairs={{0,64},{8,72},{32,96},{40,104},{64,0},{72,8},{96,32},{104,40},{1,6... | collective-permute-start | bytes 307208 | tf_op jit(solution)/shard_map/blocks/ppermute | solution.py:21
  16.2 0.2 concatenate.46
  16.4 0.9 %collective-permute-start.5 = (bf16[400,128]{1,0:T(8,128)(2,1)S(1)}, bf16[400,128]{1,0:T(8,128)(2,1)S(1)}, u32[]{:S(2)}, u32[]{:S(2)}) collective-permute-start(bf16[400,128]{1,0:T(8,128)(2,1)S(1)} %concatenate.46), channel_id=1, source_target_pairs={{0,32},{8,104},{32,64},{40,8},{64,96},{72,40},{96,0},{104,72},{1,3... | collective-permute-start | bytes 307208 | tf_op jit(solution)/shard_map/blocks/ppermute | solution.py:21
  17.3 0.2 concatenate.47
  17.5 0.7 collective-permute-start.6
  18.3 0.2 concatenate.44
  18.7 1.3 %collective-permute-start.2 = (bf16[128,1024]{1,0:T(8,128)(2,1)S(1)}, bf16[128,1024]{1,0:T(8,128)(2,1)S(1)}, u32[]{:S(2)}, u32[]{:S(2)}) collective-permute-start(bf16[128,1024]{1,0:T(8,128)(2,1)S(1)} %select_select_fusion.1), channel_id=1, source_target_pairs={{0,7},{3,4},{6,5},{8,15},{11,12},{14,13},{16,23},{19,20},{22,21},{... | collective-permute-start | bytes 786440 | tf_op jit(solution)/shard_map/panel_z/ppermute | solution.py:14
  20.0 1.3 %collective-permute-start.3 = (bf16[128,1024]{1,0:T(8,128)(2,1)S(1)}, bf16[128,1024]{1,0:T(8,128)(2,1)S(1)}, u32[]{:S(2)}, u32[]{:S(2)}) collective-permute-start(bf16[128,1024]{1,0:T(8,128)(2,1)S(1)} %select_select_fusion.1), channel_id=1, source_target_pairs={{0,1},{3,2},{8,9},{11,10},{16,17},{19,18},{24,25},{27,26},{32,33},... | collective-permute-start | bytes 786440 | tf_op jit(solution)/shard_map/panel_z/ppermute | solution.py:14
  21.3 3.1 %fusion = (bf16[1024,1024]{1,0:T(8,128)(2,1)S(1)}, bf16[1024,1024]{1,0:T(8,128)(2,1)S(1)}) fusion(f32[1024,1024]{1,0:T(8,128)} %param.5), kind=kLoop, calls=%fused_computation.2 | loop fusion | flops 4194304 | bytes 8388608 | tf_op jit(solution)/shard_map/panel_z/convert_element_type | solution.py:39
  24.4 0.1 collective-permute-done.3
  24.6 1.8 %collective-permute-start.7 = (bf16[128,1024]{1,0:T(8,128)(2,1)S(1)}, bf16[128,1024]{1,0:T(8,128)(2,1)S(1)}, u32[]{:S(2)}, u32[]{:S(2)}) collective-permute-start(bf16[128,1024]{1,0:T(8,128)(2,1)S(1)} %select_select_fusion), channel_id=1, source_target_pairs={{0,64},{8,72},{32,96},{40,104},{64,0},{72,8},{96,32},{104,40},{1,6... | collective-permute-start | bytes 786440 | tf_op jit(solution)/shard_map/panel_x/ppermute | solution.py:21
  26.4 2.4 %collective-permute-start.8 = (bf16[128,1024]{1,0:T(8,128)(2,1)S(1)}, bf16[128,1024]{1,0:T(8,128)(2,1)S(1)}, u32[]{:S(2)}, u32[]{:S(2)}) collective-permute-start(bf16[128,1024]{1,0:T(8,128)(2,1)S(1)} %select_select_fusion), channel_id=1, source_target_pairs={{0,32},{8,104},{32,64},{40,8},{64,96},{72,40},{96,0},{104,72},{1,3... | collective-permute-start | bytes 786440 | tf_op jit(solution)/shard_map/panel_x/ppermute | solution.py:21
  28.8 0.5 collective-permute-start.9
  29.6 1.9 %collective-permute-done.7 = bf16[128,1024]{1,0:T(8,128)(2,1)S(1)} collective-permute-done((bf16[128,1024]{1,0:T(8,128)(2,1)S(1)}, bf16[128,1024]{1,0:T(8,128)(2,1)S(1)}, u32[]{:S(2)}, u32[]{:S(2)}) %collective-permute-start.7) | collective-permute-done | bytes 262176 | tf_op jit(solution)/shard_map/panel_x/ppermute | solution.py:21
  31.4 8.8 %collective-permute-done.8 = bf16[128,1024]{1,0:T(8,128)(2,1)S(1)} collective-permute-done((bf16[128,1024]{1,0:T(8,128)(2,1)S(1)}, bf16[128,1024]{1,0:T(8,128)(2,1)S(1)}, u32[]{:S(2)}, u32[]{:S(2)}) %collective-permute-start.8) | collective-permute-done | bytes 262176 | tf_op jit(solution)/shard_map/panel_x/ppermute | solution.py:21
  40.2 0.6 collective-permute-done.9
  40.9 0.2 multiply_convert_fusion
  41.1 0.4 convolution_convert_fusion
  41.5 1.4 %collective-permute-start.10 = (bf16[192,1024]{1,0:T(8,128)(2,1)S(1)}, bf16[192,1024]{1,0:T(8,128)(2,1)S(1)}, u32[]{:S(2)}, u32[]{:S(2)}) collective-permute-start(bf16[192,1024]{1,0:T(8,128)(2,1)S(1)} %convolution_convert_fusion), channel_id=1, source_target_pairs={{0,8},{8,0},{1,9},{9,1},{2,10},{10,2},{3,11},{11,3},{4,12},{12,4},... | collective-permute-start | bytes 1179656 | tf_op jit(solution)/shard_map/response/ppermute | solution.py:25
  42.9 0.4 fusion.24
  43.3 1.0 %collective-permute-done.10 = bf16[192,1024]{1,0:T(8,128)(2,1)S(1)} collective-permute-done((bf16[192,1024]{1,0:T(8,128)(2,1)S(1)}, bf16[192,1024]{1,0:T(8,128)(2,1)S(1)}, u32[]{:S(2)}, u32[]{:S(2)}) %collective-permute-start.10) | collective-permute-done | bytes 393248 | tf_op jit(solution)/shard_map/response/ppermute | solution.py:25
  44.3 0.1 convert_add_fusion
  44.4 3.0 %collective-permute-start.11 = (bf16[48,1024]{1,0:T(8,128)(2,1)S(1)}, bf16[48,1024]{1,0:T(8,128)(2,1)S(1)}, u32[]{:S(2)}, u32[]{:S(2)}) collective-permute-start(bf16[48,1024]{1,0:T(8,128)(2,1)S(1)} %get-tuple-element.54), channel_id=1, source_target_pairs={{0,128},{16,144},{128,0},{144,16},{1,129},{17,145},{129,1},{145,17... | collective-permute-start | bytes 294920 | tf_op jit(solution)/shard_map/sum_y/ppermute | solution.py:10
  47.4 0.4 collective-permute-start.12
  47.8 2.3 %collective-permute-start.13 = (bf16[48,1024]{1,0:T(8,128)(2,1)S(1)}, bf16[48,1024]{1,0:T(8,128)(2,1)S(1)}, u32[]{:S(2)}, u32[]{:S(2)}) collective-permute-start(bf16[48,1024]{1,0:T(8,128)(2,1)S(1)} %get-tuple-element.55), channel_id=1, source_target_pairs={{0,144},{16,0},{128,16},{144,128},{1,145},{17,1},{129,17},{145,129... | collective-permute-start | bytes 294920 | tf_op jit(solution)/shard_map/sum_y/ppermute | solution.py:10
  50.2 1.3 %fusion.25 = f32[512,1024]{1,0:T(8,128)S(1)} fusion(bf16[512,1024]{1,0:T(8,128)(2,1)S(1)} %constant_dynamic-update-slice_fusion.4, bf16[1024,1024]{1,0:T(8,128)(2,1)S(1)} %get-tuple-element.40), kind=kOutput, calls=%fused_computation.89 | convolution fusion | flops 1073741824 | bytes 5242880 | tf_op jit(solution)/shard_map/inverse_factors/dot_general | solution.py:113
  51.5 1.3 %reduce-precision_convert_fusion.1 = (bf16[512,1024]{1,0:T(8,128)(2,1)S(1)}, bf16[512,1024]{1,0:T(8,128)(2,1)S(1)}) fusion(f32[512,1024]{1,0:T(8,128)S(1)} %fusion.25, bf16[512,1024]{1,0:T(8,128)(2,1)S(1)} %constant_dynamic-update-slice_fusion.4, bf16[1024,1024]{1,0:T(8,128)(2,1)S(1)} %get-tuple-element.39), kind=kOutput, calls=%fused_computation.4 | convolution fusion | flops 1076363264 | bytes 7340032 | tf_op jit(solution)/shard_map/inverse_factors/dot_general | solution.py:113
  52.9 0.2 pad_maximum_fusion
  53.1 0.1 fusion.5
  53.2 1.0 %collective-permute-start.14 = (bf16[48,1024]{1,0:T(8,128)(2,1)S(1)}, bf16[48,1024]{1,0:T(8,128)(2,1)S(1)}, u32[]{:S(2)}, u32[]{:S(2)}) collective-permute-start(bf16[48,1024]{1,0:T(8,128)(2,1)S(1)} %get-tuple-element.53), channel_id=1, source_target_pairs={{0,128},{16,144},{128,0},{144,16},{1,129},{17,145},{129,1},{145,17... | collective-permute-start | bytes 294920 | tf_op jit(solution)/shard_map/gather_y/ppermute | solution.py:10
  54.2 1.5 %collective-permute-start.15 = (bf16[48,1024]{1,0:T(8,128)(2,1)S(1)}, bf16[48,1024]{1,0:T(8,128)(2,1)S(1)}, u32[]{:S(2)}, u32[]{:S(2)}) collective-permute-start(bf16[48,1024]{1,0:T(8,128)(2,1)S(1)} %get-tuple-element.53), channel_id=1, source_target_pairs={{0,16},{16,128},{128,144},{144,0},{1,17},{17,129},{129,145},{145,1... | collective-permute-start | bytes 294920 | tf_op jit(solution)/shard_map/gather_y/ppermute | solution.py:10
  55.7 1.2 %collective-permute-start.16 = (bf16[48,1024]{1,0:T(8,128)(2,1)S(1)}, bf16[48,1024]{1,0:T(8,128)(2,1)S(1)}, u32[]{:S(2)}, u32[]{:S(2)}) collective-permute-start(bf16[48,1024]{1,0:T(8,128)(2,1)S(1)} %get-tuple-element.53), channel_id=1, source_target_pairs={{0,144},{16,0},{128,16},{144,128},{1,145},{17,1},{129,17},{145,129... | collective-permute-start | bytes 294920 | tf_op jit(solution)/shard_map/gather_y/ppermute | solution.py:10
  56.8 0.5 fusion.6
  57.3 1.2 %convolution_add_fusion.1 = f32[48,1024]{1,0:T(8,128)} fusion(bf16[48,1024]{1,0:T(8,128)(2,1)S(1)} %get-tuple-element.53, bf16[1024,1024]{1,0:T(8,128)(2,1)S(1)} %get-tuple-element.40, f32[96,1024]{1,0:T(8,128)S(1)} %fusion.6), kind=kOutput, calls=%fused_computation.11 | convolution fusion | flops 100761600 | bytes 2785280 | tf_op jit(solution)/shard_map/screen/dot_general | solution.py:127
  58.5 1.5 %collective-permute-done.15 = bf16[48,1024]{1,0:T(8,128)(2,1)S(1)} collective-permute-done((bf16[48,1024]{1,0:T(8,128)(2,1)S(1)}, bf16[48,1024]{1,0:T(8,128)(2,1)S(1)}, u32[]{:S(2)}, u32[]{:S(2)}) %collective-permute-start.15) | collective-permute-done | bytes 98336 | tf_op jit(solution)/shard_map/gather_y/ppermute | solution.py:10
  60.1 2.9 %collective-permute-start.17 = (bf16[192,1024]{1,0:T(8,128)(2,1)S(1)}, bf16[192,1024]{1,0:T(8,128)(2,1)S(1)}, u32[]{:S(2)}, u32[]{:S(2)}) collective-permute-start(bf16[192,1024]{1,0:T(8,128)(2,1)S(1)} %pad_maximum_fusion.1), channel_id=1, source_target_pairs={{0,8},{8,0},{1,9},{9,1},{2,10},{10,2},{3,11},{11,3},{4,12},{12,4},... | collective-permute-start | bytes 1179656 | tf_op jit(solution)/shard_map/gather_y/ppermute | solution.py:25
  63.0 1.3 %collective-permute-done.17 = bf16[192,1024]{1,0:T(8,128)(2,1)S(1)} collective-permute-done((bf16[192,1024]{1,0:T(8,128)(2,1)S(1)}, bf16[192,1024]{1,0:T(8,128)(2,1)S(1)}, u32[]{:S(2)}, u32[]{:S(2)}) %collective-permute-start.17) | collective-permute-done | bytes 393248 | tf_op jit(solution)/shard_map/gather_y/ppermute | solution.py:25
  64.3 1.0 %multiply_reduce_fusion = f32[1024]{0:T(1024)S(1)} fusion(bf16[1024,1024]{1,0:T(8,128)(2,1)S(1)} %pad_maximum_fusion, bf16[192,1024]{1,0:T(8,128)(2,1)S(1)} %collective-permute-done.17, bf16[192,1024]{1,0:T(8,128)(2,1)S(1)} %pad_maximum_fusion.1, bf16[384,512]{1,0:T(8,128)(2,1)S(1)} %bitcast.80), kind=kOutput, calls=%fused_computation.8 | convolution fusion | flops 809237504 | bytes 3280896 | tf_op jit(solution)/shard_map/sigma/dot_general | solution.py:145
  65.4 0.1 select_add_fusion
  65.5 14.4 %all_to_all.9 = f32[32,1,128]{2,1,0:T(1,128)S(1)} all-to-all(f32[32,1,128]{2,1,0:T(1,128)S(1)} %bitcast.79), channel_id=1, replica_groups=mesh['grp'=2,'x'=4,'ylo'=2,'core'=2,'col'=8] {'x','col'}, dimensions={0} | all-to-all | bytes 32768 | tf_op jit(solution)/shard_map/sigma/all_to_all | solution.py:156
  79.8 0.6 reduce_sum.29
  (45 shorter events, 0.6 us)
Async XLA Ops:
  0.6 18.0 %copy-start = (bf16[128,1536]{1,0:T(8,128)(2,1)S(1)}, bf16[128,1536]{1,0:T(8,128)(2,1)}, u32[]{:S(2)}) copy-start(bf16[128,1536]{1,0:T(8,128)(2,1)} %param.3) | copy-start | bytes 1179652
  1.7 16.9 %collective-permute-start = (bf16[128,1024]{1,0:T(8,128)(2,1)S(1)}, bf16[128,1024]{1,0:T(8,128)(2,1)S(1)}, u32[]{:S(2)}, u32[]{:S(2)}) collective-permute-start(bf16[128,1024]{1,0:T(8,128)(2,1)S(1)} %slice.39), channel_id=1, source_target_pairs={{0,3},{8,11},{16,19},{24,27},{32,35},{40,43},{48,51},{56,59},{64,6... | collective-permute-start | bytes 786440 | tf_op jit(solution)/shard_map/panel_z/ppermute | solution.py:14
  8.8 9.8 %collective-permute-start.1 = (bf16[128,1024]{1,0:T(8,128)(2,1)S(1)}, bf16[128,1024]{1,0:T(8,128)(2,1)S(1)}, u32[]{:S(2)}, u32[]{:S(2)}) collective-permute-start(bf16[128,1024]{1,0:T(8,128)(2,1)S(1)} %slice.39), channel_id=1, source_target_pairs={{0,6},{8,14},{16,22},{24,30},{32,38},{40,46},{48,54},{56,62},{64,7... | collective-permute-start | bytes 786440 | tf_op jit(solution)/shard_map/panel_z/ppermute | solution.py:14
  13.4 11.0 %collective-permute-start.4 = (bf16[400,128]{1,0:T(8,128)(2,1)S(1)}, bf16[400,128]{1,0:T(8,128)(2,1)S(1)}, u32[]{:S(2)}, u32[]{:S(2)}) collective-permute-start(bf16[400,128]{1,0:T(8,128)(2,1)S(1)} %concatenate.45), channel_id=1, source_target_pairs={{0,64},{8,72},{32,96},{40,104},{64,0},{72,8},{96,32},{104,40},{1,6... | collective-permute-start | bytes 307208 | tf_op jit(solution)/shard_map/blocks/ppermute | solution.py:21
  16.4 8.1 %collective-permute-start.5 = (bf16[400,128]{1,0:T(8,128)(2,1)S(1)}, bf16[400,128]{1,0:T(8,128)(2,1)S(1)}, u32[]{:S(2)}, u32[]{:S(2)}) collective-permute-start(bf16[400,128]{1,0:T(8,128)(2,1)S(1)} %concatenate.46), channel_id=1, source_target_pairs={{0,32},{8,104},{32,64},{40,8},{64,96},{72,40},{96,0},{104,72},{1,3... | collective-permute-start | bytes 307208 | tf_op jit(solution)/shard_map/blocks/ppermute | solution.py:21
  17.5 7.0 %collective-permute-start.6 = (bf16[400,128]{1,0:T(8,128)(2,1)S(1)}, bf16[400,128]{1,0:T(8,128)(2,1)S(1)}, u32[]{:S(2)}, u32[]{:S(2)}) collective-permute-start(bf16[400,128]{1,0:T(8,128)(2,1)S(1)} %concatenate.47), channel_id=1, source_target_pairs={{0,96},{8,40},{32,0},{40,72},{64,32},{72,104},{96,64},{104,8},{1,9... | collective-permute-start | bytes 307208 | tf_op jit(solution)/shard_map/blocks/ppermute | solution.py:21
  18.7 5.8 %collective-permute-start.2 = (bf16[128,1024]{1,0:T(8,128)(2,1)S(1)}, bf16[128,1024]{1,0:T(8,128)(2,1)S(1)}, u32[]{:S(2)}, u32[]{:S(2)}) collective-permute-start(bf16[128,1024]{1,0:T(8,128)(2,1)S(1)} %select_select_fusion.1), channel_id=1, source_target_pairs={{0,7},{3,4},{6,5},{8,15},{11,12},{14,13},{16,23},{19,20},{22,21},{... | collective-permute-start | bytes 786440 | tf_op jit(solution)/shard_map/panel_z/ppermute | solution.py:14
  20.0 4.6 %collective-permute-start.3 = (bf16[128,1024]{1,0:T(8,128)(2,1)S(1)}, bf16[128,1024]{1,0:T(8,128)(2,1)S(1)}, u32[]{:S(2)}, u32[]{:S(2)}) collective-permute-start(bf16[128,1024]{1,0:T(8,128)(2,1)S(1)} %select_select_fusion.1), channel_id=1, source_target_pairs={{0,1},{3,2},{8,9},{11,10},{16,17},{19,18},{24,25},{27,26},{32,33},... | collective-permute-start | bytes 786440 | tf_op jit(solution)/shard_map/panel_z/ppermute | solution.py:14
  24.6 6.8 %collective-permute-start.7 = (bf16[128,1024]{1,0:T(8,128)(2,1)S(1)}, bf16[128,1024]{1,0:T(8,128)(2,1)S(1)}, u32[]{:S(2)}, u32[]{:S(2)}) collective-permute-start(bf16[128,1024]{1,0:T(8,128)(2,1)S(1)} %select_select_fusion), channel_id=1, source_target_pairs={{0,64},{8,72},{32,96},{40,104},{64,0},{72,8},{96,32},{104,40},{1,6... | collective-permute-start | bytes 786440 | tf_op jit(solution)/shard_map/panel_x/ppermute | solution.py:21
  26.4 13.8 %collective-permute-start.8 = (bf16[128,1024]{1,0:T(8,128)(2,1)S(1)}, bf16[128,1024]{1,0:T(8,128)(2,1)S(1)}, u32[]{:S(2)}, u32[]{:S(2)}) collective-permute-start(bf16[128,1024]{1,0:T(8,128)(2,1)S(1)} %select_select_fusion), channel_id=1, source_target_pairs={{0,32},{8,104},{32,64},{40,8},{64,96},{72,40},{96,0},{104,72},{1,3... | collective-permute-start | bytes 786440 | tf_op jit(solution)/shard_map/panel_x/ppermute | solution.py:21
  28.8 12.1 %collective-permute-start.9 = (bf16[128,1024]{1,0:T(8,128)(2,1)S(1)}, bf16[128,1024]{1,0:T(8,128)(2,1)S(1)}, u32[]{:S(2)}, u32[]{:S(2)}) collective-permute-start(bf16[128,1024]{1,0:T(8,128)(2,1)S(1)} %select_select_fusion), channel_id=1, source_target_pairs={{0,96},{8,40},{32,0},{40,72},{64,32},{72,104},{96,64},{104,8},{1,9... | collective-permute-start | bytes 786440 | tf_op jit(solution)/shard_map/panel_x/ppermute | solution.py:21
  41.5 2.8 %collective-permute-start.10 = (bf16[192,1024]{1,0:T(8,128)(2,1)S(1)}, bf16[192,1024]{1,0:T(8,128)(2,1)S(1)}, u32[]{:S(2)}, u32[]{:S(2)}) collective-permute-start(bf16[192,1024]{1,0:T(8,128)(2,1)S(1)} %convolution_convert_fusion), channel_id=1, source_target_pairs={{0,8},{8,0},{1,9},{9,1},{2,10},{10,2},{3,11},{11,3},{4,12},{12,4},... | collective-permute-start | bytes 1179656 | tf_op jit(solution)/shard_map/response/ppermute | solution.py:25
  44.4 8.6 %collective-permute-start.11 = (bf16[48,1024]{1,0:T(8,128)(2,1)S(1)}, bf16[48,1024]{1,0:T(8,128)(2,1)S(1)}, u32[]{:S(2)}, u32[]{:S(2)}) collective-permute-start(bf16[48,1024]{1,0:T(8,128)(2,1)S(1)} %get-tuple-element.54), channel_id=1, source_target_pairs={{0,128},{16,144},{128,0},{144,16},{1,129},{17,145},{129,1},{145,17... | collective-permute-start | bytes 294920 | tf_op jit(solution)/shard_map/sum_y/ppermute | solution.py:10
  47.4 5.6 %collective-permute-start.12 = (bf16[48,1024]{1,0:T(8,128)(2,1)S(1)}, bf16[48,1024]{1,0:T(8,128)(2,1)S(1)}, u32[]{:S(2)}, u32[]{:S(2)}) collective-permute-start(bf16[48,1024]{1,0:T(8,128)(2,1)S(1)} %get-tuple-element.56), channel_id=1, source_target_pairs={{0,16},{16,128},{128,144},{144,0},{1,17},{17,129},{129,145},{145,1... | collective-permute-start | bytes 294920 | tf_op jit(solution)/shard_map/sum_y/ppermute | solution.py:10
  47.8 5.2 %collective-permute-start.13 = (bf16[48,1024]{1,0:T(8,128)(2,1)S(1)}, bf16[48,1024]{1,0:T(8,128)(2,1)S(1)}, u32[]{:S(2)}, u32[]{:S(2)}) collective-permute-start(bf16[48,1024]{1,0:T(8,128)(2,1)S(1)} %get-tuple-element.55), channel_id=1, source_target_pairs={{0,144},{16,0},{128,16},{144,128},{1,145},{17,1},{129,17},{145,129... | collective-permute-start | bytes 294920 | tf_op jit(solution)/shard_map/sum_y/ppermute | solution.py:10
  53.2 5.3 %collective-permute-start.14 = (bf16[48,1024]{1,0:T(8,128)(2,1)S(1)}, bf16[48,1024]{1,0:T(8,128)(2,1)S(1)}, u32[]{:S(2)}, u32[]{:S(2)}) collective-permute-start(bf16[48,1024]{1,0:T(8,128)(2,1)S(1)} %get-tuple-element.53), channel_id=1, source_target_pairs={{0,128},{16,144},{128,0},{144,16},{1,129},{17,145},{129,1},{145,17... | collective-permute-start | bytes 294920 | tf_op jit(solution)/shard_map/gather_y/ppermute | solution.py:10
  54.2 5.9 %collective-permute-start.15 = (bf16[48,1024]{1,0:T(8,128)(2,1)S(1)}, bf16[48,1024]{1,0:T(8,128)(2,1)S(1)}, u32[]{:S(2)}, u32[]{:S(2)}) collective-permute-start(bf16[48,1024]{1,0:T(8,128)(2,1)S(1)} %get-tuple-element.53), channel_id=1, source_target_pairs={{0,16},{16,128},{128,144},{144,0},{1,17},{17,129},{129,145},{145,1... | collective-permute-start | bytes 294920 | tf_op jit(solution)/shard_map/gather_y/ppermute | solution.py:10
  55.7 4.3 %collective-permute-start.16 = (bf16[48,1024]{1,0:T(8,128)(2,1)S(1)}, bf16[48,1024]{1,0:T(8,128)(2,1)S(1)}, u32[]{:S(2)}, u32[]{:S(2)}) collective-permute-start(bf16[48,1024]{1,0:T(8,128)(2,1)S(1)} %get-tuple-element.53), channel_id=1, source_target_pairs={{0,144},{16,0},{128,16},{144,128},{1,145},{17,1},{129,17},{145,129... | collective-permute-start | bytes 294920 | tf_op jit(solution)/shard_map/gather_y/ppermute | solution.py:10
  60.1 4.2 %collective-permute-start.17 = (bf16[192,1024]{1,0:T(8,128)(2,1)S(1)}, bf16[192,1024]{1,0:T(8,128)(2,1)S(1)}, u32[]{:S(2)}, u32[]{:S(2)}) collective-permute-start(bf16[192,1024]{1,0:T(8,128)(2,1)S(1)} %pad_maximum_fusion.1), channel_id=1, source_target_pairs={{0,8},{8,0},{1,9},{9,1},{2,10},{10,2},{3,11},{11,3},{4,12},{12,4},... | collective-permute-start | bytes 1179656 | tf_op jit(solution)/shard_map/gather_y/ppermute | solution.py:25

commit v17 on v15

--- a/solution.py
+++ b/solution.py
@@ -102,10 +102,10 @@
     with jax.named_scope("inverse_factors"):
         panels = jnp.concatenate(blocks, axis=0)
         inverse_factors = sum(
-            lax.dot_general(panels, part, (((1,), (1,)), ((), ())), preferred_element_type=F32)
+            lax.dot_general(part, panels, (((1,), (1,)), ((), ())), preferred_element_type=F32)
             for part in (inv_high, inv_rest)
         )
-        inverse_factors = jnp.concatenate(two_parts(inverse_factors), axis=0)
+        inverse_factors = jnp.concatenate(two_parts(inverse_factors), axis=1)
 
     with jax.named_scope("screen"):
         place = z * width + lax.axis_index(PLANE) * count
@@ -137,9 +137,7 @@
     with jax.named_scope("sigma"):
 
         def terms_of(rows, weights):
-            products = lax.dot_general(
-                rows, inverse_factors, (((1,), (1,)), ((), ())), preferred_element_type=F32
-            )
+            products = jnp.dot(rows, inverse_factors, preferred_element_type=F32)
             weights = jnp.concatenate([weights, weights], axis=1).astype(F32)
             return jnp.sum(products * weights, axis=0)
 

time: 80.2 us -> 80.2 us (level)
  no operation moved by 1% of the time
where the time goes in v17:
time: 80.2 us; the launch traced here: 79.9 us
  starting transfers between devices  33.6 us (42%)
  waiting for transfers between devices  15.8 us (20%)
  blocking collectives  14.1 us (18%)
  matrix products  6.78 us (8%)
  other arithmetic  5.29 us (7%)
  local copies, waits for them, and re-layouts  3.27 us (4%)
  between operations  1.17 us (1%)
    ppermute x12, starting transfers between devices, shift(): lax.ppermute(value, axis, [(i, (i + step) % size) for i in range(size)])  17.8 us
    all_to_all x1, blocking collectives, body(): terms = lax.all_to_all(copies, (X, Z), 0, 0, tiled=True)  14.1 us
    ppermute x12, waiting for transfers between devices, shift(): lax.ppermute(value, axis, [(i, (i + step) % size) for i in range(size)])  13.5 us
    ppermute x4, starting transfers between devices, along_z(): return lax.ppermute(value, Z, pairs)  12.1 us
    ppermute x2, starting transfers between devices, swap(): return lax.ppermute(value, CORE, [(0, 1), (1, 0)])  3.67 us
    convert_element_type x2, other arithmetic, two_parts(): return (high.astype(LOW), (value - high).astype(LOW))  3.22 us
    dot_general x2, matrix products, body(): lax.dot_general(part, panels, (((1,), (1,)), ((), ())), preferred_element...  2.64 us
    dot_general x2, matrix products, terms_of(): products = jnp.dot(rows, inverse_factors, preferred_element_type=F32)  1.73 us
  transfers between devices with their start and end apart: 18, of which 6 were waited for; matrix products, arithmetic and copies ran while one was open for 15% of the time, Pallas kernels for 0%

profile of v17, /device:TPU:1, one launch (start us, length us, event | category | flops | bytes accessed | tf_op | source)
XLA Modules:
  0.0 79.9 jit_solution(17449848552509108221)
XLA Ops:
  0.6 0.0 copy-start
  0.6 1.0 %slice.39 = bf16[128,1024]{1,0:T(8,128)(2,1)S(1)} slice(bf16[128,1536]{1,0:T(8,128)(2,1)} %param.3), slice={[0:128], [0:1024]} | slice | bytes 524288 | tf_op jit(solution)/shard_map/panel_z/slice | solution.py:44
  1.7 7.1 %collective-permute-start = (bf16[128,1024]{1,0:T(8,128)(2,1)S(1)}, bf16[128,1024]{1,0:T(8,128)(2,1)S(1)}, u32[]{:S(2)}, u32[]{:S(2)}) collective-permute-start(bf16[128,1024]{1,0:T(8,128)(2,1)S(1)} %slice.39), channel_id=1, source_target_pairs={{0,3},{8,11},{16,19},{24,27},{32,35},{40,43},{48,51},{56,59},{64,6... | collective-permute-start | bytes 786440 | tf_op jit(solution)/shard_map/panel_z/ppermute | solution.py:14
  8.8 2.4 %collective-permute-start.1 = (bf16[128,1024]{1,0:T(8,128)(2,1)S(1)}, bf16[128,1024]{1,0:T(8,128)(2,1)S(1)}, u32[]{:S(2)}, u32[]{:S(2)}) collective-permute-start(bf16[128,1024]{1,0:T(8,128)(2,1)S(1)} %slice.39), channel_id=1, source_target_pairs={{0,6},{8,14},{16,22},{24,30},{32,38},{40,46},{48,54},{56,62},{64,7... | collective-permute-start | bytes 786440 | tf_op jit(solution)/shard_map/panel_z/ppermute | solution.py:14
  11.2 1.2 %copy.18 = bf16[128,1536]{0,1:T(8,128)(2,1)S(1)} copy(bf16[128,1536]{1,0:T(8,128)(2,1)} %param.3) | data formatting | bytes 786432 | tf_op args[0]
  12.4 0.7 fusion.19
  13.2 0.2 concatenate.48
  13.3 2.8 %collective-permute-start.4 = (bf16[400,128]{1,0:T(8,128)(2,1)S(1)}, bf16[400,128]{1,0:T(8,128)(2,1)S(1)}, u32[]{:S(2)}, u32[]{:S(2)}) collective-permute-start(bf16[400,128]{1,0:T(8,128)(2,1)S(1)} %concatenate.48), channel_id=1, source_target_pairs={{0,64},{32,96},{64,0},{96,32},{1,65},{33,97},{65,1},{97,33},{2,66}... | collective-permute-start | bytes 307208 | tf_op jit(solution)/shard_map/blocks/ppermute | solution.py:10
  16.2 0.2 concatenate.49
  16.3 0.4 collective-permute-start.5
  16.7 0.2 concatenate.50
  16.9 2.4 %collective-permute-start.6 = (bf16[400,128]{1,0:T(8,128)(2,1)S(1)}, bf16[400,128]{1,0:T(8,128)(2,1)S(1)}, u32[]{:S(2)}, u32[]{:S(2)}) collective-permute-start(bf16[400,128]{1,0:T(8,128)(2,1)S(1)} %concatenate.50), channel_id=1, source_target_pairs={{0,96},{32,0},{64,32},{96,64},{1,97},{33,1},{65,33},{97,65},{2,98}... | collective-permute-start | bytes 307208 | tf_op jit(solution)/shard_map/blocks/ppermute | solution.py:10
  19.3 0.2 concatenate.47
  19.7 1.3 %collective-permute-start.2 = (bf16[128,1024]{1,0:T(8,128)(2,1)S(1)}, bf16[128,1024]{1,0:T(8,128)(2,1)S(1)}, u32[]{:S(2)}, u32[]{:S(2)}) collective-permute-start(bf16[128,1024]{1,0:T(8,128)(2,1)S(1)} %select_select_fusion.1), channel_id=1, source_target_pairs={{0,7},{3,4},{6,5},{8,15},{11,12},{14,13},{16,23},{19,20},{22,21},{... | collective-permute-start | bytes 786440 | tf_op jit(solution)/shard_map/panel_z/ppermute | solution.py:14
  21.0 1.3 %collective-permute-start.3 = (bf16[128,1024]{1,0:T(8,128)(2,1)S(1)}, bf16[128,1024]{1,0:T(8,128)(2,1)S(1)}, u32[]{:S(2)}, u32[]{:S(2)}) collective-permute-start(bf16[128,1024]{1,0:T(8,128)(2,1)S(1)} %select_select_fusion.1), channel_id=1, source_target_pairs={{0,1},{3,2},{8,9},{11,10},{16,17},{19,18},{24,25},{27,26},{32,33},... | collective-permute-start | bytes 786440 | tf_op jit(solution)/shard_map/panel_z/ppermute | solution.py:14
  22.3 3.1 %fusion = (bf16[1024,1024]{1,0:T(8,128)(2,1)S(1)}, bf16[1024,1024]{1,0:T(8,128)(2,1)S(1)}) fusion(f32[1024,1024]{1,0:T(8,128)} %param.5), kind=kLoop, calls=%fused_computation.2 | loop fusion | flops 4194304 | bytes 8388608 | tf_op jit(solution)/shard_map/panel_z/convert_element_type | solution.py:32
  25.5 0.9 %collective-permute-done.3 = bf16[128,1024]{1,0:T(8,128)(2,1)S(1)} collective-permute-done((bf16[128,1024]{1,0:T(8,128)(2,1)S(1)}, bf16[128,1024]{1,0:T(8,128)(2,1)S(1)}, u32[]{:S(2)}, u32[]{:S(2)}) %collective-permute-start.3) | collective-permute-done | bytes 262176 | tf_op jit(solution)/shard_map/panel_z/ppermute | solution.py:14
  26.4 0.1 collective-permute-start.7
  26.5 1.0 %collective-permute-start.8 = (bf16[128,1024]{1,0:T(8,128)(2,1)S(1)}, bf16[128,1024]{1,0:T(8,128)(2,1)S(1)}, u32[]{:S(2)}, u32[]{:S(2)}) collective-permute-start(bf16[128,1024]{1,0:T(8,128)(2,1)S(1)} %select_select_fusion), channel_id=1, source_target_pairs={{0,32},{32,64},{64,96},{96,0},{1,33},{33,65},{65,97},{97,1},{2,34}... | collective-permute-start | bytes 786440 | tf_op jit(solution)/shard_map/panel_x/ppermute | solution.py:10
  27.5 1.7 %collective-permute-start.9 = (bf16[128,1024]{1,0:T(8,128)(2,1)S(1)}, bf16[128,1024]{1,0:T(8,128)(2,1)S(1)}, u32[]{:S(2)}, u32[]{:S(2)}) collective-permute-start(bf16[128,1024]{1,0:T(8,128)(2,1)S(1)} %select_select_fusion), channel_id=1, source_target_pairs={{0,96},{32,0},{64,32},{96,64},{1,97},{33,1},{65,33},{97,65},{2,98}... | collective-permute-start | bytes 786440 | tf_op jit(solution)/shard_map/panel_x/ppermute | solution.py:10
  29.5 3.8 %collective-permute-done.7 = bf16[128,1024]{1,0:T(8,128)(2,1)S(1)} collective-permute-done((bf16[128,1024]{1,0:T(8,128)(2,1)S(1)}, bf16[128,1024]{1,0:T(8,128)(2,1)S(1)}, u32[]{:S(2)}, u32[]{:S(2)}) %collective-permute-start.7) | collective-permute-done | bytes 262176 | tf_op jit(solution)/shard_map/panel_x/ppermute | solution.py:10
  33.3 8.1 %collective-permute-done.8 = bf16[128,1024]{1,0:T(8,128)(2,1)S(1)} collective-permute-done((bf16[128,1024]{1,0:T(8,128)(2,1)S(1)}, bf16[128,1024]{1,0:T(8,128)(2,1)S(1)}, u32[]{:S(2)}, u32[]{:S(2)}) %collective-permute-start.8) | collective-permute-done | bytes 262176 | tf_op jit(solution)/shard_map/panel_x/ppermute | solution.py:10
  41.4 0.2 multiply_convert_fusion
  41.7 0.4 convolution_convert_fusion
  42.1 0.8 collective-permute-start.10
  42.9 0.4 fusion.22
  43.3 0.9 %collective-permute-done.10 = bf16[192,1024]{1,0:T(8,128)(2,1)S(1)} collective-permute-done((bf16[192,1024]{1,0:T(8,128)(2,1)S(1)}, bf16[192,1024]{1,0:T(8,128)(2,1)S(1)}, u32[]{:S(2)}, u32[]{:S(2)}) %collective-permute-start.10) | collective-permute-done | bytes 393248 | tf_op jit(solution)/shard_map/response/ppermute | solution.py:18
  44.2 0.1 convert_add_fusion
  44.4 3.0 %collective-permute-start.11 = (bf16[48,1024]{1,0:T(8,128)(2,1)S(1)}, bf16[48,1024]{1,0:T(8,128)(2,1)S(1)}, u32[]{:S(2)}, u32[]{:S(2)}) collective-permute-start(bf16[48,1024]{1,0:T(8,128)(2,1)S(1)} %get-tuple-element.56), channel_id=1, source_target_pairs={{0,128},{16,144},{128,0},{144,16},{1,129},{17,145},{129,1},{145,17... | collective-permute-start | bytes 294920 | tf_op jit(solution)/shard_map/sum_y/ppermute | solution.py:10
  47.4 0.4 collective-permute-start.12
  47.8 2.3 %collective-permute-start.13 = (bf16[48,1024]{1,0:T(8,128)(2,1)S(1)}, bf16[48,1024]{1,0:T(8,128)(2,1)S(1)}, u32[]{:S(2)}, u32[]{:S(2)}) collective-permute-start(bf16[48,1024]{1,0:T(8,128)(2,1)S(1)} %get-tuple-element.57), channel_id=1, source_target_pairs={{0,144},{16,0},{128,16},{144,128},{1,145},{17,1},{129,17},{145,129... | collective-permute-start | bytes 294920 | tf_op jit(solution)/shard_map/sum_y/ppermute | solution.py:10
  50.2 1.3 %fusion.23 = f32[1024,512]{0,1:T(8,128)S(1)} fusion(bf16[1024,1024]{1,0:T(8,128)(2,1)S(1)} %get-tuple-element.42, bf16[512,1024]{1,0:T(8,128)(2,1)S(1)} %constant_dynamic-update-slice_fusion.4), kind=kOutput, calls=%fused_computation.91 | convolution fusion | flops 1073741824 | bytes 5242880 | tf_op jit(solution)/shard_map/inverse_factors/dot_general | solution.py:105
  51.5 1.3 %reduce-precision_convert_fusion.1 = (bf16[1024,512]{0,1:T(8,128)(2,1)S(1)}, bf16[1024,512]{0,1:T(8,128)(2,1)S(1)}) fusion(f32[1024,512]{0,1:T(8,128)S(1)} %fusion.23, bf16[1024,1024]{1,0:T(8,128)(2,1)S(1)} %get-tuple-element.37, bf16[512,1024]{1,0:T(8,128)(2,1)S(1)} %constant_dynamic-update-slice_fusion.4), kind=kOutput, calls=%fused_computation.4 | convolution fusion | flops 1076363264 | bytes 7340032 | tf_op jit(solution)/shard_map/inverse_factors/dot_general | solution.py:105
  52.8 0.2 pad_maximum_fusion
  53.0 0.1 fusion.4
  53.2 1.0 %collective-permute-start.14 = (bf16[48,1024]{1,0:T(8,128)(2,1)S(1)}, bf16[48,1024]{1,0:T(8,128)(2,1)S(1)}, u32[]{:S(2)}, u32[]{:S(2)}) collective-permute-start(bf16[48,1024]{1,0:T(8,128)(2,1)S(1)} %get-tuple-element.55), channel_id=1, source_target_pairs={{0,128},{16,144},{128,0},{144,16},{1,129},{17,145},{129,1},{145,17... | collective-permute-start | bytes 294920 | tf_op jit(solution)/shard_map/gather_y/ppermute | solution.py:10
  54.1 1.5 %collective-permute-start.15 = (bf16[48,1024]{1,0:T(8,128)(2,1)S(1)}, bf16[48,1024]{1,0:T(8,128)(2,1)S(1)}, u32[]{:S(2)}, u32[]{:S(2)}) collective-permute-start(bf16[48,1024]{1,0:T(8,128)(2,1)S(1)} %get-tuple-element.55), channel_id=1, source_target_pairs={{0,16},{16,128},{128,144},{144,0},{1,17},{17,129},{129,145},{145,1... | collective-permute-start | bytes 294920 | tf_op jit(solution)/shard_map/gather_y/ppermute | solution.py:10
  55.7 1.2 %collective-permute-start.16 = (bf16[48,1024]{1,0:T(8,128)(2,1)S(1)}, bf16[48,1024]{1,0:T(8,128)(2,1)S(1)}, u32[]{:S(2)}, u32[]{:S(2)}) collective-permute-start(bf16[48,1024]{1,0:T(8,128)(2,1)S(1)} %get-tuple-element.55), channel_id=1, source_target_pairs={{0,144},{16,0},{128,16},{144,128},{1,145},{17,1},{129,17},{145,129... | collective-permute-start | bytes 294920 | tf_op jit(solution)/shard_map/gather_y/ppermute | solution.py:10
  56.8 0.5 fusion.5
  57.3 1.2 %convolution_add_fusion.1 = f32[48,1024]{1,0:T(8,128)} fusion(bf16[48,1024]{1,0:T(8,128)(2,1)S(1)} %get-tuple-element.55, bf16[1024,1024]{1,0:T(8,128)(2,1)S(1)} %get-tuple-element.42, f32[96,1024]{1,0:T(8,128)S(1)} %fusion.5), kind=kOutput, calls=%fused_computation.14 | convolution fusion | flops 100761600 | bytes 2785280 | tf_op jit(solution)/shard_map/screen/dot_general | solution.py:119
  58.5 1.5 %collective-permute-done.15 = bf16[48,1024]{1,0:T(8,128)(2,1)S(1)} collective-permute-done((bf16[48,1024]{1,0:T(8,128)(2,1)S(1)}, bf16[48,1024]{1,0:T(8,128)(2,1)S(1)}, u32[]{:S(2)}, u32[]{:S(2)}) %collective-permute-start.15) | collective-permute-done | bytes 98336 | tf_op jit(solution)/shard_map/gather_y/ppermute | solution.py:10
  60.0 2.9 %collective-permute-start.17 = (bf16[192,1024]{1,0:T(8,128)(2,1)S(1)}, bf16[192,1024]{1,0:T(8,128)(2,1)S(1)}, u32[]{:S(2)}, u32[]{:S(2)}) collective-permute-start(bf16[192,1024]{1,0:T(8,128)(2,1)S(1)} %pad_maximum_fusion.1), channel_id=1, source_target_pairs={{0,8},{8,0},{1,9},{9,1},{2,10},{10,2},{3,11},{11,3},{4,12},{12,4},... | collective-permute-start | bytes 1179656 | tf_op jit(solution)/shard_map/sigma/ppermute | solution.py:18
  63.0 0.9 %fusion.2 = f32[1024]{0:T(1024)S(1)} fusion(bf16[192,1024]{1,0:T(8,128)(2,1)S(1)} %pad_maximum_fusion.1, bf16[1024,1024]{0,1:T(8,128)(2,1)S(1)} %pad_maximum_fusion, bf16[192,512]{1,0:T(8,128)(2,1)S(1)} %bitcast.77), kind=kOutput, calls=%fused_computation.12 | convolution fusion | flops 403831808 | bytes 2691072 | tf_op jit(solution)/shard_map/sigma/dot_general | solution.py:140
  63.8 0.4 collective-permute-done.17
  64.3 0.9 %fusion.3 = f32[1024]{0:T(1024)S(1)} fusion(bf16[192,1024]{1,0:T(8,128)(2,1)S(1)} %collective-permute-done.17, bf16[1024,1024]{0,1:T(8,128)(2,1)S(1)} %pad_maximum_fusion, bf16[192,512]{1,0:T(8,128)(2,1)S(1)} %bitcast.76), kind=kOutput, calls=%fused_computation.13 | convolution fusion | flops 403831808 | bytes 2691072 | tf_op jit(solution)/shard_map/sigma/dot_general | solution.py:140
  65.2 0.1 select_add_fusion
  65.3 14.1 %all_to_all.9 = f32[32,1,128]{2,1,0:T(1,128)S(1)} all-to-all(f32[32,1,128]{2,1,0:T(1,128)S(1)} %bitcast.78), channel_id=1, replica_groups=mesh['grp'=2,'x'=4,'ylo'=2,'core'=2,'col'=8] {'x','col'}, dimensions={0} | all-to-all | bytes 32768 | tf_op jit(solution)/shard_map/sigma/all_to_all | solution.py:152
  79.4 0.6 reduce_sum.39
  (41 shorter events, 0.6 us)
Async XLA Ops:
  0.6 19.0 %copy-start = (bf16[128,1536]{1,0:T(8,128)(2,1)S(1)}, bf16[128,1536]{1,0:T(8,128)(2,1)}, u32[]{:S(2)}) copy-start(bf16[128,1536]{1,0:T(8,128)(2,1)} %param.3) | copy-start | bytes 1179652
  1.7 17.9 %collective-permute-start = (bf16[128,1024]{1,0:T(8,128)(2,1)S(1)}, bf16[128,1024]{1,0:T(8,128)(2,1)S(1)}, u32[]{:S(2)}, u32[]{:S(2)}) collective-permute-start(bf16[128,1024]{1,0:T(8,128)(2,1)S(1)} %slice.39), channel_id=1, source_target_pairs={{0,3},{8,11},{16,19},{24,27},{32,35},{40,43},{48,51},{56,59},{64,6... | collective-permute-start | bytes 786440 | tf_op jit(solution)/shard_map/panel_z/ppermute | solution.py:14
  8.8 10.8 %collective-permute-start.1 = (bf16[128,1024]{1,0:T(8,128)(2,1)S(1)}, bf16[128,1024]{1,0:T(8,128)(2,1)S(1)}, u32[]{:S(2)}, u32[]{:S(2)}) collective-permute-start(bf16[128,1024]{1,0:T(8,128)(2,1)S(1)} %slice.39), channel_id=1, source_target_pairs={{0,6},{8,14},{16,22},{24,30},{32,38},{40,46},{48,54},{56,62},{64,7... | collective-permute-start | bytes 786440 | tf_op jit(solution)/shard_map/panel_z/ppermute | solution.py:14
  13.3 12.1 %collective-permute-start.4 = (bf16[400,128]{1,0:T(8,128)(2,1)S(1)}, bf16[400,128]{1,0:T(8,128)(2,1)S(1)}, u32[]{:S(2)}, u32[]{:S(2)}) collective-permute-start(bf16[400,128]{1,0:T(8,128)(2,1)S(1)} %concatenate.48), channel_id=1, source_target_pairs={{0,64},{32,96},{64,0},{96,32},{1,65},{33,97},{65,1},{97,33},{2,66}... | collective-permute-start | bytes 307208 | tf_op jit(solution)/shard_map/blocks/ppermute | solution.py:10
  16.3 9.1 %collective-permute-start.5 = (bf16[400,128]{1,0:T(8,128)(2,1)S(1)}, bf16[400,128]{1,0:T(8,128)(2,1)S(1)}, u32[]{:S(2)}, u32[]{:S(2)}) collective-permute-start(bf16[400,128]{1,0:T(8,128)(2,1)S(1)} %concatenate.49), channel_id=1, source_target_pairs={{0,32},{32,64},{64,96},{96,0},{1,33},{33,65},{65,97},{97,1},{2,34}... | collective-permute-start | bytes 307208 | tf_op jit(solution)/shard_map/blocks/ppermute | solution.py:10
  16.9 8.6 %collective-permute-start.6 = (bf16[400,128]{1,0:T(8,128)(2,1)S(1)}, bf16[400,128]{1,0:T(8,128)(2,1)S(1)}, u32[]{:S(2)}, u32[]{:S(2)}) collective-permute-start(bf16[400,128]{1,0:T(8,128)(2,1)S(1)} %concatenate.50), channel_id=1, source_target_pairs={{0,96},{32,0},{64,32},{96,64},{1,97},{33,1},{65,33},{97,65},{2,98}... | collective-permute-start | bytes 307208 | tf_op jit(solution)/shard_map/blocks/ppermute | solution.py:10
  19.7 5.8 %collective-permute-start.2 = (bf16[128,1024]{1,0:T(8,128)(2,1)S(1)}, bf16[128,1024]{1,0:T(8,128)(2,1)S(1)}, u32[]{:S(2)}, u32[]{:S(2)}) collective-permute-start(bf16[128,1024]{1,0:T(8,128)(2,1)S(1)} %select_select_fusion.1), channel_id=1, source_target_pairs={{0,7},{3,4},{6,5},{8,15},{11,12},{14,13},{16,23},{19,20},{22,21},{... | collective-permute-start | bytes 786440 | tf_op jit(solution)/shard_map/panel_z/ppermute | solution.py:14
  21.0 5.4 %collective-permute-start.3 = (bf16[128,1024]{1,0:T(8,128)(2,1)S(1)}, bf16[128,1024]{1,0:T(8,128)(2,1)S(1)}, u32[]{:S(2)}, u32[]{:S(2)}) collective-permute-start(bf16[128,1024]{1,0:T(8,128)(2,1)S(1)} %select_select_fusion.1), channel_id=1, source_target_pairs={{0,1},{3,2},{8,9},{11,10},{16,17},{19,18},{24,25},{27,26},{32,33},... | collective-permute-start | bytes 786440 | tf_op jit(solution)/shard_map/panel_z/ppermute | solution.py:14
  26.4 6.9 %collective-permute-start.7 = (bf16[128,1024]{1,0:T(8,128)(2,1)S(1)}, bf16[128,1024]{1,0:T(8,128)(2,1)S(1)}, u32[]{:S(2)}, u32[]{:S(2)}) collective-permute-start(bf16[128,1024]{1,0:T(8,128)(2,1)S(1)} %select_select_fusion), channel_id=1, source_target_pairs={{0,64},{32,96},{64,0},{96,32},{1,65},{33,97},{65,1},{97,33},{2,66}... | collective-permute-start | bytes 786440 | tf_op jit(solution)/shard_map/panel_x/ppermute | solution.py:10
  26.5 14.9 %collective-permute-start.8 = (bf16[128,1024]{1,0:T(8,128)(2,1)S(1)}, bf16[128,1024]{1,0:T(8,128)(2,1)S(1)}, u32[]{:S(2)}, u32[]{:S(2)}) collective-permute-start(bf16[128,1024]{1,0:T(8,128)(2,1)S(1)} %select_select_fusion), channel_id=1, source_target_pairs={{0,32},{32,64},{64,96},{96,0},{1,33},{33,65},{65,97},{97,1},{2,34}... | collective-permute-start | bytes 786440 | tf_op jit(solution)/shard_map/panel_x/ppermute | solution.py:10
  27.5 13.9 %collective-permute-start.9 = (bf16[128,1024]{1,0:T(8,128)(2,1)S(1)}, bf16[128,1024]{1,0:T(8,128)(2,1)S(1)}, u32[]{:S(2)}, u32[]{:S(2)}) collective-permute-start(bf16[128,1024]{1,0:T(8,128)(2,1)S(1)} %select_select_fusion), channel_id=1, source_target_pairs={{0,96},{32,0},{64,32},{96,64},{1,97},{33,1},{65,33},{97,65},{2,98}... | collective-permute-start | bytes 786440 | tf_op jit(solution)/shard_map/panel_x/ppermute | solution.py:10
  42.1 2.1 %collective-permute-start.10 = (bf16[192,1024]{1,0:T(8,128)(2,1)S(1)}, bf16[192,1024]{1,0:T(8,128)(2,1)S(1)}, u32[]{:S(2)}, u32[]{:S(2)}) collective-permute-start(bf16[192,1024]{1,0:T(8,128)(2,1)S(1)} %convolution_convert_fusion), channel_id=1, source_target_pairs={{0,8},{8,0},{1,9},{9,1},{2,10},{10,2},{3,11},{11,3},{4,12},{12,4},... | collective-permute-start | bytes 1179656 | tf_op jit(solution)/shard_map/response/ppermute | solution.py:18
  44.4 8.6 %collective-permute-start.11 = (bf16[48,1024]{1,0:T(8,128)(2,1)S(1)}, bf16[48,1024]{1,0:T(8,128)(2,1)S(1)}, u32[]{:S(2)}, u32[]{:S(2)}) collective-permute-start(bf16[48,1024]{1,0:T(8,128)(2,1)S(1)} %get-tuple-element.56), channel_id=1, source_target_pairs={{0,128},{16,144},{128,0},{144,16},{1,129},{17,145},{129,1},{145,17... | collective-permute-start | bytes 294920 | tf_op jit(solution)/shard_map/sum_y/ppermute | solution.py:10
  47.4 5.6 %collective-permute-start.12 = (bf16[48,1024]{1,0:T(8,128)(2,1)S(1)}, bf16[48,1024]{1,0:T(8,128)(2,1)S(1)}, u32[]{:S(2)}, u32[]{:S(2)}) collective-permute-start(bf16[48,1024]{1,0:T(8,128)(2,1)S(1)} %get-tuple-element.58), channel_id=1, source_target_pairs={{0,16},{16,128},{128,144},{144,0},{1,17},{17,129},{129,145},{145,1... | collective-permute-start | bytes 294920 | tf_op jit(solution)/shard_map/sum_y/ppermute | solution.py:10
  47.8 5.2 %collective-permute-start.13 = (bf16[48,1024]{1,0:T(8,128)(2,1)S(1)}, bf16[48,1024]{1,0:T(8,128)(2,1)S(1)}, u32[]{:S(2)}, u32[]{:S(2)}) collective-permute-start(bf16[48,1024]{1,0:T(8,128)(2,1)S(1)} %get-tuple-element.57), channel_id=1, source_target_pairs={{0,144},{16,0},{128,16},{144,128},{1,145},{17,1},{129,17},{145,129... | collective-permute-start | bytes 294920 | tf_op jit(solution)/shard_map/sum_y/ppermute | solution.py:10
  53.2 5.3 %collective-permute-start.14 = (bf16[48,1024]{1,0:T(8,128)(2,1)S(1)}, bf16[48,1024]{1,0:T(8,128)(2,1)S(1)}, u32[]{:S(2)}, u32[]{:S(2)}) collective-permute-start(bf16[48,1024]{1,0:T(8,128)(2,1)S(1)} %get-tuple-element.55), channel_id=1, source_target_pairs={{0,128},{16,144},{128,0},{144,16},{1,129},{17,145},{129,1},{145,17... | collective-permute-start | bytes 294920 | tf_op jit(solution)/shard_map/gather_y/ppermute | solution.py:10
  54.1 5.9 %collective-permute-start.15 = (bf16[48,1024]{1,0:T(8,128)(2,1)S(1)}, bf16[48,1024]{1,0:T(8,128)(2,1)S(1)}, u32[]{:S(2)}, u32[]{:S(2)}) collective-permute-start(bf16[48,1024]{1,0:T(8,128)(2,1)S(1)} %get-tuple-element.55), channel_id=1, source_target_pairs={{0,16},{16,128},{128,144},{144,0},{1,17},{17,129},{129,145},{145,1... | collective-permute-start | bytes 294920 | tf_op jit(solution)/shard_map/gather_y/ppermute | solution.py:10
  55.7 4.3 %collective-permute-start.16 = (bf16[48,1024]{1,0:T(8,128)(2,1)S(1)}, bf16[48,1024]{1,0:T(8,128)(2,1)S(1)}, u32[]{:S(2)}, u32[]{:S(2)}) collective-permute-start(bf16[48,1024]{1,0:T(8,128)(2,1)S(1)} %get-tuple-element.55), channel_id=1, source_target_pairs={{0,144},{16,0},{128,16},{144,128},{1,145},{17,1},{129,17},{145,129... | collective-permute-start | bytes 294920 | tf_op jit(solution)/shard_map/gather_y/ppermute | solution.py:10
  60.0 4.2 %collective-permute-start.17 = (bf16[192,1024]{1,0:T(8,128)(2,1)S(1)}, bf16[192,1024]{1,0:T(8,128)(2,1)S(1)}, u32[]{:S(2)}, u32[]{:S(2)}) collective-permute-start(bf16[192,1024]{1,0:T(8,128)(2,1)S(1)} %pad_maximum_fusion.1), channel_id=1, source_target_pairs={{0,8},{8,0},{1,9},{9,1},{2,10},{10,2},{3,11},{11,3},{4,12},{12,4},... | collective-permute-start | bytes 1179656 | tf_op jit(solution)/shard_map/sigma/ppermute | solution.py:18

commit v18 on v17

--- a/solution.py
+++ b/solution.py
@@ -75,20 +75,28 @@
 
     with jax.named_scope("panel_x"):
         blocks = [held] + [shift(held, X, nx, k) for k in steps[1:]]
-        panels = jnp.concatenate(blocks, axis=0)
 
     with jax.named_scope("response"):
         factors = jnp.concatenate(factors, axis=1)
         weight = jnp.sum(factors[-16:-13].astype(F32), axis=0)
         factors = factors[:-16]
-        weighted = (weight[:, None] * panels.astype(F32)).astype(LOW)
         by_core = factors.reshape(ny, 2, count, -1)
         theirs, mine = (
             lax.dynamic_index_in_dim(by_core, c, 1, False).reshape(ny * count, -1)
             for c in (1 - core, core)
         )
-        sent = jnp.dot(theirs, weighted, preferred_element_type=F32).astype(LOW)
-        kept = jnp.dot(mine, weighted, preferred_element_type=F32)
+        split = 2 * own
+
+        def product(rows, part):
+            block = jnp.concatenate(blocks[:2] if part == 0 else blocks[2:], axis=0)
+            columns = slice(part * split, (part + 1) * split)
+            weighted = (weight[columns, None] * block.astype(F32)).astype(LOW)
+            return jnp.dot(rows[:, columns], weighted, preferred_element_type=F32)
+
+        early = [product(rows, 0) for rows in (theirs, mine)]
+        *early, blocks[2], blocks[3] = lax.optimization_barrier((*early, blocks[2], blocks[3]))
+        sent = (early[0] + product(theirs, 1)).astype(LOW)
+        kept = early[1] + product(mine, 1)
         kept, sent = lax.optimization_barrier((kept, swap(sent)))
         kept = (kept + sent.astype(F32)).reshape(ny, count, panel)
         kept, *blocks = lax.optimization_barrier((kept, *blocks))

time: 80.2 us -> 83.4 us (1.040)
  other arithmetic: 5.29 us -> 9.45 us
  starting transfers between devices: 33.6 us -> 31.7 us
  matrix products: 6.78 us -> 8.53 us
  waiting for transfers between devices: 15.8 us -> 14.2 us
  local copies, waits for them, and re-layouts: 3.27 us -> 4.79 us
  blocking collectives: 14.1 us -> 13.1 us
    ppermute x2, starting transfers between devices: 3.67 us -> 1.89 us  [swap(): return lax.ppermute(value, CORE, [(0, 1), (1, 0)])]
    dot_general x2 -> x4, matrix products: 0.78 us -> 2.51 us  [product(): return jnp.dot(rows[:, columns], weighted, preferred_element_type=F32)]
    unnamed x9 -> x29, local copies, waits for them, and re-layouts: 1.35 us -> 2.87 us
    convert_element_type x2, other arithmetic: 3.22 us -> 4.59 us  [two_parts(): return (high.astype(LOW), (value - high).astype(LOW))]
    add x1, other arithmetic: 0.12 us -> 1.17 us  [body(): kept = (kept + sent.astype(F32)).reshape(ny, count, panel)]
    all_to_all x1, blocking collectives: 14.1 us -> 13.1 us  [body(): terms = lax.all_to_all(copies, (X, Z), 0, 0, tiled=True)]
    ppermute x2, waiting for transfers between devices: 1.35 us -> 0.41 us  [swap(): return lax.ppermute(value, CORE, [(0, 1), (1, 0)])]
    ppermute x4, waiting for transfers between devices: 0.9 us -> 0.01 us  [along_z(): return lax.ppermute(value, Z, pairs)]
  transfers between devices with their start and end apart: 18 -> 18, of which waited for: 6 -> 4; matrix products, arithmetic and copies ran while one was open for 15% -> 19% of each run, Pallas kernels for 0% -> 0%
where the time goes in v18:
time: 83.4 us; the launch traced here: 83 us
  starting transfers between devices  31.7 us (38%)
  waiting for transfers between devices  14.2 us (17%)
  blocking collectives  13.1 us (16%)
  other arithmetic  9.45 us (11%)
  matrix products  8.53 us (10%)
  local copies, waits for them, and re-layouts  4.79 us (6%)
  between operations  1.25 us (1%)
    ppermute x12, starting transfers between devices, shift(): lax.ppermute(value, axis, [(i, (i + step) % size) for i in range(size)])  17.8 us
    ppermute x12, waiting for transfers between devices, shift(): lax.ppermute(value, axis, [(i, (i + step) % size) for i in range(size)])  13.8 us
    all_to_all x1, blocking collectives, body(): terms = lax.all_to_all(copies, (X, Z), 0, 0, tiled=True)  13.1 us
    ppermute x4, starting transfers between devices, along_z(): return lax.ppermute(value, Z, pairs)  12.1 us
    convert_element_type x2, other arithmetic, two_parts(): return (high.astype(LOW), (value - high).astype(LOW))  4.59 us
    unnamed x29, local copies, waits for them, and re-layouts  2.87 us
    dot_general x2, matrix products, body(): lax.dot_general(part, panels, (((1,), (1,)), ((), ())), preferred_element...  2.66 us
    dot_general x4, matrix products, product(): return jnp.dot(rows[:, columns], weighted, preferred_element_type=F32)  2.51 us
  transfers between devices with their start and end apart: 18, of which 4 were waited for; matrix products, arithmetic and copies ran while one was open for 19% of the time, Pallas kernels for 0%

profile of v18, /device:TPU:1, one launch (start us, length us, event | category | flops | bytes accessed | tf_op | source)
XLA Modules:
  0.0 83.0 jit_solution(14913905163632648531)
XLA Ops:
  0.6 1.0 %slice.59 = bf16[128,1024]{1,0:T(8,128)(2,1)S(1)} slice(bf16[128,1536]{1,0:T(8,128)(2,1)} %param.3), slice={[0:128], [0:1024]} | slice | bytes 524288 | tf_op jit(solution)/shard_map/panel_z/slice | solution.py:44
  1.7 7.1 %collective-permute-start = (bf16[128,1024]{1,0:T(8,128)(2,1)S(1)}, bf16[128,1024]{1,0:T(8,128)(2,1)S(1)}, u32[]{:S(2)}, u32[]{:S(2)}) collective-permute-start(bf16[128,1024]{1,0:T(8,128)(2,1)S(1)} %slice.59), channel_id=1, source_target_pairs={{0,3},{8,11},{16,19},{24,27},{32,35},{40,43},{48,51},{56,59},{64,6... | collective-permute-start | bytes 786440 | tf_op jit(solution)/shard_map/panel_z/ppermute | solution.py:14
  8.8 2.4 %collective-permute-start.1 = (bf16[128,1024]{1,0:T(8,128)(2,1)S(1)}, bf16[128,1024]{1,0:T(8,128)(2,1)S(1)}, u32[]{:S(2)}, u32[]{:S(2)}) collective-permute-start(bf16[128,1024]{1,0:T(8,128)(2,1)S(1)} %slice.59), channel_id=1, source_target_pairs={{0,6},{8,14},{16,22},{24,30},{32,38},{40,46},{48,54},{56,62},{64,7... | collective-permute-start | bytes 786440 | tf_op jit(solution)/shard_map/panel_z/ppermute | solution.py:14
  11.2 1.2 %copy.18 = bf16[128,1536]{0,1:T(8,128)(2,1)S(1)} copy(bf16[128,1536]{1,0:T(8,128)(2,1)} %param.3) | data formatting | bytes 786432 | tf_op args[0]
  12.4 0.7 fusion.27
  13.2 0.2 concatenate.53
  13.3 2.8 %collective-permute-start.4 = (bf16[400,128]{1,0:T(8,128)(2,1)S(1)}, bf16[400,128]{1,0:T(8,128)(2,1)S(1)}, u32[]{:S(2)}, u32[]{:S(2)}) collective-permute-start(bf16[400,128]{1,0:T(8,128)(2,1)S(1)} %concatenate.53), channel_id=1, source_target_pairs={{0,64},{32,96},{64,0},{96,32},{1,65},{33,97},{65,1},{97,33},{2,66}... | collective-permute-start | bytes 307208 | tf_op jit(solution)/shard_map/blocks/ppermute | solution.py:10
  16.2 0.2 concatenate.54
  16.3 0.4 collective-permute-start.5
  16.7 0.2 concatenate.55
  16.9 2.4 %collective-permute-start.6 = (bf16[400,128]{1,0:T(8,128)(2,1)S(1)}, bf16[400,128]{1,0:T(8,128)(2,1)S(1)}, u32[]{:S(2)}, u32[]{:S(2)}) collective-permute-start(bf16[400,128]{1,0:T(8,128)(2,1)S(1)} %concatenate.55), channel_id=1, source_target_pairs={{0,96},{32,0},{64,32},{96,64},{1,97},{33,1},{65,33},{97,65},{2,98}... | collective-permute-start | bytes 307208 | tf_op jit(solution)/shard_map/blocks/ppermute | solution.py:10
  19.6 0.5 broadcast_compare_fusion.2
  20.2 1.3 %collective-permute-start.2 = (bf16[128,1024]{1,0:T(8,128)(2,1)S(1)}, bf16[128,1024]{1,0:T(8,128)(2,1)S(1)}, u32[]{:S(2)}, u32[]{:S(2)}) collective-permute-start(bf16[128,1024]{1,0:T(8,128)(2,1)S(1)} %select_select_fusion.1), channel_id=1, source_target_pairs={{0,7},{3,4},{6,5},{8,15},{11,12},{14,13},{16,23},{19,20},{22,21},{... | collective-permute-start | bytes 786440 | tf_op jit(solution)/shard_map/panel_z/ppermute | solution.py:14
  21.5 1.3 %collective-permute-start.3 = (bf16[128,1024]{1,0:T(8,128)(2,1)S(1)}, bf16[128,1024]{1,0:T(8,128)(2,1)S(1)}, u32[]{:S(2)}, u32[]{:S(2)}) collective-permute-start(bf16[128,1024]{1,0:T(8,128)(2,1)S(1)} %select_select_fusion.1), channel_id=1, source_target_pairs={{0,1},{3,2},{8,9},{11,10},{16,17},{19,18},{24,25},{27,26},{32,33},... | collective-permute-start | bytes 786440 | tf_op jit(solution)/shard_map/panel_z/ppermute | solution.py:14
  22.8 4.5 %fusion = (bf16[1024,1024]{1,0:T(8,128)(2,1)S(1)}, bf16[1024,1024]{1,0:T(8,128)(2,1)}) fusion(f32[1024,1024]{1,0:T(8,128)} %param.5), kind=kLoop, calls=%fused_computation.2 | loop fusion | flops 4194304 | bytes 8388608 | tf_op jit(solution)/shard_map/panel_z/convert_element_type | solution.py:32
  27.4 0.6 collective-permute-start.8
  28.0 2.2 %collective-permute-start.9 = (bf16[128,1024]{1,0:T(8,128)(2,1)S(1)}, bf16[128,1024]{1,0:T(8,128)(2,1)S(1)}, u32[]{:S(2)}, u32[]{:S(2)}) collective-permute-start(bf16[128,1024]{1,0:T(8,128)(2,1)S(1)} %select_select_fusion), channel_id=1, source_target_pairs={{0,96},{32,0},{64,32},{96,64},{1,97},{33,1},{65,33},{97,65},{2,98}... | collective-permute-start | bytes 786440 | tf_op jit(solution)/shard_map/panel_x/ppermute | solution.py:10
  30.4 4.4 %collective-permute-done.7 = bf16[128,1024]{1,0:T(8,128)(2,1)S(1)} collective-permute-done((bf16[128,1024]{1,0:T(8,128)(2,1)S(1)}, bf16[128,1024]{1,0:T(8,128)(2,1)S(1)}, u32[]{:S(2)}, u32[]{:S(2)}) %collective-permute-start.7) | collective-permute-done | bytes 262176 | tf_op jit(solution)/shard_map/panel_x/ppermute | solution.py:10
  34.9 0.4 fusion.19
  35.2 0.4 fusion.21
  35.6 6.8 %collective-permute-done.8 = bf16[128,1024]{1,0:T(8,128)(2,1)S(1)} collective-permute-done((bf16[128,1024]{1,0:T(8,128)(2,1)S(1)}, bf16[128,1024]{1,0:T(8,128)(2,1)S(1)}, u32[]{:S(2)}, u32[]{:S(2)}) %collective-permute-start.8) | collective-permute-done | bytes 262176 | tf_op jit(solution)/shard_map/panel_x/ppermute | solution.py:10
  42.4 0.7 copy-done.3
  43.2 0.4 fusion.15
  43.5 0.9 %add_convert_fusion = bf16[192,1024]{1,0:T(8,128)(2,1)} fusion(f32[192,1024]{1,0:T(8,128)S(1)} %fusion.21, f32[192,1024]{1,0:T(8,128)S(1)} %fusion.15), kind=kLoop, calls=%fused_computation.16 | loop fusion | flops 393216 | bytes 1966080 | tf_op jit(solution)/shard_map/response/convert_element_type | solution.py:98
  44.4 0.7 collective-permute-start.10
  45.1 0.5 iota_add_fusion
  45.6 1.4 %fusion.17 = f32[192,1024]{1,0:T(8,128)S(1)} fusion(bf16[192,512]{1,0:T(8,128)(2,1)} %bitcast.66, bf16[128,1024]{1,0:T(8,128)(2,1)} %copy-done.5, bf16[128,1024]{1,0:T(8,128)(2,1)} %copy-done.3, f32[256]{0:T(256)S(1)} %get-tuple-element.85), kind=kOutput, calls=%fused_computation.43 | convolution fusion | flops 102236160 | bytes 1410048 | tf_op jit(solution)/shard_map/response/dot_general | solution.py:94
  47.2 1.2 %convert_add_fusion = f32[192,1024]{1,0:T(8,128)S(1)} fusion(f32[192,1024]{1,0:T(8,128)S(1)} %add.251, bf16[192,1024]{1,0:T(8,128)(2,1)} %collective-permute-done.10), kind=kLoop, calls=%fused_computation.15 | loop fusion | flops 393216 | bytes 1966080 | tf_op jit(solution)/shard_map/response/add | solution.py:101
  48.4 3.0 %collective-permute-start.11 = (bf16[48,1024]{1,0:T(8,128)(2,1)S(1)}, bf16[48,1024]{1,0:T(8,128)(2,1)S(1)}, u32[]{:S(2)}, u32[]{:S(2)}) collective-permute-start(bf16[48,1024]{1,0:T(8,128)(2,1)S(1)} %get-tuple-element.64), channel_id=1, source_target_pairs={{0,128},{16,144},{128,0},{144,16},{1,129},{17,145},{129,1},{145,17... | collective-permute-start | bytes 294920 | tf_op jit(solution)/shard_map/sum_y/ppermute | solution.py:10
  51.4 0.4 collective-permute-start.12
  51.8 2.3 %collective-permute-start.13 = (bf16[48,1024]{1,0:T(8,128)(2,1)S(1)}, bf16[48,1024]{1,0:T(8,128)(2,1)S(1)}, u32[]{:S(2)}, u32[]{:S(2)}) collective-permute-start(bf16[48,1024]{1,0:T(8,128)(2,1)S(1)} %get-tuple-element.65), channel_id=1, source_target_pairs={{0,144},{16,0},{128,16},{144,128},{1,145},{17,1},{129,17},{145,129... | collective-permute-start | bytes 294920 | tf_op jit(solution)/shard_map/sum_y/ppermute | solution.py:10
  54.3 1.3 %fusion.35 = f32[1024,512]{0,1:T(8,128)S(1)} fusion(bf16[1024,1024]{1,0:T(8,128)(2,1)S(1)} %get-tuple-element.50, bf16[512,1024]{1,0:T(8,128)(2,1)S(1)} %constant_dynamic-update-slice_fusion.4), kind=kOutput, calls=%fused_computation.104 | convolution fusion | flops 1073741824 | bytes 5242880 | tf_op jit(solution)/shard_map/inverse_factors/dot_general | solution.py:113
  55.6 0.3 copy-done
  55.9 1.4 %reduce-precision_convert_fusion.1 = (bf16[1024,512]{0,1:T(8,128)(2,1)S(1)}, bf16[1024,512]{0,1:T(8,128)(2,1)S(1)}) fusion(f32[1024,512]{0,1:T(8,128)S(1)} %fusion.35, bf16[1024,1024]{1,0:T(8,128)(2,1)S(1)} %copy-done, bf16[512,1024]{1,0:T(8,128)(2,1)S(1)} %constant_dynamic-update-slice_fusion.4), kind=kOutput, calls=%fused_computation.4 | convolution fusion | flops 1076363264 | bytes 7340032 | tf_op jit(solution)/shard_map/inverse_factors/dot_general | solution.py:113
  57.2 0.2 pad_maximum_fusion
  57.5 0.4 copy-done.10
  58.0 0.9 %collective-permute-start.14 = (bf16[48,1024]{1,0:T(8,128)(2,1)S(1)}, bf16[48,1024]{1,0:T(8,128)(2,1)S(1)}, u32[]{:S(2)}, u32[]{:S(2)}) collective-permute-start(bf16[48,1024]{1,0:T(8,128)(2,1)S(1)} %get-tuple-element.63), channel_id=1, source_target_pairs={{0,128},{16,144},{128,0},{144,16},{1,129},{17,145},{129,1},{145,17... | collective-permute-start | bytes 294920 | tf_op jit(solution)/shard_map/gather_y/ppermute | solution.py:10
  58.9 1.0 %collective-permute-start.15 = (bf16[48,1024]{1,0:T(8,128)(2,1)S(1)}, bf16[48,1024]{1,0:T(8,128)(2,1)S(1)}, u32[]{:S(2)}, u32[]{:S(2)}) collective-permute-start(bf16[48,1024]{1,0:T(8,128)(2,1)S(1)} %get-tuple-element.63), channel_id=1, source_target_pairs={{0,16},{16,128},{128,144},{144,0},{1,17},{17,129},{129,145},{145,1... | collective-permute-start | bytes 294920 | tf_op jit(solution)/shard_map/gather_y/ppermute | solution.py:10
  59.9 1.7 %collective-permute-start.16 = (bf16[48,1024]{1,0:T(8,128)(2,1)S(1)}, bf16[48,1024]{1,0:T(8,128)(2,1)S(1)}, u32[]{:S(2)}, u32[]{:S(2)}) collective-permute-start(bf16[48,1024]{1,0:T(8,128)(2,1)S(1)} %get-tuple-element.63), channel_id=1, source_target_pairs={{0,144},{16,0},{128,16},{144,128},{1,145},{17,1},{129,17},{145,129... | collective-permute-start | bytes 294920 | tf_op jit(solution)/shard_map/gather_y/ppermute | solution.py:10
  61.6 0.5 fusion.5
  62.1 1.2 %convolution_add_fusion.1 = f32[48,1024]{1,0:T(8,128)} fusion(bf16[48,1024]{1,0:T(8,128)(2,1)S(1)} %get-tuple-element.63, bf16[1024,1024]{1,0:T(8,128)(2,1)S(1)} %get-tuple-element.50, f32[96,1024]{1,0:T(8,128)S(1)} %fusion.5), kind=kOutput, calls=%fused_computation.12 | convolution fusion | flops 100761600 | bytes 2785280 | tf_op jit(solution)/shard_map/screen/dot_general | solution.py:127
  63.2 2.6 %collective-permute-done.15 = bf16[48,1024]{1,0:T(8,128)(2,1)S(1)} collective-permute-done((bf16[48,1024]{1,0:T(8,128)(2,1)S(1)}, bf16[48,1024]{1,0:T(8,128)(2,1)S(1)}, u32[]{:S(2)}, u32[]{:S(2)}) %collective-permute-start.15) | collective-permute-done | bytes 98336 | tf_op jit(solution)/shard_map/gather_y/ppermute | solution.py:10
  65.8 1.2 %collective-permute-start.17 = (bf16[192,1024]{1,0:T(8,128)(2,1)S(1)}, bf16[192,1024]{1,0:T(8,128)(2,1)S(1)}, u32[]{:S(2)}, u32[]{:S(2)}) collective-permute-start(bf16[192,1024]{1,0:T(8,128)(2,1)S(1)} %pad_maximum_fusion.1), channel_id=1, source_target_pairs={{0,8},{8,0},{1,9},{9,1},{2,10},{10,2},{3,11},{11,3},{4,12},{12,4},... | collective-permute-start | bytes 1179656 | tf_op jit(solution)/shard_map/sigma/ppermute | solution.py:18
  67.1 0.9 %fusion.2 = f32[1024]{0:T(1024)S(1)} fusion(bf16[192,1024]{1,0:T(8,128)(2,1)S(1)} %pad_maximum_fusion.1, bf16[1024,1024]{0,1:T(8,128)(2,1)S(1)} %pad_maximum_fusion, bf16[192,512]{1,0:T(8,128)(2,1)S(1)} %bitcast.75), kind=kOutput, calls=%fused_computation.10 | convolution fusion | flops 403831808 | bytes 2691072 | tf_op jit(solution)/shard_map/sigma/dot_general | solution.py:148
  68.0 0.4 collective-permute-done.17
  68.4 0.9 %fusion.3 = f32[1024]{0:T(1024)S(1)} fusion(bf16[192,1024]{1,0:T(8,128)(2,1)S(1)} %collective-permute-done.17, bf16[1024,1024]{0,1:T(8,128)(2,1)S(1)} %pad_maximum_fusion, bf16[192,512]{1,0:T(8,128)(2,1)S(1)} %bitcast.74), kind=kOutput, calls=%fused_computation.11 | convolution fusion | flops 403831808 | bytes 2691072 | tf_op jit(solution)/shard_map/sigma/dot_general | solution.py:148
  69.4 13.1 %all_to_all.9 = f32[32,1,128]{2,1,0:T(1,128)S(1)} all-to-all(f32[32,1,128]{2,1,0:T(1,128)S(1)} %bitcast.76), channel_id=1, replica_groups=mesh['grp'=2,'x'=4,'ylo'=2,'core'=2,'col'=8] {'x','col'}, dimensions={0} | all-to-all | bytes 32768 | tf_op jit(solution)/shard_map/sigma/all_to_all | solution.py:160
  82.4 0.6 reduce_sum.39
  (65 shorter events, 1.3 us)
Async XLA Ops:
  0.6 19.5 %copy-start.7 = (bf16[128,1536]{1,0:T(8,128)(2,1)S(1)}, bf16[128,1536]{1,0:T(8,128)(2,1)}, u32[]{:S(2)}) copy-start(bf16[128,1536]{1,0:T(8,128)(2,1)} %param.3) | copy-start | bytes 1179652
  1.7 18.4 %collective-permute-start = (bf16[128,1024]{1,0:T(8,128)(2,1)S(1)}, bf16[128,1024]{1,0:T(8,128)(2,1)S(1)}, u32[]{:S(2)}, u32[]{:S(2)}) collective-permute-start(bf16[128,1024]{1,0:T(8,128)(2,1)S(1)} %slice.59), channel_id=1, source_target_pairs={{0,3},{8,11},{16,19},{24,27},{32,35},{40,43},{48,51},{56,59},{64,6... | collective-permute-start | bytes 786440 | tf_op jit(solution)/shard_map/panel_z/ppermute | solution.py:14
  8.8 11.3 %collective-permute-start.1 = (bf16[128,1024]{1,0:T(8,128)(2,1)S(1)}, bf16[128,1024]{1,0:T(8,128)(2,1)S(1)}, u32[]{:S(2)}, u32[]{:S(2)}) collective-permute-start(bf16[128,1024]{1,0:T(8,128)(2,1)S(1)} %slice.59), channel_id=1, source_target_pairs={{0,6},{8,14},{16,22},{24,30},{32,38},{40,46},{48,54},{56,62},{64,7... | collective-permute-start | bytes 786440 | tf_op jit(solution)/shard_map/panel_z/ppermute | solution.py:14
  13.3 13.9 %collective-permute-start.4 = (bf16[400,128]{1,0:T(8,128)(2,1)S(1)}, bf16[400,128]{1,0:T(8,128)(2,1)S(1)}, u32[]{:S(2)}, u32[]{:S(2)}) collective-permute-start(bf16[400,128]{1,0:T(8,128)(2,1)S(1)} %concatenate.53), channel_id=1, source_target_pairs={{0,64},{32,96},{64,0},{96,32},{1,65},{33,97},{65,1},{97,33},{2,66}... | collective-permute-start | bytes 307208 | tf_op jit(solution)/shard_map/blocks/ppermute | solution.py:10
  16.3 10.9 %collective-permute-start.5 = (bf16[400,128]{1,0:T(8,128)(2,1)S(1)}, bf16[400,128]{1,0:T(8,128)(2,1)S(1)}, u32[]{:S(2)}, u32[]{:S(2)}) collective-permute-start(bf16[400,128]{1,0:T(8,128)(2,1)S(1)} %concatenate.54), channel_id=1, source_target_pairs={{0,32},{32,64},{64,96},{96,0},{1,33},{33,65},{65,97},{97,1},{2,34}... | collective-permute-start | bytes 307208 | tf_op jit(solution)/shard_map/blocks/ppermute | solution.py:10
  16.9 10.4 %collective-permute-start.6 = (bf16[400,128]{1,0:T(8,128)(2,1)S(1)}, bf16[400,128]{1,0:T(8,128)(2,1)S(1)}, u32[]{:S(2)}, u32[]{:S(2)}) collective-permute-start(bf16[400,128]{1,0:T(8,128)(2,1)S(1)} %concatenate.55), channel_id=1, source_target_pairs={{0,96},{32,0},{64,32},{96,64},{1,97},{33,1},{65,33},{97,65},{2,98}... | collective-permute-start | bytes 307208 | tf_op jit(solution)/shard_map/blocks/ppermute | solution.py:10
  20.2 7.1 %collective-permute-start.2 = (bf16[128,1024]{1,0:T(8,128)(2,1)S(1)}, bf16[128,1024]{1,0:T(8,128)(2,1)S(1)}, u32[]{:S(2)}, u32[]{:S(2)}) collective-permute-start(bf16[128,1024]{1,0:T(8,128)(2,1)S(1)} %select_select_fusion.1), channel_id=1, source_target_pairs={{0,7},{3,4},{6,5},{8,15},{11,12},{14,13},{16,23},{19,20},{22,21},{... | collective-permute-start | bytes 786440 | tf_op jit(solution)/shard_map/panel_z/ppermute | solution.py:14
  21.5 5.8 %collective-permute-start.3 = (bf16[128,1024]{1,0:T(8,128)(2,1)S(1)}, bf16[128,1024]{1,0:T(8,128)(2,1)S(1)}, u32[]{:S(2)}, u32[]{:S(2)}) collective-permute-start(bf16[128,1024]{1,0:T(8,128)(2,1)S(1)} %select_select_fusion.1), channel_id=1, source_target_pairs={{0,1},{3,2},{8,9},{11,10},{16,17},{19,18},{24,25},{27,26},{32,33},... | collective-permute-start | bytes 786440 | tf_op jit(solution)/shard_map/panel_z/ppermute | solution.py:14
  27.3 7.5 %collective-permute-start.7 = (bf16[128,1024]{1,0:T(8,128)(2,1)S(1)}, bf16[128,1024]{1,0:T(8,128)(2,1)S(1)}, u32[]{:S(2)}, u32[]{:S(2)}) collective-permute-start(bf16[128,1024]{1,0:T(8,128)(2,1)S(1)} %select_select_fusion), channel_id=1, source_target_pairs={{0,64},{32,96},{64,0},{96,32},{1,65},{33,97},{65,1},{97,33},{2,66}... | collective-permute-start | bytes 786440 | tf_op jit(solution)/shard_map/panel_x/ppermute | solution.py:10
  27.4 14.9 %collective-permute-start.8 = (bf16[128,1024]{1,0:T(8,128)(2,1)S(1)}, bf16[128,1024]{1,0:T(8,128)(2,1)S(1)}, u32[]{:S(2)}, u32[]{:S(2)}) collective-permute-start(bf16[128,1024]{1,0:T(8,128)(2,1)S(1)} %select_select_fusion), channel_id=1, source_target_pairs={{0,32},{32,64},{64,96},{96,0},{1,33},{33,65},{65,97},{97,1},{2,34}... | collective-permute-start | bytes 786440 | tf_op jit(solution)/shard_map/panel_x/ppermute | solution.py:10
  28.0 14.3 %collective-permute-start.9 = (bf16[128,1024]{1,0:T(8,128)(2,1)S(1)}, bf16[128,1024]{1,0:T(8,128)(2,1)S(1)}, u32[]{:S(2)}, u32[]{:S(2)}) collective-permute-start(bf16[128,1024]{1,0:T(8,128)(2,1)S(1)} %select_select_fusion), channel_id=1, source_target_pairs={{0,96},{32,0},{64,32},{96,64},{1,97},{33,1},{65,33},{97,65},{2,98}... | collective-permute-start | bytes 786440 | tf_op jit(solution)/shard_map/panel_x/ppermute | solution.py:10
  30.4 12.0 %copy-start.8 = (bf16[4,1,48,512]{3,2,1,0:T(8,128)(2,1)}, bf16[4,1,48,512]{3,2,1,0:T(8,128)(2,1)S(1)}, u32[]{:S(2)}) copy-start(bf16[4,1,48,512]{3,2,1,0:T(8,128)(2,1)S(1)} %get-tuple-element.75) | copy-start | bytes 589828
  34.9 7.5 %copy-start.1 = (bf16[128,1024]{1,0:T(8,128)(2,1)}, bf16[128,1024]{1,0:T(8,128)(2,1)S(1)}, u32[]{:S(2)}) copy-start(bf16[128,1024]{1,0:T(8,128)(2,1)S(1)} %collective-permute-done.7) | copy-start | bytes 786436
  42.4 0.7 copy-start.3
  42.4 0.8 copy-start.5
  44.4 2.8 %collective-permute-start.10 = (bf16[192,1024]{1,0:T(8,128)(2,1)}, bf16[192,1024]{1,0:T(8,128)(2,1)}, u32[]{:S(2)}, u32[]{:S(2)}) collective-permute-start(bf16[192,1024]{1,0:T(8,128)(2,1)} %add_convert_fusion), channel_id=1, source_target_pairs={{0,8},{8,0},{1,9},{9,1},{2,10},{10,2},{3,11},{11,3},{4,12},{12,4},... | collective-permute-start | bytes 1179656 | tf_op jit(solution)/shard_map/response/ppermute | solution.py:18
  47.2 7.0 %copy-start.2 = (bf16[128,1024]{1,0:T(8,128)(2,1)S(1)}, bf16[128,1024]{1,0:T(8,128)(2,1)}, u32[]{:S(2)}) copy-start(bf16[128,1024]{1,0:T(8,128)(2,1)} %copy-done.1) | copy-start | bytes 786436
  47.2 7.0 %copy-start.4 = (bf16[128,1024]{1,0:T(8,128)(2,1)S(1)}, bf16[128,1024]{1,0:T(8,128)(2,1)}, u32[]{:S(2)}) copy-start(bf16[128,1024]{1,0:T(8,128)(2,1)} %copy-done.3) | copy-start | bytes 786436
  47.2 7.0 %copy-start.6 = (bf16[128,1024]{1,0:T(8,128)(2,1)S(1)}, bf16[128,1024]{1,0:T(8,128)(2,1)}, u32[]{:S(2)}) copy-start(bf16[128,1024]{1,0:T(8,128)(2,1)} %copy-done.5) | copy-start | bytes 786436
  48.4 9.0 %collective-permute-start.11 = (bf16[48,1024]{1,0:T(8,128)(2,1)S(1)}, bf16[48,1024]{1,0:T(8,128)(2,1)S(1)}, u32[]{:S(2)}, u32[]{:S(2)}) collective-permute-start(bf16[48,1024]{1,0:T(8,128)(2,1)S(1)} %get-tuple-element.64), channel_id=1, source_target_pairs={{0,128},{16,144},{128,0},{144,16},{1,129},{17,145},{129,1},{145,17... | collective-permute-start | bytes 294920 | tf_op jit(solution)/shard_map/sum_y/ppermute | solution.py:10
  51.4 6.0 %collective-permute-start.12 = (bf16[48,1024]{1,0:T(8,128)(2,1)S(1)}, bf16[48,1024]{1,0:T(8,128)(2,1)S(1)}, u32[]{:S(2)}, u32[]{:S(2)}) collective-permute-start(bf16[48,1024]{1,0:T(8,128)(2,1)S(1)} %get-tuple-element.66), channel_id=1, source_target_pairs={{0,16},{16,128},{128,144},{144,0},{1,17},{17,129},{129,145},{145,1... | collective-permute-start | bytes 294920 | tf_op jit(solution)/shard_map/sum_y/ppermute | solution.py:10
  51.8 5.6 %collective-permute-start.13 = (bf16[48,1024]{1,0:T(8,128)(2,1)S(1)}, bf16[48,1024]{1,0:T(8,128)(2,1)S(1)}, u32[]{:S(2)}, u32[]{:S(2)}) collective-permute-start(bf16[48,1024]{1,0:T(8,128)(2,1)S(1)} %get-tuple-element.65), channel_id=1, source_target_pairs={{0,144},{16,0},{128,16},{144,128},{1,145},{17,1},{129,17},{145,129... | collective-permute-start | bytes 294920 | tf_op jit(solution)/shard_map/sum_y/ppermute | solution.py:10
  54.3 1.6 %copy-start = (bf16[1024,1024]{1,0:T(8,128)(2,1)S(1)}, bf16[1024,1024]{1,0:T(8,128)(2,1)}, u32[]{:S(2)}) copy-start(bf16[1024,1024]{1,0:T(8,128)(2,1)} %get-tuple-element.45) | copy-start | bytes 6291460
  57.2 0.7 copy-start.10
  58.0 5.2 %collective-permute-start.14 = (bf16[48,1024]{1,0:T(8,128)(2,1)S(1)}, bf16[48,1024]{1,0:T(8,128)(2,1)S(1)}, u32[]{:S(2)}, u32[]{:S(2)}) collective-permute-start(bf16[48,1024]{1,0:T(8,128)(2,1)S(1)} %get-tuple-element.63), channel_id=1, source_target_pairs={{0,128},{16,144},{128,0},{144,16},{1,129},{17,145},{129,1},{145,17... | collective-permute-start | bytes 294920 | tf_op jit(solution)/shard_map/gather_y/ppermute | solution.py:10
  58.9 6.9 %collective-permute-start.15 = (bf16[48,1024]{1,0:T(8,128)(2,1)S(1)}, bf16[48,1024]{1,0:T(8,128)(2,1)S(1)}, u32[]{:S(2)}, u32[]{:S(2)}) collective-permute-start(bf16[48,1024]{1,0:T(8,128)(2,1)S(1)} %get-tuple-element.63), channel_id=1, source_target_pairs={{0,16},{16,128},{128,144},{144,0},{1,17},{17,129},{129,145},{145,1... | collective-permute-start | bytes 294920 | tf_op jit(solution)/shard_map/gather_y/ppermute | solution.py:10
  59.9 5.9 %collective-permute-start.16 = (bf16[48,1024]{1,0:T(8,128)(2,1)S(1)}, bf16[48,1024]{1,0:T(8,128)(2,1)S(1)}, u32[]{:S(2)}, u32[]{:S(2)}) collective-permute-start(bf16[48,1024]{1,0:T(8,128)(2,1)S(1)} %get-tuple-element.63), channel_id=1, source_target_pairs={{0,144},{16,0},{128,16},{144,128},{1,145},{17,1},{129,17},{145,129... | collective-permute-start | bytes 294920 | tf_op jit(solution)/shard_map/gather_y/ppermute | solution.py:10
  65.8 2.5 %collective-permute-start.17 = (bf16[192,1024]{1,0:T(8,128)(2,1)S(1)}, bf16[192,1024]{1,0:T(8,128)(2,1)S(1)}, u32[]{:S(2)}, u32[]{:S(2)}) collective-permute-start(bf16[192,1024]{1,0:T(8,128)(2,1)S(1)} %pad_maximum_fusion.1), channel_id=1, source_target_pairs={{0,8},{8,0},{1,9},{9,1},{2,10},{10,2},{3,11},{11,3},{4,12},{12,4},... | collective-permute-start | bytes 1179656 | tf_op jit(solution)/shard_map/sigma/ppermute | solution.py:18
  68.0 1.3 %copy-start.9 = (pred[4]{0:T(512)(128)(4,1)S(1)}, pred[4]{0:T(512)(128)(4,1)}, u32[]{:S(2)}) copy-start(pred[4]{0:T(512)(128)(4,1)} %get-tuple-element.92) | copy-start | bytes 16

commit v19 on v17

--- a/solution.py
+++ b/solution.py
@@ -44,6 +44,7 @@
         piece = orbital_b[:, :panel]
         far_a = along_z(piece, (0, 3))
         far_b = along_z(piece, (0, 6))
+        orbital_b, far_a, far_b = lax.optimization_barrier((orbital_b, far_a, far_b))
 
     with jax.named_scope("blocks"):
         weight = 2.0 * gaps / (gaps * gaps + 1.0)
@@ -60,21 +61,17 @@
         factors = [rows[0]] + [shift(row, X, nx, k) for row, k in zip(rows[1:], steps[1:])]
 
     with jax.named_scope("panel_z"):
-        far_a, far_b, block_inverse, *_ = lax.optimization_barrier(
-            (far_a, far_b, block_inverse, *rows)
-        )
         held = jnp.where(z == 3, far_a, jnp.where(z == 6, far_b, piece))
         near_a = along_z(held, (0, 7), (3, 4), (6, 5))
         near_b = along_z(held, (0, 1), (3, 2))
-        inv_high, inv_rest = two_parts(block_inverse)
-        near_a, near_b, inv_high, inv_rest, *factors = lax.optimization_barrier(
-            (near_a, near_b, inv_high, inv_rest, *factors)
-        )
+        near_a, near_b, *factors = lax.optimization_barrier((near_a, near_b, *factors))
         held = jnp.where((z == 7) | (z == 4) | (z == 5), near_a, held)
         held = jnp.where((z == 1) | (z == 2), near_b, held)
 
     with jax.named_scope("panel_x"):
         blocks = [held] + [shift(held, X, nx, k) for k in steps[1:]]
+        inv_high, inv_rest = two_parts(block_inverse + 0 * held[:1, :1].astype(F32))
+        blocks[2], inv_high, inv_rest = lax.optimization_barrier((blocks[2], inv_high, inv_rest))
         panels = jnp.concatenate(blocks, axis=0)
 
     with jax.named_scope("response"):

time: 80.2 us -> 85.5 us (1.066)
  starting transfers between devices: 33.6 us -> 37 us
  blocking collectives: 14.1 us -> 15.3 us
  other arithmetic: 5.29 us -> 6.26 us
    ppermute x12, waiting for transfers between devices: 13.5 us -> 9.67 us  [shift(): lax.ppermute(value, axis, [(i, (i + step) % size) for i in range(size)])]
    ppermute x4, waiting for transfers between devices: 0.9 us -> 4.23 us  [along_z(): return lax.ppermute(value, Z, pairs)]
    ppermute x2, starting transfers between devices: 3.67 us -> 6.05 us  [swap(): return lax.ppermute(value, CORE, [(0, 1), (1, 0)])]
    unnamed x9 -> x8, local copies, waits for them, and re-layouts: 1.35 us -> 0.14 us
    all_to_all x1, blocking collectives: 14.1 us -> 15.3 us  [body(): terms = lax.all_to_all(copies, (X, Z), 0, 0, tiled=True)]
    ppermute x12, starting transfers between devices: 17.8 us -> 18.9 us  [shift(): lax.ppermute(value, axis, [(i, (i + step) % size) for i in range(size)])]
    select_n x1, other arithmetic: 0.04 us -> 0.99 us  [body(): held = jnp.where(z == 3, far_a, jnp.where(z == 6, far_b, piece))]
  transfers between devices with their start and end apart: 18 -> 18, of which waited for: 6 -> 8; matrix products, arithmetic and copies ran while one was open for 15% -> 13% of each run, Pallas kernels for 0% -> 0%
where the time goes in v19:
time: 85.5 us; the launch traced here: 85.2 us
  starting transfers between devices  37 us (43%)
  waiting for transfers between devices  15.3 us (18%)
  blocking collectives  15.3 us (18%)
  matrix products  6.74 us (8%)
  other arithmetic  6.26 us (7%)
  local copies, waits for them, and re-layouts  2.78 us (3%)
  between operations  1.89 us (2%)
    ppermute x12, starting transfers between devices, shift(): lax.ppermute(value, axis, [(i, (i + step) % size) for i in range(size)])  18.9 us
    all_to_all x1, blocking collectives, body(): terms = lax.all_to_all(copies, (X, Z), 0, 0, tiled=True)  15.3 us
    ppermute x4, starting transfers between devices, along_z(): return lax.ppermute(value, Z, pairs)  12.1 us
    ppermute x12, waiting for transfers between devices, shift(): lax.ppermute(value, axis, [(i, (i + step) % size) for i in range(size)])  9.67 us
    ppermute x2, starting transfers between devices, swap(): return lax.ppermute(value, CORE, [(0, 1), (1, 0)])  6.05 us
    ppermute x4, waiting for transfers between devices, along_z(): return lax.ppermute(value, Z, pairs)  4.23 us
    convert_element_type x2, other arithmetic, two_parts(): return (high.astype(LOW), (value - high).astype(LOW))  3.25 us
    dot_general x2, matrix products, body(): lax.dot_general(part, panels, (((1,), (1,)), ((), ())), preferred_element...  2.64 us
  transfers between devices with their start and end apart: 18, of which 8 were waited for; matrix products, arithmetic and copies ran while one was open for 13% of the time, Pallas kernels for 0%

profile of v19, /device:TPU:1, one launch (start us, length us, event | category | flops | bytes accessed | tf_op | source)
XLA Modules:
  0.0 85.2 jit_solution(1719378824534732969)
XLA Ops:
  0.6 1.0 %slice.42 = bf16[128,1024]{1,0:T(8,128)(2,1)S(1)} slice(bf16[128,1536]{1,0:T(8,128)(2,1)} %param.3), slice={[0:128], [0:1024]} | slice | bytes 524288 | tf_op jit(solution)/shard_map/panel_z/slice | solution.py:44
  1.7 7.1 %collective-permute-start = (bf16[128,1024]{1,0:T(8,128)(2,1)S(1)}, bf16[128,1024]{1,0:T(8,128)(2,1)S(1)}, u32[]{:S(2)}, u32[]{:S(2)}) collective-permute-start(bf16[128,1024]{1,0:T(8,128)(2,1)S(1)} %slice.42), channel_id=1, source_target_pairs={{0,3},{8,11},{16,19},{24,27},{32,35},{40,43},{48,51},{56,59},{64,6... | collective-permute-start | bytes 786440 | tf_op jit(solution)/shard_map/panel_z/ppermute | solution.py:14
  8.8 2.4 %collective-permute-start.1 = (bf16[128,1024]{1,0:T(8,128)(2,1)S(1)}, bf16[128,1024]{1,0:T(8,128)(2,1)S(1)}, u32[]{:S(2)}, u32[]{:S(2)}) collective-permute-start(bf16[128,1024]{1,0:T(8,128)(2,1)S(1)} %slice.42), channel_id=1, source_target_pairs={{0,6},{8,14},{16,22},{24,30},{32,38},{40,46},{48,54},{56,62},{64,7... | collective-permute-start | bytes 786440 | tf_op jit(solution)/shard_map/panel_z/ppermute | solution.py:14
  11.1 0.7 fusion.19
  11.9 1.9 %collective-permute-done = bf16[128,1024]{1,0:T(8,128)(2,1)S(1)} collective-permute-done((bf16[128,1024]{1,0:T(8,128)(2,1)S(1)}, bf16[128,1024]{1,0:T(8,128)(2,1)S(1)}, u32[]{:S(2)}, u32[]{:S(2)}) %collective-permute-start) | collective-permute-done | bytes 262176 | tf_op jit(solution)/shard_map/panel_z/ppermute | solution.py:14
  13.7 2.4 %collective-permute-done.1 = bf16[128,1024]{1,0:T(8,128)(2,1)S(1)} collective-permute-done((bf16[128,1024]{1,0:T(8,128)(2,1)S(1)}, bf16[128,1024]{1,0:T(8,128)(2,1)S(1)}, u32[]{:S(2)}, u32[]{:S(2)}) %collective-permute-start.1) | collective-permute-done | bytes 262176 | tf_op jit(solution)/shard_map/panel_z/ppermute | solution.py:14
  16.1 1.0 %select_select_fusion.1 = bf16[128,1024]{1,0:T(8,128)(2,1)S(1)} fusion(bf16[128,1024]{1,0:T(8,128)(2,1)S(1)} %collective-permute-done, bf16[128,1024]{1,0:T(8,128)(2,1)S(1)} %collective-permute-done.1, pred[]{:T(512)S(6)} %eq.85, pred[]{:T(512)S(6)} %eq.84, bf16[128,1536]{1,0:T(8,128)(2,1)} %param.3), kind=kLoop, calls=%fused_computation.20 | loop fusion | flops 262144 | bytes 1048578 | tf_op jit(solution)/shard_map/panel_z/jit(_where)/select_n | solution.py:64
  17.1 1.3 %collective-permute-start.2 = (bf16[128,1024]{1,0:T(8,128)(2,1)S(1)}, bf16[128,1024]{1,0:T(8,128)(2,1)S(1)}, u32[]{:S(2)}, u32[]{:S(2)}) collective-permute-start(bf16[128,1024]{1,0:T(8,128)(2,1)S(1)} %select_select_fusion.1), channel_id=1, source_target_pairs={{0,7},{3,4},{6,5},{8,15},{11,12},{14,13},{16,23},{19,20},{22,21},{... | collective-permute-start | bytes 786440 | tf_op jit(solution)/shard_map/panel_z/ppermute | solution.py:14
  18.4 1.3 %collective-permute-start.3 = (bf16[128,1024]{1,0:T(8,128)(2,1)S(1)}, bf16[128,1024]{1,0:T(8,128)(2,1)S(1)}, u32[]{:S(2)}, u32[]{:S(2)}) collective-permute-start(bf16[128,1024]{1,0:T(8,128)(2,1)S(1)} %select_select_fusion.1), channel_id=1, source_target_pairs={{0,1},{3,2},{8,9},{11,10},{16,17},{19,18},{24,25},{27,26},{32,33},... | collective-permute-start | bytes 786440 | tf_op jit(solution)/shard_map/panel_z/ppermute | solution.py:14
  19.9 0.2 copy.18
  20.2 0.2 concatenate.48
  20.4 2.8 %collective-permute-start.4 = (bf16[400,128]{1,0:T(8,128)(2,1)S(1)}, bf16[400,128]{1,0:T(8,128)(2,1)S(1)}, u32[]{:S(2)}, u32[]{:S(2)}) collective-permute-start(bf16[400,128]{1,0:T(8,128)(2,1)S(1)} %concatenate.48), channel_id=1, source_target_pairs={{0,64},{32,96},{64,0},{96,32},{1,65},{33,97},{65,1},{97,33},{2,66}... | collective-permute-start | bytes 307208 | tf_op jit(solution)/shard_map/blocks/ppermute | solution.py:10
  23.2 0.2 concatenate.49
  23.4 0.4 collective-permute-start.5
  23.8 0.2 concatenate.50
  24.0 2.4 %collective-permute-start.6 = (bf16[400,128]{1,0:T(8,128)(2,1)S(1)}, bf16[400,128]{1,0:T(8,128)(2,1)S(1)}, u32[]{:S(2)}, u32[]{:S(2)}) collective-permute-start(bf16[400,128]{1,0:T(8,128)(2,1)S(1)} %concatenate.50), channel_id=1, source_target_pairs={{0,96},{32,0},{64,32},{96,64},{1,97},{33,1},{65,33},{97,65},{2,98}... | collective-permute-start | bytes 307208 | tf_op jit(solution)/shard_map/blocks/ppermute | solution.py:10
  26.4 0.2 concatenate.47
  26.6 2.3 %collective-permute-done.5 = bf16[400,128]{1,0:T(8,128)(2,1)S(1)} collective-permute-done((bf16[400,128]{1,0:T(8,128)(2,1)S(1)}, bf16[400,128]{1,0:T(8,128)(2,1)S(1)}, u32[]{:S(2)}, u32[]{:S(2)}) %collective-permute-start.5) | collective-permute-done | bytes 102432 | tf_op jit(solution)/shard_map/blocks/ppermute | solution.py:10
  29.0 0.5 slice.56
  29.5 3.9 %collective-permute-start.7 = (bf16[128,1024]{1,0:T(8,128)(2,1)S(1)}, bf16[128,1024]{1,0:T(8,128)(2,1)S(1)}, u32[]{:S(2)}, u32[]{:S(2)}) collective-permute-start(bf16[128,1024]{1,0:T(8,128)(2,1)S(1)} %select_select_fusion), channel_id=1, source_target_pairs={{0,64},{32,96},{64,0},{96,32},{1,65},{33,97},{65,1},{97,33},{2,66}... | collective-permute-start | bytes 786440 | tf_op jit(solution)/shard_map/panel_x/ppermute | solution.py:10
  34.1 3.1 %fusion = (bf16[1024,1024]{1,0:T(8,128)(2,1)S(1)}, bf16[1024,1024]{1,0:T(8,128)(2,1)S(1)}) fusion(f32[1024,1024]{1,0:T(8,128)} %param.5, f32[]{:T(128)} %bitcast.12), kind=kLoop, calls=%fused_computation.2 | loop fusion | flops 5242880 | bytes 8388612 | tf_op jit(solution)/shard_map/panel_x/convert_element_type | solution.py:32
  37.4 4.9 %collective-permute-done.7 = bf16[128,1024]{1,0:T(8,128)(2,1)S(1)} collective-permute-done((bf16[128,1024]{1,0:T(8,128)(2,1)S(1)}, bf16[128,1024]{1,0:T(8,128)(2,1)S(1)}, u32[]{:S(2)}, u32[]{:S(2)}) %collective-permute-start.7) | collective-permute-done | bytes 262176 | tf_op jit(solution)/shard_map/panel_x/ppermute | solution.py:10
  42.3 0.9 %collective-permute-done.9 = bf16[128,1024]{1,0:T(8,128)(2,1)S(1)} collective-permute-done((bf16[128,1024]{1,0:T(8,128)(2,1)S(1)}, bf16[128,1024]{1,0:T(8,128)(2,1)S(1)}, u32[]{:S(2)}, u32[]{:S(2)}) %collective-permute-start.9) | collective-permute-done | bytes 262176 | tf_op jit(solution)/shard_map/panel_x/ppermute | solution.py:10
  43.2 0.2 multiply_convert_fusion
  43.4 0.4 convolution_convert_fusion
  43.8 3.2 %collective-permute-start.10 = (bf16[192,1024]{1,0:T(8,128)(2,1)S(1)}, bf16[192,1024]{1,0:T(8,128)(2,1)S(1)}, u32[]{:S(2)}, u32[]{:S(2)}) collective-permute-start(bf16[192,1024]{1,0:T(8,128)(2,1)S(1)} %convolution_convert_fusion), channel_id=1, source_target_pairs={{0,8},{8,0},{1,9},{9,1},{2,10},{10,2},{3,11},{11,3},{4,12},{12,4},... | collective-permute-start | bytes 1179656 | tf_op jit(solution)/shard_map/response/ppermute | solution.py:18
  47.0 0.4 fusion.22
  47.4 0.9 %collective-permute-done.10 = bf16[192,1024]{1,0:T(8,128)(2,1)S(1)} collective-permute-done((bf16[192,1024]{1,0:T(8,128)(2,1)S(1)}, bf16[192,1024]{1,0:T(8,128)(2,1)S(1)}, u32[]{:S(2)}, u32[]{:S(2)}) %collective-permute-start.10) | collective-permute-done | bytes 393248 | tf_op jit(solution)/shard_map/response/ppermute | solution.py:18
  48.3 0.1 convert_add_fusion
  48.5 3.0 %collective-permute-start.11 = (bf16[48,1024]{1,0:T(8,128)(2,1)S(1)}, bf16[48,1024]{1,0:T(8,128)(2,1)S(1)}, u32[]{:S(2)}, u32[]{:S(2)}) collective-permute-start(bf16[48,1024]{1,0:T(8,128)(2,1)S(1)} %get-tuple-element.58), channel_id=1, source_target_pairs={{0,128},{16,144},{128,0},{144,16},{1,129},{17,145},{129,1},{145,17... | collective-permute-start | bytes 294920 | tf_op jit(solution)/shard_map/sum_y/ppermute | solution.py:10
  51.5 0.4 collective-permute-start.12
  51.9 2.3 %collective-permute-start.13 = (bf16[48,1024]{1,0:T(8,128)(2,1)S(1)}, bf16[48,1024]{1,0:T(8,128)(2,1)S(1)}, u32[]{:S(2)}, u32[]{:S(2)}) collective-permute-start(bf16[48,1024]{1,0:T(8,128)(2,1)S(1)} %get-tuple-element.59), channel_id=1, source_target_pairs={{0,144},{16,0},{128,16},{144,128},{1,145},{17,1},{129,17},{145,129... | collective-permute-start | bytes 294920 | tf_op jit(solution)/shard_map/sum_y/ppermute | solution.py:10
  54.3 1.3 %fusion.23 = f32[1024,512]{0,1:T(8,128)S(1)} fusion(bf16[1024,1024]{1,0:T(8,128)(2,1)S(1)} %get-tuple-element.44, bf16[512,1024]{1,0:T(8,128)(2,1)S(1)} %constant_dynamic-update-slice_fusion.4), kind=kOutput, calls=%fused_computation.91 | convolution fusion | flops 1073741824 | bytes 5242880 | tf_op jit(solution)/shard_map/inverse_factors/dot_general | solution.py:102
  55.6 1.3 %reduce-precision_convert_fusion.1 = (bf16[1024,512]{0,1:T(8,128)(2,1)S(1)}, bf16[1024,512]{0,1:T(8,128)(2,1)S(1)}) fusion(f32[1024,512]{0,1:T(8,128)S(1)} %fusion.23, bf16[1024,1024]{1,0:T(8,128)(2,1)S(1)} %get-tuple-element.39, bf16[512,1024]{1,0:T(8,128)(2,1)S(1)} %constant_dynamic-update-slice_fusion.4), kind=kOutput, calls=%fused_computation.4 | convolution fusion | flops 1076363264 | bytes 7340032 | tf_op jit(solution)/shard_map/inverse_factors/dot_general | solution.py:102
  56.9 0.2 pad_maximum_fusion
  57.2 0.1 fusion.4
  57.3 1.0 %collective-permute-start.14 = (bf16[48,1024]{1,0:T(8,128)(2,1)S(1)}, bf16[48,1024]{1,0:T(8,128)(2,1)S(1)}, u32[]{:S(2)}, u32[]{:S(2)}) collective-permute-start(bf16[48,1024]{1,0:T(8,128)(2,1)S(1)} %get-tuple-element.57), channel_id=1, source_target_pairs={{0,128},{16,144},{128,0},{144,16},{1,129},{17,145},{129,1},{145,17... | collective-permute-start | bytes 294920 | tf_op jit(solution)/shard_map/gather_y/ppermute | solution.py:10
  58.3 1.5 %collective-permute-start.15 = (bf16[48,1024]{1,0:T(8,128)(2,1)S(1)}, bf16[48,1024]{1,0:T(8,128)(2,1)S(1)}, u32[]{:S(2)}, u32[]{:S(2)}) collective-permute-start(bf16[48,1024]{1,0:T(8,128)(2,1)S(1)} %get-tuple-element.57), channel_id=1, source_target_pairs={{0,16},{16,128},{128,144},{144,0},{1,17},{17,129},{129,145},{145,1... | collective-permute-start | bytes 294920 | tf_op jit(solution)/shard_map/gather_y/ppermute | solution.py:10
  59.8 1.2 %collective-permute-start.16 = (bf16[48,1024]{1,0:T(8,128)(2,1)S(1)}, bf16[48,1024]{1,0:T(8,128)(2,1)S(1)}, u32[]{:S(2)}, u32[]{:S(2)}) collective-permute-start(bf16[48,1024]{1,0:T(8,128)(2,1)S(1)} %get-tuple-element.57), channel_id=1, source_target_pairs={{0,144},{16,0},{128,16},{144,128},{1,145},{17,1},{129,17},{145,129... | collective-permute-start | bytes 294920 | tf_op jit(solution)/shard_map/gather_y/ppermute | solution.py:10
  60.9 0.5 fusion.5
  61.4 1.2 %convolution_add_fusion.1 = f32[48,1024]{1,0:T(8,128)} fusion(bf16[48,1024]{1,0:T(8,128)(2,1)S(1)} %get-tuple-element.57, bf16[1024,1024]{1,0:T(8,128)(2,1)S(1)} %get-tuple-element.44, f32[96,1024]{1,0:T(8,128)S(1)} %fusion.5), kind=kOutput, calls=%fused_computation.14 | convolution fusion | flops 100761600 | bytes 2785280 | tf_op jit(solution)/shard_map/screen/dot_general | solution.py:116
  62.6 1.5 %collective-permute-done.15 = bf16[48,1024]{1,0:T(8,128)(2,1)S(1)} collective-permute-done((bf16[48,1024]{1,0:T(8,128)(2,1)S(1)}, bf16[48,1024]{1,0:T(8,128)(2,1)S(1)}, u32[]{:S(2)}, u32[]{:S(2)}) %collective-permute-start.15) | collective-permute-done | bytes 98336 | tf_op jit(solution)/shard_map/gather_y/ppermute | solution.py:10
  64.2 2.9 %collective-permute-start.17 = (bf16[192,1024]{1,0:T(8,128)(2,1)S(1)}, bf16[192,1024]{1,0:T(8,128)(2,1)S(1)}, u32[]{:S(2)}, u32[]{:S(2)}) collective-permute-start(bf16[192,1024]{1,0:T(8,128)(2,1)S(1)} %pad_maximum_fusion.1), channel_id=1, source_target_pairs={{0,8},{8,0},{1,9},{9,1},{2,10},{10,2},{3,11},{11,3},{4,12},{12,4},... | collective-permute-start | bytes 1179656 | tf_op jit(solution)/shard_map/sigma/ppermute | solution.py:18
  67.1 0.9 %fusion.2 = f32[1024]{0:T(1024)S(1)} fusion(bf16[192,1024]{1,0:T(8,128)(2,1)S(1)} %pad_maximum_fusion.1, bf16[1024,1024]{0,1:T(8,128)(2,1)S(1)} %pad_maximum_fusion, bf16[192,512]{1,0:T(8,128)(2,1)S(1)} %bitcast.78), kind=kOutput, calls=%fused_computation.12 | convolution fusion | flops 403831808 | bytes 2691072 | tf_op jit(solution)/shard_map/sigma/dot_general | solution.py:137
  68.0 0.4 collective-permute-done.17
  68.4 0.9 fusion.3
  69.4 15.3 %all_to_all.9 = f32[32,1,128]{2,1,0:T(1,128)S(1)} all-to-all(f32[32,1,128]{2,1,0:T(1,128)S(1)} %bitcast.79), channel_id=1, replica_groups=mesh['grp'=2,'x'=4,'ylo'=2,'core'=2,'col'=8] {'x','col'}, dimensions={0} | all-to-all | bytes 32768 | tf_op jit(solution)/shard_map/sigma/all_to_all | solution.py:149
  84.6 0.6 reduce_sum.39
  (42 shorter events, 0.7 us)
Async XLA Ops:
  0.6 19.3 %copy-start = (bf16[128,1536]{1,0:T(8,128)(2,1)S(1)}, bf16[128,1536]{1,0:T(8,128)(2,1)}, u32[]{:S(2)}) copy-start(bf16[128,1536]{1,0:T(8,128)(2,1)} %param.3) | copy-start | bytes 1179652
  1.7 12.0 %collective-permute-start = (bf16[128,1024]{1,0:T(8,128)(2,1)S(1)}, bf16[128,1024]{1,0:T(8,128)(2,1)S(1)}, u32[]{:S(2)}, u32[]{:S(2)}) collective-permute-start(bf16[128,1024]{1,0:T(8,128)(2,1)S(1)} %slice.42), channel_id=1, source_target_pairs={{0,3},{8,11},{16,19},{24,27},{32,35},{40,43},{48,51},{56,59},{64,6... | collective-permute-start | bytes 786440 | tf_op jit(solution)/shard_map/panel_z/ppermute | solution.py:14
  8.8 7.3 %collective-permute-start.1 = (bf16[128,1024]{1,0:T(8,128)(2,1)S(1)}, bf16[128,1024]{1,0:T(8,128)(2,1)S(1)}, u32[]{:S(2)}, u32[]{:S(2)}) collective-permute-start(bf16[128,1024]{1,0:T(8,128)(2,1)S(1)} %slice.42), channel_id=1, source_target_pairs={{0,6},{8,14},{16,22},{24,30},{32,38},{40,46},{48,54},{56,62},{64,7... | collective-permute-start | bytes 786440 | tf_op jit(solution)/shard_map/panel_z/ppermute | solution.py:14
  17.1 11.9 %collective-permute-start.2 = (bf16[128,1024]{1,0:T(8,128)(2,1)S(1)}, bf16[128,1024]{1,0:T(8,128)(2,1)S(1)}, u32[]{:S(2)}, u32[]{:S(2)}) collective-permute-start(bf16[128,1024]{1,0:T(8,128)(2,1)S(1)} %select_select_fusion.1), channel_id=1, source_target_pairs={{0,7},{3,4},{6,5},{8,15},{11,12},{14,13},{16,23},{19,20},{22,21},{... | collective-permute-start | bytes 786440 | tf_op jit(solution)/shard_map/panel_z/ppermute | solution.py:14
  18.4 10.5 %collective-permute-start.3 = (bf16[128,1024]{1,0:T(8,128)(2,1)S(1)}, bf16[128,1024]{1,0:T(8,128)(2,1)S(1)}, u32[]{:S(2)}, u32[]{:S(2)}) collective-permute-start(bf16[128,1024]{1,0:T(8,128)(2,1)S(1)} %select_select_fusion.1), channel_id=1, source_target_pairs={{0,1},{3,2},{8,9},{11,10},{16,17},{19,18},{24,25},{27,26},{32,33},... | collective-permute-start | bytes 786440 | tf_op jit(solution)/shard_map/panel_z/ppermute | solution.py:14
  20.4 6.2 %collective-permute-start.4 = (bf16[400,128]{1,0:T(8,128)(2,1)S(1)}, bf16[400,128]{1,0:T(8,128)(2,1)S(1)}, u32[]{:S(2)}, u32[]{:S(2)}) collective-permute-start(bf16[400,128]{1,0:T(8,128)(2,1)S(1)} %concatenate.48), channel_id=1, source_target_pairs={{0,64},{32,96},{64,0},{96,32},{1,65},{33,97},{65,1},{97,33},{2,66}... | collective-permute-start | bytes 307208 | tf_op jit(solution)/shard_map/blocks/ppermute | solution.py:10
  23.4 5.5 %collective-permute-start.5 = (bf16[400,128]{1,0:T(8,128)(2,1)S(1)}, bf16[400,128]{1,0:T(8,128)(2,1)S(1)}, u32[]{:S(2)}, u32[]{:S(2)}) collective-permute-start(bf16[400,128]{1,0:T(8,128)(2,1)S(1)} %concatenate.49), channel_id=1, source_target_pairs={{0,32},{32,64},{64,96},{96,0},{1,33},{33,65},{65,97},{97,1},{2,34}... | collective-permute-start | bytes 307208 | tf_op jit(solution)/shard_map/blocks/ppermute | solution.py:10
  24.0 5.0 %collective-permute-start.6 = (bf16[400,128]{1,0:T(8,128)(2,1)S(1)}, bf16[400,128]{1,0:T(8,128)(2,1)S(1)}, u32[]{:S(2)}, u32[]{:S(2)}) collective-permute-start(bf16[400,128]{1,0:T(8,128)(2,1)S(1)} %concatenate.50), channel_id=1, source_target_pairs={{0,96},{32,0},{64,32},{96,64},{1,97},{33,1},{65,33},{97,65},{2,98}... | collective-permute-start | bytes 307208 | tf_op jit(solution)/shard_map/blocks/ppermute | solution.py:10
  29.5 7.9 %collective-permute-start.8 = (bf16[128,1024]{1,0:T(8,128)(2,1)S(1)}, bf16[128,1024]{1,0:T(8,128)(2,1)S(1)}, u32[]{:S(2)}, u32[]{:S(2)}) collective-permute-start(bf16[128,1024]{1,0:T(8,128)(2,1)S(1)} %select_select_fusion), channel_id=1, source_target_pairs={{0,32},{32,64},{64,96},{96,0},{1,33},{33,65},{65,97},{97,1},{2,34}... | collective-permute-start | bytes 786440 | tf_op jit(solution)/shard_map/panel_x/ppermute | solution.py:10
  29.5 12.8 %collective-permute-start.7 = (bf16[128,1024]{1,0:T(8,128)(2,1)S(1)}, bf16[128,1024]{1,0:T(8,128)(2,1)S(1)}, u32[]{:S(2)}, u32[]{:S(2)}) collective-permute-start(bf16[128,1024]{1,0:T(8,128)(2,1)S(1)} %select_select_fusion), channel_id=1, source_target_pairs={{0,64},{32,96},{64,0},{96,32},{1,65},{33,97},{65,1},{97,33},{2,66}... | collective-permute-start | bytes 786440 | tf_op jit(solution)/shard_map/panel_x/ppermute | solution.py:10
  33.4 9.8 %collective-permute-start.9 = (bf16[128,1024]{1,0:T(8,128)(2,1)S(1)}, bf16[128,1024]{1,0:T(8,128)(2,1)S(1)}, u32[]{:S(2)}, u32[]{:S(2)}) collective-permute-start(bf16[128,1024]{1,0:T(8,128)(2,1)S(1)} %select_select_fusion), channel_id=1, source_target_pairs={{0,96},{32,0},{64,32},{96,64},{1,97},{33,1},{65,33},{97,65},{2,98}... | collective-permute-start | bytes 786440 | tf_op jit(solution)/shard_map/panel_x/ppermute | solution.py:10
  43.8 4.5 %collective-permute-start.10 = (bf16[192,1024]{1,0:T(8,128)(2,1)S(1)}, bf16[192,1024]{1,0:T(8,128)(2,1)S(1)}, u32[]{:S(2)}, u32[]{:S(2)}) collective-permute-start(bf16[192,1024]{1,0:T(8,128)(2,1)S(1)} %convolution_convert_fusion), channel_id=1, source_target_pairs={{0,8},{8,0},{1,9},{9,1},{2,10},{10,2},{3,11},{11,3},{4,12},{12,4},... | collective-permute-start | bytes 1179656 | tf_op jit(solution)/shard_map/response/ppermute | solution.py:18
  48.5 8.6 %collective-permute-start.11 = (bf16[48,1024]{1,0:T(8,128)(2,1)S(1)}, bf16[48,1024]{1,0:T(8,128)(2,1)S(1)}, u32[]{:S(2)}, u32[]{:S(2)}) collective-permute-start(bf16[48,1024]{1,0:T(8,128)(2,1)S(1)} %get-tuple-element.58), channel_id=1, source_target_pairs={{0,128},{16,144},{128,0},{144,16},{1,129},{17,145},{129,1},{145,17... | collective-permute-start | bytes 294920 | tf_op jit(solution)/shard_map/sum_y/ppermute | solution.py:10
  51.5 5.6 %collective-permute-start.12 = (bf16[48,1024]{1,0:T(8,128)(2,1)S(1)}, bf16[48,1024]{1,0:T(8,128)(2,1)S(1)}, u32[]{:S(2)}, u32[]{:S(2)}) collective-permute-start(bf16[48,1024]{1,0:T(8,128)(2,1)S(1)} %get-tuple-element.60), channel_id=1, source_target_pairs={{0,16},{16,128},{128,144},{144,0},{1,17},{17,129},{129,145},{145,1... | collective-permute-start | bytes 294920 | tf_op jit(solution)/shard_map/sum_y/ppermute | solution.py:10
  51.9 5.2 %collective-permute-start.13 = (bf16[48,1024]{1,0:T(8,128)(2,1)S(1)}, bf16[48,1024]{1,0:T(8,128)(2,1)S(1)}, u32[]{:S(2)}, u32[]{:S(2)}) collective-permute-start(bf16[48,1024]{1,0:T(8,128)(2,1)S(1)} %get-tuple-element.59), channel_id=1, source_target_pairs={{0,144},{16,0},{128,16},{144,128},{1,145},{17,1},{129,17},{145,129... | collective-permute-start | bytes 294920 | tf_op jit(solution)/shard_map/sum_y/ppermute | solution.py:10
  57.3 5.3 %collective-permute-start.14 = (bf16[48,1024]{1,0:T(8,128)(2,1)S(1)}, bf16[48,1024]{1,0:T(8,128)(2,1)S(1)}, u32[]{:S(2)}, u32[]{:S(2)}) collective-permute-start(bf16[48,1024]{1,0:T(8,128)(2,1)S(1)} %get-tuple-element.57), channel_id=1, source_target_pairs={{0,128},{16,144},{128,0},{144,16},{1,129},{17,145},{129,1},{145,17... | collective-permute-start | bytes 294920 | tf_op jit(solution)/shard_map/gather_y/ppermute | solution.py:10
  58.3 5.9 %collective-permute-start.15 = (bf16[48,1024]{1,0:T(8,128)(2,1)S(1)}, bf16[48,1024]{1,0:T(8,128)(2,1)S(1)}, u32[]{:S(2)}, u32[]{:S(2)}) collective-permute-start(bf16[48,1024]{1,0:T(8,128)(2,1)S(1)} %get-tuple-element.57), channel_id=1, source_target_pairs={{0,16},{16,128},{128,144},{144,0},{1,17},{17,129},{129,145},{145,1... | collective-permute-start | bytes 294920 | tf_op jit(solution)/shard_map/gather_y/ppermute | solution.py:10
  59.8 4.3 %collective-permute-start.16 = (bf16[48,1024]{1,0:T(8,128)(2,1)S(1)}, bf16[48,1024]{1,0:T(8,128)(2,1)S(1)}, u32[]{:S(2)}, u32[]{:S(2)}) collective-permute-start(bf16[48,1024]{1,0:T(8,128)(2,1)S(1)} %get-tuple-element.57), channel_id=1, source_target_pairs={{0,144},{16,0},{128,16},{144,128},{1,145},{17,1},{129,17},{145,129... | collective-permute-start | bytes 294920 | tf_op jit(solution)/shard_map/gather_y/ppermute | solution.py:10
  64.2 4.2 %collective-permute-start.17 = (bf16[192,1024]{1,0:T(8,128)(2,1)S(1)}, bf16[192,1024]{1,0:T(8,128)(2,1)S(1)}, u32[]{:S(2)}, u32[]{:S(2)}) collective-permute-start(bf16[192,1024]{1,0:T(8,128)(2,1)S(1)} %pad_maximum_fusion.1), channel_id=1, source_target_pairs={{0,8},{8,0},{1,9},{9,1},{2,10},{10,2},{3,11},{11,3},{4,12},{12,4},... | collective-permute-start | bytes 1179656 | tf_op jit(solution)/shard_map/sigma/ppermute | solution.py:18
